TPU v7x, 32 devices: a whole 2x2x4 slice. The times are simulated.
32 devices in a mesh: seq: 16 (over z, x, core), dp: 2 (over y).
Axes of the slice: x: 2, y: 2, z: 4, core: 2. Of those that a mesh axis runs over, the one named last changes fastest.
Arguments:
- features: bfloat16 [2, 4096, 2048], P('dp', 'seq'), may hold values from -6 to 6
- queries: bfloat16 [2, 4096, 1024], P('dp', 'seq'), may hold values from -136 to 136
- kv_weight: bfloat16 [2048, 2048], P('dp'), may hold values from -0.125 to 0.125
- upstream: bfloat16 [2, 4096, 1024], P('dp', 'seq'), may hold values from -6 to 6
Outputs:
- attended: bfloat16 [2, 4096, 1024], P('dp', 'seq')
- query_grad: bfloat16 [2, 4096, 1024], P('dp', 'seq')
- feature_grad: bfloat16 [2, 4096, 2048], P('dp', 'seq')
- weight_grad: float32 [2048, 2048], P(('dp', 'seq'))
All inputs are finite; a program needn't handle non-finite values.
Results may differ from a plain program's by a relative error of at most 0.013.
The roundings to bfloat16 on the way count: a program that leaves them out, or rounds other values in their place, can miss the bound.
Values may be sent and summed in bfloat16 or wider, within the bound.
No kernel may reach another device: no remote copies, remote signals or barrier semaphores. Data moves between devices by JAX's collectives and lax.ppermute only.
A program may use at most 128 MiB of HBM per device.

v0:
```python
import math

import jax
import jax.numpy as jnp
from jax import lax
from jax.sharding import PartitionSpec as P

HEAD_DIM = 128
WINDOW = 2048


def passed_along(value, axis, steps):
    count = lax.axis_size(axis)
    leading, last = (max(0, -steps), min(count, count - steps))
    return lax.ppermute(value, axis, [(source, source + steps) for source in range(leading, last)])


def local(features, queries, kv_weight, upstream):
    tokens = features[0]
    query_rows = queries[0]
    upstream_rows = upstream[0]
    tok_count = tokens.shape[0]
    head_width = query_rows.shape[1]
    head_count = head_width // HEAD_DIM
    span = WINDOW // tok_count
    key_count = (span + 1) * tok_count
    score_scale = 1.0 / math.sqrt(HEAD_DIM)
    transpose_dims = (((1,), (1,)), ((), ()))
    token_dims = (((0,), (0,)), ((), ()))
    full_weight = lax.all_gather(kv_weight, "dp", axis=0, tiled=True)
    own_kv = jnp.dot(tokens, full_weight, preferred_element_type=jnp.float32).astype(jnp.bfloat16)
    earlier = []
    travelling = own_kv
    for distance in range(span):
        travelling = passed_along(travelling, "seq", 1)
        earlier.append(travelling)
    window_kv = jnp.concatenate(earlier[::-1] + [own_kv], axis=0)
    key_major = (
        window_kv[:, :head_width].reshape(key_count, head_count, HEAD_DIM).transpose(1, 0, 2)
    )
    value_major = (
        window_kv[:, head_width:].reshape(key_count, head_count, HEAD_DIM).transpose(1, 0, 2)
    )
    query_major = query_rows.reshape(tok_count, head_count, HEAD_DIM).transpose(1, 0, 2)
    grad_major = upstream_rows.reshape(tok_count, head_count, HEAD_DIM).transpose(1, 0, 2)
    first_pos = lax.axis_index("seq") * tok_count
    query_pos = lax.broadcasted_iota(jnp.int32, (tok_count, key_count), 0)
    key_pos = lax.broadcasted_iota(jnp.int32, (tok_count, key_count), 1) - span * tok_count
    allowed = (key_pos <= query_pos) & (key_pos > query_pos - WINDOW) & (first_pos + key_pos >= 0)

    def head_work(item):
        query_head, grad_head, key_head, value_head = item
        scores = (
            lax.dot_general(
                query_head, key_head, transpose_dims, preferred_element_type=jnp.float32
            )
            * score_scale
        )
        scores = jnp.where(allowed, scores, -1e30)
        row_max = jnp.max(scores, axis=-1, keepdims=True)
        exp_scores = jnp.exp(scores - row_max)
        probability = exp_scores / jnp.sum(exp_scores, axis=-1, keepdims=True)
        weights = probability.astype(jnp.bfloat16)
        attended_head = jnp.dot(weights, value_head, preferred_element_type=jnp.float32).astype(
            jnp.bfloat16
        )
        dprob = lax.dot_general(
            grad_head, value_head, transpose_dims, preferred_element_type=jnp.float32
        )
        centred = dprob - jnp.sum(probability * dprob, axis=-1, keepdims=True)
        dscore = (probability * centred * score_scale).astype(jnp.bfloat16)
        query_grad_head = jnp.dot(dscore, key_head, preferred_element_type=jnp.float32).astype(
            jnp.bfloat16
        )
        key_grad_head = lax.dot_general(
            dscore, query_head, token_dims, preferred_element_type=jnp.float32
        )
        value_grad_head = lax.dot_general(
            weights, grad_head, token_dims, preferred_element_type=jnp.float32
        )
        return (attended_head, query_grad_head, key_grad_head, value_grad_head)

    attended_all, query_grad_all, key_grad_all, value_grad_all = lax.map(
        head_work, (query_major, grad_major, key_major, value_major)
    )
    attended = attended_all.transpose(1, 0, 2).reshape(tok_count, head_width)
    query_grad = query_grad_all.transpose(1, 0, 2).reshape(tok_count, head_width)
    key_grad = key_grad_all.transpose(1, 0, 2).reshape(key_count, head_width)
    value_grad = value_grad_all.transpose(1, 0, 2).reshape(key_count, head_width)
    kv_grad_all = jnp.concatenate([key_grad, value_grad], axis=1)
    total = kv_grad_all[span * tok_count :]
    for distance in range(1, span + 1):
        portion = kv_grad_all[
            (span - distance) * tok_count : (span - distance + 1) * tok_count
        ].astype(jnp.bfloat16)
        arrived = passed_along(portion, "seq", -distance)
        total = total + arrived.astype(jnp.float32)
    kv_grad = total.astype(jnp.bfloat16)
    feature_sum = lax.dot_general(
        kv_grad, full_weight, transpose_dims, preferred_element_type=jnp.float32
    )
    feature_grad = feature_sum.astype(jnp.bfloat16)
    paired_cols = lax.all_to_all(tokens, "dp", split_axis=1, concat_axis=0, tiled=True)
    paired_grads = lax.all_gather(kv_grad, "dp", axis=0, tiled=True)
    weight_grad = lax.psum_scatter(
        lax.dot_general(paired_cols, paired_grads, token_dims, preferred_element_type=jnp.float32),
        "seq",
        scatter_dimension=0,
        tiled=True,
    )
    return (attended[None], query_grad[None], feature_grad[None], weight_grad)


def solution(mesh):
    return jax.shard_map(
        local,
        mesh=mesh,
        in_specs=(P("dp", "seq", None), P("dp", "seq", None), P("dp", None), P("dp", "seq", None)),
        out_specs=(
            P("dp", "seq", None),
            P("dp", "seq", None),
            P("dp", "seq", None),
            P(("dp", "seq"), None),
        ),
        check_vma=False,
    )
```

profile of v0, /device:TPU:0, one launch (start us, length us, event | category | flops | bytes accessed | tf_op | source)
XLA Modules:
  0.0 824.6 jit_solution(16882314783052995520)
XLA Ops:
  8.0 108.3 %all-gather.3.cloned.1.call-done = bf16[2048,2048]{1,0:T(8,128)(2,1)} async-done(((bf16[1024,2048]{1,0:T(8,128)(2,1)}), bf16[2048,2048]{1,0:T(8,128)(2,1)}) %all-gather.3.cloned.1.call-update) | async-done | bytes 8388624 | tf_op jit(solution)/shard_map/all_gather | solution.py:30
  116.3 5.7 convolution_convert_fusion.3
  126.0 13.2 %collective-permute-start.1 = (bf16[256,2048]{1,0:T(8,128)(2,1)S(1)}, bf16[256,2048]{1,0:T(8,128)(2,1)S(1)}, u32[]{:S(2)}, u32[]{:S(2)}) collective-permute-start(bf16[256,2048]{1,0:T(8,128)(2,1)S(1)} %collective-permute-done), channel_id=1, source_target_pairs={{0,2},{2,4},{4,6},{6,8},{8,10},{10,12},{12,14},{14,16},{16,18},{18... | collective-permute-start | bytes 3145736 | tf_op jit(solution)/shard_map/ppermute | solution.py:15
  141.4 13.9 %collective-permute-start.2 = (bf16[256,2048]{1,0:T(8,128)(2,1)S(1)}, bf16[256,2048]{1,0:T(8,128)(2,1)S(1)}, u32[]{:S(2)}, u32[]{:S(2)}) collective-permute-start(bf16[256,2048]{1,0:T(8,128)(2,1)S(1)} %collective-permute-done.1), channel_id=1, source_target_pairs={{0,2},{2,4},{4,6},{6,8},{8,10},{10,12},{12,14},{14,16},{16,18},{18... | collective-permute-start | bytes 3145736 | tf_op jit(solution)/shard_map/ppermute | solution.py:15
  158.5 13.9 %collective-permute-start.3 = (bf16[256,2048]{1,0:T(8,128)(2,1)S(1)}, bf16[256,2048]{1,0:T(8,128)(2,1)S(1)}, u32[]{:S(2)}, u32[]{:S(2)}) collective-permute-start(bf16[256,2048]{1,0:T(8,128)(2,1)S(1)} %collective-permute-done.2), channel_id=1, source_target_pairs={{0,2},{2,4},{4,6},{6,8},{8,10},{10,12},{12,14},{14,16},{16,18},{18... | collective-permute-start | bytes 3145736 | tf_op jit(solution)/shard_map/ppermute | solution.py:15
  175.6 13.9 %collective-permute-start.4 = (bf16[256,2048]{1,0:T(8,128)(2,1)S(1)}, bf16[256,2048]{1,0:T(8,128)(2,1)S(1)}, u32[]{:S(2)}, u32[]{:S(2)}) collective-permute-start(bf16[256,2048]{1,0:T(8,128)(2,1)S(1)} %collective-permute-done.3), channel_id=1, source_target_pairs={{0,2},{2,4},{4,6},{6,8},{8,10},{10,12},{12,14},{14,16},{16,18},{18... | collective-permute-start | bytes 3145736 | tf_op jit(solution)/shard_map/ppermute | solution.py:15
  192.7 13.9 %collective-permute-start.5 = (bf16[256,2048]{1,0:T(8,128)(2,1)S(1)}, bf16[256,2048]{1,0:T(8,128)(2,1)S(1)}, u32[]{:S(2)}, u32[]{:S(2)}) collective-permute-start(bf16[256,2048]{1,0:T(8,128)(2,1)S(1)} %collective-permute-done.4), channel_id=1, source_target_pairs={{0,2},{2,4},{4,6},{6,8},{8,10},{10,12},{12,14},{14,16},{16,18},{18... | collective-permute-start | bytes 3145736 | tf_op jit(solution)/shard_map/ppermute | solution.py:15
  209.8 14.8 %collective-permute-start.6 = (bf16[256,2048]{1,0:T(8,128)(2,1)S(1)}, bf16[256,2048]{1,0:T(8,128)(2,1)}, u32[]{:S(2)}, u32[]{:S(2)}) collective-permute-start(bf16[256,2048]{1,0:T(8,128)(2,1)S(1)} %collective-permute-done.5), channel_id=1, source_target_pairs={{0,2},{2,4},{4,6},{6,8},{8,10},{10,12},{12,14},{14,16},{16,18},{18... | collective-permute-start | bytes 3145736 | tf_op jit(solution)/shard_map/ppermute | solution.py:15
  226.0 14.7 %collective-permute-start.7 = (bf16[256,2048]{1,0:T(8,128)(2,1)}, bf16[256,2048]{1,0:T(8,128)(2,1)}, u32[]{:S(2)}, u32[]{:S(2)}) collective-permute-start(bf16[256,2048]{1,0:T(8,128)(2,1)} %collective-permute-done.6), channel_id=1, source_target_pairs={{0,2},{2,4},{4,6},{6,8},{8,10},{10,12},{12,14},{14,16},{16,18},{18... | collective-permute-start | bytes 3145736 | tf_op jit(solution)/shard_map/ppermute | solution.py:15
  244.8 2.4 constant_dynamic-update-slice_fusion.8
  247.3 2.4 constant_dynamic-update-slice_fusion.7
  257.1 6.1 slice_bitcast_fusion
  263.2 6.0 bitcast_bitcast_fusion
  269.2 116.3 %while.17 = (s32[]{:T(128)}, bf16[8,256,128]{2,1,0:T(8,128)(2,1)}, bf16[8,256,128]{2,1,0:T(8,128)(2,1)}, f32[8,2304,128]{1,2,0:T(8,128)}, f32[8,2304,128]{1,2,0:...) while((s32[]{:T(128)}, bf16[8,256,128]{2,1,0:T(8,128)(2,1)}, ...), condition=%wide.region_4.5_spmd.clone, body=%wide.region_0.4_spmd.clone.sunk | while | flops 920780032 | bytes 27557244 | solution.py:83
  271.8 2.5 fusion.89
  277.0 2.2 fusion.88
  281.4 2.3 fusion.86
  286.3 2.5 fusion.89
  295.9 2.3 fusion.86
  300.9 2.6 fusion.89
  306.1 2.2 fusion.88
  310.5 2.3 fusion.86
  315.4 2.5 fusion.89
  325.0 2.3 fusion.86
  329.9 2.5 fusion.89
  335.1 2.2 fusion.88
  339.5 2.3 fusion.86
  344.5 2.5 fusion.89
  354.0 2.3 fusion.86
  359.0 2.5 fusion.89
  364.2 2.3 fusion.88
  368.7 2.3 fusion.86
  373.6 2.5 fusion.89
  383.2 2.3 fusion.86
  385.5 9.1 %fusion.40 = bf16[2304,2048]{0,1:T(8,128)(2,1)S(1)} fusion(f32[2304,1024]{0,1:T(8,128)} %bitcast.126, f32[2304,1024]{0,1:T(8,128)} %bitcast.122), kind=kLoop, calls=%fused_computation.49 | loop fusion | flops 18874368 | bytes 28311552 | tf_op jit(solution)/shard_map/convert.7
  394.7 2.2 fusion.54
  403.6 24.7 %collective-permute-done.10 = bf16[256,2048]{0,1:T(8,128)(2,1)S(1)} collective-permute-done((bf16[256,2048]{0,1:T(8,128)(2,1)S(1)}, bf16[256,2048]{0,1:T(8,128)(2,1)S(1)}, u32[]{:S(2)}, u32[]{:S(2)}) %collective-permute-start.10) | collective-permute-done | bytes 1048608 | tf_op jit(solution)/shard_map/ppermute | solution.py:15
  429.6 35.0 %collective-permute-done.11 = bf16[256,2048]{0,1:T(8,128)(2,1)S(1)} collective-permute-done((bf16[256,2048]{0,1:T(8,128)(2,1)S(1)}, bf16[256,2048]{0,1:T(8,128)(2,1)S(1)}, u32[]{:S(2)}, u32[]{:S(2)}) %collective-permute-start.11) | collective-permute-done | bytes 1048608 | tf_op jit(solution)/shard_map/ppermute | solution.py:15
  465.9 6.4 collective-permute-done.12
  473.7 31.4 %collective-permute-done.13 = bf16[256,2048]{0,1:T(8,128)(2,1)S(1)} collective-permute-done((bf16[256,2048]{0,1:T(8,128)(2,1)}, bf16[256,2048]{0,1:T(8,128)(2,1)S(1)}, u32[]{:S(2)}, u32[]{:S(2)}) %collective-permute-start.13) | collective-permute-done | bytes 1048608 | tf_op jit(solution)/shard_map/ppermute | solution.py:15
  505.2 4.9 collective-permute-done.14
  510.0 124.0 %collective-permute-done.15 = bf16[256,2048]{0,1:T(8,128)(2,1)S(1)} collective-permute-done((bf16[256,2048]{0,1:T(8,128)(2,1)}, bf16[256,2048]{0,1:T(8,128)(2,1)S(1)}, u32[]{:S(2)}, u32[]{:S(2)}) %collective-permute-start.15) | collective-permute-done | bytes 1048608 | tf_op jit(solution)/shard_map/ppermute | solution.py:15
  637.8 11.8 %all_to_all.19 = bf16[256,2,1024]{0,2,1:T(8,128)(2,1)S(1)} all-to-all(bf16[256,2,1024]{0,2,1:T(8,128)(2,1)S(1)} %bitcast.131), channel_id=1, replica_groups=mesh['seq'=16,'dp'=2] {'dp'}, dimensions={1} | all-to-all | bytes 2097152 | tf_op jit(solution)/shard_map/all_to_all | solution.py:103
  650.2 43.8 %all-gather.5.cloned.1.call-done = bf16[512,2048]{0,1:T(8,128)(2,1)} async-done(((bf16[256,2048]{0,1:T(8,128)(2,1)}), bf16[512,2048]{0,1:T(8,128)(2,1)}) %all-gather.5.cloned.1.call-update) | async-done | bytes 2097168 | tf_op jit(solution)/shard_map/all_gather | solution.py:104
  694.0 7.2 convolution_bitcast_fusion.2
  701.2 9.2 %copy.50 = f32[1024,2048]{1,0:T(8,128)} copy(f32[1024,2048]{0,1:T(8,128)} %convolution_bitcast_fusion.2) | data formatting | bytes 16777216
  714.2 6.7 fusion.41
  720.9 97.2 %reduce-scatter.4.cloned.1.call-done = f32[64,2048]{1,0:T(8,128)} async-done(((f32[1024,2048]{1,0:T(8,128)}), f32[64,2048]{1,0:T(8,128)}) %reduce-scatter.4.cloned.1.call-update) | async-done | bytes 524304
  (130 shorter events, 120.0 us)
Async XLA Ops:
  7.2 109.1 %copy-start.1 = (bf16[1,256,2048]{2,1,0:T(8,128)(2,1)S(1)}, bf16[1,256,2048]{2,1,0:T(8,128)(2,1)}, u32[]{:S(2)}) copy-start(bf16[1,256,2048]{2,1,0:T(8,128)(2,1)} %param.6) | copy-start | bytes 3145732
  7.2 109.1 %all-gather.3.cloned.1.call-start = ((), (), s32[]{:S(2)}) async-start(), calls=%async_computation.2 | async-start | bytes 12582912 | tf_op jit(solution)/shard_map/all_gather | solution.py:30
  7.9 686.1 %all-gather.5.cloned.1.call-start = ((), (), s32[]{:S(2)}) async-start(), calls=%async_computation.3 | async-start | bytes 3145728 | tf_op jit(solution)/shard_map/all_gather | solution.py:104
  122.0 4.0 collective-permute-start
  126.0 15.4 %collective-permute-start.1 = (bf16[256,2048]{1,0:T(8,128)(2,1)S(1)}, bf16[256,2048]{1,0:T(8,128)(2,1)S(1)}, u32[]{:S(2)}, u32[]{:S(2)}) collective-permute-start(bf16[256,2048]{1,0:T(8,128)(2,1)S(1)} %collective-permute-done), channel_id=1, source_target_pairs={{0,2},{2,4},{4,6},{6,8},{8,10},{10,12},{12,14},{14,16},{16,18},{18... | collective-permute-start | bytes 3145736 | tf_op jit(solution)/shard_map/ppermute | solution.py:15
  141.4 16.1 %collective-permute-start.2 = (bf16[256,2048]{1,0:T(8,128)(2,1)S(1)}, bf16[256,2048]{1,0:T(8,128)(2,1)S(1)}, u32[]{:S(2)}, u32[]{:S(2)}) collective-permute-start(bf16[256,2048]{1,0:T(8,128)(2,1)S(1)} %collective-permute-done.1), channel_id=1, source_target_pairs={{0,2},{2,4},{4,6},{6,8},{8,10},{10,12},{12,14},{14,16},{16,18},{18... | collective-permute-start | bytes 3145736 | tf_op jit(solution)/shard_map/ppermute | solution.py:15
  157.5 1.0 copy-start.2
  158.5 16.1 %collective-permute-start.3 = (bf16[256,2048]{1,0:T(8,128)(2,1)S(1)}, bf16[256,2048]{1,0:T(8,128)(2,1)S(1)}, u32[]{:S(2)}, u32[]{:S(2)}) collective-permute-start(bf16[256,2048]{1,0:T(8,128)(2,1)S(1)} %collective-permute-done.2), channel_id=1, source_target_pairs={{0,2},{2,4},{4,6},{6,8},{8,10},{10,12},{12,14},{14,16},{16,18},{18... | collective-permute-start | bytes 3145736 | tf_op jit(solution)/shard_map/ppermute | solution.py:15
  174.6 1.0 copy-start.4
  175.6 16.1 %collective-permute-start.4 = (bf16[256,2048]{1,0:T(8,128)(2,1)S(1)}, bf16[256,2048]{1,0:T(8,128)(2,1)S(1)}, u32[]{:S(2)}, u32[]{:S(2)}) collective-permute-start(bf16[256,2048]{1,0:T(8,128)(2,1)S(1)} %collective-permute-done.3), channel_id=1, source_target_pairs={{0,2},{2,4},{4,6},{6,8},{8,10},{10,12},{12,14},{14,16},{16,18},{18... | collective-permute-start | bytes 3145736 | tf_op jit(solution)/shard_map/ppermute | solution.py:15
  191.7 1.0 copy-start.6
  192.7 16.1 %collective-permute-start.5 = (bf16[256,2048]{1,0:T(8,128)(2,1)S(1)}, bf16[256,2048]{1,0:T(8,128)(2,1)S(1)}, u32[]{:S(2)}, u32[]{:S(2)}) collective-permute-start(bf16[256,2048]{1,0:T(8,128)(2,1)S(1)} %collective-permute-done.4), channel_id=1, source_target_pairs={{0,2},{2,4},{4,6},{6,8},{8,10},{10,12},{12,14},{14,16},{16,18},{18... | collective-permute-start | bytes 3145736 | tf_op jit(solution)/shard_map/ppermute | solution.py:15
  208.8 1.0 copy-start.8
  209.8 16.2 %collective-permute-start.6 = (bf16[256,2048]{1,0:T(8,128)(2,1)S(1)}, bf16[256,2048]{1,0:T(8,128)(2,1)}, u32[]{:S(2)}, u32[]{:S(2)}) collective-permute-start(bf16[256,2048]{1,0:T(8,128)(2,1)S(1)} %collective-permute-done.5), channel_id=1, source_target_pairs={{0,2},{2,4},{4,6},{6,8},{8,10},{10,12},{12,14},{14,16},{16,18},{18... | collective-permute-start | bytes 3145736 | tf_op jit(solution)/shard_map/ppermute | solution.py:15
  226.0 18.8 %collective-permute-start.7 = (bf16[256,2048]{1,0:T(8,128)(2,1)}, bf16[256,2048]{1,0:T(8,128)(2,1)}, u32[]{:S(2)}, u32[]{:S(2)}) collective-permute-start(bf16[256,2048]{1,0:T(8,128)(2,1)} %collective-permute-done.6), channel_id=1, source_target_pairs={{0,2},{2,4},{4,6},{6,8},{8,10},{10,12},{12,14},{14,16},{16,18},{18... | collective-permute-start | bytes 3145736 | tf_op jit(solution)/shard_map/ppermute | solution.py:15
  244.8 4.9 copy-start.9
  247.3 3.5 copy-start.7
  249.7 2.1 copy-start.5
  250.8 2.1 copy-start.3
  385.5 248.6 %slice-start = ((s8[9437184]{0:T(1024)(128)(4,1)}), s8[4194304]{0:T(1024)(128)(4,1)S(1)}, s32[]{:S(2)}) async-start(s8[9437184]{0:T(1024)(128)(4,1)} %bitcast.123), calls=%async_computation.5 | async-start | bytes 8388608
  385.5 248.6 %slice-start.1 = ((s8[9437184]{0:T(1024)(128)(4,1)}), s8[4194304]{0:T(1024)(128)(4,1)S(1)}, s32[]{:S(2)}) async-start(s8[9437184]{0:T(1024)(128)(4,1)} %bitcast.123), calls=%async_computation.6 | async-start | bytes 8388608
  385.5 248.6 %slice-start.3 = ((s8[9437184]{0:T(1024)(128)(4,1)}), s8[4194304]{0:T(1024)(128)(4,1)S(1)}, s32[]{:S(2)}) async-start(s8[9437184]{0:T(1024)(128)(4,1)} %bitcast.127), calls=%async_computation.8 | async-start | bytes 8388608
  385.5 248.6 %slice-start.4 = ((s8[9437184]{0:T(1024)(128)(4,1)}), s8[4194304]{0:T(1024)(128)(4,1)S(1)}, s32[]{:S(2)}) async-start(s8[9437184]{0:T(1024)(128)(4,1)} %bitcast.127), calls=%async_computation.9 | async-start | bytes 8388608
  394.6 239.5 %slice-start.2 = ((s8[9437184]{0:T(1024)(128)(4,1)}), s8[1048576]{0:T(1024)(128)(4,1)S(1)}, s32[]{:S(2)}) async-start(s8[9437184]{0:T(1024)(128)(4,1)} %bitcast.123), calls=%async_computation.7 | async-start | bytes 2097152
  394.7 239.5 %slice-start.5 = ((s8[9437184]{0:T(1024)(128)(4,1)}), s8[1048576]{0:T(1024)(128)(4,1)S(1)}, s32[]{:S(2)}) async-start(s8[9437184]{0:T(1024)(128)(4,1)} %bitcast.127), calls=%async_computation.10 | async-start | bytes 2097152
  396.9 31.4 %collective-permute-start.10 = (bf16[256,2048]{0,1:T(8,128)(2,1)S(1)}, bf16[256,2048]{0,1:T(8,128)(2,1)S(1)}, u32[]{:S(2)}, u32[]{:S(2)}) collective-permute-start(bf16[256,2048]{0,1:T(8,128)(2,1)S(1)} %get-tuple-element.178), channel_id=1, source_target_pairs={{6,0},{8,2},{10,4},{12,6},{14,8},{16,10},{18,12},{20,14},{22,16},{... | collective-permute-start | bytes 3145736 | tf_op jit(solution)/shard_map/ppermute | solution.py:15
  398.4 66.1 %collective-permute-start.11 = (bf16[256,2048]{0,1:T(8,128)(2,1)S(1)}, bf16[256,2048]{0,1:T(8,128)(2,1)S(1)}, u32[]{:S(2)}, u32[]{:S(2)}) collective-permute-start(bf16[256,2048]{0,1:T(8,128)(2,1)S(1)} %get-tuple-element.177), channel_id=1, source_target_pairs={{8,0},{10,2},{12,4},{14,6},{16,8},{18,10},{20,12},{22,14},{24,16},... | collective-permute-start | bytes 3145736 | tf_op jit(solution)/shard_map/ppermute | solution.py:15
  399.7 72.5 %collective-permute-start.12 = (bf16[256,2048]{0,1:T(8,128)(2,1)S(1)}, bf16[256,2048]{0,1:T(8,128)(2,1)S(1)}, u32[]{:S(2)}, u32[]{:S(2)}) collective-permute-start(bf16[256,2048]{0,1:T(8,128)(2,1)S(1)} %get-tuple-element.176), channel_id=1, source_target_pairs={{10,0},{12,2},{14,4},{16,6},{18,8},{20,10},{22,12},{24,14},{26,16}... | collective-permute-start | bytes 3145736 | tf_op jit(solution)/shard_map/ppermute | solution.py:15
  401.0 104.1 %collective-permute-start.13 = (bf16[256,2048]{0,1:T(8,128)(2,1)}, bf16[256,2048]{0,1:T(8,128)(2,1)S(1)}, u32[]{:S(2)}, u32[]{:S(2)}) collective-permute-start(bf16[256,2048]{0,1:T(8,128)(2,1)} %get-tuple-element.175), channel_id=1, source_target_pairs={{12,0},{14,2},{16,4},{18,6},{20,8},{22,10},{24,12},{26,14},{28,16}... | collective-permute-start | bytes 3145736 | tf_op jit(solution)/shard_map/ppermute | solution.py:15
  402.3 107.7 %collective-permute-start.14 = (bf16[256,2048]{0,1:T(8,128)(2,1)}, bf16[256,2048]{0,1:T(8,128)(2,1)S(1)}, u32[]{:S(2)}, u32[]{:S(2)}) collective-permute-start(bf16[256,2048]{0,1:T(8,128)(2,1)} %get-tuple-element.174), channel_id=1, source_target_pairs={{14,0},{16,2},{18,4},{20,6},{22,8},{24,10},{26,12},{28,14},{30,16}... | collective-permute-start | bytes 3145736 | tf_op jit(solution)/shard_map/ppermute | solution.py:15
  428.3 205.8 %collective-permute-start.15 = (bf16[256,2048]{0,1:T(8,128)(2,1)}, bf16[256,2048]{0,1:T(8,128)(2,1)S(1)}, u32[]{:S(2)}, u32[]{:S(2)}) collective-permute-start(bf16[256,2048]{0,1:T(8,128)(2,1)} %get-tuple-element.173), channel_id=1, source_target_pairs={{16,0},{18,2},{20,4},{22,6},{24,8},{26,10},{28,12},{30,14},{17,1},... | collective-permute-start | bytes 3145736 | tf_op jit(solution)/shard_map/ppermute | solution.py:15
  464.6 169.5 %collective-permute-start.8 = (bf16[256,2048]{0,1:T(8,128)(2,1)}, bf16[256,2048]{0,1:T(8,128)(2,1)S(1)}, u32[]{:S(2)}, u32[]{:S(2)}) collective-permute-start(bf16[256,2048]{0,1:T(8,128)(2,1)} %get-tuple-element.172), channel_id=1, source_target_pairs={{2,0},{4,2},{6,4},{8,6},{10,8},{12,10},{14,12},{16,14},{18,16},{20... | collective-permute-start | bytes 3145736 | tf_op jit(solution)/shard_map/ppermute | solution.py:15
  472.2 161.8 %collective-permute-start.9 = (bf16[256,2048]{0,1:T(8,128)(2,1)S(1)}, bf16[256,2048]{0,1:T(8,128)(2,1)S(1)}, u32[]{:S(2)}, u32[]{:S(2)}) collective-permute-start(bf16[256,2048]{0,1:T(8,128)(2,1)S(1)} %get-tuple-element.179), channel_id=1, source_target_pairs={{4,0},{6,2},{8,4},{10,6},{12,8},{14,10},{16,12},{18,14},{20,16},{2... | collective-permute-start | bytes 3145736 | tf_op jit(solution)/shard_map/ppermute | solution.py:15
  636.3 181.8 %reduce-scatter.4.cloned.1.call-start = ((), (), s32[]{:S(2)}) async-start(), calls=%async_computation.4 | async-start | bytes 8912896
  710.4 1.0 copy-start.10
  710.4 2.4 copy-start.11
  710.4 3.7 copy-start
Sparse Core Ops, SparseCore 0:
  9.6 106.6 all-gather.2
  636.4 57.5 all-gather.4
  710.5 107.5 reduce-scatter.3
where the time goes:
time: 827 us; the launch traced here: 825 us
  waiting for transfers between devices  491 us (59%)
  matrix products  126 us (15%)
  starting transfers between devices  111 us (13%)
  local copies, waits for them, and re-layouts  49.5 us (6%)
  other arithmetic  21 us (3%)
  between operations  14 us (2%)
  blocking collectives  11.8 us (1%)
    ppermute x16, waiting for transfers between devices, passed_along(): lax.ppermute(value, axis, [(source, source + steps) for source in range(l...  241 us
    ppermute x16, starting transfers between devices, passed_along(): lax.ppermute(value, axis, [(source, source + steps) for source in range(l...  111 us
    all_gather x1, waiting for transfers between devices, local(): full_weight = lax.all_gather(kv_weight, 'dp', axis=0, tiled=True)  108 us
    unnamed x4, waiting for transfers between devices  97.9 us
    all_gather x1, waiting for transfers between devices, local(): paired_grads = lax.all_gather(kv_grad, 'dp', axis=0, tiled=True)  43.8 us
    unnamed x49, local copies, waits for them, and re-layouts  37 us
    dot_general x8, matrix products, head_work(): lax.dot_general(weights, grad_head, token_dims, preferred_element_type=jn...  20.1 us
    dot_general x8, matrix products, head_work(): jnp.dot(weights, value_head, preferred_element_type=jnp.float32)  18.6 us
  transfers between devices with their start and end apart: 19, of which 16 were waited for; matrix products, arithmetic and copies ran while one was open for 2% of the time, Pallas kernels for 0%

commit v1 on v0

v1 whole, which is shorter than its diff:
```python
import functools
import math

import jax
import jax.numpy as jnp
from jax import lax
from jax.experimental import pallas as pl
from jax.experimental.pallas import tpu as pltpu
from jax.sharding import PartitionSpec as P

HEAD_DIM = 128
WINDOW = 2048
LANES = 4
SCORE_SCALE = 1.0 / math.sqrt(HEAD_DIM)
EXP2_SCALE = SCORE_SCALE * math.log2(math.e)
MASKED = -1e30
MINOR_DIMS = (((1,), (1,)), ((), ()))
MAJOR_DIMS = (((0,), (0,)), ((), ()))


def exchanged(value, bits):
    count = lax.axis_size("seq")
    return lax.ppermute(value, "seq", [(source, source ^ bits) for source in range(count)])


def shifted(value, rows):
    count = lax.axis_size("seq")
    steps = rows * LANES
    leading, last = (max(0, -steps), min(count, count - steps))
    return lax.ppermute(value, "seq", [(source, source + steps) for source in range(leading, last)])


def swapped(value):
    return lax.ppermute(value, "dp", [(0, 1), (1, 0)])


def by_sublane(block, reduce):
    return reduce(block.reshape(block.shape[0] // 8, 8, block.shape[1]), axis=0)


def attention_kernel(
    row_ref, qu_ref, far_ref, near_ref, own_ref,
    out_ref, far_grad_ref, near_grad_ref, own_grad_ref,
    window, turned, total, scores, dprobs,
    *, blocks, span, size,
):
    step = pl.program_id(1)
    row_tokens = blocks * size

    @pl.when(step == 0)
    def _():
        window[:row_tokens] = far_ref[...]
        window[row_tokens : 2 * row_tokens] = near_ref[...]
        window[2 * row_tokens :] = own_ref[...]
        total[...] = jnp.zeros_like(total)
        for block in range(3 * blocks):
            turned[block] = window[block * size : (block + 1) * size].T

    query = qu_ref[0]
    cotangent = qu_ref[1]
    first = row_ref[0] * blocks + step - span
    key_pos = lax.broadcasted_iota(jnp.int32, (size, size), 0)
    query_pos = lax.broadcasted_iota(jnp.int32, (size, size), 1)

    def rows_of(block):
        return pl.ds((step + block) * size, size)

    peak = jnp.full((8, size), MASKED, jnp.float32)
    for block in range(span + 1):
        key = window[rows_of(block), :HEAD_DIM]
        score = lax.dot_general(key, query, MINOR_DIMS, preferred_element_type=jnp.float32)
        if block == span:
            allowed = key_pos <= query_pos
        elif block == 0:
            allowed = (key_pos > query_pos) & (first >= 0)
        else:
            allowed = first + block >= 0
        score = jnp.where(allowed, score, MASKED)
        scores[block * size : (block + 1) * size] = score
        peak = jnp.maximum(peak, by_sublane(score, jnp.max))
    peak = jnp.max(peak, axis=0, keepdims=True)
    mass = jnp.zeros((8, size), jnp.float32)
    pull = jnp.zeros((8, size), jnp.float32)
    for block in range(span + 1):
        value = window[rows_of(block), HEAD_DIM:]
        held = slice(block * size, (block + 1) * size)
        grown = jnp.exp2((scores[held] - peak) * EXP2_SCALE)
        dprob = lax.dot_general(value, cotangent, MINOR_DIMS, preferred_element_type=jnp.float32)
        mass = mass + by_sublane(grown, jnp.sum)
        pull = pull + by_sublane(grown * dprob, jnp.sum)
        scores[held] = grown
        dprobs[held] = dprob
    share = 1.0 / jnp.sum(mass, axis=0, keepdims=True)
    centre = jnp.sum(pull, axis=0, keepdims=True) * share
    attended = jnp.zeros((HEAD_DIM, size), jnp.float32)
    query_grad = jnp.zeros((HEAD_DIM, size), jnp.float32)
    for block in range(span + 1):
        held = slice(block * size, (block + 1) * size)
        probability = scores[held] * share
        weights = probability.astype(jnp.bfloat16)
        dscore = (probability * (dprobs[held] - centre) * SCORE_SCALE).astype(jnp.bfloat16)
        key_turned = turned[step + block, :HEAD_DIM]
        value_turned = turned[step + block, HEAD_DIM:]
        attended += jnp.dot(value_turned, weights, preferred_element_type=jnp.float32)
        query_grad += jnp.dot(key_turned, dscore, preferred_element_type=jnp.float32)
        total[rows_of(block), :HEAD_DIM] += jnp.dot(
            dscore, query, preferred_element_type=jnp.float32
        )
        total[rows_of(block), HEAD_DIM:] += jnp.dot(
            weights, cotangent, preferred_element_type=jnp.float32
        )
    out_ref[0] = attended.T.astype(jnp.bfloat16)
    out_ref[1] = query_grad.T.astype(jnp.bfloat16)

    @pl.when(step == blocks - 1)
    def _():
        far_grad_ref[...] = total[:row_tokens].astype(jnp.bfloat16)
        near_grad_ref[...] = total[row_tokens : 2 * row_tokens]
        own_grad_ref[...] = total[2 * row_tokens :]


def attention(row, query_pair, far, near, own, size):
    _, row_tokens, width = query_pair.shape
    heads = width // HEAD_DIM
    blocks = row_tokens // size
    span = WINDOW // size
    pair_spec = pl.BlockSpec((2, size, HEAD_DIM), lambda head, step, *_: (0, step, head))
    kv_spec = pl.BlockSpec((row_tokens, 2 * HEAD_DIM), lambda head, step, *_: (0, head))
    kv_shape = (row_tokens, 2 * width)
    cells = heads * row_tokens * (span + 1) * size
    return pl.pallas_call(
        functools.partial(attention_kernel, blocks=blocks, span=span, size=size),
        grid_spec=pltpu.PrefetchScalarGridSpec(
            num_scalar_prefetch=1,
            grid=(heads, blocks),
            in_specs=[pair_spec, kv_spec, kv_spec, kv_spec],
            out_specs=[pair_spec, kv_spec, kv_spec, kv_spec],
            scratch_shapes=[
                pltpu.VMEM((3 * row_tokens, 2 * HEAD_DIM), jnp.bfloat16),
                pltpu.VMEM((3 * blocks, 2 * HEAD_DIM, size), jnp.bfloat16),
                pltpu.VMEM((3 * row_tokens, 2 * HEAD_DIM), jnp.float32),
                pltpu.VMEM(((span + 1) * size, size), jnp.float32),
                pltpu.VMEM(((span + 1) * size, size), jnp.float32),
            ],
        ),
        out_shape=[
            jax.ShapeDtypeStruct(query_pair.shape, jnp.bfloat16),
            jax.ShapeDtypeStruct(kv_shape, jnp.bfloat16),
            jax.ShapeDtypeStruct(kv_shape, jnp.float32),
            jax.ShapeDtypeStruct(kv_shape, jnp.float32),
        ],
        compiler_params=pltpu.CompilerParams(vmem_limit_bytes=48 * 2**20),
        cost_estimate=pl.CostEstimate(
            flops=12 * cells * HEAD_DIM, bytes_accessed=9 * 2**20, transcendentals=cells
        ),
        name="window_attention",
    )(row, query_pair, far, near, own)


def placed(pieces, lane, axis):
    size = pieces[0].shape[axis]
    shape = list(pieces[0].shape)
    shape[axis] = size * LANES
    whole = jnp.zeros(shape, pieces[0].dtype)
    for bits, piece in enumerate(pieces):
        whole = lax.dynamic_update_slice_in_dim(whole, piece, (lane ^ bits) * size, axis)
    return whole


def dealt(value, lane, axis):
    size = value.shape[axis] // LANES
    pieces = []
    for bits in range(LANES):
        piece = lax.dynamic_slice_in_dim(value, (lane ^ bits) * size, size, axis)
        pieces.append(exchanged(piece, bits) if bits else piece)
    return pieces


def local(features, queries, kv_weight, upstream):
    tokens = features[0]
    size = tokens.shape[0]
    weight_rows, kv_width = kv_weight.shape
    width = kv_width // 2
    lane_width = width // LANES
    heads = lane_width // HEAD_DIM
    rows = lax.axis_size("seq") // LANES
    place = lax.axis_index("seq")
    lane = place % LANES
    row = place // LANES
    half = lax.axis_index("dp")
    core = place % 2

    key_cols = lax.dynamic_slice_in_dim(kv_weight, lane * lane_width, lane_width, 1)
    value_cols = lax.dynamic_slice_in_dim(kv_weight, width + lane * lane_width, lane_width, 1)
    lane_weight = jnp.concatenate(
        [
            part[:, head * HEAD_DIM : (head + 1) * HEAD_DIM]
            for head in range(heads)
            for part in (key_cols, value_cols)
        ],
        axis=1,
    )
    other_lane_weight = swapped(lane_weight)
    across = exchanged(tokens, 2)
    beside = exchanged(tokens, 1)
    diagonal = exchanged(across, 1)
    row_tokens = placed([tokens, beside, across, diagonal], lane, 0)
    whole_weight = jnp.zeros((2 * weight_rows, lane_weight.shape[1]), jnp.bfloat16)
    whole_weight = lax.dynamic_update_slice_in_dim(whole_weight, lane_weight, half * weight_rows, 0)
    whole_weight = lax.dynamic_update_slice_in_dim(
        whole_weight, other_lane_weight, (1 - half) * weight_rows, 0
    )
    own = jnp.dot(row_tokens, whole_weight, preferred_element_type=jnp.float32).astype(jnp.bfloat16)
    near = shifted(own, 1)
    far = shifted(near, 1)

    query_pair = placed(dealt(jnp.concatenate([queries, upstream], 0), lane, 2), lane, 1)

    part_rows = weight_rows // 2
    fetched = swapped(lax.dynamic_slice_in_dim(kv_weight, core * part_rows, part_rows, 0))
    passed = exchanged(fetched, 1)

    out_pair, far_grad, near_grad, own_grad = attention(
        row[None], query_pair, far, near, own, size
    )
    carried = shifted(far_grad, -1).astype(jnp.float32)
    carried = shifted((near_grad + carried).astype(jnp.bfloat16), -1).astype(jnp.float32)
    kv_grad = (own_grad + carried).astype(jnp.bfloat16)

    out_pair = placed(dealt(out_pair, lane, 1), lane, 2)

    lane_grads = dealt(kv_grad, lane, 0)
    token_grad = placed([piece[:, None] for piece in lane_grads], lane, 1)
    token_grad = (
        token_grad.reshape(size, LANES, heads, 2, HEAD_DIM)
        .transpose(0, 3, 1, 2, 4)
        .reshape(size, kv_width)
    )

    def against(weight):
        return lax.dot_general(
            token_grad, weight, MINOR_DIMS, preferred_element_type=jnp.float32
        ).astype(jnp.bfloat16)

    feature_grad = jnp.zeros((size, 2 * weight_rows), jnp.bfloat16)
    for piece, start in (
        (kv_weight, half * weight_rows),
        (fetched, (1 - half) * weight_rows + core * part_rows),
        (passed, (1 - half) * weight_rows + (1 - core) * part_rows),
    ):
        feature_grad = lax.dynamic_update_slice_in_dim(feature_grad, against(piece), start, 1)

    partial = lax.dot_general(row_tokens, kv_grad, MAJOR_DIMS, preferred_element_type=jnp.float32)

    def halved(pairs, bit, send):
        kept = lax.dynamic_index_in_dim(pairs, bit, 1, keepdims=False)
        given = lax.dynamic_index_in_dim(pairs, 1 - bit, 1, keepdims=False)
        return kept + send(given.astype(jnp.bfloat16)).astype(jnp.float32)

    lane_cols = partial.shape[1]
    partial = halved(partial.reshape(1, 2, weight_rows, lane_cols), half, swapped)
    partial = partial.reshape(rows, weight_rows // rows, lane_cols)
    distance = 1
    while distance < rows:
        partial = halved(
            partial.reshape(partial.shape[0] // 2, 2, weight_rows // rows, lane_cols),
            (row // distance) % 2,
            functools.partial(exchanged, bits=distance * LANES),
        )
        distance *= 2
    pieces = dealt(partial[0], lane, 0)
    weight_grad = placed([piece[:, None] for piece in pieces], lane, 1)
    weight_grad = (
        weight_grad.reshape(-1, LANES, heads, 2, HEAD_DIM)
        .transpose(0, 3, 1, 2, 4)
        .reshape(-1, kv_width)
    )
    return (out_pair[:1], out_pair[1:], feature_grad[None], weight_grad)


def solution(mesh):
    return jax.shard_map(
        local,
        mesh=mesh,
        in_specs=(P("dp", "seq", None), P("dp", "seq", None), P("dp", None), P("dp", "seq", None)),
        out_specs=(
            P("dp", "seq", None),
            P("dp", "seq", None),
            P("dp", "seq", None),
            P(("dp", "seq"), None),
        ),
        check_vma=False,
    )
```

time: 827 us -> 241 us (0.29)
  waiting for transfers between devices: 491 us -> 142 us
  matrix products: 126 us -> 10.7 us
  starting transfers between devices: 111 us -> 33.3 us
  local copies, waits for them, and re-layouts: 49.5 us -> 21.2 us
  Pallas kernels: 0 us -> 25.6 us
  other arithmetic: 21 us -> 6.64 us
  between operations: 14 us -> 1.34 us
  blocking collectives: 11.8 us -> 0 us
    all_gather x2 -> x0, waiting for transfers between devices: 152 us -> none  [the longest x1 108 us: local(): full_weight = lax.all_gather(kv_weight, 'dp', axis=0, tiled=True)]
    dot_general x51 -> x5, matrix products: 126 us -> 10.7 us  [the longest x3 6.04 us: against(): lax.dot_general(token_grad, weight, MINOR_DIMS, preferred_element_type=jn...]
    ppermute x16 -> x25, waiting for transfers between devices: 241 us -> 142 us  [the longest x18 68.2 us: exchanged(): lax.ppermute(value, 'seq', [(source, source ^ bits) for source in range(c...]
    unnamed x4 -> x0, waiting for transfers between devices: 97.9 us -> none
    ppermute x16 -> x25, starting transfers between devices: 111 us -> 33.3 us  [the longest x18 17.6 us: exchanged(): lax.ppermute(value, 'seq', [(source, source ^ bits) for source in range(c...]
    unnamed x49 -> x29, local copies, waits for them, and re-layouts: 37 us -> 3.05 us
    pallas_call x0 -> x1, Pallas kernels: none -> 25.6 us  [attention(): pl.pallas_call(functools.partial(attention_kernel, blocks=blocks, span=sp...]
    all_to_all x1 -> x0, blocking collectives: 11.8 us -> none  [local(): lax.all_to_all(tokens, 'dp', split_axis=1, concat_axis=0, tiled=True)]
  transfers between devices with their start and end apart: 19 -> 25, of which waited for: 16 -> 17; matrix products, arithmetic and copies ran while one was open for 2% -> 13% of each run, Pallas kernels for 0% -> 0%
where the time goes in v1:
time: 241 us; the launch traced here: 240 us
  waiting for transfers between devices  142 us (59%)
  starting transfers between devices  33.3 us (14%)
  Pallas kernels  25.6 us (11%)
  local copies, waits for them, and re-layouts  21.2 us (9%)
  matrix products  10.7 us (4%)
  other arithmetic  6.64 us (3%)
    ppermute x18, waiting for transfers between devices, exchanged(): lax.ppermute(value, 'seq', [(source, source ^ bits) for source in range(c...  68.2 us
    ppermute x4, waiting for transfers between devices, shifted(): lax.ppermute(value, 'seq', [(source, source + steps) for source in range(...  45 us
    ppermute x3, waiting for transfers between devices, swapped(): return lax.ppermute(value, 'dp', [(0, 1), (1, 0)])  28.4 us
    pallas_call x1, Pallas kernels, attention(): pl.pallas_call(functools.partial(attention_kernel, blocks=blocks, span=sp...  25.6 us
    ppermute x18, starting transfers between devices, exchanged(): lax.ppermute(value, 'seq', [(source, source ^ bits) for source in range(c...  17.6 us
    ppermute x4, starting transfers between devices, shifted(): lax.ppermute(value, 'seq', [(source, source + steps) for source in range(...  11 us
    dot_general x3, matrix products, against(): lax.dot_general(token_grad, weight, MINOR_DIMS, preferred_element_type=jn...  6.04 us
    dynamic_update_slice x18, local copies, waits for them, and re-layouts, placed(): lax.dynamic_update_slice_in_dim(whole, piece, (lane ^ bits) * size, axis)  6.01 us
  transfers between devices with their start and end apart: 25, of which 17 were waited for; matrix products, arithmetic and copies ran while one was open for 13% of the time, Pallas kernels for 0%

profile of v1, /device:TPU:0, one launch (start us, length us, event | category | flops | bytes accessed | tf_op | source)
XLA Modules:
  0.0 240.4 jit_solution(15112940225242011309)
XLA Ops:
  0.6 3.0 %collective-permute-start.4 = (bf16[256,2048]{1,0:T(8,128)(2,1)}, bf16[256,2048]{1,0:T(8,128)(2,1)}, u32[]{:S(2)}, u32[]{:S(2)}) collective-permute-start(bf16[256,2048]{1,0:T(8,128)(2,1)} %bitcast.71), channel_id=1, source_target_pairs={{0,4},{2,6},{4,0},{6,2},{8,12},{10,14},{12,8},{14,10},{16,20},{18,... | collective-permute-start | bytes 3145736 | tf_op jit(solution)/shard_map/ppermute | solution.py:23
  3.6 1.3 constant_dynamic-slice_fusion.13
  5.1 1.1 pad_maximum_fusion
  6.2 1.5 collective-permute-start.6
  7.7 19.4 %collective-permute-done.4 = bf16[256,2048]{1,0:T(8,128)(2,1)} collective-permute-done((bf16[256,2048]{1,0:T(8,128)(2,1)}, bf16[256,2048]{1,0:T(8,128)(2,1)}, u32[]{:S(2)}, u32[]{:S(2)}) %collective-permute-start.4) | collective-permute-done | bytes 1048608 | tf_op jit(solution)/shard_map/ppermute | solution.py:23
  27.8 3.4 %collective-permute-done.6 = bf16[1024,512]{1,0:T(8,128)(2,1)} collective-permute-done((bf16[1024,512]{1,0:T(8,128)(2,1)}, bf16[1024,512]{1,0:T(8,128)(2,1)}, u32[]{:S(2)}, u32[]{:S(2)}) %collective-permute-start.6) | collective-permute-done | bytes 1048608 | tf_op jit(solution)/shard_map/ppermute | solution.py:34
  31.1 1.3 constant_dynamic-update-slice_fusion.7
  32.5 1.3 constant_dynamic-update-slice_fusion.11
  33.8 1.3 constant_dynamic-update-slice_fusion.10
  35.3 2.3 convolution_convert_fusion.own_ref
  37.6 3.5 %collective-permute-start.7 = (bf16[1024,512]{1,0:T(8,128)(2,1)S(1)}, bf16[1024,512]{1,0:T(8,128)(2,1)S(1)}, u32[]{:S(2)}, u32[]{:S(2)}) collective-permute-start(bf16[1024,512]{1,0:T(8,128)(2,1)S(1)} %convolution_convert_fusion.own_ref), channel_id=1, source_target_pairs={{0,8},{2,10},{4,12},{6,14},{8,16},{10,18},{12,20},{14,22},{16,24},... | collective-permute-start | bytes 3145736 | tf_op jit(solution)/shard_map/ppermute | solution.py:30
  41.2 21.1 %collective-permute-done.7.near_ref = bf16[1024,512]{1,0:T(8,128)(2,1)S(1)} collective-permute-done((bf16[1024,512]{1,0:T(8,128)(2,1)S(1)}, bf16[1024,512]{1,0:T(8,128)(2,1)S(1)}, u32[]{:S(2)}, u32[]{:S(2)}) %collective-permute-start.7) | collective-permute-done | bytes 1048608 | tf_op jit(solution)/shard_map/ppermute | solution.py:30
  62.3 4.4 %collective-permute-start.8 = (bf16[1024,512]{1,0:T(8,128)(2,1)S(1)}, bf16[1024,512]{1,0:T(8,128)(2,1)S(1)}, u32[]{:S(2)}, u32[]{:S(2)}) collective-permute-start(bf16[1024,512]{1,0:T(8,128)(2,1)S(1)} %collective-permute-done.7.near_ref), channel_id=1, source_target_pairs={{0,8},{2,10},{4,12},{6,14},{8,16},{10,18},{12,20},{14,22},{16,24},... | collective-permute-start | bytes 3145736 | tf_op jit(solution)/shard_map/ppermute | solution.py:30
  68.4 1.3 collective-permute-start.2
  70.8 6.6 %collective-permute-done.1 = bf16[2,256,256]{2,1,0:T(8,128)(2,1)} collective-permute-done((bf16[2,256,256]{2,1,0:T(8,128)(2,1)}, bf16[2,256,256]{2,1,0:T(8,128)(2,1)}, u32[]{:S(2)}, u32[]{:S(2)}) %collective-permute-start.1) | collective-permute-done | bytes 262176 | tf_op jit(solution)/shard_map/ppermute | solution.py:23
  78.3 3.9 %collective-permute-done.2 = bf16[2,256,256]{2,1,0:T(8,128)(2,1)} collective-permute-done((bf16[2,256,256]{2,1,0:T(8,128)(2,1)S(1)}, bf16[2,256,256]{2,1,0:T(8,128)(2,1)}, u32[]{:S(2)}, u32[]{:S(2)}) %collective-permute-start.2) | collective-permute-done | bytes 262176 | tf_op jit(solution)/shard_map/ppermute | solution.py:23
  83.2 3.9 %collective-permute-done.8.far_ref = bf16[1024,512]{1,0:T(8,128)(2,1)S(1)} collective-permute-done((bf16[1024,512]{1,0:T(8,128)(2,1)S(1)}, bf16[1024,512]{1,0:T(8,128)(2,1)S(1)}, u32[]{:S(2)}, u32[]{:S(2)}) %collective-permute-start.8) | collective-permute-done | bytes 1048608 | tf_op jit(solution)/shard_map/ppermute | solution.py:30
  88.0 1.2 copy-done.1
  89.2 25.6 %window_attention.1 = (bf16[2,1024,256]{2,1,0:T(8,128)(2,1)S(1)}, bf16[1024,512]{1,0:T(8,128)(2,1)S(1)}, f32[1024,512]{1,0:T(8,128)}, f32[1024,512]{1,0:T(8,128)}) custom-call(s32[1]{0:T(128)} %bitcast.row_ref, bf16[2,1024,256]{2,1,0:T(8,128)(2,1)S(1)} %constant_dynamic-update-slice_fusion.13.qu_ref, bf16[1024,512]{1,0:T(8,128)(2,1)S(1)} %copy-done.1, ...), custom_call_target="tpu_custom_call" | custom-call | flops 7247757312 | bytes 9437184 | tf_op jit(solution)/shard_map/window_attention/pallas_call | solution.py:131
  114.8 1.4 collective-permute-start.12
  116.3 1.7 constant_dynamic-slice_fusion
  117.9 1.5 collective-permute-start.17
  119.5 20.0 %collective-permute-done.12 = bf16[1024,512]{1,0:T(8,128)(2,1)S(1)} collective-permute-done((bf16[1024,512]{1,0:T(8,128)(2,1)S(1)}, bf16[1024,512]{1,0:T(8,128)(2,1)S(1)}, u32[]{:S(2)}, u32[]{:S(2)}) %collective-permute-start.12) | collective-permute-done | bytes 1048608 | tf_op jit(solution)/shard_map/ppermute | solution.py:30
  139.5 1.3 add_convert_fusion.1
  140.8 1.6 collective-permute-start.13
  142.5 20.1 %collective-permute-done.17 = bf16[512,2048]{1,0:T(8,128)(2,1)} collective-permute-done((bf16[512,2048]{1,0:T(8,128)(2,1)}, bf16[512,2048]{1,0:T(8,128)(2,1)}, u32[]{:S(2)}, u32[]{:S(2)}) %collective-permute-start.17) | collective-permute-done | bytes 2097184 | tf_op jit(solution)/shard_map/ppermute | solution.py:34
  164.8 1.7 add_convert_fusion
  167.3 2.4 fusion.9
  169.9 1.6 collective-permute-start.19
  172.6 3.8 %collective-permute-done.11 = bf16[2,256,256]{2,1,0:T(8,128)(2,1)S(1)} collective-permute-done((bf16[2,256,256]{2,1,0:T(8,128)(2,1)S(1)}, bf16[2,256,256]{2,1,0:T(8,128)(2,1)S(1)}, u32[]{:S(2)}, u32[]{:S(2)}) %collective-permute-start.11) | collective-permute-done | bytes 262176 | tf_op jit(solution)/shard_map/ppermute | solution.py:23
  176.6 1.2 collective-permute-start.14
  180.5 1.1 copy.16
  181.6 5.4 %collective-permute-done.15 = bf16[256,512]{1,0:T(8,128)(2,1)} collective-permute-done((bf16[256,512]{1,0:T(8,128)(2,1)S(1)}, bf16[256,512]{1,0:T(8,128)(2,1)}, u32[]{:S(2)}, u32[]{:S(2)}) %collective-permute-start.15) | collective-permute-done | bytes 262176 | tf_op jit(solution)/shard_map/ppermute | solution.py:23
  187.0 1.1 copy.17
  188.1 2.6 %collective-permute-done.16 = bf16[256,512]{1,0:T(8,128)(2,1)S(1)} collective-permute-done((bf16[256,512]{1,0:T(8,128)(2,1)S(1)}, bf16[256,512]{1,0:T(8,128)(2,1)S(1)}, u32[]{:S(2)}, u32[]{:S(2)}) %collective-permute-start.16) | collective-permute-done | bytes 262176 | tf_op jit(solution)/shard_map/ppermute | solution.py:23
  190.9 4.9 %collective-permute-done.19 = bf16[1,1024,512]{2,1,0:T(8,128)(2,1)} collective-permute-done((bf16[1,1024,512]{2,1,0:T(8,128)(2,1)S(1)}, bf16[1,1024,512]{2,1,0:T(8,128)(2,1)}, u32[]{:S(2)}, u32[]{:S(2)}) %collective-permute-start.19) | collective-permute-done | bytes 1048608 | tf_op jit(solution)/shard_map/ppermute | solution.py:34
  195.8 2.3 bitcast_add_fusion
  198.2 3.2 %collective-permute-start.20 = (bf16[2,256,512]{2,1,0:T(8,128)(2,1)S(1)}, bf16[2,256,512]{2,1,0:T(8,128)(2,1)S(1)}, u32[]{:S(2)}, u32[]{:S(2)}) collective-permute-start(bf16[2,256,512]{2,1,0:T(8,128)(2,1)S(1)} %fusion.7), channel_id=1, source_target_pairs={{0,8},{2,10},{4,12},{6,14},{8,0},{10,2},{12,4},{14,6},{16,24},{18,... | collective-permute-start | bytes 1572872 | tf_op jit(solution)/shard_map/ppermute | solution.py:23
  201.6 1.3 fusion.1
  202.9 10.4 %collective-permute-done.20 = bf16[2,256,512]{2,1,0:T(8,128)(2,1)S(1)} collective-permute-done((bf16[2,256,512]{2,1,0:T(8,128)(2,1)S(1)}, bf16[2,256,512]{2,1,0:T(8,128)(2,1)S(1)}, u32[]{:S(2)}, u32[]{:S(2)}) %collective-permute-start.20) | collective-permute-done | bytes 524320 | tf_op jit(solution)/shard_map/ppermute | solution.py:23
  213.5 3.0 %collective-permute-start.21 = (bf16[1,256,512]{2,1,0:T(8,128)(2,1)S(1)}, bf16[1,256,512]{2,1,0:T(8,128)(2,1)S(1)}, u32[]{:S(2)}, u32[]{:S(2)}) collective-permute-start(bf16[1,256,512]{2,1,0:T(8,128)(2,1)S(1)} %dynamic-slice_convert_fusion.1), channel_id=1, source_target_pairs={{0,16},{2,18},{4,20},{6,22},{8,24},{10,26},{12,28},{14,30},{16,0},... | collective-permute-start | bytes 786440 | tf_op jit(solution)/shard_map/ppermute | solution.py:23
  216.5 2.4 fusion.3
  218.8 8.8 %collective-permute-done.21 = bf16[1,256,512]{2,1,0:T(8,128)(2,1)S(1)} collective-permute-done((bf16[1,256,512]{2,1,0:T(8,128)(2,1)S(1)}, bf16[1,256,512]{2,1,0:T(8,128)(2,1)S(1)}, u32[]{:S(2)}, u32[]{:S(2)}) %collective-permute-start.21) | collective-permute-done | bytes 262176 | tf_op jit(solution)/shard_map/ppermute | solution.py:23
  227.8 2.4 fusion.5
  230.6 1.5 collective-permute-start.24
  232.2 4.3 %collective-permute-done.23 = f32[64,512]{1,0:T(8,128)S(1)} collective-permute-done((f32[64,512]{1,0:T(8,128)S(1)}, f32[64,512]{1,0:T(8,128)S(1)}, u32[]{:S(2)}, u32[]{:S(2)}) %collective-permute-start.23) | collective-permute-done | bytes 131104 | tf_op jit(solution)/shard_map/ppermute | solution.py:23
  236.6 2.0 collective-permute-done.24
  239.2 1.2 reshape.59
  (88 shorter events, 15.5 us)
Async XLA Ops:
  0.6 26.5 %collective-permute-start.4 = (bf16[256,2048]{1,0:T(8,128)(2,1)}, bf16[256,2048]{1,0:T(8,128)(2,1)}, u32[]{:S(2)}, u32[]{:S(2)}) collective-permute-start(bf16[256,2048]{1,0:T(8,128)(2,1)} %bitcast.71), channel_id=1, source_target_pairs={{0,4},{2,6},{4,0},{6,2},{8,12},{10,14},{12,8},{14,10},{16,20},{18,... | collective-permute-start | bytes 3145736 | tf_op jit(solution)/shard_map/ppermute | solution.py:23
  5.1 2.6 %copy-start.9 = (bf16[1,256,2048]{2,1,0:T(8,128)(2,1)S(1)}, bf16[1,256,2048]{2,1,0:T(8,128)(2,1)}, u32[]{:S(2)}) copy-start(bf16[1,256,2048]{2,1,0:T(8,128)(2,1)} %param.4) | copy-start | bytes 3145732
  6.2 24.9 %collective-permute-start.6 = (bf16[1024,512]{1,0:T(8,128)(2,1)}, bf16[1024,512]{1,0:T(8,128)(2,1)}, u32[]{:S(2)}, u32[]{:S(2)}) collective-permute-start(bf16[1024,512]{1,0:T(8,128)(2,1)} %get-tuple-element.26), channel_id=1, source_target_pairs={{0,1},{1,0},{2,3},{3,2},{4,5},{5,4},{6,7},{7,6},{8,9},{9,8},{10,11... | collective-permute-start | bytes 3145736 | tf_op jit(solution)/shard_map/ppermute | solution.py:34
  7.7 24.7 %collective-permute-start.3 = (bf16[256,2048]{1,0:T(8,128)(2,1)S(1)}, bf16[256,2048]{1,0:T(8,128)(2,1)}, u32[]{:S(2)}, u32[]{:S(2)}) collective-permute-start(bf16[256,2048]{1,0:T(8,128)(2,1)S(1)} %bitcast.72), channel_id=1, source_target_pairs={{0,2},{2,0},{4,6},{6,4},{8,10},{10,8},{12,14},{14,12},{16,18},{18,... | collective-permute-start | bytes 3145736 | tf_op jit(solution)/shard_map/ppermute | solution.py:23
  27.1 8.0 %collective-permute-start.5 = (bf16[256,2048]{1,0:T(8,128)(2,1)}, bf16[256,2048]{1,0:T(8,128)(2,1)S(1)}, u32[]{:S(2)}, u32[]{:S(2)}) collective-permute-start(bf16[256,2048]{1,0:T(8,128)(2,1)} %collective-permute-done.4), channel_id=1, source_target_pairs={{0,2},{2,0},{4,6},{6,4},{8,10},{10,8},{12,14},{14,12},{16,18},{18,... | collective-permute-start | bytes 3145736 | tf_op jit(solution)/shard_map/ppermute | solution.py:23
  35.3 2.4 copy-start.2
  35.3 31.5 %copy-start.11 = (bf16[1,256,1024]{2,1,0:T(8,128)(2,1)S(1)}, bf16[1,256,1024]{2,1,0:T(8,128)(2,1)}, u32[]{:S(2)}) copy-start(bf16[1,256,1024]{2,1,0:T(8,128)(2,1)} %param.5) | copy-start | bytes 1572868
  35.3 31.6 %copy-start.12 = (bf16[1,256,1024]{2,1,0:T(8,128)(2,1)S(1)}, bf16[1,256,1024]{2,1,0:T(8,128)(2,1)}, u32[]{:S(2)}) copy-start(bf16[1,256,1024]{2,1,0:T(8,128)(2,1)} %param.7) | copy-start | bytes 1572868
  37.6 30.3 %copy-start.13 = (bf16[1024,512]{1,0:T(8,128)(2,1)}, bf16[1024,512]{1,0:T(8,128)(2,1)S(1)}, u32[]{:S(2)}) copy-start(bf16[1024,512]{1,0:T(8,128)(2,1)S(1)} %convolution_convert_fusion.own_ref) | copy-start | bytes 3145732
  37.6 24.7 %collective-permute-start.7 = (bf16[1024,512]{1,0:T(8,128)(2,1)S(1)}, bf16[1024,512]{1,0:T(8,128)(2,1)S(1)}, u32[]{:S(2)}, u32[]{:S(2)}) collective-permute-start(bf16[1024,512]{1,0:T(8,128)(2,1)S(1)} %convolution_convert_fusion.own_ref), channel_id=1, source_target_pairs={{0,8},{2,10},{4,12},{6,14},{8,16},{10,18},{12,20},{14,22},{16,24},... | collective-permute-start | bytes 3145736 | tf_op jit(solution)/shard_map/ppermute | solution.py:30
  62.3 24.7 %collective-permute-start.8 = (bf16[1024,512]{1,0:T(8,128)(2,1)S(1)}, bf16[1024,512]{1,0:T(8,128)(2,1)S(1)}, u32[]{:S(2)}, u32[]{:S(2)}) collective-permute-start(bf16[1024,512]{1,0:T(8,128)(2,1)S(1)} %collective-permute-done.7.near_ref), channel_id=1, source_target_pairs={{0,8},{2,10},{4,12},{6,14},{8,16},{10,18},{12,20},{14,22},{16,24},... | collective-permute-start | bytes 3145736 | tf_op jit(solution)/shard_map/ppermute | solution.py:30
  67.9 1.9 collective-permute-start
  67.9 9.4 %collective-permute-start.1 = (bf16[2,256,256]{2,1,0:T(8,128)(2,1)}, bf16[2,256,256]{2,1,0:T(8,128)(2,1)}, u32[]{:S(2)}, u32[]{:S(2)}) collective-permute-start(bf16[2,256,256]{2,1,0:T(8,128)(2,1)} %get-tuple-element.29), channel_id=1, source_target_pairs={{0,4},{2,6},{4,0},{6,2},{8,12},{10,14},{12,8},{14,10},{16,20},{18,... | collective-permute-start | bytes 786440 | tf_op jit(solution)/shard_map/ppermute | solution.py:23
  68.4 13.7 %collective-permute-start.2 = (bf16[2,256,256]{2,1,0:T(8,128)(2,1)S(1)}, bf16[2,256,256]{2,1,0:T(8,128)(2,1)}, u32[]{:S(2)}, u32[]{:S(2)}) collective-permute-start(bf16[2,256,256]{2,1,0:T(8,128)(2,1)S(1)} %get-tuple-element.28), channel_id=1, source_target_pairs={{0,6},{2,4},{4,2},{6,0},{8,14},{10,12},{12,10},{14,8},{16,22},{18,... | collective-permute-start | bytes 786440 | tf_op jit(solution)/shard_map/ppermute | solution.py:23
  87.0 1.0 copy-start
  88.0 1.2 copy-start.1
  89.2 27.0 %copy-start.4 = (bf16[1024,2048]{1,0:T(8,128)(2,1)S(1)}, bf16[1024,2048]{1,0:T(8,128)(2,1)}, u32[]{:S(2)}) copy-start(bf16[1024,2048]{1,0:T(8,128)(2,1)} %param.6) | copy-start | bytes 12582916
  114.8 24.6 %copy-start.8 = (f32[1024,512]{1,0:T(8,128)S(1)}, f32[1024,512]{1,0:T(8,128)}, u32[]{:S(2)}) copy-start(f32[1024,512]{1,0:T(8,128)} %get-tuple-element.10) | copy-start | bytes 6291460
  114.8 24.6 %collective-permute-start.12 = (bf16[1024,512]{1,0:T(8,128)(2,1)S(1)}, bf16[1024,512]{1,0:T(8,128)(2,1)S(1)}, u32[]{:S(2)}, u32[]{:S(2)}) collective-permute-start(bf16[1024,512]{1,0:T(8,128)(2,1)S(1)} %get-tuple-element.11), channel_id=1, source_target_pairs={{8,0},{10,2},{12,4},{14,6},{16,8},{18,10},{20,12},{22,14},{24,16},... | collective-permute-start | bytes 3145736 | tf_op jit(solution)/shard_map/ppermute | solution.py:30
  117.9 44.7 %collective-permute-start.17 = (bf16[512,2048]{1,0:T(8,128)(2,1)}, bf16[512,2048]{1,0:T(8,128)(2,1)}, u32[]{:S(2)}, u32[]{:S(2)}) collective-permute-start(bf16[512,2048]{1,0:T(8,128)(2,1)} %constant_dynamic-slice_fusion), channel_id=1, source_target_pairs={{0,1},{1,0},{2,3},{3,2},{4,5},{5,4},{6,7},{7,6},{8,9},{9,8},{10,11... | collective-permute-start | bytes 6291464 | tf_op jit(solution)/shard_map/ppermute | solution.py:34
  140.8 24.0 %copy-start.7 = (f32[1024,512]{1,0:T(8,128)S(1)}, f32[1024,512]{1,0:T(8,128)}, u32[]{:S(2)}) copy-start(f32[1024,512]{1,0:T(8,128)} %get-tuple-element.9) | copy-start | bytes 6291460
  140.8 24.0 %collective-permute-start.13 = (bf16[1024,512]{1,0:T(8,128)(2,1)}, bf16[1024,512]{1,0:T(8,128)(2,1)}, u32[]{:S(2)}, u32[]{:S(2)}) collective-permute-start(bf16[1024,512]{1,0:T(8,128)(2,1)} %add_convert_fusion.1), channel_id=1, source_target_pairs={{8,0},{10,2},{12,4},{14,6},{16,8},{18,10},{20,12},{22,14},{24,16},... | collective-permute-start | bytes 3145736 | tf_op jit(solution)/shard_map/ppermute | solution.py:30
  162.6 65.2 %collective-permute-start.18 = (bf16[512,2048]{1,0:T(8,128)(2,1)}, bf16[512,2048]{1,0:T(8,128)(2,1)}, u32[]{:S(2)}, u32[]{:S(2)}) collective-permute-start(bf16[512,2048]{1,0:T(8,128)(2,1)} %collective-permute-done.17), channel_id=1, source_target_pairs={{0,2},{2,0},{4,6},{6,4},{8,10},{10,8},{12,14},{14,12},{16,18},{18,... | collective-permute-start | bytes 6291464 | tf_op jit(solution)/shard_map/ppermute | solution.py:23
  162.8 8.7 %collective-permute-start.9 = (bf16[2,256,256]{2,1,0:T(8,128)(2,1)S(1)}, bf16[2,256,256]{2,1,0:T(8,128)(2,1)S(1)}, u32[]{:S(2)}, u32[]{:S(2)}) collective-permute-start(bf16[2,256,256]{2,1,0:T(8,128)(2,1)S(1)} %get-tuple-element.24), channel_id=1, source_target_pairs={{0,2},{2,0},{4,6},{6,4},{8,10},{10,8},{12,14},{14,12},{16,18},{18,... | collective-permute-start | bytes 786440 | tf_op jit(solution)/shard_map/ppermute | solution.py:23
  163.4 9.2 %collective-permute-start.10 = (bf16[2,256,256]{2,1,0:T(8,128)(2,1)S(1)}, bf16[2,256,256]{2,1,0:T(8,128)(2,1)S(1)}, u32[]{:S(2)}, u32[]{:S(2)}) collective-permute-start(bf16[2,256,256]{2,1,0:T(8,128)(2,1)S(1)} %get-tuple-element.23), channel_id=1, source_target_pairs={{0,4},{2,6},{4,0},{6,2},{8,12},{10,14},{12,8},{14,10},{16,20},{18,... | collective-permute-start | bytes 786440 | tf_op jit(solution)/shard_map/ppermute | solution.py:23
  163.9 12.6 %collective-permute-start.11 = (bf16[2,256,256]{2,1,0:T(8,128)(2,1)S(1)}, bf16[2,256,256]{2,1,0:T(8,128)(2,1)S(1)}, u32[]{:S(2)}, u32[]{:S(2)}) collective-permute-start(bf16[2,256,256]{2,1,0:T(8,128)(2,1)S(1)} %get-tuple-element.22), channel_id=1, source_target_pairs={{0,6},{2,4},{4,2},{6,0},{8,14},{10,12},{12,10},{14,8},{16,22},{18,... | collective-permute-start | bytes 786440 | tf_op jit(solution)/shard_map/ppermute | solution.py:23
  164.8 2.5 %copy-start.3 = (bf16[1024,2048]{1,0:T(8,128)(2,1)S(1)}, bf16[1024,2048]{1,0:T(8,128)(2,1)}, u32[]{:S(2)}) copy-start(bf16[1024,2048]{1,0:T(8,128)(2,1)} %copy-done.2) | copy-start | bytes 12582916
  169.7 6.8 %copy-start.6 = (f32[2048,512]{1,0:T(8,128)}, f32[2048,512]{1,0:T(8,128)S(1)}, u32[]{:S(2)}) copy-start(f32[2048,512]{1,0:T(8,128)S(1)} %fusion.9) | copy-start | bytes 12582916
  169.9 25.9 %collective-permute-start.19 = (bf16[1,1024,512]{2,1,0:T(8,128)(2,1)S(1)}, bf16[1,1024,512]{2,1,0:T(8,128)(2,1)}, u32[]{:S(2)}, u32[]{:S(2)}) collective-permute-start(bf16[1,1024,512]{2,1,0:T(8,128)(2,1)S(1)} %fusion.6), channel_id=1, source_target_pairs={{0,1},{1,0},{2,3},{3,2},{4,5},{5,4},{6,7},{7,6},{8,9},{9,8},{10,11... | collective-permute-start | bytes 3145736 | tf_op jit(solution)/shard_map/ppermute | solution.py:34
  176.6 3.9 %collective-permute-start.14 = (bf16[256,512]{1,0:T(8,128)(2,1)S(1)}, bf16[256,512]{1,0:T(8,128)(2,1)}, u32[]{:S(2)}, u32[]{:S(2)}) collective-permute-start(bf16[256,512]{1,0:T(8,128)(2,1)S(1)} %get-tuple-element.18), channel_id=1, source_target_pairs={{0,2},{2,0},{4,6},{6,4},{8,10},{10,8},{12,14},{14,12},{16,18},{18,... | collective-permute-start | bytes 786440 | tf_op jit(solution)/shard_map/ppermute | solution.py:23
  177.7 9.3 %collective-permute-start.15 = (bf16[256,512]{1,0:T(8,128)(2,1)S(1)}, bf16[256,512]{1,0:T(8,128)(2,1)}, u32[]{:S(2)}, u32[]{:S(2)}) collective-permute-start(bf16[256,512]{1,0:T(8,128)(2,1)S(1)} %get-tuple-element.17), channel_id=1, source_target_pairs={{0,4},{2,6},{4,0},{6,2},{8,12},{10,14},{12,8},{14,10},{16,20},{18,... | collective-permute-start | bytes 786440 | tf_op jit(solution)/shard_map/ppermute | solution.py:23
  179.4 11.4 %collective-permute-start.16 = (bf16[256,512]{1,0:T(8,128)(2,1)S(1)}, bf16[256,512]{1,0:T(8,128)(2,1)S(1)}, u32[]{:S(2)}, u32[]{:S(2)}) collective-permute-start(bf16[256,512]{1,0:T(8,128)(2,1)S(1)} %get-tuple-element.16), channel_id=1, source_target_pairs={{0,6},{2,4},{4,2},{6,0},{8,14},{10,12},{12,10},{14,8},{16,22},{18,... | collective-permute-start | bytes 786440 | tf_op jit(solution)/shard_map/ppermute | solution.py:23
  198.1 3.5 %copy-start.5 = (bf16[1024,2048]{1,0:T(8,128)(2,1)S(1)}, bf16[1024,2048]{1,0:T(8,128)(2,1)}, u32[]{:S(2)}) copy-start(bf16[1024,2048]{1,0:T(8,128)(2,1)} %param.6) | copy-start | bytes 12582916
  198.2 15.1 %collective-permute-start.20 = (bf16[2,256,512]{2,1,0:T(8,128)(2,1)S(1)}, bf16[2,256,512]{2,1,0:T(8,128)(2,1)S(1)}, u32[]{:S(2)}, u32[]{:S(2)}) collective-permute-start(bf16[2,256,512]{2,1,0:T(8,128)(2,1)S(1)} %fusion.7), channel_id=1, source_target_pairs={{0,8},{2,10},{4,12},{6,14},{8,0},{10,2},{12,4},{14,6},{16,24},{18,... | collective-permute-start | bytes 1572872 | tf_op jit(solution)/shard_map/ppermute | solution.py:23
  213.5 14.1 %collective-permute-start.21 = (bf16[1,256,512]{2,1,0:T(8,128)(2,1)S(1)}, bf16[1,256,512]{2,1,0:T(8,128)(2,1)S(1)}, u32[]{:S(2)}, u32[]{:S(2)}) collective-permute-start(bf16[1,256,512]{2,1,0:T(8,128)(2,1)S(1)} %dynamic-slice_convert_fusion.1), channel_id=1, source_target_pairs={{0,16},{2,18},{4,20},{6,22},{8,24},{10,26},{12,28},{14,30},{16,0},... | collective-permute-start | bytes 786440 | tf_op jit(solution)/shard_map/ppermute | solution.py:23
  227.7 4.5 %collective-permute-start.22 = (f32[64,512]{1,0:T(8,128)S(1)}, f32[64,512]{1,0:T(8,128)S(1)}, u32[]{:S(2)}, u32[]{:S(2)}) collective-permute-start(f32[64,512]{1,0:T(8,128)S(1)} %get-tuple-element.34), channel_id=1, source_target_pairs={{0,2},{2,0},{4,6},{6,4},{8,10},{10,8},{12,14},{14,12},{16,18},{18,... | collective-permute-start | bytes 393224 | tf_op jit(solution)/shard_map/ppermute | solution.py:23
  230.2 10.2 %copy-start.10 = (bf16[1,256,2048]{2,1,0:T(8,128)(2,1)}, bf16[1,256,2048]{2,1,0:T(8,128)(2,1)S(1)}, u32[]{:S(2)}) copy-start(bf16[1,256,2048]{2,1,0:T(8,128)(2,1)S(1)} %fusion.5) | copy-start | bytes 3145732
  230.2 6.4 %collective-permute-start.23 = (f32[64,512]{1,0:T(8,128)S(1)}, f32[64,512]{1,0:T(8,128)S(1)}, u32[]{:S(2)}, u32[]{:S(2)}) collective-permute-start(f32[64,512]{1,0:T(8,128)S(1)} %get-tuple-element.33), channel_id=1, source_target_pairs={{0,4},{2,6},{4,0},{6,2},{8,12},{10,14},{12,8},{14,10},{16,20},{18,... | collective-permute-start | bytes 393224 | tf_op jit(solution)/shard_map/ppermute | solution.py:23
  230.6 7.9 %collective-permute-start.24 = (f32[64,512]{1,0:T(8,128)S(1)}, f32[64,512]{1,0:T(8,128)S(1)}, u32[]{:S(2)}, u32[]{:S(2)}) collective-permute-start(f32[64,512]{1,0:T(8,128)S(1)} %get-tuple-element.32), channel_id=1, source_target_pairs={{0,6},{2,4},{4,2},{6,0},{8,14},{10,12},{12,10},{14,8},{16,22},{18,... | collective-permute-start | bytes 393224 | tf_op jit(solution)/shard_map/ppermute | solution.py:23

commit v2 on v1

--- a/solution.py
+++ b/solution.py
@@ -34,6 +34,10 @@
     return lax.ppermute(value, "dp", [(0, 1), (1, 0)])
 
 
+def after(value, *others):
+    return lax.optimization_barrier((value, *others))[0]
+
+
 def by_sublane(block, reduce):
     return reduce(block.reshape(block.shape[0] // 8, 8, block.shape[1]), axis=0)
 
@@ -44,7 +48,7 @@
     window, turned, total, scores, dprobs,
     *, blocks, span, size,
 ):
-    step = pl.program_id(1)
+    step = pl.program_id(0)
     row_tokens = blocks * size
 
     @pl.when(step == 0)
@@ -119,22 +123,22 @@
         own_grad_ref[...] = total[2 * row_tokens :]
 
 
-def attention(row, query_pair, far, near, own, size):
-    _, row_tokens, width = query_pair.shape
-    heads = width // HEAD_DIM
+def attention(row, query_pair, head, far, near, own, size):
+    row_tokens = query_pair.shape[1]
     blocks = row_tokens // size
     span = WINDOW // size
-    pair_spec = pl.BlockSpec((2, size, HEAD_DIM), lambda head, step, *_: (0, step, head))
-    kv_spec = pl.BlockSpec((row_tokens, 2 * HEAD_DIM), lambda head, step, *_: (0, head))
-    kv_shape = (row_tokens, 2 * width)
-    cells = heads * row_tokens * (span + 1) * size
+    pair_in = pl.BlockSpec((2, size, HEAD_DIM), lambda step, *_: (0, step, head))
+    pair_out = pl.BlockSpec((2, size, HEAD_DIM), lambda step, *_: (0, step, 0))
+    kv_shape = (row_tokens, 2 * HEAD_DIM)
+    kv_spec = pl.BlockSpec(kv_shape, lambda step, *_: (0, 0))
+    cells = row_tokens * (span + 1) * size
     return pl.pallas_call(
         functools.partial(attention_kernel, blocks=blocks, span=span, size=size),
         grid_spec=pltpu.PrefetchScalarGridSpec(
             num_scalar_prefetch=1,
-            grid=(heads, blocks),
-            in_specs=[pair_spec, kv_spec, kv_spec, kv_spec],
-            out_specs=[pair_spec, kv_spec, kv_spec, kv_spec],
+            grid=(blocks,),
+            in_specs=[pair_in, kv_spec, kv_spec, kv_spec],
+            out_specs=[pair_out, kv_spec, kv_spec, kv_spec],
             scratch_shapes=[
                 pltpu.VMEM((3 * row_tokens, 2 * HEAD_DIM), jnp.bfloat16),
                 pltpu.VMEM((3 * blocks, 2 * HEAD_DIM, size), jnp.bfloat16),
@@ -144,14 +148,14 @@
             ],
         ),
         out_shape=[
-            jax.ShapeDtypeStruct(query_pair.shape, jnp.bfloat16),
+            jax.ShapeDtypeStruct((2, row_tokens, HEAD_DIM), jnp.bfloat16),
             jax.ShapeDtypeStruct(kv_shape, jnp.bfloat16),
             jax.ShapeDtypeStruct(kv_shape, jnp.float32),
             jax.ShapeDtypeStruct(kv_shape, jnp.float32),
         ],
         compiler_params=pltpu.CompilerParams(vmem_limit_bytes=48 * 2**20),
         cost_estimate=pl.CostEstimate(
-            flops=12 * cells * HEAD_DIM, bytes_accessed=9 * 2**20, transcendentals=cells
+            flops=12 * cells * HEAD_DIM, bytes_accessed=5 * 2**20, transcendentals=cells
         ),
         name="window_attention",
     )(row, query_pair, far, near, own)
@@ -210,9 +214,16 @@
     whole_weight = lax.dynamic_update_slice_in_dim(
         whole_weight, other_lane_weight, (1 - half) * weight_rows, 0
     )
-    own = jnp.dot(row_tokens, whole_weight, preferred_element_type=jnp.float32).astype(jnp.bfloat16)
-    near = shifted(own, 1)
-    far = shifted(near, 1)
+    owns, nears, fars = [], [], []
+    for head in range(heads):
+        head_weight = whole_weight[:, head * 2 * HEAD_DIM : (head + 1) * 2 * HEAD_DIM]
+        if head:
+            head_weight = after(head_weight, nears[-1])
+        own = jnp.dot(row_tokens, head_weight, preferred_element_type=jnp.float32)
+        own = own.astype(jnp.bfloat16)
+        owns.append(own)
+        nears.append(shifted(own, 1))
+        fars.append(shifted(nears[-1], 1))
 
     query_pair = placed(dealt(jnp.concatenate([queries, upstream], 0), lane, 2), lane, 1)
 
@@ -220,17 +231,25 @@
     fetched = swapped(lax.dynamic_slice_in_dim(kv_weight, core * part_rows, part_rows, 0))
     passed = exchanged(fetched, 1)
 
-    out_pair, far_grad, near_grad, own_grad = attention(
-        row[None], query_pair, far, near, own, size
-    )
-    carried = shifted(far_grad, -1).astype(jnp.float32)
-    carried = shifted((near_grad + carried).astype(jnp.bfloat16), -1).astype(jnp.float32)
-    kv_grad = (own_grad + carried).astype(jnp.bfloat16)
-
-    out_pair = placed(dealt(out_pair, lane, 1), lane, 2)
-
-    lane_grads = dealt(kv_grad, lane, 0)
-    token_grad = placed([piece[:, None] for piece in lane_grads], lane, 1)
+    out_pairs, kv_grads = [], []
+    for head in range(heads):
+        out_pair, far_grad, near_grad, own_grad = attention(
+            row[None], query_pair, head, fars[head], nears[head], owns[head], size
+        )
+        out_pairs.append(out_pair)
+        carried = shifted(far_grad, -1).astype(jnp.float32)
+        carried = shifted((near_grad + carried).astype(jnp.bfloat16), -1).astype(jnp.float32)
+        kv_grads.append((own_grad + carried).astype(jnp.bfloat16))
+
+    out_pair = placed(dealt(jnp.concatenate(out_pairs, 2), lane, 1), lane, 2)
+
+    token_grad = jnp.stack(
+        [
+            placed([piece[:, None] for piece in dealt(kv_grad, lane, 0)], lane, 1)
+            for kv_grad in kv_grads
+        ],
+        2,
+    )
     token_grad = (
         token_grad.reshape(size, LANES, heads, 2, HEAD_DIM)
         .transpose(0, 3, 1, 2, 4)
@@ -250,28 +269,32 @@
     ):
         feature_grad = lax.dynamic_update_slice_in_dim(feature_grad, against(piece), start, 1)
 
-    partial = lax.dot_general(row_tokens, kv_grad, MAJOR_DIMS, preferred_element_type=jnp.float32)
-
     def halved(pairs, bit, send):
         kept = lax.dynamic_index_in_dim(pairs, bit, 1, keepdims=False)
         given = lax.dynamic_index_in_dim(pairs, 1 - bit, 1, keepdims=False)
         return kept + send(given.astype(jnp.bfloat16)).astype(jnp.float32)
 
-    lane_cols = partial.shape[1]
-    partial = halved(partial.reshape(1, 2, weight_rows, lane_cols), half, swapped)
-    partial = partial.reshape(rows, weight_rows // rows, lane_cols)
-    distance = 1
-    while distance < rows:
-        partial = halved(
-            partial.reshape(partial.shape[0] // 2, 2, weight_rows // rows, lane_cols),
-            (row // distance) % 2,
-            functools.partial(exchanged, bits=distance * LANES),
+    weight_grads = []
+    for kv_grad in kv_grads:
+        partial = lax.dot_general(
+            row_tokens, kv_grad, MAJOR_DIMS, preferred_element_type=jnp.float32
         )
-        distance *= 2
-    pieces = dealt(partial[0], lane, 0)
-    weight_grad = placed([piece[:, None] for piece in pieces], lane, 1)
+        cols = partial.shape[1]
+        partial = halved(partial.reshape(1, 2, weight_rows, cols), half, swapped)
+        partial = partial.reshape(rows, weight_rows // rows, cols)
+        distance = 1
+        while distance < rows:
+            partial = halved(
+                partial.reshape(partial.shape[0] // 2, 2, weight_rows // rows, cols),
+                (row // distance) % 2,
+                functools.partial(exchanged, bits=distance * LANES),
+            )
+            distance *= 2
+        pieces = dealt(partial[0], lane, 0)
+        weight_grads.append(placed([piece[:, None] for piece in pieces], lane, 1))
     weight_grad = (
-        weight_grad.reshape(-1, LANES, heads, 2, HEAD_DIM)
+        jnp.stack(weight_grads, 2)
+        .reshape(-1, LANES, heads, 2, HEAD_DIM)
         .transpose(0, 3, 1, 2, 4)
         .reshape(-1, kv_width)
     )

time: 241 us -> 211 us (0.88)
  waiting for transfers between devices: 142 us -> 95.8 us
  starting transfers between devices: 33.3 us -> 46.3 us
  local copies, waits for them, and re-layouts: 21.2 us -> 23.8 us
    ppermute x3 -> x4, waiting for transfers between devices: 28.4 us -> 3.37 us  [swapped(): return lax.ppermute(value, 'dp', [(0, 1), (1, 0)])]
    ppermute x4 -> x8, waiting for transfers between devices: 45 us -> 34.1 us  [shifted(): lax.ppermute(value, 'seq', [(source, source + steps) for source in range(...]
    ppermute x18 -> x26, waiting for transfers between devices: 68.2 us -> 58.4 us  [exchanged(): lax.ppermute(value, 'seq', [(source, source ^ bits) for source in range(c...]
    ppermute x4 -> x8, starting transfers between devices: 11 us -> 20.5 us  [shifted(): lax.ppermute(value, 'seq', [(source, source + steps) for source in range(...]
    convert_element_type x3 -> x6, local copies, waits for them, and re-layouts: 0.26 us -> 2.96 us  [halved(): return kept + send(given.astype(jnp.bfloat16)).astype(jnp.float32)]
    broadcast_in_dim x4 -> x0, local copies, waits for them, and re-layouts: 2.42 us -> none  [local(): token_grad = placed([piece[:, None] for piece in lane_grads], lane, 1)]
    pallas_call x1 -> x2, Pallas kernels: 25.6 us -> 23.5 us  [attention(): pl.pallas_call(functools.partial(attention_kernel, blocks=blocks, span=sp...]
    ppermute x18 -> x26, starting transfers between devices: 17.6 us -> 19.7 us  [exchanged(): lax.ppermute(value, 'seq', [(source, source ^ bits) for source in range(c...]
  transfers between devices with their start and end apart: 25 -> 38, of which waited for: 17 -> 18; matrix products, arithmetic and copies ran while one was open for 13% -> 17% of each run, Pallas kernels for 0% -> 11%
where the time goes in v2:
time: 211 us; the launch traced here: 210 us
  waiting for transfers between devices  95.8 us (45%)
  starting transfers between devices  46.3 us (22%)
  local copies, waits for them, and re-layouts  23.8 us (11%)
  Pallas kernels  23.5 us (11%)
  matrix products  12.6 us (6%)
  other arithmetic  6.4 us (3%)
    ppermute x26, waiting for transfers between devices, exchanged(): lax.ppermute(value, 'seq', [(source, source ^ bits) for source in range(c...  58.4 us
    ppermute x8, waiting for transfers between devices, shifted(): lax.ppermute(value, 'seq', [(source, source + steps) for source in range(...  34.1 us
    pallas_call x2, Pallas kernels, attention(): pl.pallas_call(functools.partial(attention_kernel, blocks=blocks, span=sp...  23.5 us
    ppermute x8, starting transfers between devices, shifted(): lax.ppermute(value, 'seq', [(source, source + steps) for source in range(...  20.5 us
    ppermute x26, starting transfers between devices, exchanged(): lax.ppermute(value, 'seq', [(source, source ^ bits) for source in range(c...  19.7 us
    ppermute x4, starting transfers between devices, swapped(): return lax.ppermute(value, 'dp', [(0, 1), (1, 0)])  6.14 us
    dynamic_update_slice x25, local copies, waits for them, and re-layouts, placed(): lax.dynamic_update_slice_in_dim(whole, piece, (lane ^ bits) * size, axis)  6.07 us
    dot_general x3, matrix products, against(): lax.dot_general(token_grad, weight, MINOR_DIMS, preferred_element_type=jn...  6.04 us
  transfers between devices with their start and end apart: 38, of which 18 were waited for; matrix products, arithmetic and copies ran while one was open for 17% of the time, Pallas kernels for 11%

profile of v2, /device:TPU:0, one launch (start us, length us, event | category | flops | bytes accessed | tf_op | source)
XLA Modules:
  0.0 209.9 jit_solution(6592030340855473650)
XLA Ops:
  0.6 3.0 %collective-permute-start.4 = (bf16[256,2048]{1,0:T(8,128)(2,1)}, bf16[256,2048]{1,0:T(8,128)(2,1)}, u32[]{:S(2)}, u32[]{:S(2)}) collective-permute-start(bf16[256,2048]{1,0:T(8,128)(2,1)} %bitcast.113), channel_id=1, source_target_pairs={{0,4},{2,6},{4,0},{6,2},{8,12},{10,14},{12,8},{14,10},{16,20},{18,... | collective-permute-start | bytes 3145736 | tf_op jit(solution)/shard_map/ppermute | solution.py:23
  3.6 1.3 constant_dynamic-slice_fusion.16
  6.2 1.5 collective-permute-start.6
  7.7 19.4 %collective-permute-done.4 = bf16[256,2048]{1,0:T(8,128)(2,1)} collective-permute-done((bf16[256,2048]{1,0:T(8,128)(2,1)}, bf16[256,2048]{1,0:T(8,128)(2,1)}, u32[]{:S(2)}, u32[]{:S(2)}) %collective-permute-start.4) | collective-permute-done | bytes 1048608 | tf_op jit(solution)/shard_map/ppermute | solution.py:23
  27.8 3.4 %collective-permute-done.6 = bf16[1024,512]{1,0:T(8,128)(2,1)} collective-permute-done((bf16[1024,512]{1,0:T(8,128)(2,1)}, bf16[1024,512]{1,0:T(8,128)(2,1)}, u32[]{:S(2)}, u32[]{:S(2)}) %collective-permute-start.6) | collective-permute-done | bytes 1048608 | tf_op jit(solution)/shard_map/ppermute | solution.py:34
  31.1 1.3 constant_dynamic-update-slice_fusion.11
  32.5 1.3 constant_dynamic-update-slice_fusion.15
  33.8 1.3 constant_dynamic-update-slice_fusion.14
  36.5 3.5 %collective-permute-start.7 = (bf16[1024,256]{1,0:T(8,128)(2,1)S(1)}, bf16[1024,256]{1,0:T(8,128)(2,1)S(1)}, u32[]{:S(2)}, u32[]{:S(2)}) collective-permute-start(bf16[1024,256]{1,0:T(8,128)(2,1)S(1)} %convolution_convert_fusion.2.own_ref), channel_id=1, source_target_pairs={{0,8},{2,10},{4,12},{6,14},{8,16},{10,18},{12,20},{14,22},{16,24},... | collective-permute-start | bytes 1572872 | tf_op jit(solution)/shard_map/ppermute | solution.py:30
  40.3 9.8 %collective-permute-done.7.near_ref = bf16[1024,256]{1,0:T(8,128)(2,1)S(1)} collective-permute-done((bf16[1024,256]{1,0:T(8,128)(2,1)S(1)}, bf16[1024,256]{1,0:T(8,128)(2,1)S(1)}, u32[]{:S(2)}, u32[]{:S(2)}) %collective-permute-start.7) | collective-permute-done | bytes 524320 | tf_op jit(solution)/shard_map/ppermute | solution.py:30
  51.3 4.4 %collective-permute-start.9 = (bf16[1024,256]{1,0:T(8,128)(2,1)S(1)}, bf16[1024,256]{1,0:T(8,128)(2,1)S(1)}, u32[]{:S(2)}, u32[]{:S(2)}) collective-permute-start(bf16[1024,256]{1,0:T(8,128)(2,1)S(1)} %convolution_convert_fusion.1.own_ref), channel_id=1, source_target_pairs={{0,8},{2,10},{4,12},{6,14},{8,16},{10,18},{12,20},{14,22},{16,24},... | collective-permute-start | bytes 1572872 | tf_op jit(solution)/shard_map/ppermute | solution.py:30
  57.3 1.3 collective-permute-start.2
  58.6 4.2 %collective-permute-start.8 = (bf16[1024,256]{1,0:T(8,128)(2,1)S(1)}, bf16[1024,256]{1,0:T(8,128)(2,1)}, u32[]{:S(2)}, u32[]{:S(2)}) collective-permute-start(bf16[1024,256]{1,0:T(8,128)(2,1)S(1)} %collective-permute-done.7.near_ref), channel_id=1, source_target_pairs={{0,8},{2,10},{4,12},{6,14},{8,16},{10,18},{12,20},{14,22},{16,24},... | collective-permute-start | bytes 1572872 | tf_op jit(solution)/shard_map/ppermute | solution.py:30
  62.8 3.2 %constant_dynamic-slice_fusion = bf16[512,2048]{1,0:T(8,128)(2,1)} fusion(bf16[1024,2048]{1,0:T(8,128)(2,1)} %param.6, s32[]{:T(128)S(6)} %select_n.173), kind=kLoop, calls=%fused_computation.53 | loop fusion | bytes 4194308 | tf_op jit(solution)/shard_map/dynamic_slice | solution.py:231
  66.0 1.5 collective-permute-start.24
  69.5 2.7 %collective-permute-start.10 = (bf16[1024,256]{1,0:T(8,128)(2,1)S(1)}, bf16[1024,256]{1,0:T(8,128)(2,1)S(1)}, u32[]{:S(2)}, u32[]{:S(2)}) collective-permute-start(bf16[1024,256]{1,0:T(8,128)(2,1)S(1)} %collective-permute-done.9.near_ref), channel_id=1, source_target_pairs={{0,8},{2,10},{4,12},{6,14},{8,16},{10,18},{12,20},{14,22},{16,24},... | collective-permute-start | bytes 1572872 | tf_op jit(solution)/shard_map/ppermute | solution.py:30
  73.2 4.9 %collective-permute-done.8.far_ref = bf16[1024,256]{1,0:T(8,128)(2,1)} collective-permute-done((bf16[1024,256]{1,0:T(8,128)(2,1)S(1)}, bf16[1024,256]{1,0:T(8,128)(2,1)}, u32[]{:S(2)}, u32[]{:S(2)}) %collective-permute-start.8) | collective-permute-done | bytes 524320 | tf_op jit(solution)/shard_map/ppermute | solution.py:30
  78.2 12.3 %window_attention.2 = (bf16[2,1024,128]{2,1,0:T(8,128)(2,1)S(1)}, bf16[1024,256]{1,0:T(8,128)(2,1)S(1)}, f32[1024,256]{1,0:T(8,128)S(1)}, f32[1024,256]{1,0:T(8,128)S(1)}) custom-call(s32[1]{0:T(128)} %bitcast.row_ref, bf16[2,1024,256]{2,1,0:T(8,128)(2,1)S(1)} %constant_dynamic-update-slice_fusion.17.qu_ref, ...), custom_call_target="tpu_custom_call" | custom-call | flops 3623878656 | bytes 5242880 | tf_op jit(solution)/shard_map/window_attention/pallas_call | solution.py:135
  90.5 1.5 collective-permute-start.14
  92.1 11.3 %window_attention.3 = (bf16[2,1024,128]{2,1,0:T(8,128)(2,1)S(1)}, bf16[1024,256]{1,0:T(8,128)(2,1)S(1)}, f32[1024,256]{1,0:T(8,128)S(1)}, f32[1024,256]{1,0:T(8,128)S(1)}) custom-call(s32[1]{0:T(128)} %bitcast.row_ref, bf16[2,1024,256]{2,1,0:T(8,128)(2,1)S(1)} %constant_dynamic-update-slice_fusion.17.qu_ref, ...), custom_call_target="tpu_custom_call" | custom-call | flops 3623878656 | bytes 5242880 | tf_op jit(solution)/shard_map/window_attention/pallas_call | solution.py:135
  105.8 1.3 collective-permute-start.15
  107.1 1.3 collective-permute-start.19
  108.4 4.5 %collective-permute-done.12 = bf16[2,256,256]{2,1,0:T(8,128)(2,1)S(1)} collective-permute-done((bf16[2,256,256]{2,1,0:T(8,128)(2,1)S(1)}, bf16[2,256,256]{2,1,0:T(8,128)(2,1)S(1)}, u32[]{:S(2)}, u32[]{:S(2)}) %collective-permute-start.12) | collective-permute-done | bytes 262176 | tf_op jit(solution)/shard_map/ppermute | solution.py:23
  113.0 4.7 %collective-permute-done.13 = bf16[2,256,256]{2,1,0:T(8,128)(2,1)S(1)} collective-permute-done((bf16[2,256,256]{2,1,0:T(8,128)(2,1)S(1)}, bf16[2,256,256]{2,1,0:T(8,128)(2,1)S(1)}, u32[]{:S(2)}, u32[]{:S(2)}) %collective-permute-start.13) | collective-permute-done | bytes 262176 | tf_op jit(solution)/shard_map/ppermute | solution.py:23
  118.7 4.9 %collective-permute-done.15 = bf16[1024,256]{1,0:T(8,128)(2,1)S(1)} collective-permute-done((bf16[1024,256]{1,0:T(8,128)(2,1)S(1)}, bf16[1024,256]{1,0:T(8,128)(2,1)S(1)}, u32[]{:S(2)}, u32[]{:S(2)}) %collective-permute-start.15) | collective-permute-done | bytes 524320 | tf_op jit(solution)/shard_map/ppermute | solution.py:30
  123.8 1.3 fusion.12
  125.2 1.6 collective-permute-start.26
  128.0 6.5 %collective-permute-done.19 = bf16[1024,256]{1,0:T(8,128)(2,1)S(1)} collective-permute-done((bf16[1024,256]{1,0:T(8,128)(2,1)S(1)}, bf16[1024,256]{1,0:T(8,128)(2,1)S(1)}, u32[]{:S(2)}, u32[]{:S(2)}) %collective-permute-start.19) | collective-permute-done | bytes 524320 | tf_op jit(solution)/shard_map/ppermute | solution.py:30
  135.6 1.5 collective-permute-start.20
  138.1 2.2 %collective-permute-done.18 = bf16[256,256]{1,0:T(8,128)(2,1)S(1)} collective-permute-done((bf16[256,256]{1,0:T(8,128)(2,1)S(1)}, bf16[256,256]{1,0:T(8,128)(2,1)S(1)}, u32[]{:S(2)}, u32[]{:S(2)}) %collective-permute-start.18) | collective-permute-done | bytes 131104 | tf_op jit(solution)/shard_map/ppermute | solution.py:23
  140.4 1.5 bitcast_add_fusion.1
  142.7 2.0 collective-permute-start.27
  144.7 7.9 %collective-permute-done.20 = bf16[1024,256]{1,0:T(8,128)(2,1)} collective-permute-done((bf16[1024,256]{1,0:T(8,128)(2,1)}, bf16[1024,256]{1,0:T(8,128)(2,1)}, u32[]{:S(2)}, u32[]{:S(2)}) %collective-permute-start.20) | collective-permute-done | bytes 524320 | tf_op jit(solution)/shard_map/ppermute | solution.py:30
  153.8 2.7 %fusion.13 = f32[2048,256]{1,0:T(8,128)} fusion(bf16[1024,2048]{1,0:T(8,128)(2,1)S(1)} %copy-done.2, bf16[1024,256]{1,0:T(8,128)(2,1)S(1)} %add_convert_fusion), kind=kOutput, calls=%fused_computation.96 | convolution fusion | flops 1073741824 | bytes 6815744 | tf_op jit(solution)/shard_map/dot_general | solution.py:279
  156.7 1.5 collective-permute-start.22
  158.6 2.1 fusion.8
  160.7 1.5 collective-permute-start.32
  163.2 1.8 collective-permute-done.23
  165.5 1.9 copy-done.3
  167.4 1.3 fusion.1
  168.7 2.4 %fusion.3 = bf16[1,256,2048]{2,1,0:T(8,128)(2,1)S(1)} fusion(bf16[1,256,2048]{2,1,0:T(8,128)(2,1)S(1)} %fusion.1, s32[]{:T(128)S(6)} %select_n.174, bf16[256,2048]{0,1:T(8,128)(2,1)S(1)} %bitcast.116, bf16[512,2048]{1,0:T(8,128)(2,1)} %collective-permute-done.24), kind=kOutput, calls=%fused_computation.8 | convolution fusion | flops 537001984 | bytes 3407876 | tf_op jit(solution)/shard_map/dot_general | solution.py:260
  171.2 3.2 %collective-permute-start.28 = (bf16[1,256,256]{2,1,0:T(8,128)(2,1)S(1)}, bf16[1,256,256]{2,1,0:T(8,128)(2,1)S(1)}, u32[]{:S(2)}, u32[]{:S(2)}) collective-permute-start(bf16[1,256,256]{2,1,0:T(8,128)(2,1)S(1)} %dynamic-slice_convert_fusion.3), channel_id=1, source_target_pairs={{0,16},{2,18},{4,20},{6,22},{8,24},{10,26},{12,28},{14,30},{16,0},... | collective-permute-start | bytes 393224 | tf_op jit(solution)/shard_map/ppermute | solution.py:23
  174.4 2.4 %fusion.5 = bf16[1,256,2048]{2,1,0:T(8,128)(2,1)S(1)} fusion(bf16[1,256,2048]{2,1,0:T(8,128)(2,1)S(1)} %fusion.3, s32[]{:T(128)S(6)} %select_n.175, bf16[256,2048]{0,1:T(8,128)(2,1)S(1)} %bitcast.117, bf16[512,2048]{1,0:T(8,128)(2,1)} %collective-permute-done.25), kind=kOutput, calls=%fused_computation.10 | convolution fusion | flops 537001984 | bytes 3407876 | tf_op jit(solution)/shard_map/dot_general | solution.py:260
  176.8 4.8 %collective-permute-done.28 = bf16[1,256,256]{2,1,0:T(8,128)(2,1)S(1)} collective-permute-done((bf16[1,256,256]{2,1,0:T(8,128)(2,1)S(1)}, bf16[1,256,256]{2,1,0:T(8,128)(2,1)S(1)}, u32[]{:S(2)}, u32[]{:S(2)}) %collective-permute-start.28) | collective-permute-done | bytes 131104 | tf_op jit(solution)/shard_map/ppermute | solution.py:23
  185.0 1.6 collective-permute-done.30
  186.6 7.0 %collective-permute-done.33 = bf16[2,256,256]{2,1,0:T(8,128)(2,1)S(1)} collective-permute-done((bf16[2,256,256]{2,1,0:T(8,128)(2,1)S(1)}, bf16[2,256,256]{2,1,0:T(8,128)(2,1)S(1)}, u32[]{:S(2)}, u32[]{:S(2)}) %collective-permute-start.33) | collective-permute-done | bytes 262176 | tf_op jit(solution)/shard_map/ppermute | solution.py:23
  194.1 8.2 %collective-permute-done.34 = bf16[1,256,256]{2,1,0:T(8,128)(2,1)S(1)} collective-permute-done((bf16[1,256,256]{2,1,0:T(8,128)(2,1)S(1)}, bf16[1,256,256]{2,1,0:T(8,128)(2,1)S(1)}, u32[]{:S(2)}, u32[]{:S(2)}) %collective-permute-start.34) | collective-permute-done | bytes 131104 | tf_op jit(solution)/shard_map/ppermute | solution.py:23
  204.4 2.9 %collective-permute-done.36 = f32[64,256]{1,0:T(8,128)S(1)} collective-permute-done((f32[64,256]{1,0:T(8,128)S(1)}, f32[64,256]{1,0:T(8,128)S(1)}, u32[]{:S(2)}, u32[]{:S(2)}) %collective-permute-start.36) | collective-permute-done | bytes 65568 | tf_op jit(solution)/shard_map/ppermute | solution.py:23
  (137 shorter events, 28.8 us)
Async XLA Ops:
  0.6 26.5 %collective-permute-start.4 = (bf16[256,2048]{1,0:T(8,128)(2,1)}, bf16[256,2048]{1,0:T(8,128)(2,1)}, u32[]{:S(2)}, u32[]{:S(2)}) collective-permute-start(bf16[256,2048]{1,0:T(8,128)(2,1)} %bitcast.113), channel_id=1, source_target_pairs={{0,4},{2,6},{4,0},{6,2},{8,12},{10,14},{12,8},{14,10},{16,20},{18,... | collective-permute-start | bytes 3145736 | tf_op jit(solution)/shard_map/ppermute | solution.py:23
  5.1 2.6 %copy-start.6 = (bf16[1,256,2048]{2,1,0:T(8,128)(2,1)S(1)}, bf16[1,256,2048]{2,1,0:T(8,128)(2,1)}, u32[]{:S(2)}) copy-start(bf16[1,256,2048]{2,1,0:T(8,128)(2,1)} %param.4) | copy-start | bytes 3145732
  6.2 24.9 %collective-permute-start.6 = (bf16[1024,512]{1,0:T(8,128)(2,1)}, bf16[1024,512]{1,0:T(8,128)(2,1)}, u32[]{:S(2)}, u32[]{:S(2)}) collective-permute-start(bf16[1024,512]{1,0:T(8,128)(2,1)} %get-tuple-element.32), channel_id=1, source_target_pairs={{0,1},{1,0},{2,3},{3,2},{4,5},{5,4},{6,7},{7,6},{8,9},{9,8},{10,11... | collective-permute-start | bytes 3145736 | tf_op jit(solution)/shard_map/ppermute | solution.py:34
  7.7 24.7 %collective-permute-start.3 = (bf16[256,2048]{1,0:T(8,128)(2,1)S(1)}, bf16[256,2048]{1,0:T(8,128)(2,1)}, u32[]{:S(2)}, u32[]{:S(2)}) collective-permute-start(bf16[256,2048]{1,0:T(8,128)(2,1)S(1)} %bitcast.114), channel_id=1, source_target_pairs={{0,2},{2,0},{4,6},{6,4},{8,10},{10,8},{12,14},{14,12},{16,18},{18,... | collective-permute-start | bytes 3145736 | tf_op jit(solution)/shard_map/ppermute | solution.py:23
  27.1 8.0 %collective-permute-start.5 = (bf16[256,2048]{1,0:T(8,128)(2,1)}, bf16[256,2048]{1,0:T(8,128)(2,1)S(1)}, u32[]{:S(2)}, u32[]{:S(2)}) collective-permute-start(bf16[256,2048]{1,0:T(8,128)(2,1)} %collective-permute-done.4), channel_id=1, source_target_pairs={{0,2},{2,0},{4,6},{6,4},{8,10},{10,8},{12,14},{14,12},{16,18},{18,... | collective-permute-start | bytes 3145736 | tf_op jit(solution)/shard_map/ppermute | solution.py:23
  35.3 14.8 %copy-start = (bf16[1024,2048]{1,0:T(8,128)(2,1)}, bf16[1024,2048]{1,0:T(8,128)(2,1)S(1)}, u32[]{:S(2)}) copy-start(bf16[1024,2048]{1,0:T(8,128)(2,1)S(1)} %constant_dynamic-update-slice_fusion.13) | copy-start | bytes 12582916
  35.3 4.8 %copy-start.8 = (bf16[1,256,1024]{2,1,0:T(8,128)(2,1)S(1)}, bf16[1,256,1024]{2,1,0:T(8,128)(2,1)}, u32[]{:S(2)}) copy-start(bf16[1,256,1024]{2,1,0:T(8,128)(2,1)} %param.5) | copy-start | bytes 1572868
  35.3 4.8 %copy-start.9 = (bf16[1,256,1024]{2,1,0:T(8,128)(2,1)S(1)}, bf16[1,256,1024]{2,1,0:T(8,128)(2,1)}, u32[]{:S(2)}) copy-start(bf16[1,256,1024]{2,1,0:T(8,128)(2,1)} %param.7) | copy-start | bytes 1572868
  36.5 13.5 %collective-permute-start.7 = (bf16[1024,256]{1,0:T(8,128)(2,1)S(1)}, bf16[1024,256]{1,0:T(8,128)(2,1)S(1)}, u32[]{:S(2)}, u32[]{:S(2)}) collective-permute-start(bf16[1024,256]{1,0:T(8,128)(2,1)S(1)} %convolution_convert_fusion.2.own_ref), channel_id=1, source_target_pairs={{0,8},{2,10},{4,12},{6,14},{8,16},{10,18},{12,20},{14,22},{16,24},... | collective-permute-start | bytes 1572872 | tf_op jit(solution)/shard_map/ppermute | solution.py:30
  51.3 18.2 %collective-permute-start.9 = (bf16[1024,256]{1,0:T(8,128)(2,1)S(1)}, bf16[1024,256]{1,0:T(8,128)(2,1)S(1)}, u32[]{:S(2)}, u32[]{:S(2)}) collective-permute-start(bf16[1024,256]{1,0:T(8,128)(2,1)S(1)} %convolution_convert_fusion.1.own_ref), channel_id=1, source_target_pairs={{0,8},{2,10},{4,12},{6,14},{8,16},{10,18},{12,20},{14,22},{16,24},... | collective-permute-start | bytes 1572872 | tf_op jit(solution)/shard_map/ppermute | solution.py:30
  56.7 9.3 %collective-permute-start = (bf16[2,256,256]{2,1,0:T(8,128)(2,1)}, bf16[2,256,256]{2,1,0:T(8,128)(2,1)}, u32[]{:S(2)}, u32[]{:S(2)}) collective-permute-start(bf16[2,256,256]{2,1,0:T(8,128)(2,1)} %get-tuple-element.36), channel_id=1, source_target_pairs={{0,2},{2,0},{4,6},{6,4},{8,10},{10,8},{12,14},{14,12},{16,18},{18,... | collective-permute-start | bytes 786440 | tf_op jit(solution)/shard_map/ppermute | solution.py:23
  56.7 11.8 %collective-permute-start.1 = (bf16[2,256,256]{2,1,0:T(8,128)(2,1)}, bf16[2,256,256]{2,1,0:T(8,128)(2,1)}, u32[]{:S(2)}, u32[]{:S(2)}) collective-permute-start(bf16[2,256,256]{2,1,0:T(8,128)(2,1)} %get-tuple-element.35), channel_id=1, source_target_pairs={{0,4},{2,6},{4,0},{6,2},{8,12},{10,14},{12,8},{14,10},{16,20},{18,... | collective-permute-start | bytes 786440 | tf_op jit(solution)/shard_map/ppermute | solution.py:23
  57.3 15.0 %collective-permute-start.2 = (bf16[2,256,256]{2,1,0:T(8,128)(2,1)S(1)}, bf16[2,256,256]{2,1,0:T(8,128)(2,1)}, u32[]{:S(2)}, u32[]{:S(2)}) collective-permute-start(bf16[2,256,256]{2,1,0:T(8,128)(2,1)S(1)} %get-tuple-element.34), channel_id=1, source_target_pairs={{0,6},{2,4},{4,2},{6,0},{8,14},{10,12},{12,10},{14,8},{16,22},{18,... | collective-permute-start | bytes 786440 | tf_op jit(solution)/shard_map/ppermute | solution.py:23
  58.6 19.6 %collective-permute-start.8 = (bf16[1024,256]{1,0:T(8,128)(2,1)S(1)}, bf16[1024,256]{1,0:T(8,128)(2,1)}, u32[]{:S(2)}, u32[]{:S(2)}) collective-permute-start(bf16[1024,256]{1,0:T(8,128)(2,1)S(1)} %collective-permute-done.7.near_ref), channel_id=1, source_target_pairs={{0,8},{2,10},{4,12},{6,14},{8,16},{10,18},{12,20},{14,22},{16,24},... | collective-permute-start | bytes 1572872 | tf_op jit(solution)/shard_map/ppermute | solution.py:30
  66.0 69.5 %collective-permute-start.24 = (bf16[512,2048]{1,0:T(8,128)(2,1)}, bf16[512,2048]{1,0:T(8,128)(2,1)}, u32[]{:S(2)}, u32[]{:S(2)}) collective-permute-start(bf16[512,2048]{1,0:T(8,128)(2,1)} %constant_dynamic-slice_fusion), channel_id=1, source_target_pairs={{0,1},{1,0},{2,3},{3,2},{4,5},{5,4},{6,7},{7,6},{8,9},{9,8},{10,11... | collective-permute-start | bytes 6291464 | tf_op jit(solution)/shard_map/ppermute | solution.py:34
  69.5 22.5 %collective-permute-start.10 = (bf16[1024,256]{1,0:T(8,128)(2,1)S(1)}, bf16[1024,256]{1,0:T(8,128)(2,1)S(1)}, u32[]{:S(2)}, u32[]{:S(2)}) collective-permute-start(bf16[1024,256]{1,0:T(8,128)(2,1)S(1)} %collective-permute-done.9.near_ref), channel_id=1, source_target_pairs={{0,8},{2,10},{4,12},{6,14},{8,16},{10,18},{12,20},{14,22},{16,24},... | collective-permute-start | bytes 1572872 | tf_op jit(solution)/shard_map/ppermute | solution.py:30
  90.5 15.2 %collective-permute-start.14 = (bf16[1024,256]{1,0:T(8,128)(2,1)S(1)}, bf16[1024,256]{1,0:T(8,128)(2,1)S(1)}, u32[]{:S(2)}, u32[]{:S(2)}) collective-permute-start(bf16[1024,256]{1,0:T(8,128)(2,1)S(1)} %get-tuple-element.18), channel_id=1, source_target_pairs={{8,0},{10,2},{12,4},{14,6},{16,8},{18,10},{20,12},{22,14},{24,16},... | collective-permute-start | bytes 1572872 | tf_op jit(solution)/shard_map/ppermute | solution.py:30
  103.7 3.4 %collective-permute-start.11 = (bf16[2,256,256]{2,1,0:T(8,128)(2,1)S(1)}, bf16[2,256,256]{2,1,0:T(8,128)(2,1)S(1)}, u32[]{:S(2)}, u32[]{:S(2)}) collective-permute-start(bf16[2,256,256]{2,1,0:T(8,128)(2,1)S(1)} %get-tuple-element.30), channel_id=1, source_target_pairs={{0,2},{2,0},{4,6},{6,4},{8,10},{10,8},{12,14},{14,12},{16,18},{18,... | collective-permute-start | bytes 786440 | tf_op jit(solution)/shard_map/ppermute | solution.py:23
  103.8 9.2 %collective-permute-start.12 = (bf16[2,256,256]{2,1,0:T(8,128)(2,1)S(1)}, bf16[2,256,256]{2,1,0:T(8,128)(2,1)S(1)}, u32[]{:S(2)}, u32[]{:S(2)}) collective-permute-start(bf16[2,256,256]{2,1,0:T(8,128)(2,1)S(1)} %get-tuple-element.29), channel_id=1, source_target_pairs={{0,4},{2,6},{4,0},{6,2},{8,12},{10,14},{12,8},{14,10},{16,20},{18,... | collective-permute-start | bytes 786440 | tf_op jit(solution)/shard_map/ppermute | solution.py:23
  104.4 13.3 %collective-permute-start.13 = (bf16[2,256,256]{2,1,0:T(8,128)(2,1)S(1)}, bf16[2,256,256]{2,1,0:T(8,128)(2,1)S(1)}, u32[]{:S(2)}, u32[]{:S(2)}) collective-permute-start(bf16[2,256,256]{2,1,0:T(8,128)(2,1)S(1)} %get-tuple-element.28), channel_id=1, source_target_pairs={{0,6},{2,4},{4,2},{6,0},{8,14},{10,12},{12,10},{14,8},{16,22},{18,... | collective-permute-start | bytes 786440 | tf_op jit(solution)/shard_map/ppermute | solution.py:23
  105.8 17.9 %collective-permute-start.15 = (bf16[1024,256]{1,0:T(8,128)(2,1)S(1)}, bf16[1024,256]{1,0:T(8,128)(2,1)S(1)}, u32[]{:S(2)}, u32[]{:S(2)}) collective-permute-start(bf16[1024,256]{1,0:T(8,128)(2,1)S(1)} %add_convert_fusion.3), channel_id=1, source_target_pairs={{8,0},{10,2},{12,4},{14,6},{16,8},{18,10},{20,12},{22,14},{24,16},... | collective-permute-start | bytes 1572872 | tf_op jit(solution)/shard_map/ppermute | solution.py:30
  107.1 27.5 %collective-permute-start.19 = (bf16[1024,256]{1,0:T(8,128)(2,1)S(1)}, bf16[1024,256]{1,0:T(8,128)(2,1)S(1)}, u32[]{:S(2)}, u32[]{:S(2)}) collective-permute-start(bf16[1024,256]{1,0:T(8,128)(2,1)S(1)} %get-tuple-element.21), channel_id=1, source_target_pairs={{8,0},{10,2},{12,4},{14,6},{16,8},{18,10},{20,12},{22,14},{24,16},... | collective-permute-start | bytes 1572872 | tf_op jit(solution)/shard_map/ppermute | solution.py:30
  117.7 6.1 %copy-start.1 = (bf16[1024,2048]{1,0:T(8,128)(2,1)S(1)}, bf16[1024,2048]{1,0:T(8,128)(2,1)}, u32[]{:S(2)}) copy-start(bf16[1024,2048]{1,0:T(8,128)(2,1)} %copy-done) | copy-start | bytes 12582916
  125.1 10.3 %copy-start.5 = (f32[2048,256]{1,0:T(8,128)}, f32[2048,256]{1,0:T(8,128)S(1)}, u32[]{:S(2)}) copy-start(f32[2048,256]{1,0:T(8,128)S(1)} %fusion.12) | copy-start | bytes 6291460
  125.2 15.2 %collective-permute-start.26 = (bf16[1,1024,256]{2,1,0:T(8,128)(2,1)S(1)}, bf16[1,1024,256]{2,1,0:T(8,128)(2,1)S(1)}, u32[]{:S(2)}, u32[]{:S(2)}) collective-permute-start(bf16[1,1024,256]{2,1,0:T(8,128)(2,1)S(1)} %fusion.7), channel_id=1, source_target_pairs={{0,1},{1,0},{2,3},{3,2},{4,5},{5,4},{6,7},{7,6},{8,9},{9,8},{10,11... | collective-permute-start | bytes 1572872 | tf_op jit(solution)/shard_map/ppermute | solution.py:34
  127.5 9.7 %collective-permute-start.16 = (bf16[256,256]{1,0:T(8,128)(2,1)}, bf16[256,256]{1,0:T(8,128)(2,1)S(1)}, u32[]{:S(2)}, u32[]{:S(2)}) collective-permute-start(bf16[256,256]{1,0:T(8,128)(2,1)} %get-tuple-element.40), channel_id=1, source_target_pairs={{0,2},{2,0},{4,6},{6,4},{8,10},{10,8},{12,14},{14,12},{16,18},{18,... | collective-permute-start | bytes 393224 | tf_op jit(solution)/shard_map/ppermute | solution.py:23
  127.5 10.5 %collective-permute-start.17 = (bf16[256,256]{1,0:T(8,128)(2,1)S(1)}, bf16[256,256]{1,0:T(8,128)(2,1)S(1)}, u32[]{:S(2)}, u32[]{:S(2)}) collective-permute-start(bf16[256,256]{1,0:T(8,128)(2,1)S(1)} %get-tuple-element.39), channel_id=1, source_target_pairs={{0,4},{2,6},{4,0},{6,2},{8,12},{10,14},{12,8},{14,10},{16,20},{18,... | collective-permute-start | bytes 393224 | tf_op jit(solution)/shard_map/ppermute | solution.py:23
  134.5 5.7 %collective-permute-start.18 = (bf16[256,256]{1,0:T(8,128)(2,1)S(1)}, bf16[256,256]{1,0:T(8,128)(2,1)S(1)}, u32[]{:S(2)}, u32[]{:S(2)}) collective-permute-start(bf16[256,256]{1,0:T(8,128)(2,1)S(1)} %get-tuple-element.38), channel_id=1, source_target_pairs={{0,6},{2,4},{4,2},{6,0},{8,14},{10,12},{12,10},{14,8},{16,22},{18,... | collective-permute-start | bytes 393224 | tf_op jit(solution)/shard_map/ppermute | solution.py:23
  135.6 17.0 %collective-permute-start.20 = (bf16[1024,256]{1,0:T(8,128)(2,1)}, bf16[1024,256]{1,0:T(8,128)(2,1)}, u32[]{:S(2)}, u32[]{:S(2)}) collective-permute-start(bf16[1024,256]{1,0:T(8,128)(2,1)} %add_convert_fusion.1), channel_id=1, source_target_pairs={{8,0},{10,2},{12,4},{14,6},{16,8},{18,10},{20,12},{22,14},{24,16},... | collective-permute-start | bytes 1572872 | tf_op jit(solution)/shard_map/ppermute | solution.py:30
  137.2 37.2 %collective-permute-start.25 = (bf16[512,2048]{1,0:T(8,128)(2,1)}, bf16[512,2048]{1,0:T(8,128)(2,1)}, u32[]{:S(2)}, u32[]{:S(2)}) collective-permute-start(bf16[512,2048]{1,0:T(8,128)(2,1)} %collective-permute-done.24), channel_id=1, source_target_pairs={{0,2},{2,0},{4,6},{6,4},{8,10},{10,8},{12,14},{14,12},{16,18},{18,... | collective-permute-start | bytes 6291464 | tf_op jit(solution)/shard_map/ppermute | solution.py:23
  140.4 13.3 %copy-start.2 = (bf16[1024,2048]{1,0:T(8,128)(2,1)S(1)}, bf16[1024,2048]{1,0:T(8,128)(2,1)}, u32[]{:S(2)}) copy-start(bf16[1024,2048]{1,0:T(8,128)(2,1)} %copy-done) | copy-start | bytes 12582916
  142.7 28.4 %collective-permute-start.27 = (bf16[2,256,256]{2,1,0:T(8,128)(2,1)}, bf16[2,256,256]{2,1,0:T(8,128)(2,1)S(1)}, u32[]{:S(2)}, u32[]{:S(2)}) collective-permute-start(bf16[2,256,256]{2,1,0:T(8,128)(2,1)} %fusion.9), channel_id=1, source_target_pairs={{0,8},{2,10},{4,12},{6,14},{8,0},{10,2},{12,4},{14,6},{16,24},{18,... | collective-permute-start | bytes 786440 | tf_op jit(solution)/shard_map/ppermute | solution.py:23
  156.6 4.1 %collective-permute-start.21 = (bf16[256,256]{1,0:T(8,128)(2,1)S(1)}, bf16[256,256]{1,0:T(8,128)(2,1)S(1)}, u32[]{:S(2)}, u32[]{:S(2)}) collective-permute-start(bf16[256,256]{1,0:T(8,128)(2,1)S(1)} %get-tuple-element.44), channel_id=1, source_target_pairs={{0,2},{2,0},{4,6},{6,4},{8,10},{10,8},{12,14},{14,12},{16,18},{18,... | collective-permute-start | bytes 393224 | tf_op jit(solution)/shard_map/ppermute | solution.py:23
  156.7 6.3 %collective-permute-start.22 = (bf16[256,256]{1,0:T(8,128)(2,1)S(1)}, bf16[256,256]{1,0:T(8,128)(2,1)S(1)}, u32[]{:S(2)}, u32[]{:S(2)}) collective-permute-start(bf16[256,256]{1,0:T(8,128)(2,1)S(1)} %get-tuple-element.43), channel_id=1, source_target_pairs={{0,4},{2,6},{4,0},{6,2},{8,12},{10,14},{12,8},{14,10},{16,20},{18,... | collective-permute-start | bytes 393224 | tf_op jit(solution)/shard_map/ppermute | solution.py:23
  158.2 6.7 %collective-permute-start.23 = (bf16[256,256]{1,0:T(8,128)(2,1)S(1)}, bf16[256,256]{1,0:T(8,128)(2,1)S(1)}, u32[]{:S(2)}, u32[]{:S(2)}) collective-permute-start(bf16[256,256]{1,0:T(8,128)(2,1)S(1)} %get-tuple-element.42), channel_id=1, source_target_pairs={{0,6},{2,4},{4,2},{6,0},{8,14},{10,12},{12,10},{14,8},{16,22},{18,... | collective-permute-start | bytes 393224 | tf_op jit(solution)/shard_map/ppermute | solution.py:23
  160.7 22.9 %collective-permute-start.32 = (bf16[1,1024,256]{2,1,0:T(8,128)(2,1)}, bf16[1,1024,256]{2,1,0:T(8,128)(2,1)}, u32[]{:S(2)}, u32[]{:S(2)}) collective-permute-start(bf16[1,1024,256]{2,1,0:T(8,128)(2,1)} %fusion.8), channel_id=1, source_target_pairs={{0,1},{1,0},{2,3},{3,2},{4,5},{5,4},{6,7},{7,6},{8,9},{9,8},{10,11... | collective-permute-start | bytes 1572872 | tf_op jit(solution)/shard_map/ppermute | solution.py:34
  165.2 2.2 %copy-start.3 = (bf16[1024,2048]{1,0:T(8,128)(2,1)S(1)}, bf16[1024,2048]{1,0:T(8,128)(2,1)}, u32[]{:S(2)}) copy-start(bf16[1024,2048]{1,0:T(8,128)(2,1)} %param.6) | copy-start | bytes 12582916
  171.2 12.5 %copy-start.4 = (f32[2048,256]{1,0:T(8,128)S(1)}, f32[2048,256]{1,0:T(8,128)}, u32[]{:S(2)}) copy-start(f32[2048,256]{1,0:T(8,128)} %fusion.13) | copy-start | bytes 6291460
  171.2 10.4 %collective-permute-start.28 = (bf16[1,256,256]{2,1,0:T(8,128)(2,1)S(1)}, bf16[1,256,256]{2,1,0:T(8,128)(2,1)S(1)}, u32[]{:S(2)}, u32[]{:S(2)}) collective-permute-start(bf16[1,256,256]{2,1,0:T(8,128)(2,1)S(1)} %dynamic-slice_convert_fusion.3), channel_id=1, source_target_pairs={{0,16},{2,18},{4,20},{6,22},{8,24},{10,26},{12,28},{14,30},{16,0},... | collective-permute-start | bytes 393224 | tf_op jit(solution)/shard_map/ppermute | solution.py:23
  176.8 8.1 %copy-start.7 = (bf16[1,256,2048]{2,1,0:T(8,128)(2,1)}, bf16[1,256,2048]{2,1,0:T(8,128)(2,1)S(1)}, u32[]{:S(2)}) copy-start(bf16[1,256,2048]{2,1,0:T(8,128)(2,1)S(1)} %fusion.5) | copy-start | bytes 3145732
  181.6 3.3 %collective-permute-start.29 = (f32[64,256]{1,0:T(8,128)S(1)}, f32[64,256]{1,0:T(8,128)S(1)}, u32[]{:S(2)}, u32[]{:S(2)}) collective-permute-start(f32[64,256]{1,0:T(8,128)S(1)} %get-tuple-element.48), channel_id=1, source_target_pairs={{0,2},{2,0},{4,6},{6,4},{8,10},{10,8},{12,14},{14,12},{16,18},{18,... | collective-permute-start | bytes 196616 | tf_op jit(solution)/shard_map/ppermute | solution.py:23
  181.8 4.8 %collective-permute-start.30 = (f32[64,256]{1,0:T(8,128)S(1)}, f32[64,256]{1,0:T(8,128)S(1)}, u32[]{:S(2)}, u32[]{:S(2)}) collective-permute-start(f32[64,256]{1,0:T(8,128)S(1)} %get-tuple-element.47), channel_id=1, source_target_pairs={{0,4},{2,6},{4,0},{6,2},{8,12},{10,14},{12,8},{14,10},{16,20},{18,... | collective-permute-start | bytes 196616 | tf_op jit(solution)/shard_map/ppermute | solution.py:23
  183.0 11.1 %collective-permute-start.31 = (f32[64,256]{1,0:T(8,128)S(1)}, f32[64,256]{1,0:T(8,128)S(1)}, u32[]{:S(2)}, u32[]{:S(2)}) collective-permute-start(f32[64,256]{1,0:T(8,128)S(1)} %get-tuple-element.46), channel_id=1, source_target_pairs={{0,6},{2,4},{4,2},{6,0},{8,14},{10,12},{12,10},{14,8},{16,22},{18,... | collective-permute-start | bytes 196616 | tf_op jit(solution)/shard_map/ppermute | solution.py:23
  184.9 8.6 %collective-permute-start.33 = (bf16[2,256,256]{2,1,0:T(8,128)(2,1)S(1)}, bf16[2,256,256]{2,1,0:T(8,128)(2,1)S(1)}, u32[]{:S(2)}, u32[]{:S(2)}) collective-permute-start(bf16[2,256,256]{2,1,0:T(8,128)(2,1)S(1)} %fusion.10), channel_id=1, source_target_pairs={{0,8},{2,10},{4,12},{6,14},{8,0},{10,2},{12,4},{14,6},{16,24},{18,... | collective-permute-start | bytes 786440 | tf_op jit(solution)/shard_map/ppermute | solution.py:23
  193.6 8.7 %collective-permute-start.34 = (bf16[1,256,256]{2,1,0:T(8,128)(2,1)S(1)}, bf16[1,256,256]{2,1,0:T(8,128)(2,1)S(1)}, u32[]{:S(2)}, u32[]{:S(2)}) collective-permute-start(bf16[1,256,256]{2,1,0:T(8,128)(2,1)S(1)} %dynamic-slice_convert_fusion.2), channel_id=1, source_target_pairs={{0,16},{2,18},{4,20},{6,22},{8,24},{10,26},{12,28},{14,30},{16,0},... | collective-permute-start | bytes 393224 | tf_op jit(solution)/shard_map/ppermute | solution.py:23
  202.3 2.0 collective-permute-start.35
  202.4 4.9 %collective-permute-start.36 = (f32[64,256]{1,0:T(8,128)S(1)}, f32[64,256]{1,0:T(8,128)S(1)}, u32[]{:S(2)}, u32[]{:S(2)}) collective-permute-start(f32[64,256]{1,0:T(8,128)S(1)} %get-tuple-element.50), channel_id=1, source_target_pairs={{0,4},{2,6},{4,0},{6,2},{8,12},{10,14},{12,8},{14,10},{16,20},{18,... | collective-permute-start | bytes 196616 | tf_op jit(solution)/shard_map/ppermute | solution.py:23
  203.6 4.3 %collective-permute-start.37 = (f32[64,256]{1,0:T(8,128)S(1)}, f32[64,256]{1,0:T(8,128)S(1)}, u32[]{:S(2)}, u32[]{:S(2)}) collective-permute-start(f32[64,256]{1,0:T(8,128)S(1)} %get-tuple-element.49), channel_id=1, source_target_pairs={{0,6},{2,4},{4,2},{6,0},{8,14},{10,12},{12,10},{14,8},{16,22},{18,... | collective-permute-start | bytes 196616 | tf_op jit(solution)/shard_map/ppermute | solution.py:23

commit v3 on v0

v3 whole, which is shorter than its diff:
```python
import functools
import math

import jax
import jax.numpy as jnp
from jax import lax
from jax.experimental import pallas as pl
from jax.experimental.pallas import tpu as pltpu
from jax.sharding import PartitionSpec as P

HEAD_DIM = 128
WINDOW = 2048
LANES = 4
VMEM_GRANT = 24 * 2**20
SCORE_SCALE = 1.0 / math.sqrt(HEAD_DIM)
EXP2_SCALE = SCORE_SCALE * math.log2(math.e)
MASKED = -1e30
MINOR_DIMS = (((1,), (1,)), ((), ()))
MAJOR_DIMS = (((0,), (0,)), ((), ()))


def exchanged(value, bits):
    count = lax.axis_size("seq")
    return lax.ppermute(value, "seq", [(source, source ^ bits) for source in range(count)])


def shifted(value, rows):
    count = lax.axis_size("seq")
    steps = rows * LANES
    leading, last = (max(0, -steps), min(count, count - steps))
    return lax.ppermute(value, "seq", [(source, source + steps) for source in range(leading, last)])


def turned_round(value, rows):
    count = lax.axis_size("seq")
    pairs = [(source, (source + rows * LANES) % count) for source in range(count)]
    return lax.ppermute(value, "seq", pairs)


def moved(value, bits, across):
    count = lax.axis_size("seq")
    pairs = [
        (2 * place + side, 2 * (place ^ bits) + (side ^ across))
        for place in range(count)
        for side in range(2)
    ]
    return lax.ppermute(value, ("seq", "dp"), pairs)


def swapped(value):
    return lax.ppermute(value, "dp", [(0, 1), (1, 0)])


def by_sublane(block, reduce):
    return reduce(block.reshape(block.shape[0] // 8, 8, block.shape[1]), axis=0)


def product(left, right):
    return jnp.dot(left, right, preferred_element_type=jnp.float32)


def product_minor(left, right):
    return lax.dot_general(left, right, MINOR_DIMS, preferred_element_type=jnp.float32)


def take_kernel(_, weight_ref, out_ref):
    out_ref[...] = weight_ref[...]


def take_columns(at, weight, waits):
    depth, width = weight.shape
    columns = width // HEAD_DIM
    heads = columns // 2 // LANES

    def source(index, at_ref):
        return (0, index % 2 * (columns // 2) + at_ref[0] * heads + index // 2)

    return pl.pallas_call(
        ordered(take_kernel, 1, len(waits), 1, 0),
        grid_spec=pltpu.PrefetchScalarGridSpec(
            num_scalar_prefetch=1,
            grid=(2 * heads,),
            in_specs=[pl.BlockSpec((depth, HEAD_DIM), source)]
            + [pl.BlockSpec(memory_space=pl.ANY)] * len(waits),
            out_specs=pl.BlockSpec((depth, HEAD_DIM), lambda index, _: (0, index)),
        ),
        out_shape=jax.ShapeDtypeStruct((depth, 2 * heads * HEAD_DIM), weight.dtype),
        compiler_params=pltpu.CompilerParams(vmem_limit_bytes=VMEM_GRANT),
        cost_estimate=time_estimate(1),
        name="take_columns",
    )(at, weight, *waits)


def project_kernel(at_ref, *refs, heads):
    tokens, here_ref, there_ref, outs = refs[:LANES], refs[LANES], refs[LANES + 1], refs[-heads:]
    lane, half = at_ref[0], at_ref[1]
    depth = here_ref.shape[0]
    for bits, piece in enumerate(tokens):
        here = piece[:, at_offset(half, depth)]
        there = piece[:, at_offset(1 - half, depth)]
        whole = product(here, here_ref[...]) + product(there, there_ref[...])
        held = at_offset(lane ^ bits, piece.shape[0])
        width = whole.shape[1] // heads
        for head, out in enumerate(outs):
            out[held] = whole[:, head * width : (head + 1) * width].astype(jnp.bfloat16)


def project(at, tokens, weights):
    heads = weights[0].shape[1] // (2 * HEAD_DIM)
    whole = jax.ShapeDtypeStruct((LANES * tokens[0].shape[0], 2 * HEAD_DIM), jnp.bfloat16)
    return small_call(
        functools.partial(project_kernel, heads=heads),
        "project", at, (*tokens, *weights), [whole] * heads, cost=4,
    )


def visits(blocks):
    for turn in range(blocks):
        whole = [(1, lane, None) for lane in range(blocks)]
        yield 0, turn, whole + [(0, lane, "low" if lane == turn else None) for lane in range(turn + 1)]
        yield 1, turn, [(1, lane, "high" if lane == turn else None) for lane in range(turn, blocks)]


def masked(score, near, edge, near_bias):
    if edge:
        key_pos = lax.broadcasted_iota(jnp.int32, score.shape, 0)
        query_pos = lax.broadcasted_iota(jnp.int32, score.shape, 1)
        allowed = key_pos <= query_pos if edge == "low" else key_pos > query_pos
        score = jnp.where(allowed, score, MASKED)
    return score + near_bias if near else score


def stats_kernel(
    at_ref, own_pair, next_pair, own_ref, near_ref, own_out, next_out, scores, *, blocks, size
):
    near_bias = jnp.where(at_ref[0] > 0, 0.0, MASKED)
    window = (own_ref, near_ref)
    pairs = (own_pair, next_pair)
    outs = (own_out, next_out)
    for turn, (side, block, keys) in enumerate(visits(blocks)):
        held = slice(block * size, (block + 1) * size)
        peak = jnp.full((8, size), MASKED, jnp.float32)
        for index, (near, lane, edge) in enumerate(keys):
            key = window[near][lane * size : (lane + 1) * size, :HEAD_DIM]
            score = masked(product_minor(key, pairs[side][0, held]), near, edge, near_bias)
            scores[turn % 2, index] = score
            peak = jnp.maximum(peak, by_sublane(score, jnp.max))
        peak = jnp.max(peak, axis=0, keepdims=True)
        mass = jnp.zeros((8, size), jnp.float32)
        pull = jnp.zeros((8, size), jnp.float32)
        for index, (near, lane, edge) in enumerate(keys):
            value = window[near][lane * size : (lane + 1) * size, HEAD_DIM:]
            grown = jnp.exp2((scores[turn % 2, index] - peak) * EXP2_SCALE)
            mass = mass + by_sublane(grown, jnp.sum)
            pull = pull + by_sublane(grown * product_minor(value, pairs[side][1, held]), jnp.sum)
        out = outs[side]
        out[0:1, held] = peak
        out[1:2, held] = jnp.sum(mass, axis=0, keepdims=True)
        out[2:3, held] = jnp.sum(pull, axis=0, keepdims=True)
        out[3:, held] = jnp.zeros((5, size), jnp.float32)


def settled(here, there, there_valid):
    here_peak = here[0:1]
    there_peak = jnp.where(there_valid, there[0:1], MASKED)
    peak = jnp.maximum(here_peak, there_peak)
    here_factor = jnp.exp2((here_peak - peak) * EXP2_SCALE)
    there_factor = jnp.exp2((there_peak - peak) * EXP2_SCALE)
    mass = here[1:2] * here_factor + there[1:2] * there_factor
    pull = here[2:3] * here_factor + there[2:3] * there_factor
    share = jnp.where(mass > 0, 1.0 / mass, 0.0)
    return peak, share, pull * share


def gradient_kernel(
    at_ref, own_pair, next_pair, own_ref, near_ref,
    own_stats, far_stats, next_stats, main_stats,
    own_out, next_out, near_grad, own_grad,
    turned, queries, cotangents, own_weights, own_dscores, near_weights, near_dscores,
    *, blocks, size,
):
    near_valid = at_ref[0] > 0
    near_bias = jnp.where(near_valid, 0.0, MASKED)
    window = (own_ref, near_ref)
    row_tokens = blocks * size
    pairs = (own_pair, next_pair)
    outs = (own_out, next_out)
    weights = (own_weights, near_weights)
    dscores = (own_dscores, near_dscores)
    figures = (
        settled(own_stats[...], far_stats[...], near_valid),
        settled(next_stats[...], main_stats[...], True),
    )
    for side in range(2):
        queries[side * row_tokens : (side + 1) * row_tokens] = pairs[side][0]
        cotangents[side * row_tokens : (side + 1) * row_tokens] = pairs[side][1]
        for block in range(blocks):
            held = slice(block * size, (block + 1) * size)
            turned[side, :, held] = window[side][held].T
    for side, block, keys in visits(blocks):
        held = slice(block * size, (block + 1) * size)
        column = slice(side * row_tokens + block * size, side * row_tokens + (block + 1) * size)
        peak, share, centre = (figure[:, held] for figure in figures[side])
        scaled = share * SCORE_SCALE
        for near, lane, edge in keys:
            rows = slice(lane * size, (lane + 1) * size)
            score = product_minor(window[near][rows, :HEAD_DIM], pairs[side][0, held])
            dprob = product_minor(window[near][rows, HEAD_DIM:], pairs[side][1, held])
            grown = jnp.exp2((masked(score, near, edge, near_bias) - peak) * EXP2_SCALE)
            weights[near][rows, column] = (grown * share).astype(jnp.bfloat16)
            dscores[near][rows, column] = (grown * ((dprob - centre) * scaled)).astype(jnp.bfloat16)
        rows = slice(block * size if side else 0, row_tokens)
        attended = product(turned[1, HEAD_DIM:, rows], near_weights[rows, column])
        query_grad = product(turned[1, :HEAD_DIM, rows], near_dscores[rows, column])
        if not side:
            rows = slice(0, (block + 1) * size)
            attended += product(turned[0, HEAD_DIM:, rows], own_weights[rows, column])
            query_grad += product(turned[0, :HEAD_DIM, rows], own_dscores[rows, column])
        outs[side][0, held] = attended.T.astype(outs[side].dtype)
        outs[side][1, held] = query_grad.T.astype(outs[side].dtype)
    for lane in range(blocks):
        rows = slice(lane * size, (lane + 1) * size)
        met = slice(0, row_tokens + (lane + 1) * size)
        near_grad[rows, :HEAD_DIM] = product(near_dscores[rows, met], queries[met]).astype(
            jnp.bfloat16
        )
        near_grad[rows, HEAD_DIM:] = product(near_weights[rows, met], cotangents[met]).astype(
            jnp.bfloat16
        )
        met = slice(lane * size, row_tokens)
        own_grad[rows, :HEAD_DIM] = product(own_dscores[rows, met], queries[met])
        own_grad[rows, HEAD_DIM:] = product(own_weights[rows, met], cotangents[met])


def kernel_call(kernel, name, at, own_pair, next_pair, kvs, stats, out_shape, scratch, size, waits, cost, grant):
    row_tokens = own_pair.shape[1]
    blocks = row_tokens // size

    return pl.pallas_call(
        ordered(
            functools.partial(kernel, blocks=blocks, size=size),
            2 + len(kvs) + len(stats),
            len(waits),
            len(out_shape),
            0,
        ),
        grid_spec=pltpu.PrefetchScalarGridSpec(
            num_scalar_prefetch=1,
            grid=(1,),
            in_specs=[whole_block(value) for value in (own_pair, next_pair, *kvs, *stats)]
            + [pl.BlockSpec(memory_space=pl.ANY)] * len(waits),
            out_specs=[whole_block(value) for value in out_shape],
            scratch_shapes=scratch,
        ),
        out_shape=out_shape,
        compiler_params=pltpu.CompilerParams(vmem_limit_bytes=grant),
        cost_estimate=time_estimate(cost),
        name=name,
    )(at, own_pair, next_pair, *kvs, *stats, *waits)


def softmax_stats(at, own_pair, next_pair, kvs, size):
    row_tokens = own_pair.shape[1]
    return kernel_call(
        stats_kernel, "softmax_stats", at, own_pair, next_pair, kvs, (),
        [jax.ShapeDtypeStruct((8, row_tokens), jnp.float32)] * 2,
        [pltpu.VMEM((2, 2 * row_tokens // size, size, size), jnp.float32)],
        size, (), 4, 16 * 2**20,
    )


def attention_grads(at, own_pair, next_pair, kvs, stats, size, waits):
    row_tokens = own_pair.shape[1]
    low = jnp.bfloat16
    return kernel_call(
        gradient_kernel, "attention_grads", at, own_pair, next_pair, kvs, stats,
        [
            jax.ShapeDtypeStruct((2, row_tokens, HEAD_DIM), jnp.float32),
            jax.ShapeDtypeStruct((2, row_tokens, HEAD_DIM), low),
            jax.ShapeDtypeStruct((row_tokens, 2 * HEAD_DIM), low),
            jax.ShapeDtypeStruct((row_tokens, 2 * HEAD_DIM), jnp.float32),
        ],
        [
            pltpu.VMEM((2, 2 * HEAD_DIM, row_tokens), low),
            pltpu.VMEM((2 * row_tokens, HEAD_DIM), low),
            pltpu.VMEM((2 * row_tokens, HEAD_DIM), low),
            pltpu.VMEM((row_tokens, row_tokens), low),
            pltpu.VMEM((row_tokens, row_tokens), low),
            pltpu.VMEM((row_tokens, 2 * row_tokens), low),
            pltpu.VMEM((row_tokens, 2 * row_tokens), low),
        ],
        size, waits, 8, 36 * 2**20,
    )


def at_offset(index, size):
    return pl.ds(pl.multiple_of(index * size, size), size)


def ordered(kernel, inputs, waits, outputs, through):
    def body(*refs):
        first = 1 + inputs + waits + through
        kept = first + outputs
        return kernel(*refs[: 1 + inputs], *refs[first:kept], *refs[kept + through :])

    return body


def time_estimate(microseconds):
    return pl.CostEstimate(
        flops=microseconds * 10**9, bytes_accessed=microseconds * 3 * 10**6, transcendentals=0
    )


def whole_block(value):
    return pl.BlockSpec(value.shape, lambda *_: (0,) * len(value.shape))


def small_call(
    kernel, name, at, operands, out_shape, scratch=(), waits=(), through=(), cost=1
):
    anywhere = pl.BlockSpec(memory_space=pl.ANY)
    first = 1 + len(operands) + len(waits)
    return pl.pallas_call(
        ordered(kernel, len(operands), len(waits), len(out_shape), len(through)),
        grid=(1,),
        in_specs=[pl.BlockSpec(memory_space=pltpu.SMEM)]
        + [whole_block(value) for value in operands]
        + [anywhere] * (len(waits) + len(through)),
        out_specs=[whole_block(value) for value in out_shape] + [anywhere] * len(through),
        out_shape=[
            *out_shape,
            *(jax.ShapeDtypeStruct(value.shape, value.dtype) for value in through),
        ],
        input_output_aliases={
            first + index: len(out_shape) + index for index in range(len(through))
        },
        scratch_shapes=list(scratch),
        compiler_params=pltpu.CompilerParams(vmem_limit_bytes=VMEM_GRANT),
        cost_estimate=time_estimate(cost),
        name=name,
    )(at, *operands, *waits, *through)


def mixed_kernel(_, held_ref, passed_ref, out):
    out[0] = held_ref[...]
    out[1] = passed_ref[1]


def go_round(at, pieces):
    own, held, given = pieces
    beside = exchanged(given, 1)
    shape = jax.ShapeDtypeStruct(given.shape, given.dtype)
    (both,) = small_call(mixed_kernel, "mix", at, (held, beside), [shape])
    across = exchanged(both, 2)
    return own, beside, across


def deal_kernel(at_ref, query_ref, cotangent_ref, *outs, heads):
    lane = at_ref[0]
    for head in range(heads):
        own, held, given = outs[3 * head : 3 * head + 3]
        for bits, out in enumerate((own, given.at[0], held, given.at[1])):
            column = at_offset((lane ^ bits) * heads + head, HEAD_DIM)
            out[0] = query_ref[0, :, column]
            out[1] = cotangent_ref[0, :, column]


def deal_heads(at, queries, upstream):
    _, size, width = queries.shape
    heads = width // LANES // HEAD_DIM
    piece = jax.ShapeDtypeStruct((2, size, HEAD_DIM), jnp.bfloat16)
    pair = jax.ShapeDtypeStruct((2, *piece.shape), jnp.bfloat16)
    outs = small_call(
        functools.partial(deal_kernel, heads=heads),
        "deal_heads", at, (queries, upstream), [piece, piece, pair] * heads,
    )
    return [outs[3 * head : 3 * head + 3] for head in range(heads)]


def place_rows_kernel(at_ref, own, beside, across, out):
    size = own.shape[1]
    for bits, piece in enumerate((own, beside.at[0], across.at[0], across.at[1])):
        out[:, at_offset(at_ref[0] ^ bits, size)] = piece[...]


def place_rows(at, found, waits, through):
    own, beside, across = found
    kinds, size, width = own.shape
    whole = jax.ShapeDtypeStruct((kinds, LANES * size, width), own.dtype)
    return small_call(
        place_rows_kernel, "place_rows", at, (own, beside, across), [whole],
        waits=waits, through=through,
    )


def settle_kernel(at_ref, own_out, arrived, own, held, given):
    size = own.shape[1]
    for bits, out in enumerate((own, given.at[0], held, given.at[1])):
        rows = at_offset(at_ref[0] ^ bits, size)
        out[...] = (own_out[:, rows] + arrived[:, rows].astype(jnp.float32)).astype(jnp.bfloat16)


def settle_out(at, own_out, arrived, waits):
    kinds, count, width = own_out.shape
    piece = jax.ShapeDtypeStruct((kinds, count // LANES, width), jnp.bfloat16)
    pair = jax.ShapeDtypeStruct((2, *piece.shape), jnp.bfloat16)
    return small_call(
        settle_kernel, "settle_out", at, (own_out, arrived), [piece, piece, pair], waits=waits
    )


def place_heads_kernel(at_ref, *refs, heads):
    outs = refs[3 * heads :]
    for head in range(heads):
        own, beside, across = refs[3 * head : 3 * head + 3]
        for bits, piece in enumerate((own, beside.at[0], across.at[0], across.at[1])):
            column = at_offset((at_ref[0] ^ bits) * heads + head, HEAD_DIM)
            for kind, out in enumerate(outs):
                out[0, :, column] = piece[kind]


def place_heads(at, found):
    heads = len(found)
    kinds, size, width = found[0][0].shape
    whole = jax.ShapeDtypeStruct((1, size, LANES * heads * width), jnp.bfloat16)
    return small_call(
        functools.partial(place_heads_kernel, heads=heads),
        "place_heads", at, [value for part in found for value in part],
        [whole] * kinds,
    )


def spread_kernel(at_ref, *refs, rows, before):
    tokens, own_ref, arrived_ref = refs[:LANES], refs[LANES], refs[LANES + 1]
    earlier = refs[LANES + 2 : LANES + 2 + before]
    own, held, given, kept_ref, sent_ref = refs[LANES + 2 + before : -2]
    kv_pieces = (own, given.at[0], held, given.at[1])
    if before:
        earlier = (earlier[0], earlier[2].at[0], earlier[1], earlier[2].at[1])
    turned, partial = refs[-2:]
    lane, half = at_ref[0], at_ref[1]
    size, depth = tokens[0].shape
    cols = own_ref.shape[1]
    for bits, piece in enumerate(kv_pieces):
        held = at_offset(lane ^ bits, size)
        kv_grad = (own_ref[held] + arrived_ref[held].astype(jnp.float32)).astype(jnp.bfloat16)
        if before:
            piece[:, : own.shape[1] - cols] = earlier[bits][...]
        piece[:, own.shape[1] - cols :] = kv_grad
        turned[:, bits * size : (bits + 1) * size] = kv_grad.T
    step = 256
    for start in range(0, depth, step):
        found = None
        for bits, piece in enumerate(tokens):
            term = product(turned[:, bits * size : (bits + 1) * size], piece[:, start : start + step])
            found = term if found is None else found + term
        partial[start : start + step] = found.T
    chunk = kept_ref.shape[1]
    for out, side in ((kept_ref, half), (sent_ref, 1 - half)):
        for index in range(rows):
            out[index] = partial[at_offset(side * rows + index, chunk)].astype(out.dtype)


def spread(at, tokens, own_grad, arrived, earlier, rows, waits, through):
    size, depth = tokens[0].shape
    cols = own_grad.shape[1]
    chunk = depth // 2 // rows
    shape = (rows, chunk, cols)
    width = cols + (earlier[0].shape[1] if earlier else 0)
    piece = jax.ShapeDtypeStruct((size, width), jnp.bfloat16)
    outs = small_call(
        functools.partial(spread_kernel, rows=rows, before=len(earlier)),
        "spread", at, (*tokens, own_grad, arrived, *earlier),
        [
            piece,
            piece,
            jax.ShapeDtypeStruct((2, size, width), jnp.bfloat16),
            jax.ShapeDtypeStruct(shape, jnp.float32),
            jax.ShapeDtypeStruct(shape, jnp.bfloat16),
        ],
        [pltpu.VMEM((cols, LANES * size), jnp.bfloat16), pltpu.VMEM((depth, cols), jnp.float32)],
        waits=waits,
        through=through,
        cost=0,
    )
    return outs[:3], outs[3], outs[4], outs[5:]


def feature_kernel(at_ref, *refs, heads, counts):
    (own, beside, across), weights, (out_ref, tokens) = refs[:3], refs[3:-2], refs[-2:]
    pieces = (own, beside.at[0], across.at[0], across.at[1])
    step = pl.program_id(0)
    width = tokens.shape[1] // 2

    @pl.when(step == 0)
    def _():
        for head in range(heads):
            for bits in range(LANES):
                piece = pieces[bits][:, 2 * head * HEAD_DIM : 2 * (head + 1) * HEAD_DIM]
                column = (at_ref[0] ^ bits) * heads + head
                tokens[:, at_offset(column, HEAD_DIM)] = piece[:, :HEAD_DIM]
                tokens[:, at_offset(column + width // HEAD_DIM, HEAD_DIM)] = piece[:, HEAD_DIM:]

    first = 0
    for weight, count in zip(weights, counts):

        @pl.when((step >= first) & (step < first + count))
        def _(weight=weight):
            out_ref[0] = product_minor(tokens[...], weight[...]).astype(jnp.bfloat16)

        first += count


def feature_grads(at, found, weights, waits):
    pieces = found
    size = pieces[0].shape[0]
    heads = pieces[0].shape[1] // (2 * HEAD_DIM)
    step = 512
    counts = [weight.shape[0] // step for weight in weights]
    depth = sum(counts) * step
    starts = [sum(counts[:index]) for index in range(len(counts))]
    side, part = counts[0], counts[1]

    def place(index, at_ref):
        half, core = at_ref[1], at_ref[2]
        other = (1 - half) * side
        fetched = other + core * part + index - starts[1]
        passed = other + (1 - core) * part + index - starts[2]
        return jnp.where(
            index < starts[1],
            half * side + index,
            jnp.where(index < starts[2], fetched, passed),
        )

    def weight_spec(weight, start, count):
        return pl.BlockSpec(
            (step, weight.shape[1]), lambda index, _: (jnp.clip(index - start, 0, count - 1), 0)
        )

    return pl.pallas_call(
        ordered(
            functools.partial(feature_kernel, heads=heads, counts=counts),
            len(pieces) + len(weights),
            len(waits),
            1,
            0,
        ),
        grid_spec=pltpu.PrefetchScalarGridSpec(
            num_scalar_prefetch=1,
            grid=(sum(counts),),
            in_specs=[whole_block(piece) for piece in pieces]
            + [weight_spec(*found) for found in zip(weights, starts, counts)]
            + [pl.BlockSpec(memory_space=pl.ANY)] * len(waits),
            out_specs=pl.BlockSpec((1, size, step), lambda index, at_ref: (0, 0, place(index, at_ref))),
            scratch_shapes=[pltpu.VMEM((size, weights[0].shape[1]), jnp.bfloat16)],
        ),
        out_shape=jax.ShapeDtypeStruct((1, size, depth), jnp.bfloat16),
        compiler_params=pltpu.CompilerParams(vmem_limit_bytes=VMEM_GRANT),
        cost_estimate=time_estimate(6),
        name="feature_grads",
    )(at, *pieces, *weights, *waits)


def place_weight_kernel(at_ref, *refs, heads):
    *pieces, out = refs
    width = out.shape[1] // 2
    for bits, piece in enumerate(pieces):
        for head in range(heads):
            column = (at_ref[0] ^ bits) * heads + head
            start = 2 * head * HEAD_DIM
            out[:, at_offset(column, HEAD_DIM)] = piece[:, start : start + HEAD_DIM]
            out[:, at_offset(column + width // HEAD_DIM, HEAD_DIM)] = piece[
                :, start + HEAD_DIM : start + 2 * HEAD_DIM
            ]


def place_weight(at, pieces, waits):
    count, cols = pieces[0].shape
    whole = jax.ShapeDtypeStruct((count, LANES * cols), jnp.float32)
    return small_call(
        functools.partial(place_weight_kernel, heads=cols // (2 * HEAD_DIM)),
        "place_weight", at, pieces, [whole], waits=waits,
    )[0]


def merge_kernel(at_ref, *refs, place):
    *inputs, kept_ref, sent_ref = refs
    bit = at_ref[place]
    for index in range(kept_ref.shape[0]):
        for out, high in ((kept_ref, bit), (sent_ref, 1 - bit)):
            found = inputs[0][2 * index + high]
            for arrived in inputs[1:]:
                found = found + arrived[2 * index + high].astype(jnp.float32)
            out[index] = found.astype(out.dtype)


def merge(at, place, kept, arrived, waits=()):
    shape = (kept.shape[0] // 2, *kept.shape[1:])
    return small_call(
        functools.partial(merge_kernel, place=place),
        "merge", at, (kept, *arrived),
        [jax.ShapeDtypeStruct(shape, jnp.float32), jax.ShapeDtypeStruct(shape, jnp.bfloat16)],
        waits=waits,
    )


def finish_kernel(at_ref, *refs, heads, each):
    inputs, outs = refs[: heads * each], refs[heads * each : -1]
    total = refs[-1]
    size = outs[0].shape[0]
    cols = inputs[0].shape[2]
    for head in range(heads):
        found = inputs[head * each][0]
        for arrived in inputs[head * each + 1 : (head + 1) * each]:
            found = found + arrived[0].astype(jnp.float32)
        total[:, head * cols : (head + 1) * cols] = found
    for bits, out in enumerate(outs):
        out[...] = total[at_offset(at_ref[0] ^ bits, size)]


def finish(at, parts, waits):
    _, chunk, cols = parts[0][0].shape
    heads = len(parts)
    piece = jax.ShapeDtypeStruct((chunk // LANES, heads * cols), jnp.float32)
    return small_call(
        functools.partial(finish_kernel, heads=heads, each=len(parts[0])),
        "finish", at, [value for part in parts for value in part], [piece] * LANES,
        [pltpu.VMEM((chunk, heads * cols), jnp.float32)],
        waits=waits,
    )


def passed_round(pieces):
    return [exchanged(piece, bits) if bits else piece for bits, piece in enumerate(pieces)]


def local(features, queries, kv_weight, upstream):
    tokens = features[0]
    size = tokens.shape[0]
    weight_rows, kv_width = kv_weight.shape
    width = kv_width // 2
    lane_width = width // LANES
    heads = lane_width // HEAD_DIM
    rows = lax.axis_size("seq") // LANES
    place = lax.axis_index("seq")
    lane = place % LANES
    row = place // LANES
    half = lax.axis_index("dp")
    core = place % 2

    here = jnp.stack([lane, half]).astype(jnp.int32)
    dealt = deal_heads(here, queries, upstream)
    lane_weight = take_columns(here, kv_weight, dealt[0][:1])
    other_lane_weight = swapped(lane_weight)
    across = exchanged(tokens, 2)
    beside = exchanged(tokens, 1)
    diagonal = exchanged(across, 1)
    row_tokens = (tokens, beside, across, diagonal)

    owns = project(here, row_tokens, (lane_weight, other_lane_weight))
    windows = [(own, shifted(own, 1)) for own in owns]

    part_rows = weight_rows // 2
    through = [lax.dynamic_slice_in_dim(kv_weight, core * part_rows, part_rows, 0)]
    own_pairs = []
    for pieces in dealt:
        own_pair, *handed = place_rows(here, go_round(here, pieces), owns[:1], through)
        if through:
            (part,) = handed
        through = []
        own_pairs.append(own_pair)
    next_pairs = [shifted(own_pair, -1) for own_pair in own_pairs]

    fetched = swapped(part)

    at = jnp.stack([row, lane]).astype(jnp.int32)
    shared = []
    for head in range(heads):
        own_stats, next_stats = softmax_stats(
            at, own_pairs[head], next_pairs[head], windows[head], size
        )
        shared.append(
            (own_stats, turned_round(next_stats, 1), next_stats, turned_round(own_stats, -1))
        )
    gained = [
        attention_grads(
            at, own_pairs[head], next_pairs[head], windows[head], shared[head], size,
            (shared[-1][0],),
        )
        for head in range(heads)
    ]

    bits = jnp.stack([(row >> index) % 2 for index in range(rows.bit_length() - 1)])
    kv_pieces, parts, out_pieces = [], [], []
    waits, through = (gained[-1][3],), (fetched,)
    for head, (own_out, next_out, near_grad, own_grad) in enumerate(gained):
        if head:
            through = (next_out,)
        else:
            next_out = shifted(next_out, 1)
        kv_pieces, kept, sent, (handed,) = spread(
            here, row_tokens, own_grad, shifted(near_grad, -1), kv_pieces, rows, waits, through
        )
        if head:
            next_out = shifted(handed, 1)
        else:
            fetched = handed
            passed = exchanged(fetched, 1)
        out_pieces.append(go_round(here, settle_out(here, own_out, next_out, (sent,))))
        arrived = [swapped(sent)]
        waits = ()
        distance = 1
        while distance < rows:
            kept, sent = merge(bits, distance.bit_length() - 1, kept, arrived)
            arrived = [moved(sent, distance * LANES, 0)]
            if not waits:
                waits = (sent,)
            distance *= 2
        parts.append((kept, *arrived))
    kv_found = go_round(here, kv_pieces)

    feature_grad = feature_grads(
        jnp.stack([lane, half, core]).astype(jnp.int32),
        kv_found,
        (kv_weight, fetched, passed),
        (sent,),
    )
    attended, query_grad = place_heads(here, out_pieces)
    pieces = passed_round(finish(here, parts, (feature_grad,)))
    weight_grad = place_weight(here, pieces, (attended,))
    return (attended, query_grad, feature_grad, weight_grad)


def solution(mesh):
    return jax.shard_map(
        local,
        mesh=mesh,
        in_specs=(P("dp", "seq", None), P("dp", "seq", None), P("dp", None), P("dp", "seq", None)),
        out_specs=(
            P("dp", "seq", None),
            P("dp", "seq", None),
            P("dp", "seq", None),
            P(("dp", "seq"), None),
        ),
        check_vma=False,
    )
```

time: 827 us -> 193 us (0.23)
  waiting for transfers between devices: 491 us -> 51.3 us
  matrix products: 126 us -> 0 us
  Pallas kernels: 0 us -> 68.8 us
  starting transfers between devices: 111 us -> 55.5 us
  local copies, waits for them, and re-layouts: 49.5 us -> 15.1 us
  other arithmetic: 21 us -> 0.3 us
  between operations: 14 us -> 1.06 us
  blocking collectives: 11.8 us -> 0 us
    ppermute x16 -> x37, waiting for transfers between devices: 241 us -> 51.3 us  [the longest x17 19 us: exchanged(): lax.ppermute(value, 'seq', [(source, source ^ bits) for source in range(c...]
    all_gather x2 -> x0, waiting for transfers between devices: 152 us -> none  [the longest x1 108 us: local(): full_weight = lax.all_gather(kv_weight, 'dp', axis=0, tiled=True)]
    dot_general x51 -> x0, matrix products: 126 us -> none  [the longest x8 20.1 us: head_work(): lax.dot_general(weights, grad_head, token_dims, preferred_element_type=jn...]
    unnamed x4 -> x0, waiting for transfers between devices: 97.9 us -> none
    pallas_call x0 -> x26, Pallas kernels: none -> 68.8 us  [the longest x4 30.5 us: kernel_call(): pl.pallas_call(ordered(functools.partial(kernel, blocks=blocks, size=size...]
    ppermute x16 -> x37, starting transfers between devices: 111 us -> 55.5 us  [the longest x8 24.4 us: shifted(): lax.ppermute(value, 'seq', [(source, source + steps) for source in range(...]
    unnamed x49 -> x54, local copies, waits for them, and re-layouts: 37 us -> 13.2 us
    all_to_all x1 -> x0, blocking collectives: 11.8 us -> none  [local(): lax.all_to_all(tokens, 'dp', split_axis=1, concat_axis=0, tiled=True)]
  transfers between devices with their start and end apart: 19 -> 37, of which waited for: 16 -> 16; matrix products, arithmetic and copies ran while one was open for 2% -> 1% of each run, Pallas kernels for 0% -> 33%
where the time goes in v3:
time: 193 us; the launch traced here: 192 us
  Pallas kernels  68.8 us (36%)
  starting transfers between devices  55.5 us (29%)
  waiting for transfers between devices  51.3 us (27%)
  local copies, waits for them, and re-layouts  15.1 us (8%)
    pallas_call x4, Pallas kernels, kernel_call(): pl.pallas_call(ordered(functools.partial(kernel, blocks=blocks, size=size...  30.5 us
    pallas_call x20, Pallas kernels, small_call(): pl.pallas_call(ordered(kernel, len(operands), len(waits), len(out_shape),...  29.1 us
    ppermute x8, starting transfers between devices, shifted(): lax.ppermute(value, 'seq', [(source, source + steps) for source in range(...  24.4 us
    ppermute x17, waiting for transfers between devices, exchanged(): lax.ppermute(value, 'seq', [(source, source ^ bits) for source in range(c...  19 us
    ppermute x4, waiting for transfers between devices, swapped(): return lax.ppermute(value, 'dp', [(0, 1), (1, 0)])  13.7 us
    ppermute x8, waiting for transfers between devices, shifted(): lax.ppermute(value, 'seq', [(source, source + steps) for source in range(...  13.6 us
    unnamed x54, local copies, waits for them, and re-layouts  13.2 us
    ppermute x17, starting transfers between devices, exchanged(): lax.ppermute(value, 'seq', [(source, source ^ bits) for source in range(c...  12.2 us
  transfers between devices with their start and end apart: 37, of which 16 were waited for; matrix products, arithmetic and copies ran while one was open for 1% of the time, Pallas kernels for 33%

profile of v3, /device:TPU:0, one launch (start us, length us, event | category | flops | bytes accessed | tf_op | source)
XLA Modules:
  0.0 192.1 jit_solution(1080311234472182372)
XLA Ops:
  0.6 3.0 %collective-permute-start.3 = (bf16[256,2048]{1,0:T(8,128)(2,1)}, bf16[256,2048]{1,0:T(8,128)(2,1)S(1)}, u32[]{:S(2)}, u32[]{:S(2)}) collective-permute-start(bf16[256,2048]{1,0:T(8,128)(2,1)} %bitcast.7), channel_id=1, source_target_pairs={{0,4},{2,6},{4,0},{6,2},{8,12},{10,14},{12,8},{14,10},{16,20},{18,... | collective-permute-start | bytes 3145736 | tf_op jit(solution)/shard_map/ppermute | solution.py:24
  5.8 1.5 deal_heads.1
  9.3 2.2 %copy-done = bf16[1024,2048]{1,0:T(8,128)(2,1)S(1)} copy-done((bf16[1024,2048]{1,0:T(8,128)(2,1)S(1)}, bf16[1024,2048]{1,0:T(8,128)(2,1)}, u32[]{:S(2)}) %copy-start) | copy-done | bytes 4194328
  11.5 2.3 %take_columns.1.refs_5_ = bf16[1024,512]{1,0:T(8,128)(2,1)} custom-call(s32[2]{0:T(128)S(1)} %pad_add_fusion.refs_0_, bf16[1024,2048]{1,0:T(8,128)(2,1)S(1)} %copy-done, bf16[2,256,128]{2,1,0:T(8,128)(2,1)S(1)} %get-tuple-element.58.refs_2_.refs_1_), custom_call_target="tpu_custom_call" | custom-call | flops 1000000000 | bytes 3000000 | tf_op jit(solution)/shard_map/take_columns/pallas_call | solution.py:78
  13.8 1.5 collective-permute-start.5
  15.3 11.7 %collective-permute-done.3.refs_3_ = bf16[256,2048]{1,0:T(8,128)(2,1)S(1)} collective-permute-done((bf16[256,2048]{1,0:T(8,128)(2,1)}, bf16[256,2048]{1,0:T(8,128)(2,1)S(1)}, u32[]{:S(2)}, u32[]{:S(2)}) %collective-permute-start.3) | collective-permute-done | bytes 1048608 | tf_op jit(solution)/shard_map/ppermute | solution.py:24
  27.5 1.9 constant_dynamic-slice_fusion.refs_5_
  31.4 1.8 collective-permute-start.1
  33.2 6.5 %collective-permute-done.5.refs_6_ = bf16[1024,512]{1,0:T(8,128)(2,1)} collective-permute-done((bf16[1024,512]{1,0:T(8,128)(2,1)}, bf16[1024,512]{1,0:T(8,128)(2,1)}, u32[]{:S(2)}, u32[]{:S(2)}) %collective-permute-start.5) | collective-permute-done | bytes 1048608 | tf_op jit(solution)/shard_map/ppermute | solution.py:51
  39.7 5.2 %project.1 = (bf16[1024,256]{1,0:T(8,128)(2,1)}, bf16[1024,256]{1,0:T(8,128)(2,1)}) custom-call(s32[2]{0:T(128)S(1)} %pad_add_fusion.refs_0_, bf16[256,2048]{1,0:T(8,128)(2,1)S(1)} %bitcast.9, bf16[256,2048]{1,0:T(8,128)(2,1)S(1)} %collective-permute-done.2.refs_2_, bf16[256,2048]{1,0:T(8,128)(2,1)S(1)} %collective-permute-done.3.refs_3_, ...), custom_call_target="tpu_custom_call" | custom-call | flops 4000000000 | bytes 12000000 | tf_op jit(solution)/shard_map/project/pallas_call | solution.py:324
  44.9 4.4 %collective-permute-start.7 = (bf16[1024,256]{1,0:T(8,128)(2,1)}, bf16[1024,256]{1,0:T(8,128)(2,1)}, u32[]{:S(2)}, u32[]{:S(2)}) collective-permute-start(bf16[1024,256]{1,0:T(8,128)(2,1)} %get-tuple-element.61.refs_4_.refs_3_), channel_id=1, source_target_pairs={{0,8},{2,10},{4,12},{6,14},{8,16},{10,18},{12,20},{14,22},{16,24},... | collective-permute-start | bytes 1572872 | tf_op jit(solution)/shard_map/ppermute | solution.py:31
  49.4 1.8 place_rows.2
  51.2 1.4 collective-permute-start.6
  54.2 5.3 %collective-permute-start.13 = (bf16[1024,256]{1,0:T(8,128)(2,1)}, bf16[1024,256]{1,0:T(8,128)(2,1)}, u32[]{:S(2)}, u32[]{:S(2)}) collective-permute-start(bf16[1024,256]{1,0:T(8,128)(2,1)} %get-tuple-element.68.refs_3_), channel_id=1, source_target_pairs={{0,8},{2,10},{4,12},{6,14},{8,16},{10,18},{12,20},{14,22},{16,24},... | collective-permute-start | bytes 1572872 | tf_op jit(solution)/shard_map/ppermute | solution.py:31
  59.5 1.8 collective-permute-done.11.refs_3_
  61.3 1.9 place_rows.3.refs_1_
  63.2 1.3 collective-permute-start.12
  64.5 1.5 collective-permute-start.18
  66.8 5.3 %softmax_stats.2 = (f32[8,1024]{1,0:T(8,128)S(1)}, f32[8,1024]{1,0:T(8,128)S(1)}) custom-call(s32[2]{0:T(128)S(1)} %pad_add_fusion.1.refs_0_, bf16[2,1024,128]{2,1,0:T(8,128)(2,1)} %get-tuple-element.62.refs_1_, bf16[2,1024,128]{2,1,0:T(8,128)(2,1)} %collective-permute-done.6.refs_2_, bf16[1024,256]{1,0:T(8,128)(2,1)} %get-tuple-element.61.refs_4_.refs_3_, ...), custom_call_target="tpu_custom_call" | custom-call | flops 4000000000 | bytes 12000000 | tf_op jit(solution)/shard_map/softmax_stats/pallas_call | solution.py:239
  72.1 4.8 %collective-permute-start.9 = (f32[8,1024]{1,0:T(8,128)S(1)}, f32[8,1024]{1,0:T(8,128)S(1)}, u32[]{:S(2)}, u32[]{:S(2)}) collective-permute-start(f32[8,1024]{1,0:T(8,128)S(1)} %get-tuple-element.63.refs_5_), channel_id=1, source_target_pairs={{0,24},{2,26},{4,28},{6,30},{8,0},{10,2},{12,4},{14,6},{16,8},{18,... | collective-permute-start | bytes 98312 | tf_op jit(solution)/shard_map/ppermute | solution.py:37
  76.9 1.6 collective-permute-done.12.refs_2_
  78.5 5.3 %softmax_stats.3 = (f32[8,1024]{1,0:T(8,128)S(1)}, f32[8,1024]{1,0:T(8,128)S(1)}) custom-call(s32[2]{0:T(128)S(1)} %pad_add_fusion.1.refs_0_, bf16[2,1024,128]{2,1,0:T(8,128)(2,1)} %place_rows.3.refs_1_, bf16[2,1024,128]{2,1,0:T(8,128)(2,1)} %collective-permute-done.12.refs_2_, bf16[1024,256]{1,0:T(8,128)(2,1)} %get-tuple-element.68.refs_3_, ...), custom_call_target="tpu_custom_call" | custom-call | flops 4000000000 | bytes 12000000 | tf_op jit(solution)/shard_map/softmax_stats/pallas_call | solution.py:239
  83.8 2.1 %collective-permute-start.16 = (f32[8,1024]{1,0:T(8,128)S(1)}, f32[8,1024]{1,0:T(8,128)S(1)}, u32[]{:S(2)}, u32[]{:S(2)}) collective-permute-start(f32[8,1024]{1,0:T(8,128)S(1)} %get-tuple-element.74.refs_7_), channel_id=1, source_target_pairs={{0,8},{2,10},{4,12},{6,14},{8,16},{10,18},{12,20},{14,22},{16,24},... | collective-permute-start | bytes 98312 | tf_op jit(solution)/shard_map/ppermute | solution.py:37
  85.9 1.7 collective-permute-start.17
  87.7 9.6 %attention_grads.2 = (f32[2,1024,128]{2,1,0:T(8,128)S(1)}, bf16[2,1024,128]{2,1,0:T(8,128)(2,1)S(1)}, bf16[1024,256]{1,0:T(8,128)(2,1)S(1)}, f32[1024,256]{1,0:T(8,128)S(1)}) custom-call(s32[2]{0:T(128)S(1)} %pad_add_fusion.1.refs_0_, bf16[2,1024,128]{2,1,0:T(8,128)(2,1)} %get-tuple-element.62.refs_1_, bf16[2,1024,128]{2,1,0:T(8,128)(2,1)} %collective-permute-done.6.refs_2_, ...), custom_call_target="tpu_custom_call" | custom-call | flops 8000000000 | bytes 24000000 | tf_op jit(solution)/shard_map/attention_grads/pallas_call | solution.py:239
  99.1 1.5 collective-permute-start.15
  100.6 10.3 %attention_grads.3 = (f32[2,1024,128]{2,1,0:T(8,128)S(1)}, bf16[2,1024,128]{2,1,0:T(8,128)(2,1)S(1)}, bf16[1024,256]{1,0:T(8,128)(2,1)}, f32[1024,256]{1,0:T(8,128)S(1)}) custom-call(s32[2]{0:T(128)S(1)} %pad_add_fusion.1.refs_0_, bf16[2,1024,128]{2,1,0:T(8,128)(2,1)} %place_rows.3.refs_1_, bf16[2,1024,128]{2,1,0:T(8,128)(2,1)} %collective-permute-done.12.refs_2_, ...), custom_call_target="tpu_custom_call" | custom-call | flops 8000000000 | bytes 24000000 | tf_op jit(solution)/shard_map/attention_grads/pallas_call | solution.py:239
  111.6 3.9 %spread.2 = (bf16[256,256]{1,0:T(8,128)(2,1)S(1)}, bf16[256,256]{1,0:T(8,128)(2,1)S(1)}, bf16[2,256,256]{2,1,0:T(8,128)(2,1)S(1)}, f32[4,256,256]{2,1,0:T(8,128)...) custom-call(s32[2]{0:T(128)S(1)} %pad_add_fusion.refs_0_, ...), custom_call_target="tpu_custom_call", output_to_operand_aliasing={{5}: (8, {})} | custom-call | tf_op jit(solution)/shard_map/spread/pallas_call | solution.py:324
  117.2 1.9 collective-permute-start.22
  119.1 1.3 collective-permute-start.21
  120.5 5.2 %collective-permute-start.14 = (bf16[2,1024,128]{2,1,0:T(8,128)(2,1)}, bf16[2,1024,128]{2,1,0:T(8,128)(2,1)S(1)}, u32[]{:S(2)}, u32[]{:S(2)}) collective-permute-start(bf16[2,1024,128]{2,1,0:T(8,128)(2,1)} %copy-done.14), channel_id=1, source_target_pairs={{0,8},{2,10},{4,12},{6,14},{8,16},{10,18},{12,20},{14,22},{16,24},... | collective-permute-start | bytes 1572872 | tf_op jit(solution)/shard_map/ppermute | solution.py:31
  125.7 6.2 %collective-permute-done.22.refs_2_ = bf16[4,256,256]{2,1,0:T(8,128)(2,1)} collective-permute-done((bf16[4,256,256]{2,1,0:T(8,128)(2,1)}, bf16[4,256,256]{2,1,0:T(8,128)(2,1)}, u32[]{:S(2)}, u32[]{:S(2)}) %collective-permute-start.22) | collective-permute-done | bytes 524320 | tf_op jit(solution)/shard_map/ppermute | solution.py:51
  132.0 1.2 copy-done.11
  133.2 1.2 merge.4
  134.4 1.8 collective-permute-done.21.refs_6_
  136.2 3.1 %spread.3 = (bf16[256,512]{1,0:T(8,128)(2,1)S(1)}, bf16[256,512]{1,0:T(8,128)(2,1)S(1)}, bf16[2,256,512]{2,1,0:T(8,128)(2,1)S(1)}, f32[4,256,256]{2,1,0:T(8,128)...) custom-call(s32[2]{0:T(128)S(1)} %pad_add_fusion.refs_0_, ...), custom_call_target="tpu_custom_call", output_to_operand_aliasing={{5}: (11, {})} | custom-call | tf_op jit(solution)/shard_map/spread/pallas_call | solution.py:324
  139.3 3.9 %collective-permute-start.23 = (bf16[2,1024,128]{2,1,0:T(8,128)(2,1)S(1)}, bf16[2,1024,128]{2,1,0:T(8,128)(2,1)S(1)}, u32[]{:S(2)}, u32[]{:S(2)}) collective-permute-start(bf16[2,1024,128]{2,1,0:T(8,128)(2,1)S(1)} %get-tuple-element.89), channel_id=1, source_target_pairs={{0,8},{2,10},{4,12},{6,14},{8,16},{10,18},{12,20},{14,22},{16,24},... | collective-permute-start | bytes 1572872 | tf_op jit(solution)/shard_map/ppermute | solution.py:31
  146.3 8.9 %collective-permute-done.23.refs_2_ = bf16[2,1024,128]{2,1,0:T(8,128)(2,1)S(1)} collective-permute-done((bf16[2,1024,128]{2,1,0:T(8,128)(2,1)S(1)}, bf16[2,1024,128]{2,1,0:T(8,128)(2,1)S(1)}, u32[]{:S(2)}, u32[]{:S(2)}) %collective-permute-start.23) | collective-permute-done | bytes 524320 | tf_op jit(solution)/shard_map/ppermute | solution.py:31
  158.0 1.6 collective-permute-start.30
  160.4 1.4 collective-permute-start.20
  164.1 4.4 %collective-permute-done.30.refs_2_ = bf16[2,256,256]{2,1,0:T(8,128)(2,1)S(1)} collective-permute-done((bf16[2,256,256]{2,1,0:T(8,128)(2,1)S(1)}, bf16[2,256,256]{2,1,0:T(8,128)(2,1)S(1)}, u32[]{:S(2)}, u32[]{:S(2)}) %collective-permute-start.30) | collective-permute-done | bytes 262176 | tf_op jit(solution)/shard_map/ppermute | solution.py:47
  168.5 2.3 %collective-permute-start.25 = (bf16[2,2,256,128]{3,2,1,0:T(8,128)(2,1)S(1)}, bf16[2,2,256,128]{3,2,1,0:T(8,128)(2,1)S(1)}, u32[]{:S(2)}, u32[]{:S(2)}) collective-permute-start(bf16[2,2,256,128]{3,2,1,0:T(8,128)(2,1)S(1)} %mix.8), channel_id=1, source_target_pairs={{0,4},{2,6},{4,0},{6,2},{8,12},{10,14},{12,8},{14,10},{16,20},{18,... | collective-permute-start | bytes 786440 | tf_op jit(solution)/shard_map/ppermute | solution.py:24
  172.2 6.9 %feature_grads.1.refs_5_ = bf16[1,256,2048]{2,1,0:T(8,128)(2,1)} custom-call(s32[3]{0:T(128)S(1)} %pad_add_fusion.3.refs_0_, bf16[256,512]{1,0:T(8,128)(2,1)S(1)} %get-tuple-element.96.refs_1_, bf16[2,256,512]{2,1,0:T(8,128)(2,1)S(1)} %collective-permute-done.26.refs_2_, bf16[2,256,512]{2,1,0:T(8,128)(2,1)S(1)} %collective-permute-done.27.refs_3_, ...), custom_call_target="tpu_custom_call" | custom-call | flops 6000000000 | bytes 18000000 | tf_op jit(solution)/shard_map/feature_grads/pallas_call | solution.py:541
  179.4 1.2 copy-done.15
  183.3 1.8 place_heads.1
  185.1 2.7 %collective-permute-done.35.refs_3_ = f32[64,512]{1,0:T(8,128)S(1)} collective-permute-done((f32[64,512]{1,0:T(8,128)S(1)}, f32[64,512]{1,0:T(8,128)S(1)}, u32[]{:S(2)}, u32[]{:S(2)}) %collective-permute-start.35) | collective-permute-done | bytes 131104 | tf_op jit(solution)/shard_map/ppermute | solution.py:24
  187.7 1.9 collective-permute-done.36.refs_4_
  190.7 1.4 place_weight.1
  (111 shorter events, 27.5 us)
Async XLA Ops:
  0.6 26.4 %collective-permute-start.3 = (bf16[256,2048]{1,0:T(8,128)(2,1)}, bf16[256,2048]{1,0:T(8,128)(2,1)S(1)}, u32[]{:S(2)}, u32[]{:S(2)}) collective-permute-start(bf16[256,2048]{1,0:T(8,128)(2,1)} %bitcast.7), channel_id=1, source_target_pairs={{0,4},{2,6},{4,0},{6,2},{8,12},{10,14},{12,8},{14,10},{16,20},{18,... | collective-permute-start | bytes 3145736 | tf_op jit(solution)/shard_map/ppermute | solution.py:24
  3.6 36.1 %collective-permute-start.2 = (bf16[256,2048]{1,0:T(8,128)(2,1)}, bf16[256,2048]{1,0:T(8,128)(2,1)S(1)}, u32[]{:S(2)}, u32[]{:S(2)}) collective-permute-start(bf16[256,2048]{1,0:T(8,128)(2,1)} %bitcast.8), channel_id=1, source_target_pairs={{0,2},{2,0},{4,6},{6,4},{8,10},{10,8},{12,14},{14,12},{16,18},{18,... | collective-permute-start | bytes 3145736 | tf_op jit(solution)/shard_map/ppermute | solution.py:24
  13.8 25.9 %collective-permute-start.5 = (bf16[1024,512]{1,0:T(8,128)(2,1)}, bf16[1024,512]{1,0:T(8,128)(2,1)}, u32[]{:S(2)}, u32[]{:S(2)}) collective-permute-start(bf16[1024,512]{1,0:T(8,128)(2,1)} %take_columns.1.refs_5_), channel_id=1, source_target_pairs={{0,1},{1,0},{2,3},{3,2},{4,5},{5,4},{6,7},{7,6},{8,9},{9,8},{10,11... | collective-permute-start | bytes 3145736 | tf_op jit(solution)/shard_map/ppermute | solution.py:51
  27.0 12.7 %collective-permute-start.4 = (bf16[256,2048]{1,0:T(8,128)(2,1)S(1)}, bf16[256,2048]{1,0:T(8,128)(2,1)}, u32[]{:S(2)}, u32[]{:S(2)}) collective-permute-start(bf16[256,2048]{1,0:T(8,128)(2,1)S(1)} %collective-permute-done.3.refs_3_), channel_id=1, source_target_pairs={{0,2},{2,0},{4,6},{6,4},{8,10},{10,8},{12,14},{14,12},{16,18},{18,... | collective-permute-start | bytes 3145736 | tf_op jit(solution)/shard_map/ppermute | solution.py:24
  27.0 3.4 %collective-permute-start = (bf16[2,2,256,128]{3,2,1,0:T(8,128)(2,1)}, bf16[2,2,256,128]{3,2,1,0:T(8,128)(2,1)}, u32[]{:S(2)}, u32[]{:S(2)}) collective-permute-start(bf16[2,2,256,128]{3,2,1,0:T(8,128)(2,1)} %get-tuple-element.59), channel_id=1, source_target_pairs={{0,2},{2,0},{4,6},{6,4},{8,10},{10,8},{12,14},{14,12},{16,18},{18,... | collective-permute-start | bytes 786440 | tf_op jit(solution)/shard_map/ppermute | solution.py:24
  27.5 25.1 %collective-permute-start.10 = (bf16[2,2,256,128]{3,2,1,0:T(8,128)(2,1)S(1)}, bf16[2,2,256,128]{3,2,1,0:T(8,128)(2,1)}, u32[]{:S(2)}, u32[]{:S(2)}) collective-permute-start(bf16[2,2,256,128]{3,2,1,0:T(8,128)(2,1)S(1)} %get-tuple-element.66), channel_id=1, source_target_pairs={{0,2},{2,0},{4,6},{6,4},{8,10},{10,8},{12,14},{14,12},{16,18},{18,... | collective-permute-start | bytes 786440 | tf_op jit(solution)/shard_map/ppermute | solution.py:24
  29.4 10.3 %copy-start.2 = (bf16[1,256,2048]{2,1,0:T(8,128)(2,1)S(1)}, bf16[1,256,2048]{2,1,0:T(8,128)(2,1)}, u32[]{:S(2)}) copy-start(bf16[1,256,2048]{2,1,0:T(8,128)(2,1)} %param.4) | copy-start | bytes 3145732
  31.4 18.0 %collective-permute-start.1 = (bf16[2,2,256,128]{3,2,1,0:T(8,128)(2,1)S(1)}, bf16[2,2,256,128]{3,2,1,0:T(8,128)(2,1)S(1)}, u32[]{:S(2)}, u32[]{:S(2)}) collective-permute-start(bf16[2,2,256,128]{3,2,1,0:T(8,128)(2,1)S(1)} %mix.5), channel_id=1, source_target_pairs={{0,4},{2,6},{4,0},{6,2},{8,12},{10,14},{12,8},{14,10},{16,20},{18,... | collective-permute-start | bytes 786440 | tf_op jit(solution)/shard_map/ppermute | solution.py:24
  44.9 7.7 %copy-start.24 = (bf16[2,256,128]{2,1,0:T(8,128)(2,1)S(1)}, bf16[2,256,128]{2,1,0:T(8,128)(2,1)}, u32[]{:S(2)}) copy-start(bf16[2,256,128]{2,1,0:T(8,128)(2,1)} %copy-done.23) | copy-start | bytes 393220
  44.9 21.1 %collective-permute-start.7 = (bf16[1024,256]{1,0:T(8,128)(2,1)}, bf16[1024,256]{1,0:T(8,128)(2,1)}, u32[]{:S(2)}, u32[]{:S(2)}) collective-permute-start(bf16[1024,256]{1,0:T(8,128)(2,1)} %get-tuple-element.61.refs_4_.refs_3_), channel_id=1, source_target_pairs={{0,8},{2,10},{4,12},{6,14},{8,16},{10,18},{12,20},{14,22},{16,24},... | collective-permute-start | bytes 1572872 | tf_op jit(solution)/shard_map/ppermute | solution.py:31
  51.2 12.0 %copy-start.5 = (bf16[512,2048]{1,0:T(8,128)(2,1)}, bf16[512,2048]{1,0:T(8,128)(2,1)S(1)}, u32[]{:S(2)}) copy-start(bf16[512,2048]{1,0:T(8,128)(2,1)S(1)} %get-tuple-element.76) | copy-start | bytes 6291460
  51.2 10.2 %copy-start.22 = (bf16[2,256,128]{2,1,0:T(8,128)(2,1)S(1)}, bf16[2,256,128]{2,1,0:T(8,128)(2,1)}, u32[]{:S(2)}) copy-start(bf16[2,256,128]{2,1,0:T(8,128)(2,1)} %copy-done.21) | copy-start | bytes 393220
  51.2 15.6 %collective-permute-start.6 = (bf16[2,1024,128]{2,1,0:T(8,128)(2,1)}, bf16[2,1024,128]{2,1,0:T(8,128)(2,1)}, u32[]{:S(2)}, u32[]{:S(2)}) collective-permute-start(bf16[2,1024,128]{2,1,0:T(8,128)(2,1)} %get-tuple-element.62.refs_1_), channel_id=1, source_target_pairs={{8,0},{10,2},{12,4},{14,6},{16,8},{18,10},{20,12},{22,14},{24,16},... | collective-permute-start | bytes 1572872 | tf_op jit(solution)/shard_map/ppermute | solution.py:31
  53.6 7.7 %collective-permute-start.11 = (bf16[2,2,256,128]{3,2,1,0:T(8,128)(2,1)S(1)}, bf16[2,2,256,128]{3,2,1,0:T(8,128)(2,1)S(1)}, u32[]{:S(2)}, u32[]{:S(2)}) collective-permute-start(bf16[2,2,256,128]{3,2,1,0:T(8,128)(2,1)S(1)} %mix.6), channel_id=1, source_target_pairs={{0,4},{2,6},{4,0},{6,2},{8,12},{10,14},{12,8},{14,10},{16,20},{18,... | collective-permute-start | bytes 786440 | tf_op jit(solution)/shard_map/ppermute | solution.py:24
  54.2 22.7 %collective-permute-start.13 = (bf16[1024,256]{1,0:T(8,128)(2,1)}, bf16[1024,256]{1,0:T(8,128)(2,1)}, u32[]{:S(2)}, u32[]{:S(2)}) collective-permute-start(bf16[1024,256]{1,0:T(8,128)(2,1)} %get-tuple-element.68.refs_3_), channel_id=1, source_target_pairs={{0,8},{2,10},{4,12},{6,14},{8,16},{10,18},{12,20},{14,22},{16,24},... | collective-permute-start | bytes 1572872 | tf_op jit(solution)/shard_map/ppermute | solution.py:31
  63.2 15.4 %collective-permute-start.12 = (bf16[2,1024,128]{2,1,0:T(8,128)(2,1)}, bf16[2,1024,128]{2,1,0:T(8,128)(2,1)}, u32[]{:S(2)}, u32[]{:S(2)}) collective-permute-start(bf16[2,1024,128]{2,1,0:T(8,128)(2,1)} %place_rows.3.refs_1_), channel_id=1, source_target_pairs={{8,0},{10,2},{12,4},{14,6},{16,8},{18,10},{20,12},{22,14},{24,16},... | collective-permute-start | bytes 1572872 | tf_op jit(solution)/shard_map/ppermute | solution.py:31
  64.5 47.0 %collective-permute-start.18 = (bf16[512,2048]{1,0:T(8,128)(2,1)}, bf16[512,2048]{1,0:T(8,128)(2,1)}, u32[]{:S(2)}, u32[]{:S(2)}) collective-permute-start(bf16[512,2048]{1,0:T(8,128)(2,1)} %copy-done.5), channel_id=1, source_target_pairs={{0,1},{1,0},{2,3},{3,2},{4,5},{5,4},{6,7},{7,6},{8,9},{9,8},{10,11... | collective-permute-start | bytes 6291464 | tf_op jit(solution)/shard_map/ppermute | solution.py:51
  72.1 15.6 %collective-permute-start.9 = (f32[8,1024]{1,0:T(8,128)S(1)}, f32[8,1024]{1,0:T(8,128)S(1)}, u32[]{:S(2)}, u32[]{:S(2)}) collective-permute-start(f32[8,1024]{1,0:T(8,128)S(1)} %get-tuple-element.63.refs_5_), channel_id=1, source_target_pairs={{0,24},{2,26},{4,28},{6,30},{8,0},{10,2},{12,4},{14,6},{16,8},{18,... | collective-permute-start | bytes 98312 | tf_op jit(solution)/shard_map/ppermute | solution.py:37
  76.9 10.8 %collective-permute-start.8 = (f32[8,1024]{1,0:T(8,128)S(1)}, f32[8,1024]{1,0:T(8,128)S(1)}, u32[]{:S(2)}, u32[]{:S(2)}) collective-permute-start(f32[8,1024]{1,0:T(8,128)S(1)} %get-tuple-element.64.refs_7_), channel_id=1, source_target_pairs={{0,8},{2,10},{4,12},{6,14},{8,16},{10,18},{12,20},{14,22},{16,24},... | collective-permute-start | bytes 98312 | tf_op jit(solution)/shard_map/ppermute | solution.py:37
  83.8 16.8 %collective-permute-start.16 = (f32[8,1024]{1,0:T(8,128)S(1)}, f32[8,1024]{1,0:T(8,128)S(1)}, u32[]{:S(2)}, u32[]{:S(2)}) collective-permute-start(f32[8,1024]{1,0:T(8,128)S(1)} %get-tuple-element.74.refs_7_), channel_id=1, source_target_pairs={{0,8},{2,10},{4,12},{6,14},{8,16},{10,18},{12,20},{14,22},{16,24},... | collective-permute-start | bytes 98312 | tf_op jit(solution)/shard_map/ppermute | solution.py:37
  85.9 14.6 %collective-permute-start.17 = (f32[8,1024]{1,0:T(8,128)S(1)}, f32[8,1024]{1,0:T(8,128)S(1)}, u32[]{:S(2)}, u32[]{:S(2)}) collective-permute-start(f32[8,1024]{1,0:T(8,128)S(1)} %get-tuple-element.69.refs_9_.refs_5_), channel_id=1, source_target_pairs={{0,24},{2,26},{4,28},{6,30},{8,0},{10,2},{12,4},{14,6},{16,8},{18,... | collective-permute-start | bytes 98312 | tf_op jit(solution)/shard_map/ppermute | solution.py:37
  99.1 12.5 %collective-permute-start.15 = (bf16[1024,256]{1,0:T(8,128)(2,1)S(1)}, bf16[1024,256]{1,0:T(8,128)(2,1)S(1)}, u32[]{:S(2)}, u32[]{:S(2)}) collective-permute-start(bf16[1024,256]{1,0:T(8,128)(2,1)S(1)} %get-tuple-element.73), channel_id=1, source_target_pairs={{8,0},{10,2},{12,4},{14,6},{16,8},{18,10},{20,12},{22,14},{24,16},... | collective-permute-start | bytes 1572872 | tf_op jit(solution)/shard_map/ppermute | solution.py:31
  110.9 4.5 %copy-start.17 = (f32[2,1024,128]{2,1,0:T(8,128)}, f32[2,1024,128]{2,1,0:T(8,128)S(1)}, u32[]{:S(2)}) copy-start(f32[2,1024,128]{2,1,0:T(8,128)S(1)} %get-tuple-element.81.refs_1_) | copy-start | bytes 3145732
  117.2 55.1 %collective-permute-start.28 = (bf16[512,2048]{1,0:T(8,128)(2,1)}, bf16[512,2048]{1,0:T(8,128)(2,1)}, u32[]{:S(2)}, u32[]{:S(2)}) collective-permute-start(bf16[512,2048]{1,0:T(8,128)(2,1)} %get-tuple-element.99.refs_5_), channel_id=1, source_target_pairs={{0,2},{2,0},{4,6},{6,4},{8,10},{10,8},{12,14},{14,12},{16,18},{18,... | collective-permute-start | bytes 6291464 | tf_op jit(solution)/shard_map/ppermute | solution.py:24
  117.2 14.8 %collective-permute-start.22 = (bf16[4,256,256]{2,1,0:T(8,128)(2,1)}, bf16[4,256,256]{2,1,0:T(8,128)(2,1)}, u32[]{:S(2)}, u32[]{:S(2)}) collective-permute-start(bf16[4,256,256]{2,1,0:T(8,128)(2,1)} %get-tuple-element.77.refs_3_), channel_id=1, source_target_pairs={{0,1},{1,0},{2,3},{3,2},{4,5},{5,4},{6,7},{7,6},{8,9},{9,8},{10,11... | collective-permute-start | bytes 1572872 | tf_op jit(solution)/shard_map/ppermute | solution.py:51
  119.1 17.1 %collective-permute-start.21 = (bf16[1024,256]{1,0:T(8,128)(2,1)}, bf16[1024,256]{1,0:T(8,128)(2,1)}, u32[]{:S(2)}, u32[]{:S(2)}) collective-permute-start(bf16[1024,256]{1,0:T(8,128)(2,1)} %get-tuple-element.82), channel_id=1, source_target_pairs={{8,0},{10,2},{12,4},{14,6},{16,8},{18,10},{20,12},{22,14},{24,16},... | collective-permute-start | bytes 1572872 | tf_op jit(solution)/shard_map/ppermute | solution.py:31
  120.4 15.7 %copy-start.4 = (f32[1024,256]{1,0:T(8,128)S(1)}, f32[1024,256]{1,0:T(8,128)}, u32[]{:S(2)}) copy-start(f32[1024,256]{1,0:T(8,128)} %copy-done.3) | copy-start | bytes 3145732
  120.4 15.7 %copy-start.7 = (bf16[2,1024,128]{2,1,0:T(8,128)(2,1)S(1)}, bf16[2,1024,128]{2,1,0:T(8,128)(2,1)}, u32[]{:S(2)}) copy-start(bf16[2,1024,128]{2,1,0:T(8,128)(2,1)} %copy-done.6) | copy-start | bytes 1572868
  120.4 15.7 %copy-start.9 = (bf16[256,256]{1,0:T(8,128)(2,1)S(1)}, bf16[256,256]{1,0:T(8,128)(2,1)}, u32[]{:S(2)}) copy-start(bf16[256,256]{1,0:T(8,128)(2,1)} %copy-done.8) | copy-start | bytes 393220
  120.5 23.7 %collective-permute-start.14 = (bf16[2,1024,128]{2,1,0:T(8,128)(2,1)}, bf16[2,1024,128]{2,1,0:T(8,128)(2,1)S(1)}, u32[]{:S(2)}, u32[]{:S(2)}) collective-permute-start(bf16[2,1024,128]{2,1,0:T(8,128)(2,1)} %copy-done.14), channel_id=1, source_target_pairs={{0,8},{2,10},{4,12},{6,14},{8,16},{10,18},{12,20},{14,22},{16,24},... | collective-permute-start | bytes 1572872 | tf_op jit(solution)/shard_map/ppermute | solution.py:31
  136.1 8.1 %copy-start.20 = (f32[2,1024,128]{2,1,0:T(8,128)S(1)}, f32[2,1024,128]{2,1,0:T(8,128)}, u32[]{:S(2)}) copy-start(f32[2,1024,128]{2,1,0:T(8,128)} %copy-done.19) | copy-start | bytes 3145732
  139.2 5.7 %collective-permute-start.26 = (bf16[2,256,512]{2,1,0:T(8,128)(2,1)S(1)}, bf16[2,256,512]{2,1,0:T(8,128)(2,1)S(1)}, u32[]{:S(2)}, u32[]{:S(2)}) collective-permute-start(bf16[2,256,512]{2,1,0:T(8,128)(2,1)S(1)} %get-tuple-element.97), channel_id=1, source_target_pairs={{0,2},{2,0},{4,6},{6,4},{8,10},{10,8},{12,14},{14,12},{16,18},{18,... | collective-permute-start | bytes 1572872 | tf_op jit(solution)/shard_map/ppermute | solution.py:24
  139.3 15.9 %collective-permute-start.23 = (bf16[2,1024,128]{2,1,0:T(8,128)(2,1)S(1)}, bf16[2,1024,128]{2,1,0:T(8,128)(2,1)S(1)}, u32[]{:S(2)}, u32[]{:S(2)}) collective-permute-start(bf16[2,1024,128]{2,1,0:T(8,128)(2,1)S(1)} %get-tuple-element.89), channel_id=1, source_target_pairs={{0,8},{2,10},{4,12},{6,14},{8,16},{10,18},{12,20},{14,22},{16,24},... | collective-permute-start | bytes 1572872 | tf_op jit(solution)/shard_map/ppermute | solution.py:31
  143.2 14.1 %collective-permute-start.29 = (bf16[4,256,256]{2,1,0:T(8,128)(2,1)S(1)}, bf16[4,256,256]{2,1,0:T(8,128)(2,1)S(1)}, u32[]{:S(2)}, u32[]{:S(2)}) collective-permute-start(bf16[4,256,256]{2,1,0:T(8,128)(2,1)S(1)} %get-tuple-element.90.refs_3_), channel_id=1, source_target_pairs={{0,1},{1,0},{2,3},{3,2},{4,5},{5,4},{6,7},{7,6},{8,9},{9,8},{10,11... | collective-permute-start | bytes 1572872 | tf_op jit(solution)/shard_map/ppermute | solution.py:51
  144.9 10.8 %copy-start.18 = (f32[2,1024,128]{2,1,0:T(8,128)S(1)}, f32[2,1024,128]{2,1,0:T(8,128)}, u32[]{:S(2)}) copy-start(f32[2,1024,128]{2,1,0:T(8,128)} %copy-done.17) | copy-start | bytes 3145732
  144.9 13.1 %collective-permute-start.19 = (bf16[2,2,256,128]{3,2,1,0:T(8,128)(2,1)S(1)}, bf16[2,2,256,128]{3,2,1,0:T(8,128)(2,1)S(1)}, u32[]{:S(2)}, u32[]{:S(2)}) collective-permute-start(bf16[2,2,256,128]{3,2,1,0:T(8,128)(2,1)S(1)} %get-tuple-element.79), channel_id=1, source_target_pairs={{0,2},{2,0},{4,6},{6,4},{8,10},{10,8},{12,14},{14,12},{16,18},{18,... | collective-permute-start | bytes 786440 | tf_op jit(solution)/shard_map/ppermute | solution.py:24
  145.0 15.4 %collective-permute-start.31 = (bf16[2,256,256]{2,1,0:T(8,128)(2,1)S(1)}, bf16[2,256,256]{2,1,0:T(8,128)(2,1)S(1)}, u32[]{:S(2)}, u32[]{:S(2)}) collective-permute-start(bf16[2,256,256]{2,1,0:T(8,128)(2,1)S(1)} %get-tuple-element.87.refs_10_), channel_id=1, source_target_pairs={{0,8},{1,9},{2,10},{3,11},{4,12},{5,13},{6,14},{7,15},{8,0},{9,1},... | collective-permute-start | bytes 786440 | tf_op jit(solution)/shard_map/ppermute | solution.py:47
  155.2 16.2 %collective-permute-start.27 = (bf16[2,256,512]{2,1,0:T(8,128)(2,1)S(1)}, bf16[2,256,512]{2,1,0:T(8,128)(2,1)S(1)}, u32[]{:S(2)}, u32[]{:S(2)}) collective-permute-start(bf16[2,256,512]{2,1,0:T(8,128)(2,1)S(1)} %mix.9), channel_id=1, source_target_pairs={{0,4},{2,6},{4,0},{6,2},{8,12},{10,14},{12,8},{14,10},{16,20},{18,... | collective-permute-start | bytes 1572872 | tf_op jit(solution)/shard_map/ppermute | solution.py:24
  157.3 5.0 %collective-permute-start.24 = (bf16[2,2,256,128]{3,2,1,0:T(8,128)(2,1)S(1)}, bf16[2,2,256,128]{3,2,1,0:T(8,128)(2,1)S(1)}, u32[]{:S(2)}, u32[]{:S(2)}) collective-permute-start(bf16[2,2,256,128]{3,2,1,0:T(8,128)(2,1)S(1)} %get-tuple-element.92), channel_id=1, source_target_pairs={{0,2},{2,0},{4,6},{6,4},{8,10},{10,8},{12,14},{14,12},{16,18},{18,... | collective-permute-start | bytes 786440 | tf_op jit(solution)/shard_map/ppermute | solution.py:24
  158.0 10.5 %collective-permute-start.30 = (bf16[2,256,256]{2,1,0:T(8,128)(2,1)S(1)}, bf16[2,256,256]{2,1,0:T(8,128)(2,1)S(1)}, u32[]{:S(2)}, u32[]{:S(2)}) collective-permute-start(bf16[2,256,256]{2,1,0:T(8,128)(2,1)S(1)} %get-tuple-element.102), channel_id=1, source_target_pairs={{0,8},{1,9},{2,10},{3,11},{4,12},{5,13},{6,14},{7,15},{8,0},{9,1},... | collective-permute-start | bytes 786440 | tf_op jit(solution)/shard_map/ppermute | solution.py:47
  160.4 22.9 %collective-permute-start.20 = (bf16[2,2,256,128]{3,2,1,0:T(8,128)(2,1)S(1)}, bf16[2,2,256,128]{3,2,1,0:T(8,128)(2,1)S(1)}, u32[]{:S(2)}, u32[]{:S(2)}) collective-permute-start(bf16[2,2,256,128]{3,2,1,0:T(8,128)(2,1)S(1)} %mix.7), channel_id=1, source_target_pairs={{0,4},{2,6},{4,0},{6,2},{8,12},{10,14},{12,8},{14,10},{16,20},{18,... | collective-permute-start | bytes 786440 | tf_op jit(solution)/shard_map/ppermute | solution.py:24
  162.4 16.7 %collective-permute-start.32 = (bf16[1,256,256]{2,1,0:T(8,128)(2,1)S(1)}, bf16[1,256,256]{2,1,0:T(8,128)(2,1)S(1)}, u32[]{:S(2)}, u32[]{:S(2)}) collective-permute-start(bf16[1,256,256]{2,1,0:T(8,128)(2,1)S(1)} %get-tuple-element.106), channel_id=1, source_target_pairs={{0,16},{1,17},{2,18},{3,19},{4,20},{5,21},{6,22},{7,23},{8,24},{9,... | collective-permute-start | bytes 393224 | tf_op jit(solution)/shard_map/ppermute | solution.py:47
  163.5 8.8 %copy-start.1 = (bf16[1024,2048]{1,0:T(8,128)(2,1)S(1)}, bf16[1024,2048]{1,0:T(8,128)(2,1)}, u32[]{:S(2)}) copy-start(bf16[1024,2048]{1,0:T(8,128)(2,1)} %refs_4_.1) | copy-start | bytes 12582916
  168.5 14.8 %collective-permute-start.25 = (bf16[2,2,256,128]{3,2,1,0:T(8,128)(2,1)S(1)}, bf16[2,2,256,128]{3,2,1,0:T(8,128)(2,1)S(1)}, u32[]{:S(2)}, u32[]{:S(2)}) collective-permute-start(bf16[2,2,256,128]{3,2,1,0:T(8,128)(2,1)S(1)} %mix.8), channel_id=1, source_target_pairs={{0,4},{2,6},{4,0},{6,2},{8,12},{10,14},{12,8},{14,10},{16,20},{18,... | collective-permute-start | bytes 786440 | tf_op jit(solution)/shard_map/ppermute | solution.py:24
  171.4 8.1 %collective-permute-start.33 = (bf16[1,256,256]{2,1,0:T(8,128)(2,1)S(1)}, bf16[1,256,256]{2,1,0:T(8,128)(2,1)S(1)}, u32[]{:S(2)}, u32[]{:S(2)}) collective-permute-start(bf16[1,256,256]{2,1,0:T(8,128)(2,1)S(1)} %get-tuple-element.103.refs_7_), channel_id=1, source_target_pairs={{0,16},{1,17},{2,18},{3,19},{4,20},{5,21},{6,22},{7,23},{8,24},{9,... | collective-permute-start | bytes 393224 | tf_op jit(solution)/shard_map/ppermute | solution.py:47
  181.3 3.8 %collective-permute-start.34 = (f32[64,512]{1,0:T(8,128)S(1)}, f32[64,512]{1,0:T(8,128)S(1)}, u32[]{:S(2)}, u32[]{:S(2)}) collective-permute-start(f32[64,512]{1,0:T(8,128)S(1)} %get-tuple-element.109), channel_id=1, source_target_pairs={{0,2},{2,0},{4,6},{6,4},{8,10},{10,8},{12,14},{14,12},{16,18},{18,... | collective-permute-start | bytes 393224 | tf_op jit(solution)/shard_map/ppermute | solution.py:24
  181.4 6.4 %collective-permute-start.35 = (f32[64,512]{1,0:T(8,128)S(1)}, f32[64,512]{1,0:T(8,128)S(1)}, u32[]{:S(2)}, u32[]{:S(2)}) collective-permute-start(f32[64,512]{1,0:T(8,128)S(1)} %get-tuple-element.110), channel_id=1, source_target_pairs={{0,4},{2,6},{4,0},{6,2},{8,12},{10,14},{12,8},{14,10},{16,20},{18,... | collective-permute-start | bytes 393224 | tf_op jit(solution)/shard_map/ppermute | solution.py:24
  182.4 7.2 %collective-permute-start.36 = (f32[64,512]{1,0:T(8,128)S(1)}, f32[64,512]{1,0:T(8,128)S(1)}, u32[]{:S(2)}, u32[]{:S(2)}) collective-permute-start(f32[64,512]{1,0:T(8,128)S(1)} %get-tuple-element.111), channel_id=1, source_target_pairs={{0,6},{2,4},{4,2},{6,0},{8,14},{10,12},{12,10},{14,8},{16,22},{18,... | collective-permute-start | bytes 393224 | tf_op jit(solution)/shard_map/ppermute | solution.py:24
  (16 other events, 25.1 us)

commit v4 on v3

--- a/solution.py
+++ b/solution.py
@@ -61,34 +61,6 @@
 
 def product_minor(left, right):
     return lax.dot_general(left, right, MINOR_DIMS, preferred_element_type=jnp.float32)
-
-
-def take_kernel(_, weight_ref, out_ref):
-    out_ref[...] = weight_ref[...]
-
-
-def take_columns(at, weight, waits):
-    depth, width = weight.shape
-    columns = width // HEAD_DIM
-    heads = columns // 2 // LANES
-
-    def source(index, at_ref):
-        return (0, index % 2 * (columns // 2) + at_ref[0] * heads + index // 2)
-
-    return pl.pallas_call(
-        ordered(take_kernel, 1, len(waits), 1, 0),
-        grid_spec=pltpu.PrefetchScalarGridSpec(
-            num_scalar_prefetch=1,
-            grid=(2 * heads,),
-            in_specs=[pl.BlockSpec((depth, HEAD_DIM), source)]
-            + [pl.BlockSpec(memory_space=pl.ANY)] * len(waits),
-            out_specs=pl.BlockSpec((depth, HEAD_DIM), lambda index, _: (0, index)),
-        ),
-        out_shape=jax.ShapeDtypeStruct((depth, 2 * heads * HEAD_DIM), weight.dtype),
-        compiler_params=pltpu.CompilerParams(vmem_limit_bytes=VMEM_GRANT),
-        cost_estimate=time_estimate(1),
-        name="take_columns",
-    )(at, weight, *waits)
 
 
 def project_kernel(at_ref, *refs, heads):
@@ -174,17 +146,19 @@
 
 def gradient_kernel(
     at_ref, own_pair, next_pair, own_ref, near_ref,
-    own_stats, far_stats, next_stats, main_stats,
-    own_out, next_out, near_grad, own_grad,
-    turned, queries, cotangents, own_weights, own_dscores, near_weights, near_dscores,
-    *, blocks, size,
+    own_stats, far_stats, next_stats, main_stats, *refs, blocks, size,
 ):
+    *earlier, own_out, next_out, near_grad, own_grad = refs[:-7]
+    turned, queries, cotangents, own_weights, own_dscores, near_weights, near_dscores = refs[-7:]
+    joined = next_out.shape[2] - HEAD_DIM
+    if earlier:
+        next_out[:, :, :joined] = earlier[0][...]
     near_valid = at_ref[0] > 0
     near_bias = jnp.where(near_valid, 0.0, MASKED)
     window = (own_ref, near_ref)
     row_tokens = blocks * size
     pairs = (own_pair, next_pair)
-    outs = (own_out, next_out)
+    outs = (own_out, next_out.at[:, :, joined:])
     weights = (own_weights, near_weights)
     dscores = (own_dscores, near_dscores)
     figures = (
@@ -265,18 +239,19 @@
         stats_kernel, "softmax_stats", at, own_pair, next_pair, kvs, (),
         [jax.ShapeDtypeStruct((8, row_tokens), jnp.float32)] * 2,
         [pltpu.VMEM((2, 2 * row_tokens // size, size, size), jnp.float32)],
-        size, (), 4, 16 * 2**20,
-    )
-
-
-def attention_grads(at, own_pair, next_pair, kvs, stats, size, waits):
+        size, (), 4, 20 * 2**20,
+    )
+
+
+def attention_grads(at, own_pair, next_pair, kvs, stats, earlier, size, waits):
     row_tokens = own_pair.shape[1]
     low = jnp.bfloat16
+    width = HEAD_DIM + (earlier[0].shape[2] if earlier else 0)
     return kernel_call(
-        gradient_kernel, "attention_grads", at, own_pair, next_pair, kvs, stats,
+        gradient_kernel, "attention_grads", at, own_pair, next_pair, kvs, (*stats, *earlier),
         [
             jax.ShapeDtypeStruct((2, row_tokens, HEAD_DIM), jnp.float32),
-            jax.ShapeDtypeStruct((2, row_tokens, HEAD_DIM), low),
+            jax.ShapeDtypeStruct((2, row_tokens, width), low),
             jax.ShapeDtypeStruct((row_tokens, 2 * HEAD_DIM), low),
             jax.ShapeDtypeStruct((row_tokens, 2 * HEAD_DIM), jnp.float32),
         ],
@@ -289,7 +264,7 @@
             pltpu.VMEM((row_tokens, 2 * row_tokens), low),
             pltpu.VMEM((row_tokens, 2 * row_tokens), low),
         ],
-        size, waits, 8, 36 * 2**20,
+        size, waits, 8, 40 * 2**20,
     )
 
 
@@ -310,6 +285,10 @@
     return pl.CostEstimate(
         flops=microseconds * 10**9, bytes_accessed=microseconds * 3 * 10**6, transcendentals=0
     )
+
+
+def work_estimate(microseconds):
+    return pl.CostEstimate(flops=microseconds * 10**9, bytes_accessed=0, transcendentals=0)
 
 
 def whole_block(value):
@@ -326,8 +305,10 @@
         grid=(1,),
         in_specs=[pl.BlockSpec(memory_space=pltpu.SMEM)]
         + [whole_block(value) for value in operands]
-        + [anywhere] * (len(waits) + len(through)),
-        out_specs=[whole_block(value) for value in out_shape] + [anywhere] * len(through),
+        + [anywhere] * len(waits)
+        + [pl.BlockSpec(memory_space=pltpu.HBM)] * len(through),
+        out_specs=[whole_block(value) for value in out_shape]
+        + [pl.BlockSpec(memory_space=pltpu.HBM)] * len(through),
         out_shape=[
             *out_shape,
             *(jax.ShapeDtypeStruct(value.shape, value.dtype) for value in through),
@@ -356,79 +337,123 @@
     return own, beside, across
 
 
-def deal_kernel(at_ref, query_ref, cotangent_ref, *outs, heads):
-    lane = at_ref[0]
-    for head in range(heads):
-        own, held, given = outs[3 * head : 3 * head + 3]
-        for bits, out in enumerate((own, given.at[0], held, given.at[1])):
-            column = at_offset((lane ^ bits) * heads + head, HEAD_DIM)
-            out[0] = query_ref[0, :, column]
-            out[1] = cotangent_ref[0, :, column]
-
-
-def deal_heads(at, queries, upstream):
+def deal_kernel(at_ref, query_ref, cotangent_ref, *refs):
+    columns, outs, taken_ref = refs[: -LANES - 1], refs[-LANES - 1 : -1], refs[-1]
+    width = outs[0].shape[2]
+    for bits, out in enumerate(outs):
+        held = at_offset(at_ref[0] ^ bits, width)
+        out[0] = query_ref[0, :, held]
+        out[1] = cotangent_ref[0, :, held]
+    for index, column in enumerate(columns):
+        taken_ref[:, index * HEAD_DIM : (index + 1) * HEAD_DIM] = column[...]
+
+
+def deal(at, queries, upstream, weight):
     _, size, width = queries.shape
+    depth = weight.shape[0]
     heads = width // LANES // HEAD_DIM
-    piece = jax.ShapeDtypeStruct((2, size, HEAD_DIM), jnp.bfloat16)
-    pair = jax.ShapeDtypeStruct((2, *piece.shape), jnp.bfloat16)
+    piece = jax.ShapeDtypeStruct((2, size, width // LANES), jnp.bfloat16)
+    taken = jax.ShapeDtypeStruct((depth, 2 * heads * HEAD_DIM), weight.dtype)
+
+    def column(index):
+        first = index % 2 * (width // HEAD_DIM) + index // 2
+        return pl.BlockSpec((depth, HEAD_DIM), lambda _, at_ref: (0, first + at_ref[0] * heads))
+
+    outs = pl.pallas_call(
+        deal_kernel,
+        grid_spec=pltpu.PrefetchScalarGridSpec(
+            num_scalar_prefetch=1,
+            grid=(1,),
+            in_specs=[whole_block(queries), whole_block(upstream)]
+            + [column(index) for index in range(2 * heads)],
+            out_specs=[whole_block(piece)] * LANES + [whole_block(taken)],
+        ),
+        out_shape=[piece] * LANES + [taken],
+        compiler_params=pltpu.CompilerParams(vmem_limit_bytes=VMEM_GRANT),
+        cost_estimate=work_estimate(2),
+        name="deal",
+    )(at, queries, upstream, *[weight] * (2 * heads))
+    return outs[:LANES], outs[LANES]
+
+
+def take_rows_kernel(_, weight_ref, out_ref):
+    out_ref[...] = weight_ref[...]
+
+
+def take_rows(at, weight):
+    shape = (weight.shape[0] // 2, weight.shape[1])
+    return pl.pallas_call(
+        take_rows_kernel,
+        grid_spec=pltpu.PrefetchScalarGridSpec(
+            num_scalar_prefetch=1,
+            grid=(1,),
+            in_specs=[pl.BlockSpec(shape, lambda _, at_ref: (at_ref[2], 0))],
+            out_specs=pl.BlockSpec(shape, lambda *_: (0, 0)),
+        ),
+        out_shape=jax.ShapeDtypeStruct(shape, weight.dtype),
+        compiler_params=pltpu.CompilerParams(vmem_limit_bytes=VMEM_GRANT),
+        cost_estimate=work_estimate(2),
+        name="take_rows",
+    )(at, weight)
+
+
+def place_rows_kernel(at_ref, *refs):
+    pieces, outs = refs[:LANES], refs[LANES:]
+    size = pieces[0].shape[1]
+    for bits, piece in enumerate(pieces):
+        for head, out in enumerate(outs):
+            column = slice(head * HEAD_DIM, (head + 1) * HEAD_DIM)
+            out[:, at_offset(at_ref[0] ^ bits, size)] = piece[:, :, column]
+
+
+def place_rows(at, pieces, waits, through):
+    kinds, size, width = pieces[0].shape
+    heads = width // HEAD_DIM
+    whole = jax.ShapeDtypeStruct((kinds, LANES * size, HEAD_DIM), pieces[0].dtype)
     outs = small_call(
-        functools.partial(deal_kernel, heads=heads),
-        "deal_heads", at, (queries, upstream), [piece, piece, pair] * heads,
-    )
-    return [outs[3 * head : 3 * head + 3] for head in range(heads)]
-
-
-def place_rows_kernel(at_ref, own, beside, across, out):
-    size = own.shape[1]
-    for bits, piece in enumerate((own, beside.at[0], across.at[0], across.at[1])):
-        out[:, at_offset(at_ref[0] ^ bits, size)] = piece[...]
-
-
-def place_rows(at, found, waits, through):
-    own, beside, across = found
-    kinds, size, width = own.shape
-    whole = jax.ShapeDtypeStruct((kinds, LANES * size, width), own.dtype)
-    return small_call(
-        place_rows_kernel, "place_rows", at, (own, beside, across), [whole],
-        waits=waits, through=through,
-    )
-
-
-def settle_kernel(at_ref, own_out, arrived, own, held, given):
+        place_rows_kernel, "place_rows", at, pieces, [whole] * heads, waits=waits, through=through
+    )
+    return outs[:heads], outs[heads:]
+
+
+TOKEN = jax.ShapeDtypeStruct((8, 128), jnp.float32)
+
+
+def settle_kernel(at_ref, *refs, heads):
+    own_outs, arrived, (own, held, given) = refs[:heads], refs[heads], refs[heads + 1 :]
     size = own.shape[1]
     for bits, out in enumerate((own, given.at[0], held, given.at[1])):
         rows = at_offset(at_ref[0] ^ bits, size)
-        out[...] = (own_out[:, rows] + arrived[:, rows].astype(jnp.float32)).astype(jnp.bfloat16)
-
-
-def settle_out(at, own_out, arrived, waits):
-    kinds, count, width = own_out.shape
+        for head, own_out in enumerate(own_outs):
+            column = slice(head * HEAD_DIM, (head + 1) * HEAD_DIM)
+            whole = own_out[:, rows] + arrived[:, rows, column].astype(jnp.float32)
+            out[:, :, column] = whole.astype(jnp.bfloat16)
+
+
+def settle_outs(at, own_outs, arrived, waits):
+    kinds, count, width = arrived.shape
     piece = jax.ShapeDtypeStruct((kinds, count // LANES, width), jnp.bfloat16)
     pair = jax.ShapeDtypeStruct((2, *piece.shape), jnp.bfloat16)
     return small_call(
-        settle_kernel, "settle_out", at, (own_out, arrived), [piece, piece, pair], waits=waits
-    )
-
-
-def place_heads_kernel(at_ref, *refs, heads):
-    outs = refs[3 * heads :]
-    for head in range(heads):
-        own, beside, across = refs[3 * head : 3 * head + 3]
-        for bits, piece in enumerate((own, beside.at[0], across.at[0], across.at[1])):
-            column = at_offset((at_ref[0] ^ bits) * heads + head, HEAD_DIM)
-            for kind, out in enumerate(outs):
-                out[0, :, column] = piece[kind]
+        functools.partial(settle_kernel, heads=len(own_outs)),
+        "settle_outs", at, (*own_outs, arrived), [piece, piece, pair], waits=waits,
+    )
+
+
+def place_heads_kernel(at_ref, own, beside, across, *outs):
+    *outs, token = outs
+    token[...] = jnp.zeros_like(token)
+    width = own.shape[2]
+    for bits, piece in enumerate((own, beside.at[0], across.at[0], across.at[1])):
+        column = at_offset(at_ref[0] ^ bits, width)
+        for kind, out in enumerate(outs):
+            out[0, :, column] = piece[kind]
 
 
 def place_heads(at, found):
-    heads = len(found)
-    kinds, size, width = found[0][0].shape
-    whole = jax.ShapeDtypeStruct((1, size, LANES * heads * width), jnp.bfloat16)
-    return small_call(
-        functools.partial(place_heads_kernel, heads=heads),
-        "place_heads", at, [value for part in found for value in part],
-        [whole] * kinds,
-    )
+    kinds, size, width = found[0].shape
+    whole = jax.ShapeDtypeStruct((1, size, LANES * width), jnp.bfloat16)
+    return small_call(place_heads_kernel, "place_heads", at, found, [whole] * kinds + [TOKEN])
 
 
 def spread_kernel(at_ref, *refs, rows, before):
@@ -488,13 +513,14 @@
 
 
 def feature_kernel(at_ref, *refs, heads, counts):
-    (own, beside, across), weights, (out_ref, tokens) = refs[:3], refs[3:-2], refs[-2:]
+    (own, beside, across), weights, (out_ref, token, tokens) = refs[:3], refs[3:-3], refs[-3:]
     pieces = (own, beside.at[0], across.at[0], across.at[1])
     step = pl.program_id(0)
     width = tokens.shape[1] // 2
 
     @pl.when(step == 0)
     def _():
+        token[...] = jnp.zeros_like(token)
         for head in range(heads):
             for bits in range(LANES):
                 piece = pieces[bits][:, 2 * head * HEAD_DIM : 2 * (head + 1) * HEAD_DIM]
@@ -543,7 +569,7 @@
             functools.partial(feature_kernel, heads=heads, counts=counts),
             len(pieces) + len(weights),
             len(waits),
-            1,
+            2,
             0,
         ),
         grid_spec=pltpu.PrefetchScalarGridSpec(
@@ -552,10 +578,13 @@
             in_specs=[whole_block(piece) for piece in pieces]
             + [weight_spec(*found) for found in zip(weights, starts, counts)]
             + [pl.BlockSpec(memory_space=pl.ANY)] * len(waits),
-            out_specs=pl.BlockSpec((1, size, step), lambda index, at_ref: (0, 0, place(index, at_ref))),
+            out_specs=[
+                pl.BlockSpec((1, size, step), lambda index, at_ref: (0, 0, place(index, at_ref))),
+                whole_block(TOKEN),
+            ],
             scratch_shapes=[pltpu.VMEM((size, weights[0].shape[1]), jnp.bfloat16)],
         ),
-        out_shape=jax.ShapeDtypeStruct((1, size, depth), jnp.bfloat16),
+        out_shape=[jax.ShapeDtypeStruct((1, size, depth), jnp.bfloat16), TOKEN],
         compiler_params=pltpu.CompilerParams(vmem_limit_bytes=VMEM_GRANT),
         cost_estimate=time_estimate(6),
         name="feature_grads",
@@ -649,9 +678,8 @@
     half = lax.axis_index("dp")
     core = place % 2
 
-    here = jnp.stack([lane, half]).astype(jnp.int32)
-    dealt = deal_heads(here, queries, upstream)
-    lane_weight = take_columns(here, kv_weight, dealt[0][:1])
+    here = jnp.stack([lane, half, core]).astype(jnp.int32)
+    pair_pieces, lane_weight = deal(here, queries, upstream, kv_weight)
     other_lane_weight = swapped(lane_weight)
     across = exchanged(tokens, 2)
     beside = exchanged(tokens, 1)
@@ -661,15 +689,8 @@
     owns = project(here, row_tokens, (lane_weight, other_lane_weight))
     windows = [(own, shifted(own, 1)) for own in owns]
 
-    part_rows = weight_rows // 2
-    through = [lax.dynamic_slice_in_dim(kv_weight, core * part_rows, part_rows, 0)]
-    own_pairs = []
-    for pieces in dealt:
-        own_pair, *handed = place_rows(here, go_round(here, pieces), owns[:1], through)
-        if through:
-            (part,) = handed
-        through = []
-        own_pairs.append(own_pair)
+    part = take_rows(here, kv_weight)
+    own_pairs, (part,) = place_rows(here, passed_round(pair_pieces), owns[:1], (part,))
     next_pairs = [shifted(own_pair, -1) for own_pair in own_pairs]
 
     fetched = swapped(part)
@@ -683,52 +704,54 @@
         shared.append(
             (own_stats, turned_round(next_stats, 1), next_stats, turned_round(own_stats, -1))
         )
-    gained = [
-        attention_grads(
-            at, own_pairs[head], next_pairs[head], windows[head], shared[head], size,
-            (shared[-1][0],),
+    gained, next_out = [], ()
+    for head in range(heads):
+        gained.append(
+            attention_grads(
+                at, own_pairs[head], next_pairs[head], windows[head], shared[head], next_out, size,
+                (shared[-1][0],),
+            )
         )
-        for head in range(heads)
-    ]
+        next_out = (gained[-1][1],)
+    own_outs = [found[0] for found in gained]
 
     bits = jnp.stack([(row >> index) % 2 for index in range(rows.bit_length() - 1)])
-    kv_pieces, parts, out_pieces = [], [], []
+    kv_pieces, parts = [], []
     waits, through = (gained[-1][3],), (fetched,)
-    for head, (own_out, next_out, near_grad, own_grad) in enumerate(gained):
-        if head:
-            through = (next_out,)
-        else:
-            next_out = shifted(next_out, 1)
-        kv_pieces, kept, sent, (handed,) = spread(
+    arrived_out = shifted(next_out[0], 1)
+    for head, (_, _, near_grad, own_grad) in enumerate(gained):
+        kv_pieces, kept, sent, handed = spread(
             here, row_tokens, own_grad, shifted(near_grad, -1), kv_pieces, rows, waits, through
         )
-        if head:
-            next_out = shifted(handed, 1)
-        else:
-            fetched = handed
+        if through:
+            (fetched,) = handed
             passed = exchanged(fetched, 1)
-        out_pieces.append(go_round(here, settle_out(here, own_out, next_out, (sent,))))
+        if head == heads - 1:
+            kv_found = go_round(here, kv_pieces)
+            out_found = go_round(here, settle_outs(here, own_outs, arrived_out, (sent,)))
+        waits, through = (), ()
         arrived = [swapped(sent)]
-        waits = ()
         distance = 1
         while distance < rows:
-            kept, sent = merge(bits, distance.bit_length() - 1, kept, arrived)
+            last = head == heads - 1 and 2 * distance == rows
+            kept, sent = merge(
+                bits, distance.bit_length() - 1, kept, arrived, kv_found[2:] if last else ()
+            )
             arrived = [moved(sent, distance * LANES, 0)]
             if not waits:
                 waits = (sent,)
             distance *= 2
         parts.append((kept, *arrived))
-    kv_found = go_round(here, kv_pieces)
-
-    feature_grad = feature_grads(
-        jnp.stack([lane, half, core]).astype(jnp.int32),
+
+    feature_grad, feature_token = feature_grads(
+        here,
         kv_found,
         (kv_weight, fetched, passed),
         (sent,),
     )
-    attended, query_grad = place_heads(here, out_pieces)
-    pieces = passed_round(finish(here, parts, (feature_grad,)))
-    weight_grad = place_weight(here, pieces, (attended,))
+    attended, query_grad, token = place_heads(here, out_found)
+    pieces = passed_round(finish(here, parts, (feature_token,)))
+    weight_grad = place_weight(here, pieces, (token,))
     return (attended, query_grad, feature_grad, weight_grad)
 
 

time: 193 us -> 183 us (0.948)
  waiting for transfers between devices: 51.3 us -> 60.4 us
  Pallas kernels: 68.8 us -> 60.3 us
  local copies, waits for them, and re-layouts: 15.1 us -> 9.48 us
  starting transfers between devices: 55.5 us -> 50.6 us
    pallas_call x20 -> x14, Pallas kernels: 29.1 us -> 20.6 us  [small_call(): pl.pallas_call(ordered(kernel, len(operands), len(waits), len(out_shape),...]
    ppermute x8 -> x7, starting transfers between devices: 24.4 us -> 19.8 us  [shifted(): lax.ppermute(value, 'seq', [(source, source + steps) for source in range(...]
    ppermute x17 -> x14, waiting for transfers between devices: 19 us -> 23 us  [exchanged(): lax.ppermute(value, 'seq', [(source, source ^ bits) for source in range(c...]
    ppermute x4, waiting for transfers between devices: 13.7 us -> 17.7 us  [swapped(): return lax.ppermute(value, 'dp', [(0, 1), (1, 0)])]
    unnamed x54 -> x40, local copies, waits for them, and re-layouts: 13.2 us -> 9.48 us
    ppermute x17 -> x14, starting transfers between devices: 12.2 us -> 9.04 us  [exchanged(): lax.ppermute(value, 'seq', [(source, source ^ bits) for source in range(c...]
    ppermute x4, starting transfers between devices: 8.72 us -> 11.7 us  [turned_round(): return lax.ppermute(value, 'seq', pairs)]
    ppermute x4, waiting for transfers between devices: 4.95 us -> 7.07 us  [moved(): return lax.ppermute(value, ('seq', 'dp'), pairs)]
  transfers between devices with their start and end apart: 37 -> 33, of which waited for: 16 -> 15; matrix products, arithmetic and copies ran while one was open for 1% -> 0% of each run, Pallas kernels for 33% -> 30%
where the time goes in v4:
time: 183 us; the launch traced here: 182 us
  waiting for transfers between devices  60.4 us (33%)
  Pallas kernels  60.3 us (33%)
  starting transfers between devices  50.6 us (28%)
  local copies, waits for them, and re-layouts  9.48 us (5%)
    pallas_call x4, Pallas kernels, kernel_call(): pl.pallas_call(ordered(functools.partial(kernel, blocks=blocks, size=size...  31 us
    ppermute x14, waiting for transfers between devices, exchanged(): lax.ppermute(value, 'seq', [(source, source ^ bits) for source in range(c...  23 us
    pallas_call x14, Pallas kernels, small_call(): pl.pallas_call(ordered(kernel, len(operands), len(waits), len(out_shape),...  20.6 us
    ppermute x7, starting transfers between devices, shifted(): lax.ppermute(value, 'seq', [(source, source + steps) for source in range(...  19.8 us
    ppermute x4, waiting for transfers between devices, swapped(): return lax.ppermute(value, 'dp', [(0, 1), (1, 0)])  17.7 us
    ppermute x7, waiting for transfers between devices, shifted(): lax.ppermute(value, 'seq', [(source, source + steps) for source in range(...  12.6 us
    ppermute x4, starting transfers between devices, turned_round(): return lax.ppermute(value, 'seq', pairs)  11.7 us
    unnamed x40, local copies, waits for them, and re-layouts  9.48 us
  transfers between devices with their start and end apart: 33, of which 15 were waited for; matrix products, arithmetic and copies ran while one was open for 0% of the time, Pallas kernels for 30%

profile of v4, /device:TPU:0, one launch (start us, length us, event | category | flops | bytes accessed | tf_op | source)
XLA Modules:
  0.0 181.9 jit_solution(17781508538154105291)
XLA Ops:
  0.6 3.0 %collective-permute-start.4 = (bf16[256,2048]{1,0:T(8,128)(2,1)}, bf16[256,2048]{1,0:T(8,128)(2,1)S(1)}, u32[]{:S(2)}, u32[]{:S(2)}) collective-permute-start(bf16[256,2048]{1,0:T(8,128)(2,1)} %bitcast.7), channel_id=1, source_target_pairs={{0,4},{2,6},{4,0},{6,2},{8,12},{10,14},{12,8},{14,10},{16,20},{18,... | collective-permute-start | bytes 3145736 | tf_op jit(solution)/shard_map/ppermute | solution.py:24
  3.7 2.2 %copy-done = bf16[1024,2048]{1,0:T(8,128)(2,1)S(1)} copy-done((bf16[1024,2048]{1,0:T(8,128)(2,1)S(1)}, bf16[1024,2048]{1,0:T(8,128)(2,1)}, u32[]{:S(2)}) %copy-start) | copy-done | bytes 4194328
  9.1 1.6 collective-permute-start.6
  10.7 16.3 %collective-permute-done.4.refs_3_ = bf16[256,2048]{1,0:T(8,128)(2,1)S(1)} collective-permute-done((bf16[256,2048]{1,0:T(8,128)(2,1)}, bf16[256,2048]{1,0:T(8,128)(2,1)S(1)}, u32[]{:S(2)}, u32[]{:S(2)}) %collective-permute-start.4) | collective-permute-done | bytes 1048608 | tf_op jit(solution)/shard_map/ppermute | solution.py:24
  27.5 1.7 collective-permute-start.1
  30.0 4.7 %collective-permute-done.6.refs_6_ = bf16[1024,512]{1,0:T(8,128)(2,1)S(1)} collective-permute-done((bf16[1024,512]{1,0:T(8,128)(2,1)S(1)}, bf16[1024,512]{1,0:T(8,128)(2,1)S(1)}, u32[]{:S(2)}, u32[]{:S(2)}) %collective-permute-start.6) | collective-permute-done | bytes 1048608 | tf_op jit(solution)/shard_map/ppermute | solution.py:51
  34.8 3.9 %project.1 = (bf16[1024,256]{1,0:T(8,128)(2,1)}, bf16[1024,256]{1,0:T(8,128)(2,1)}) custom-call(s32[3]{0:T(128)S(1)} %pad_add_fusion.at_ref.refs_0_._, bf16[256,2048]{1,0:T(8,128)(2,1)S(1)} %bitcast.9, bf16[256,2048]{1,0:T(8,128)(2,1)S(1)} %collective-permute-done.3.refs_2_, bf16[256,2048]{1,0:T(8,128)(2,1)S(1)} %collective-permute-done.4.refs_3_, ...), custom_call_target="tpu_custom_call" | custom-call | flops 4000000000 | bytes 12000000 | tf_op jit(solution)/shard_map/project/pallas_call | solution.py:303
  38.7 1.9 %collective-permute-done.2.refs_4_ = bf16[2,256,256]{2,1,0:T(8,128)(2,1)S(1)} collective-permute-done((bf16[2,256,256]{2,1,0:T(8,128)(2,1)S(1)}, bf16[2,256,256]{2,1,0:T(8,128)(2,1)S(1)}, u32[]{:S(2)}, u32[]{:S(2)}) %collective-permute-start.2) | collective-permute-done | bytes 262176 | tf_op jit(solution)/shard_map/ppermute | solution.py:24
  40.6 1.7 place_rows.1
  42.3 1.3 copy-done.13
  43.6 1.3 collective-permute-start.7
  44.9 5.4 %collective-permute-start.8 = (bf16[1024,256]{1,0:T(8,128)(2,1)}, bf16[1024,256]{1,0:T(8,128)(2,1)}, u32[]{:S(2)}, u32[]{:S(2)}) collective-permute-start(bf16[1024,256]{1,0:T(8,128)(2,1)} %get-tuple-element.62.refs_5_.refs_3_), channel_id=1, source_target_pairs={{0,8},{2,10},{4,12},{6,14},{8,16},{10,18},{12,20},{14,22},{16,24},... | collective-permute-start | bytes 1572872 | tf_op jit(solution)/shard_map/ppermute | solution.py:31
  50.3 1.3 collective-permute-start.11
  51.6 5.4 %collective-permute-start.12 = (bf16[1024,256]{1,0:T(8,128)(2,1)}, bf16[1024,256]{1,0:T(8,128)(2,1)}, u32[]{:S(2)}, u32[]{:S(2)}) collective-permute-start(bf16[1024,256]{1,0:T(8,128)(2,1)} %get-tuple-element.67.refs_3_), channel_id=1, source_target_pairs={{0,8},{2,10},{4,12},{6,14},{8,16},{10,18},{12,20},{14,22},{16,24},... | collective-permute-start | bytes 1572872 | tf_op jit(solution)/shard_map/ppermute | solution.py:31
  57.0 1.5 collective-permute-start.18
  58.6 2.0 %collective-permute-done.7.refs_2_ = bf16[2,1024,128]{2,1,0:T(8,128)(2,1)} collective-permute-done((bf16[2,1024,128]{2,1,0:T(8,128)(2,1)}, bf16[2,1024,128]{2,1,0:T(8,128)(2,1)}, u32[]{:S(2)}, u32[]{:S(2)}) %collective-permute-start.7) | collective-permute-done | bytes 524320 | tf_op jit(solution)/shard_map/ppermute | solution.py:31
  60.6 1.4 collective-permute-done.8.refs_4_
  62.0 5.3 %softmax_stats.2 = (f32[8,1024]{1,0:T(8,128)S(1)}, f32[8,1024]{1,0:T(8,128)S(1)}) custom-call(s32[2]{0:T(128)S(1)} %pad_add_fusion.1.refs_0_, bf16[2,1024,128]{2,1,0:T(8,128)(2,1)} %get-tuple-element.63.refs_1_, bf16[2,1024,128]{2,1,0:T(8,128)(2,1)} %collective-permute-done.7.refs_2_, bf16[1024,256]{1,0:T(8,128)(2,1)} %get-tuple-element.62.refs_5_.refs_3_, ...), custom_call_target="tpu_custom_call" | custom-call | flops 4000000000 | bytes 12000000 | tf_op jit(solution)/shard_map/softmax_stats/pallas_call | solution.py:213
  67.3 5.3 %collective-permute-start.10 = (f32[8,1024]{1,0:T(8,128)S(1)}, f32[8,1024]{1,0:T(8,128)S(1)}, u32[]{:S(2)}, u32[]{:S(2)}) collective-permute-start(f32[8,1024]{1,0:T(8,128)S(1)} %get-tuple-element.64.refs_5_), channel_id=1, source_target_pairs={{0,24},{2,26},{4,28},{6,30},{8,0},{10,2},{12,4},{14,6},{16,8},{18,... | collective-permute-start | bytes 98312 | tf_op jit(solution)/shard_map/ppermute | solution.py:37
  73.1 5.3 %softmax_stats.3 = (f32[8,1024]{1,0:T(8,128)S(1)}, f32[8,1024]{1,0:T(8,128)S(1)}) custom-call(s32[2]{0:T(128)S(1)} %pad_add_fusion.1.refs_0_, bf16[2,1024,128]{2,1,0:T(8,128)(2,1)} %get-tuple-element.66.refs_1_, bf16[2,1024,128]{2,1,0:T(8,128)(2,1)} %collective-permute-done.11.refs_2_, bf16[1024,256]{1,0:T(8,128)(2,1)} %get-tuple-element.67.refs_3_, ...), custom_call_target="tpu_custom_call" | custom-call | flops 4000000000 | bytes 12000000 | tf_op jit(solution)/shard_map/softmax_stats/pallas_call | solution.py:213
  78.4 2.5 %collective-permute-start.13 = (f32[8,1024]{1,0:T(8,128)S(1)}, f32[8,1024]{1,0:T(8,128)S(1)}, u32[]{:S(2)}, u32[]{:S(2)}) collective-permute-start(f32[8,1024]{1,0:T(8,128)S(1)} %get-tuple-element.70.refs_7_), channel_id=1, source_target_pairs={{0,8},{2,10},{4,12},{6,14},{8,16},{10,18},{12,20},{14,22},{16,24},... | collective-permute-start | bytes 98312 | tf_op jit(solution)/shard_map/ppermute | solution.py:37
  81.0 3.8 %collective-permute-start.14 = (f32[8,1024]{1,0:T(8,128)S(1)}, f32[8,1024]{1,0:T(8,128)S(1)}, u32[]{:S(2)}, u32[]{:S(2)}) collective-permute-start(f32[8,1024]{1,0:T(8,128)S(1)} %get-tuple-element.68.refs_9_.refs_5_.refs_10_), channel_id=1, source_target_pairs={{0,24},{2,26},{4,28},{6,30},{8,0},{10,2},{12,4},{14,6},{16,8},{18,... | collective-permute-start | bytes 98312 | tf_op jit(solution)/shard_map/ppermute | solution.py:37
  84.8 9.6 %attention_grads.2 = (f32[2,1024,128]{2,1,0:T(8,128)S(1)}, bf16[2,1024,128]{2,1,0:T(8,128)(2,1)S(1)}, bf16[1024,256]{1,0:T(8,128)(2,1)S(1)}, f32[1024,256]{1,0:T(8,128)S(1)}) custom-call(s32[2]{0:T(128)S(1)} %pad_add_fusion.1.refs_0_, bf16[2,1024,128]{2,1,0:T(8,128)(2,1)} %get-tuple-element.63.refs_1_, bf16[2,1024,128]{2,1,0:T(8,128)(2,1)} %collective-permute-done.7.refs_2_, ...), custom_call_target="tpu_custom_call" | custom-call | flops 8000000000 | bytes 24000000 | tf_op jit(solution)/shard_map/attention_grads/pallas_call | solution.py:213
  95.4 1.5 collective-permute-start.17
  96.9 10.8 %attention_grads.3 = (f32[2,1024,128]{2,1,0:T(8,128)S(1)}, bf16[2,1024,256]{2,1,0:T(8,128)(2,1)}, bf16[1024,256]{1,0:T(8,128)(2,1)}, f32[1024,256]{1,0:T(8,128)S(1)}) custom-call(s32[2]{0:T(128)S(1)} %pad_add_fusion.1.refs_0_, bf16[2,1024,128]{2,1,0:T(8,128)(2,1)} %get-tuple-element.66.refs_1_, bf16[2,1024,128]{2,1,0:T(8,128)(2,1)} %collective-permute-done.11.refs_2_, ...), custom_call_target="tpu_custom_call" | custom-call | flops 8000000000 | bytes 24000000 | tf_op jit(solution)/shard_map/attention_grads/pallas_call | solution.py:213
  107.8 2.1 %collective-permute-done.17.refs_6_ = bf16[1024,256]{1,0:T(8,128)(2,1)S(1)} collective-permute-done((bf16[1024,256]{1,0:T(8,128)(2,1)S(1)}, bf16[1024,256]{1,0:T(8,128)(2,1)S(1)}, u32[]{:S(2)}, u32[]{:S(2)}) %collective-permute-start.17) | collective-permute-done | bytes 524320 | tf_op jit(solution)/shard_map/ppermute | solution.py:31
  109.9 2.9 %spread.2 = (bf16[256,256]{1,0:T(8,128)(2,1)S(1)}, bf16[256,256]{1,0:T(8,128)(2,1)S(1)}, bf16[2,256,256]{2,1,0:T(8,128)(2,1)S(1)}, f32[4,256,256]{2,1,0:T(8,128)...) custom-call(s32[3]{0:T(128)S(1)} %pad_add_fusion.at_ref.refs_0_._, ...), custom_call_target="tpu_custom_call", output_to_operand_aliasing={{5}: (8, {})} | custom-call | tf_op jit(solution)/shard_map/spread/pallas_call | solution.py:303
  114.4 1.5 collective-permute-start.19
  116.0 3.4 %collective-permute-start.15 = (bf16[2,1024,256]{2,1,0:T(8,128)(2,1)}, bf16[2,1024,256]{2,1,0:T(8,128)(2,1)}, u32[]{:S(2)}, u32[]{:S(2)}) collective-permute-start(bf16[2,1024,256]{2,1,0:T(8,128)(2,1)} %get-tuple-element.73), channel_id=1, source_target_pairs={{0,8},{2,10},{4,12},{6,14},{8,16},{10,18},{12,20},{14,22},{16,24},... | collective-permute-start | bytes 3145736 | tf_op jit(solution)/shard_map/ppermute | solution.py:31
  119.4 1.5 collective-permute-start.16
  121.0 8.0 %collective-permute-done.19.refs_2_ = bf16[4,256,256]{2,1,0:T(8,128)(2,1)} collective-permute-done((bf16[4,256,256]{2,1,0:T(8,128)(2,1)}, bf16[4,256,256]{2,1,0:T(8,128)(2,1)}, u32[]{:S(2)}, u32[]{:S(2)}) %collective-permute-start.19) | collective-permute-done | bytes 524320 | tf_op jit(solution)/shard_map/ppermute | solution.py:51
  129.1 1.2 copy-done.15
  130.3 1.1 merge.4
  131.5 3.9 %collective-permute-done.16.refs_6_ = bf16[1024,256]{1,0:T(8,128)(2,1)} collective-permute-done((bf16[1024,256]{1,0:T(8,128)(2,1)}, bf16[1024,256]{1,0:T(8,128)(2,1)}, u32[]{:S(2)}, u32[]{:S(2)}) %collective-permute-start.16) | collective-permute-done | bytes 524320 | tf_op jit(solution)/shard_map/ppermute | solution.py:31
  135.4 2.8 %spread.3 = (bf16[256,512]{1,0:T(8,128)(2,1)S(1)}, bf16[256,512]{1,0:T(8,128)(2,1)S(1)}, bf16[2,256,512]{2,1,0:T(8,128)(2,1)S(1)}, f32[4,256,256]{2,1,0:T(8,128)S(1)}, bf16[4,256,256]{2,1,0:T(8,128)(2,1)S(1)}) custom-call(s32[3]{0:T(128)S(1)} %pad_add_fusion.at_ref.refs_0_._, bf16[256,2048]{1,0:T(8,128)(2,1)S(1)} %bitcast.11, ...), custom_call_target="tpu_custom_call" | custom-call | tf_op jit(solution)/shard_map/spread/pallas_call | solution.py:303
  138.8 2.7 %collective-permute-done.15.refs_3_ = bf16[2,1024,256]{2,1,0:T(8,128)(2,1)} collective-permute-done((bf16[2,1024,256]{2,1,0:T(8,128)(2,1)}, bf16[2,1024,256]{2,1,0:T(8,128)(2,1)}, u32[]{:S(2)}, u32[]{:S(2)}) %collective-permute-start.15) | collective-permute-done | bytes 1048608 | tf_op jit(solution)/shard_map/ppermute | solution.py:31
  141.5 1.5 settle_outs.1
  143.7 1.6 collective-permute-start.23
  145.2 2.5 %collective-permute-start.27 = (bf16[2,256,256]{2,1,0:T(8,128)(2,1)S(1)}, bf16[2,256,256]{2,1,0:T(8,128)(2,1)S(1)}, u32[]{:S(2)}, u32[]{:S(2)}) collective-permute-start(bf16[2,256,256]{2,1,0:T(8,128)(2,1)S(1)} %get-tuple-element.84.refs_10_), channel_id=1, source_target_pairs={{0,8},{1,9},{2,10},{3,11},{4,12},{5,13},{6,14},{7,15},{8,0},{9,1},... | collective-permute-start | bytes 786440 | tf_op jit(solution)/shard_map/ppermute | solution.py:47
  147.7 4.9 %collective-permute-done.25.refs_2_ = bf16[4,256,256]{2,1,0:T(8,128)(2,1)S(1)} collective-permute-done((bf16[4,256,256]{2,1,0:T(8,128)(2,1)S(1)}, bf16[4,256,256]{2,1,0:T(8,128)(2,1)S(1)}, u32[]{:S(2)}, u32[]{:S(2)}) %collective-permute-start.25) | collective-permute-done | bytes 524320 | tf_op jit(solution)/shard_map/ppermute | solution.py:51
  155.0 2.3 %collective-permute-start.28 = (bf16[1,256,256]{2,1,0:T(8,128)(2,1)S(1)}, bf16[1,256,256]{2,1,0:T(8,128)(2,1)S(1)}, u32[]{:S(2)}, u32[]{:S(2)}) collective-permute-start(bf16[1,256,256]{2,1,0:T(8,128)(2,1)S(1)} %get-tuple-element.102), channel_id=1, source_target_pairs={{0,16},{1,17},{2,18},{3,19},{4,20},{5,21},{6,22},{7,23},{8,24},{9,... | collective-permute-start | bytes 393224 | tf_op jit(solution)/shard_map/ppermute | solution.py:47
  158.0 6.0 %collective-permute-done.26.refs_2_ = bf16[2,256,256]{2,1,0:T(8,128)(2,1)S(1)} collective-permute-done((bf16[2,256,256]{2,1,0:T(8,128)(2,1)S(1)}, bf16[2,256,256]{2,1,0:T(8,128)(2,1)S(1)}, u32[]{:S(2)}, u32[]{:S(2)}) %collective-permute-start.26) | collective-permute-done | bytes 262176 | tf_op jit(solution)/shard_map/ppermute | solution.py:47
  164.7 6.9 %feature_grads.1 = (bf16[1,256,2048]{2,1,0:T(8,128)(2,1)}, f32[8,128]{1,0:T(8,128)S(1)}) custom-call(s32[3]{0:T(128)S(1)} %pad_add_fusion.at_ref.refs_0_._, bf16[256,512]{1,0:T(8,128)(2,1)S(1)} %get-tuple-element.91.refs_1_, bf16[2,256,512]{2,1,0:T(8,128)(2,1)S(1)} %collective-permute-done.22.refs_2_, ...), custom_call_target="tpu_custom_call" | custom-call | flops 6000000000 | bytes 18000000 | tf_op jit(solution)/shard_map/feature_grads/pallas_call | solution.py:567
  172.3 1.6 collective-permute-start.31
  174.2 1.6 place_heads.1
  175.8 2.8 %collective-permute-done.31.refs_3_ = f32[64,512]{1,0:T(8,128)S(1)} collective-permute-done((f32[64,512]{1,0:T(8,128)S(1)}, f32[64,512]{1,0:T(8,128)S(1)}, u32[]{:S(2)}, u32[]{:S(2)}) %collective-permute-start.31) | collective-permute-done | bytes 131104 | tf_op jit(solution)/shard_map/ppermute | solution.py:24
  178.7 1.9 %collective-permute-done.32.refs_4_ = f32[64,512]{1,0:T(8,128)S(1)} collective-permute-done((f32[64,512]{1,0:T(8,128)S(1)}, f32[64,512]{1,0:T(8,128)S(1)}, u32[]{:S(2)}, u32[]{:S(2)}) %collective-permute-start.32) | collective-permute-done | bytes 131104 | tf_op jit(solution)/shard_map/ppermute | solution.py:24
  180.6 1.4 place_weight.1
  (82 shorter events, 13.7 us)
Async XLA Ops:
  0.6 26.4 %collective-permute-start.4 = (bf16[256,2048]{1,0:T(8,128)(2,1)}, bf16[256,2048]{1,0:T(8,128)(2,1)S(1)}, u32[]{:S(2)}, u32[]{:S(2)}) collective-permute-start(bf16[256,2048]{1,0:T(8,128)(2,1)} %bitcast.7), channel_id=1, source_target_pairs={{0,4},{2,6},{4,0},{6,2},{8,12},{10,14},{12,8},{14,10},{16,20},{18,... | collective-permute-start | bytes 3145736 | tf_op jit(solution)/shard_map/ppermute | solution.py:24
  3.6 26.3 %collective-permute-start.3 = (bf16[256,2048]{1,0:T(8,128)(2,1)}, bf16[256,2048]{1,0:T(8,128)(2,1)S(1)}, u32[]{:S(2)}, u32[]{:S(2)}) collective-permute-start(bf16[256,2048]{1,0:T(8,128)(2,1)} %bitcast.8), channel_id=1, source_target_pairs={{0,2},{2,0},{4,6},{6,4},{8,10},{10,8},{12,14},{14,12},{16,18},{18,... | collective-permute-start | bytes 3145736 | tf_op jit(solution)/shard_map/ppermute | solution.py:24
  3.7 2.2 %copy-start = (bf16[1024,2048]{1,0:T(8,128)(2,1)S(1)}, bf16[1024,2048]{1,0:T(8,128)(2,1)}, u32[]{:S(2)}) copy-start(bf16[1024,2048]{1,0:T(8,128)(2,1)} %refs_4_.1) | copy-start | bytes 12582916
  8.0 21.3 %copy-start.1 = (bf16[1024,2048]{1,0:T(8,128)(2,1)S(1)}, bf16[1024,2048]{1,0:T(8,128)(2,1)}, u32[]{:S(2)}) copy-start(bf16[1024,2048]{1,0:T(8,128)(2,1)} %refs_4_.1) | copy-start | bytes 12582916
  9.1 25.6 %collective-permute-start.6 = (bf16[1024,512]{1,0:T(8,128)(2,1)S(1)}, bf16[1024,512]{1,0:T(8,128)(2,1)S(1)}, u32[]{:S(2)}, u32[]{:S(2)}) collective-permute-start(bf16[1024,512]{1,0:T(8,128)(2,1)S(1)} %get-tuple-element.61.refs_5_), channel_id=1, source_target_pairs={{0,1},{1,0},{2,3},{3,2},{4,5},{5,4},{6,7},{7,6},{8,9},{9,8},{10,11... | collective-permute-start | bytes 3145736 | tf_op jit(solution)/shard_map/ppermute | solution.py:51
  27.0 7.7 %collective-permute-start.5 = (bf16[256,2048]{1,0:T(8,128)(2,1)S(1)}, bf16[256,2048]{1,0:T(8,128)(2,1)S(1)}, u32[]{:S(2)}, u32[]{:S(2)}) collective-permute-start(bf16[256,2048]{1,0:T(8,128)(2,1)S(1)} %collective-permute-done.4.refs_3_), channel_id=1, source_target_pairs={{0,2},{2,0},{4,6},{6,4},{8,10},{10,8},{12,14},{14,12},{16,18},{18,... | collective-permute-start | bytes 3145736 | tf_op jit(solution)/shard_map/ppermute | solution.py:24
  27.0 11.7 %collective-permute-start = (bf16[2,256,256]{2,1,0:T(8,128)(2,1)S(1)}, bf16[2,256,256]{2,1,0:T(8,128)(2,1)S(1)}, u32[]{:S(2)}, u32[]{:S(2)}) collective-permute-start(bf16[2,256,256]{2,1,0:T(8,128)(2,1)S(1)} %get-tuple-element.58), channel_id=1, source_target_pairs={{0,2},{2,0},{4,6},{6,4},{8,10},{10,8},{12,14},{14,12},{16,18},{18,... | collective-permute-start | bytes 786440 | tf_op jit(solution)/shard_map/ppermute | solution.py:24
  27.5 7.2 %copy-start.3 = (bf16[1,256,2048]{2,1,0:T(8,128)(2,1)S(1)}, bf16[1,256,2048]{2,1,0:T(8,128)(2,1)}, u32[]{:S(2)}) copy-start(bf16[1,256,2048]{2,1,0:T(8,128)(2,1)} %param.4) | copy-start | bytes 3145732
  27.5 11.2 %collective-permute-start.1 = (bf16[2,256,256]{2,1,0:T(8,128)(2,1)S(1)}, bf16[2,256,256]{2,1,0:T(8,128)(2,1)S(1)}, u32[]{:S(2)}, u32[]{:S(2)}) collective-permute-start(bf16[2,256,256]{2,1,0:T(8,128)(2,1)S(1)} %get-tuple-element.59), channel_id=1, source_target_pairs={{0,4},{2,6},{4,0},{6,2},{8,12},{10,14},{12,8},{14,10},{16,20},{18,... | collective-permute-start | bytes 786440 | tf_op jit(solution)/shard_map/ppermute | solution.py:24
  30.0 10.6 %collective-permute-start.2 = (bf16[2,256,256]{2,1,0:T(8,128)(2,1)S(1)}, bf16[2,256,256]{2,1,0:T(8,128)(2,1)S(1)}, u32[]{:S(2)}, u32[]{:S(2)}) collective-permute-start(bf16[2,256,256]{2,1,0:T(8,128)(2,1)S(1)} %get-tuple-element.60), channel_id=1, source_target_pairs={{0,6},{2,4},{4,2},{6,0},{8,14},{10,12},{12,10},{14,8},{16,22},{18,... | collective-permute-start | bytes 786440 | tf_op jit(solution)/shard_map/ppermute | solution.py:24
  34.8 3.9 %copy-start.4 = (bf16[256,2048]{1,0:T(8,128)(2,1)}, bf16[256,2048]{1,0:T(8,128)(2,1)S(1)}, u32[]{:S(2)}) copy-start(bf16[256,2048]{1,0:T(8,128)(2,1)S(1)} %collective-permute-done.5.refs_4_) | copy-start | bytes 3145732
  42.3 1.3 copy-start.13
  43.6 17.0 %collective-permute-start.7 = (bf16[2,1024,128]{2,1,0:T(8,128)(2,1)}, bf16[2,1024,128]{2,1,0:T(8,128)(2,1)}, u32[]{:S(2)}, u32[]{:S(2)}) collective-permute-start(bf16[2,1024,128]{2,1,0:T(8,128)(2,1)} %get-tuple-element.63.refs_1_), channel_id=1, source_target_pairs={{8,0},{10,2},{12,4},{14,6},{16,8},{18,10},{20,12},{22,14},{24,16},... | collective-permute-start | bytes 1572872 | tf_op jit(solution)/shard_map/ppermute | solution.py:31
  44.9 17.1 %collective-permute-start.8 = (bf16[1024,256]{1,0:T(8,128)(2,1)}, bf16[1024,256]{1,0:T(8,128)(2,1)}, u32[]{:S(2)}, u32[]{:S(2)}) collective-permute-start(bf16[1024,256]{1,0:T(8,128)(2,1)} %get-tuple-element.62.refs_5_.refs_3_), channel_id=1, source_target_pairs={{0,8},{2,10},{4,12},{6,14},{8,16},{10,18},{12,20},{14,22},{16,24},... | collective-permute-start | bytes 1572872 | tf_op jit(solution)/shard_map/ppermute | solution.py:31
  50.3 22.4 %collective-permute-start.11 = (bf16[2,1024,128]{2,1,0:T(8,128)(2,1)}, bf16[2,1024,128]{2,1,0:T(8,128)(2,1)}, u32[]{:S(2)}, u32[]{:S(2)}) collective-permute-start(bf16[2,1024,128]{2,1,0:T(8,128)(2,1)} %get-tuple-element.66.refs_1_), channel_id=1, source_target_pairs={{8,0},{10,2},{12,4},{14,6},{16,8},{18,10},{20,12},{22,14},{24,16},... | collective-permute-start | bytes 1572872 | tf_op jit(solution)/shard_map/ppermute | solution.py:31
  51.6 21.6 %collective-permute-start.12 = (bf16[1024,256]{1,0:T(8,128)(2,1)}, bf16[1024,256]{1,0:T(8,128)(2,1)}, u32[]{:S(2)}, u32[]{:S(2)}) collective-permute-start(bf16[1024,256]{1,0:T(8,128)(2,1)} %get-tuple-element.67.refs_3_), channel_id=1, source_target_pairs={{0,8},{2,10},{4,12},{6,14},{8,16},{10,18},{12,20},{14,22},{16,24},... | collective-permute-start | bytes 1572872 | tf_op jit(solution)/shard_map/ppermute | solution.py:31
  57.0 52.8 %collective-permute-start.18 = (bf16[512,2048]{1,0:T(8,128)(2,1)}, bf16[512,2048]{1,0:T(8,128)(2,1)}, u32[]{:S(2)}, u32[]{:S(2)}) collective-permute-start(bf16[512,2048]{1,0:T(8,128)(2,1)} %copy-done.13), channel_id=1, source_target_pairs={{0,1},{1,0},{2,3},{3,2},{4,5},{5,4},{6,7},{7,6},{8,9},{9,8},{10,11... | collective-permute-start | bytes 6291464 | tf_op jit(solution)/shard_map/ppermute | solution.py:51
  67.3 17.5 %collective-permute-start.10 = (f32[8,1024]{1,0:T(8,128)S(1)}, f32[8,1024]{1,0:T(8,128)S(1)}, u32[]{:S(2)}, u32[]{:S(2)}) collective-permute-start(f32[8,1024]{1,0:T(8,128)S(1)} %get-tuple-element.64.refs_5_), channel_id=1, source_target_pairs={{0,24},{2,26},{4,28},{6,30},{8,0},{10,2},{12,4},{14,6},{16,8},{18,... | collective-permute-start | bytes 98312 | tf_op jit(solution)/shard_map/ppermute | solution.py:37
  72.7 12.1 %collective-permute-start.9 = (f32[8,1024]{1,0:T(8,128)S(1)}, f32[8,1024]{1,0:T(8,128)S(1)}, u32[]{:S(2)}, u32[]{:S(2)}) collective-permute-start(f32[8,1024]{1,0:T(8,128)S(1)} %get-tuple-element.65.refs_7_), channel_id=1, source_target_pairs={{0,8},{2,10},{4,12},{6,14},{8,16},{10,18},{12,20},{14,22},{16,24},... | collective-permute-start | bytes 98312 | tf_op jit(solution)/shard_map/ppermute | solution.py:37
  78.4 18.5 %collective-permute-start.13 = (f32[8,1024]{1,0:T(8,128)S(1)}, f32[8,1024]{1,0:T(8,128)S(1)}, u32[]{:S(2)}, u32[]{:S(2)}) collective-permute-start(f32[8,1024]{1,0:T(8,128)S(1)} %get-tuple-element.70.refs_7_), channel_id=1, source_target_pairs={{0,8},{2,10},{4,12},{6,14},{8,16},{10,18},{12,20},{14,22},{16,24},... | collective-permute-start | bytes 98312 | tf_op jit(solution)/shard_map/ppermute | solution.py:37
  81.0 15.9 %collective-permute-start.14 = (f32[8,1024]{1,0:T(8,128)S(1)}, f32[8,1024]{1,0:T(8,128)S(1)}, u32[]{:S(2)}, u32[]{:S(2)}) collective-permute-start(f32[8,1024]{1,0:T(8,128)S(1)} %get-tuple-element.68.refs_9_.refs_5_.refs_10_), channel_id=1, source_target_pairs={{0,24},{2,26},{4,28},{6,30},{8,0},{10,2},{12,4},{14,6},{16,8},{18,... | collective-permute-start | bytes 98312 | tf_op jit(solution)/shard_map/ppermute | solution.py:37
  95.4 14.5 %collective-permute-start.17 = (bf16[1024,256]{1,0:T(8,128)(2,1)S(1)}, bf16[1024,256]{1,0:T(8,128)(2,1)S(1)}, u32[]{:S(2)}, u32[]{:S(2)}) collective-permute-start(bf16[1024,256]{1,0:T(8,128)(2,1)S(1)} %get-tuple-element.77), channel_id=1, source_target_pairs={{8,0},{10,2},{12,4},{14,6},{16,8},{18,10},{20,12},{22,14},{24,16},... | collective-permute-start | bytes 1572872 | tf_op jit(solution)/shard_map/ppermute | solution.py:31
  96.9 13.0 %copy-start.5 = (bf16[256,2048]{1,0:T(8,128)(2,1)S(1)}, bf16[256,2048]{1,0:T(8,128)(2,1)}, u32[]{:S(2)}) copy-start(bf16[256,2048]{1,0:T(8,128)(2,1)} %copy-done.4) | copy-start | bytes 3145732
  107.8 5.0 %copy-start.7 = (f32[1024,256]{1,0:T(8,128)}, f32[1024,256]{1,0:T(8,128)S(1)}, u32[]{:S(2)}) copy-start(f32[1024,256]{1,0:T(8,128)S(1)} %get-tuple-element.74.refs_7_.refs_5_) | copy-start | bytes 3145732
  107.8 5.0 %copy-start.18 = (f32[2,1024,128]{2,1,0:T(8,128)}, f32[2,1024,128]{2,1,0:T(8,128)S(1)}, u32[]{:S(2)}) copy-start(f32[2,1024,128]{2,1,0:T(8,128)S(1)} %get-tuple-element.72.refs_2_) | copy-start | bytes 3145732
  114.4 50.2 %collective-permute-start.24 = (bf16[512,2048]{1,0:T(8,128)(2,1)}, bf16[512,2048]{1,0:T(8,128)(2,1)}, u32[]{:S(2)}, u32[]{:S(2)}) collective-permute-start(bf16[512,2048]{1,0:T(8,128)(2,1)} %get-tuple-element.94.refs_5_), channel_id=1, source_target_pairs={{0,2},{2,0},{4,6},{6,4},{8,10},{10,8},{12,14},{14,12},{16,18},{18,... | collective-permute-start | bytes 6291464 | tf_op jit(solution)/shard_map/ppermute | solution.py:24
  114.4 14.7 %collective-permute-start.19 = (bf16[4,256,256]{2,1,0:T(8,128)(2,1)}, bf16[4,256,256]{2,1,0:T(8,128)(2,1)}, u32[]{:S(2)}, u32[]{:S(2)}) collective-permute-start(bf16[4,256,256]{2,1,0:T(8,128)(2,1)} %get-tuple-element.83), channel_id=1, source_target_pairs={{0,1},{1,0},{2,3},{3,2},{4,5},{5,4},{6,7},{7,6},{8,9},{9,8},{10,11... | collective-permute-start | bytes 1572872 | tf_op jit(solution)/shard_map/ppermute | solution.py:51
  116.0 25.5 %collective-permute-start.15 = (bf16[2,1024,256]{2,1,0:T(8,128)(2,1)}, bf16[2,1024,256]{2,1,0:T(8,128)(2,1)}, u32[]{:S(2)}, u32[]{:S(2)}) collective-permute-start(bf16[2,1024,256]{2,1,0:T(8,128)(2,1)} %get-tuple-element.73), channel_id=1, source_target_pairs={{0,8},{2,10},{4,12},{6,14},{8,16},{10,18},{12,20},{14,22},{16,24},... | collective-permute-start | bytes 3145736 | tf_op jit(solution)/shard_map/ppermute | solution.py:31
  119.4 16.0 %collective-permute-start.16 = (bf16[1024,256]{1,0:T(8,128)(2,1)}, bf16[1024,256]{1,0:T(8,128)(2,1)}, u32[]{:S(2)}, u32[]{:S(2)}) collective-permute-start(bf16[1024,256]{1,0:T(8,128)(2,1)} %get-tuple-element.75), channel_id=1, source_target_pairs={{8,0},{10,2},{12,4},{14,6},{16,8},{18,10},{20,12},{22,14},{24,16},... | collective-permute-start | bytes 1572872 | tf_op jit(solution)/shard_map/ppermute | solution.py:31
  120.9 14.4 %copy-start.6 = (bf16[256,2048]{1,0:T(8,128)(2,1)S(1)}, bf16[256,2048]{1,0:T(8,128)(2,1)}, u32[]{:S(2)}) copy-start(bf16[256,2048]{1,0:T(8,128)(2,1)} %copy-done.4) | copy-start | bytes 3145732
  120.9 14.4 %copy-start.8 = (f32[1024,256]{1,0:T(8,128)S(1)}, f32[1024,256]{1,0:T(8,128)}, u32[]{:S(2)}) copy-start(f32[1024,256]{1,0:T(8,128)} %copy-done.7) | copy-start | bytes 3145732
  121.0 14.4 %copy-start.12 = (bf16[256,256]{1,0:T(8,128)(2,1)S(1)}, bf16[256,256]{1,0:T(8,128)(2,1)}, u32[]{:S(2)}) copy-start(bf16[256,256]{1,0:T(8,128)(2,1)} %copy-done.11) | copy-start | bytes 393220
  129.1 1.2 copy-start.15
  135.3 6.2 %copy-start.17 = (f32[2,1024,128]{2,1,0:T(8,128)S(1)}, f32[2,1024,128]{2,1,0:T(8,128)}, u32[]{:S(2)}) copy-start(f32[2,1024,128]{2,1,0:T(8,128)} %copy-done.16) | copy-start | bytes 3145732
  135.4 6.2 %copy-start.19 = (f32[2,1024,128]{2,1,0:T(8,128)S(1)}, f32[2,1024,128]{2,1,0:T(8,128)}, u32[]{:S(2)}) copy-start(f32[2,1024,128]{2,1,0:T(8,128)} %copy-done.18) | copy-start | bytes 3145732
  138.2 4.9 %collective-permute-start.22 = (bf16[2,256,512]{2,1,0:T(8,128)(2,1)S(1)}, bf16[2,256,512]{2,1,0:T(8,128)(2,1)S(1)}, u32[]{:S(2)}, u32[]{:S(2)}) collective-permute-start(bf16[2,256,512]{2,1,0:T(8,128)(2,1)S(1)} %get-tuple-element.92), channel_id=1, source_target_pairs={{0,2},{2,0},{4,6},{6,4},{8,10},{10,8},{12,14},{14,12},{16,18},{18,... | collective-permute-start | bytes 1572872 | tf_op jit(solution)/shard_map/ppermute | solution.py:24
  138.3 14.3 %collective-permute-start.25 = (bf16[4,256,256]{2,1,0:T(8,128)(2,1)S(1)}, bf16[4,256,256]{2,1,0:T(8,128)(2,1)S(1)}, u32[]{:S(2)}, u32[]{:S(2)}) collective-permute-start(bf16[4,256,256]{2,1,0:T(8,128)(2,1)S(1)} %get-tuple-element.85.refs_4_), channel_id=1, source_target_pairs={{0,1},{1,0},{2,3},{3,2},{4,5},{5,4},{6,7},{7,6},{8,9},{9,8},{10,11... | collective-permute-start | bytes 1572872 | tf_op jit(solution)/shard_map/ppermute | solution.py:51
  143.0 14.3 %collective-permute-start.20 = (bf16[2,2,256,256]{3,2,1,0:T(8,128)(2,1)S(1)}, bf16[2,2,256,256]{3,2,1,0:T(8,128)(2,1)S(1)}, u32[]{:S(2)}, u32[]{:S(2)}) collective-permute-start(bf16[2,2,256,256]{3,2,1,0:T(8,128)(2,1)S(1)} %get-tuple-element.87), channel_id=1, source_target_pairs={{0,2},{2,0},{4,6},{6,4},{8,10},{10,8},{12,14},{14,12},{16,18},{18,... | collective-permute-start | bytes 1572872 | tf_op jit(solution)/shard_map/ppermute | solution.py:24
  143.7 20.3 %collective-permute-start.23 = (bf16[2,256,512]{2,1,0:T(8,128)(2,1)S(1)}, bf16[2,256,512]{2,1,0:T(8,128)(2,1)S(1)}, u32[]{:S(2)}, u32[]{:S(2)}) collective-permute-start(bf16[2,256,512]{2,1,0:T(8,128)(2,1)S(1)} %mix.3), channel_id=1, source_target_pairs={{0,4},{2,6},{4,0},{6,2},{8,12},{10,14},{12,8},{14,10},{16,20},{18,... | collective-permute-start | bytes 1572872 | tf_op jit(solution)/shard_map/ppermute | solution.py:24
  145.2 9.2 %collective-permute-start.27 = (bf16[2,256,256]{2,1,0:T(8,128)(2,1)S(1)}, bf16[2,256,256]{2,1,0:T(8,128)(2,1)S(1)}, u32[]{:S(2)}, u32[]{:S(2)}) collective-permute-start(bf16[2,256,256]{2,1,0:T(8,128)(2,1)S(1)} %get-tuple-element.84.refs_10_), channel_id=1, source_target_pairs={{0,8},{1,9},{2,10},{3,11},{4,12},{5,13},{6,14},{7,15},{8,0},{9,1},... | collective-permute-start | bytes 786440 | tf_op jit(solution)/shard_map/ppermute | solution.py:47
  153.3 10.7 %collective-permute-start.26 = (bf16[2,256,256]{2,1,0:T(8,128)(2,1)S(1)}, bf16[2,256,256]{2,1,0:T(8,128)(2,1)S(1)}, u32[]{:S(2)}, u32[]{:S(2)}) collective-permute-start(bf16[2,256,256]{2,1,0:T(8,128)(2,1)S(1)} %get-tuple-element.97), channel_id=1, source_target_pairs={{0,8},{1,9},{2,10},{3,11},{4,12},{5,13},{6,14},{7,15},{8,0},{9,1},... | collective-permute-start | bytes 786440 | tf_op jit(solution)/shard_map/ppermute | solution.py:47
  155.0 16.6 %collective-permute-start.28 = (bf16[1,256,256]{2,1,0:T(8,128)(2,1)S(1)}, bf16[1,256,256]{2,1,0:T(8,128)(2,1)S(1)}, u32[]{:S(2)}, u32[]{:S(2)}) collective-permute-start(bf16[1,256,256]{2,1,0:T(8,128)(2,1)S(1)} %get-tuple-element.102), channel_id=1, source_target_pairs={{0,16},{1,17},{2,18},{3,19},{4,20},{5,21},{6,22},{7,23},{8,24},{9,... | collective-permute-start | bytes 393224 | tf_op jit(solution)/shard_map/ppermute | solution.py:47
  157.3 7.4 %copy-start.2 = (bf16[1024,2048]{1,0:T(8,128)(2,1)S(1)}, bf16[1024,2048]{1,0:T(8,128)(2,1)}, u32[]{:S(2)}) copy-start(bf16[1024,2048]{1,0:T(8,128)(2,1)} %refs_4_.1) | copy-start | bytes 12582916
  157.9 16.3 %collective-permute-start.21 = (bf16[2,2,256,256]{3,2,1,0:T(8,128)(2,1)S(1)}, bf16[2,2,256,256]{3,2,1,0:T(8,128)(2,1)S(1)}, u32[]{:S(2)}, u32[]{:S(2)}) collective-permute-start(bf16[2,2,256,256]{3,2,1,0:T(8,128)(2,1)S(1)} %mix.2), channel_id=1, source_target_pairs={{0,4},{2,6},{4,0},{6,2},{8,12},{10,14},{12,8},{14,10},{16,20},{18,... | collective-permute-start | bytes 1572872 | tf_op jit(solution)/shard_map/ppermute | solution.py:24
  164.6 7.0 %collective-permute-start.29 = (bf16[1,256,256]{2,1,0:T(8,128)(2,1)S(1)}, bf16[1,256,256]{2,1,0:T(8,128)(2,1)S(1)}, u32[]{:S(2)}, u32[]{:S(2)}) collective-permute-start(bf16[1,256,256]{2,1,0:T(8,128)(2,1)S(1)} %get-tuple-element.98.refs_7_), channel_id=1, source_target_pairs={{0,16},{1,17},{2,18},{3,19},{4,20},{5,21},{6,22},{7,23},{8,24},{9,... | collective-permute-start | bytes 393224 | tf_op jit(solution)/shard_map/ppermute | solution.py:47
  172.2 3.6 %collective-permute-start.30 = (f32[64,512]{1,0:T(8,128)S(1)}, f32[64,512]{1,0:T(8,128)S(1)}, u32[]{:S(2)}, u32[]{:S(2)}) collective-permute-start(f32[64,512]{1,0:T(8,128)S(1)} %get-tuple-element.106), channel_id=1, source_target_pairs={{0,2},{2,0},{4,6},{6,4},{8,10},{10,8},{12,14},{14,12},{16,18},{18,... | collective-permute-start | bytes 393224 | tf_op jit(solution)/shard_map/ppermute | solution.py:24
  172.3 6.4 %collective-permute-start.31 = (f32[64,512]{1,0:T(8,128)S(1)}, f32[64,512]{1,0:T(8,128)S(1)}, u32[]{:S(2)}, u32[]{:S(2)}) collective-permute-start(f32[64,512]{1,0:T(8,128)S(1)} %get-tuple-element.107), channel_id=1, source_target_pairs={{0,4},{2,6},{4,0},{6,2},{8,12},{10,14},{12,8},{14,10},{16,20},{18,... | collective-permute-start | bytes 393224 | tf_op jit(solution)/shard_map/ppermute | solution.py:24
  173.9 6.7 %collective-permute-start.32 = (f32[64,512]{1,0:T(8,128)S(1)}, f32[64,512]{1,0:T(8,128)S(1)}, u32[]{:S(2)}, u32[]{:S(2)}) collective-permute-start(f32[64,512]{1,0:T(8,128)S(1)} %get-tuple-element.108), channel_id=1, source_target_pairs={{0,6},{2,4},{4,2},{6,0},{8,14},{10,12},{12,10},{14,8},{16,22},{18,... | collective-permute-start | bytes 393224 | tf_op jit(solution)/shard_map/ppermute | solution.py:24
  (5 other events, 4.7 us)

commit v5 on v4

--- a/solution.py
+++ b/solution.py
@@ -100,6 +100,17 @@
         allowed = key_pos <= query_pos if edge == "low" else key_pos > query_pos
         score = jnp.where(allowed, score, MASKED)
     return score + near_bias if near else score
+
+
+def turn_kernel(_, near_ref, out_ref):
+    size = out_ref.shape[0]
+    for start in range(0, near_ref.shape[0], size):
+        out_ref[:, start : start + size] = near_ref[start : start + size].T
+
+
+def turned_over(at, near):
+    shape = jax.ShapeDtypeStruct((near.shape[1], near.shape[0]), near.dtype)
+    return small_call(turn_kernel, "turn", at, (near,), [shape])[0]
 
 
 def stats_kernel(
@@ -145,11 +156,12 @@
 
 
 def gradient_kernel(
-    at_ref, own_pair, next_pair, own_ref, near_ref,
+    at_ref, own_pair, next_pair, own_ref, near_ref, near_turned,
     own_stats, far_stats, next_stats, main_stats, *refs, blocks, size,
 ):
     *earlier, own_out, next_out, near_grad, own_grad = refs[:-7]
-    turned, queries, cotangents, own_weights, own_dscores, near_weights, near_dscores = refs[-7:]
+    own_turned, queries, cotangents, own_weights, own_dscores, near_weights, near_dscores = refs[-7:]
+    turned = (own_turned, near_turned)
     joined = next_out.shape[2] - HEAD_DIM
     if earlier:
         next_out[:, :, :joined] = earlier[0][...]
@@ -168,9 +180,9 @@
     for side in range(2):
         queries[side * row_tokens : (side + 1) * row_tokens] = pairs[side][0]
         cotangents[side * row_tokens : (side + 1) * row_tokens] = pairs[side][1]
-        for block in range(blocks):
-            held = slice(block * size, (block + 1) * size)
-            turned[side, :, held] = window[side][held].T
+    for block in range(blocks):
+        held = slice(block * size, (block + 1) * size)
+        own_turned[:, held] = own_ref[held].T
     for side, block, keys in visits(blocks):
         held = slice(block * size, (block + 1) * size)
         column = slice(side * row_tokens + block * size, side * row_tokens + (block + 1) * size)
@@ -184,12 +196,12 @@
             weights[near][rows, column] = (grown * share).astype(jnp.bfloat16)
             dscores[near][rows, column] = (grown * ((dprob - centre) * scaled)).astype(jnp.bfloat16)
         rows = slice(block * size if side else 0, row_tokens)
-        attended = product(turned[1, HEAD_DIM:, rows], near_weights[rows, column])
-        query_grad = product(turned[1, :HEAD_DIM, rows], near_dscores[rows, column])
+        attended = product(turned[1][HEAD_DIM:, rows], near_weights[rows, column])
+        query_grad = product(turned[1][:HEAD_DIM, rows], near_dscores[rows, column])
         if not side:
             rows = slice(0, (block + 1) * size)
-            attended += product(turned[0, HEAD_DIM:, rows], own_weights[rows, column])
-            query_grad += product(turned[0, :HEAD_DIM, rows], own_dscores[rows, column])
+            attended += product(turned[0][HEAD_DIM:, rows], own_weights[rows, column])
+            query_grad += product(turned[0][:HEAD_DIM, rows], own_dscores[rows, column])
         outs[side][0, held] = attended.T.astype(outs[side].dtype)
         outs[side][1, held] = query_grad.T.astype(outs[side].dtype)
     for lane in range(blocks):
@@ -233,13 +245,13 @@
     )(at, own_pair, next_pair, *kvs, *stats, *waits)
 
 
-def softmax_stats(at, own_pair, next_pair, kvs, size):
+def softmax_stats(at, own_pair, next_pair, kvs, size, waits):
     row_tokens = own_pair.shape[1]
     return kernel_call(
         stats_kernel, "softmax_stats", at, own_pair, next_pair, kvs, (),
         [jax.ShapeDtypeStruct((8, row_tokens), jnp.float32)] * 2,
         [pltpu.VMEM((2, 2 * row_tokens // size, size, size), jnp.float32)],
-        size, (), 4, 20 * 2**20,
+        size, waits, 4, 20 * 2**20,
     )
 
 
@@ -256,7 +268,7 @@
             jax.ShapeDtypeStruct((row_tokens, 2 * HEAD_DIM), jnp.float32),
         ],
         [
-            pltpu.VMEM((2, 2 * HEAD_DIM, row_tokens), low),
+            pltpu.VMEM((2 * HEAD_DIM, row_tokens), low),
             pltpu.VMEM((2 * row_tokens, HEAD_DIM), low),
             pltpu.VMEM((2 * row_tokens, HEAD_DIM), low),
             pltpu.VMEM((row_tokens, row_tokens), low),
@@ -696,10 +708,11 @@
     fetched = swapped(part)
 
     at = jnp.stack([row, lane]).astype(jnp.int32)
-    shared = []
+    shared, turns = [], []
     for head in range(heads):
+        turns.append(turned_over(at, windows[head][1]))
         own_stats, next_stats = softmax_stats(
-            at, own_pairs[head], next_pairs[head], windows[head], size
+            at, own_pairs[head], next_pairs[head], windows[head], size, (turns[-1],)
         )
         shared.append(
             (own_stats, turned_round(next_stats, 1), next_stats, turned_round(own_stats, -1))
@@ -708,7 +721,8 @@
     for head in range(heads):
         gained.append(
             attention_grads(
-                at, own_pairs[head], next_pairs[head], windows[head], shared[head], next_out, size,
+                at, own_pairs[head], next_pairs[head], (*windows[head], turns[head]),
+                shared[head], next_out, size,
                 (shared[-1][0],),
             )
         )

time: 183 us -> 178 us (0.973)
  starting transfers between devices: 50.6 us -> 43.9 us
  waiting for transfers between devices: 60.4 us -> 62.4 us
    ppermute x4, starting transfers between devices: 11.7 us -> 5.96 us  [turned_round(): return lax.ppermute(value, 'seq', pairs)]
    ppermute x7, waiting for transfers between devices: 12.6 us -> 17.4 us  [shifted(): lax.ppermute(value, 'seq', [(source, source + steps) for source in range(...]
    pallas_call x4, Pallas kernels: 31 us -> 28.5 us  [kernel_call(): pl.pallas_call(ordered(functools.partial(kernel, blocks=blocks, size=size...]
    ppermute x7, starting transfers between devices: 19.8 us -> 17.6 us  [shifted(): lax.ppermute(value, 'seq', [(source, source + steps) for source in range(...]
    ppermute x14, waiting for transfers between devices: 23 us -> 21.1 us  [exchanged(): lax.ppermute(value, 'seq', [(source, source ^ bits) for source in range(c...]
    pallas_call x14 -> x16, Pallas kernels: 20.6 us -> 22.2 us  [small_call(): pl.pallas_call(ordered(kernel, len(operands), len(waits), len(out_shape),...]
    unnamed x40 -> x48, local copies, waits for them, and re-layouts: 9.48 us -> 10.3 us
  transfers between devices with their start and end apart: 33 -> 33, of which waited for: 15 -> 13; matrix products, arithmetic and copies ran while one was open for 0% -> 0% of each run, Pallas kernels for 30% -> 31%
where the time goes in v5:
time: 178 us; the launch traced here: 177 us
  waiting for transfers between devices  62.4 us (35%)
  Pallas kernels  59.4 us (33%)
  starting transfers between devices  43.9 us (25%)
  local copies, waits for them, and re-layouts  10.3 us (6%)
    pallas_call x4, Pallas kernels, kernel_call(): pl.pallas_call(ordered(functools.partial(kernel, blocks=blocks, size=size...  28.5 us
    pallas_call x16, Pallas kernels, small_call(): pl.pallas_call(ordered(kernel, len(operands), len(waits), len(out_shape),...  22.2 us
    ppermute x14, waiting for transfers between devices, exchanged(): lax.ppermute(value, 'seq', [(source, source ^ bits) for source in range(c...  21.1 us
    ppermute x4, waiting for transfers between devices, swapped(): return lax.ppermute(value, 'dp', [(0, 1), (1, 0)])  18.1 us
    ppermute x7, starting transfers between devices, shifted(): lax.ppermute(value, 'seq', [(source, source + steps) for source in range(...  17.6 us
    ppermute x7, waiting for transfers between devices, shifted(): lax.ppermute(value, 'seq', [(source, source + steps) for source in range(...  17.4 us
    unnamed x48, local copies, waits for them, and re-layouts  10.3 us
    ppermute x14, starting transfers between devices, exchanged(): lax.ppermute(value, 'seq', [(source, source ^ bits) for source in range(c...  8.89 us
  transfers between devices with their start and end apart: 33, of which 13 were waited for; matrix products, arithmetic and copies ran while one was open for 0% of the time, Pallas kernels for 31%

profile of v5, /device:TPU:0, one launch (start us, length us, event | category | flops | bytes accessed | tf_op | source)
XLA Modules:
  0.0 177.2 jit_solution(3395729635791956352)
XLA Ops:
  0.6 3.0 %collective-permute-start.4 = (bf16[256,2048]{1,0:T(8,128)(2,1)}, bf16[256,2048]{1,0:T(8,128)(2,1)S(1)}, u32[]{:S(2)}, u32[]{:S(2)}) collective-permute-start(bf16[256,2048]{1,0:T(8,128)(2,1)} %bitcast.7), channel_id=1, source_target_pairs={{0,4},{2,6},{4,0},{6,2},{8,12},{10,14},{12,8},{14,10},{16,20},{18,... | collective-permute-start | bytes 3145736 | tf_op jit(solution)/shard_map/ppermute | solution.py:24
  3.7 2.2 %copy-done = bf16[1024,2048]{1,0:T(8,128)(2,1)S(1)} copy-done((bf16[1024,2048]{1,0:T(8,128)(2,1)S(1)}, bf16[1024,2048]{1,0:T(8,128)(2,1)}, u32[]{:S(2)}) %copy-start) | copy-done | bytes 4194328
  8.0 1.1 deal.1
  9.1 1.6 collective-permute-start.6
  10.7 16.3 %collective-permute-done.4.refs_3_ = bf16[256,2048]{1,0:T(8,128)(2,1)S(1)} collective-permute-done((bf16[256,2048]{1,0:T(8,128)(2,1)}, bf16[256,2048]{1,0:T(8,128)(2,1)S(1)}, u32[]{:S(2)}, u32[]{:S(2)}) %collective-permute-start.4) | collective-permute-done | bytes 1048608 | tf_op jit(solution)/shard_map/ppermute | solution.py:24
  27.5 1.7 collective-permute-start.1
  30.0 4.7 %collective-permute-done.6.refs_6_ = bf16[1024,512]{1,0:T(8,128)(2,1)S(1)} collective-permute-done((bf16[1024,512]{1,0:T(8,128)(2,1)S(1)}, bf16[1024,512]{1,0:T(8,128)(2,1)S(1)}, u32[]{:S(2)}, u32[]{:S(2)}) %collective-permute-start.6) | collective-permute-done | bytes 1048608 | tf_op jit(solution)/shard_map/ppermute | solution.py:51
  34.8 3.7 %project.1 = (bf16[1024,256]{1,0:T(8,128)(2,1)}, bf16[1024,256]{1,0:T(8,128)(2,1)S(1)}) custom-call(s32[3]{0:T(128)S(1)} %pad_add_fusion.at_ref.refs_0_._, bf16[256,2048]{1,0:T(8,128)(2,1)S(1)} %bitcast.9, bf16[256,2048]{1,0:T(8,128)(2,1)S(1)} %collective-permute-done.3.refs_2_, bf16[256,2048]{1,0:T(8,128)(2,1)S(1)} %collective-permute-done.4.refs_3_, ...), custom_call_target="tpu_custom_call" | custom-call | flops 4000000000 | bytes 12000000 | tf_op jit(solution)/shard_map/project/pallas_call | solution.py:315
  38.4 4.3 %collective-permute-start.8 = (bf16[1024,256]{1,0:T(8,128)(2,1)}, bf16[1024,256]{1,0:T(8,128)(2,1)}, u32[]{:S(2)}, u32[]{:S(2)}) collective-permute-start(bf16[1024,256]{1,0:T(8,128)(2,1)} %get-tuple-element.62.refs_5_.refs_3_), channel_id=1, source_target_pairs={{0,8},{2,10},{4,12},{6,14},{8,16},{10,18},{12,20},{14,22},{16,24},... | collective-permute-start | bytes 1572872 | tf_op jit(solution)/shard_map/ppermute | solution.py:31
  42.7 1.5 place_rows.1
  44.3 1.3 copy-done.13
  46.4 1.3 collective-permute-start.7
  47.7 4.6 %collective-permute-start.12 = (bf16[1024,256]{1,0:T(8,128)(2,1)}, bf16[1024,256]{1,0:T(8,128)(2,1)S(1)}, u32[]{:S(2)}, u32[]{:S(2)}) collective-permute-start(bf16[1024,256]{1,0:T(8,128)(2,1)} %copy-done.16), channel_id=1, source_target_pairs={{0,8},{2,10},{4,12},{6,14},{8,16},{10,18},{12,20},{14,22},{16,24},... | collective-permute-start | bytes 1572872 | tf_op jit(solution)/shard_map/ppermute | solution.py:31
  52.3 1.3 collective-permute-start.11
  53.6 1.6 collective-permute-start.18
  55.2 1.2 turn.2.refs_5_
  56.5 7.0 %collective-permute-done.7.refs_2_ = bf16[2,1024,128]{2,1,0:T(8,128)(2,1)} collective-permute-done((bf16[2,1024,128]{2,1,0:T(8,128)(2,1)}, bf16[2,1024,128]{2,1,0:T(8,128)(2,1)}, u32[]{:S(2)}, u32[]{:S(2)}) %collective-permute-start.7) | collective-permute-done | bytes 524320 | tf_op jit(solution)/shard_map/ppermute | solution.py:31
  63.4 5.3 %softmax_stats.2 = (f32[8,1024]{1,0:T(8,128)S(1)}, f32[8,1024]{1,0:T(8,128)S(1)}) custom-call(s32[2]{0:T(128)S(1)} %pad_add_fusion.1.refs_0_, bf16[2,1024,128]{2,1,0:T(8,128)(2,1)} %get-tuple-element.63.refs_1_, bf16[2,1024,128]{2,1,0:T(8,128)(2,1)} %collective-permute-done.7.refs_2_, bf16[1024,256]{1,0:T(8,128)(2,1)} %get-tuple-element.62.refs_5_.refs_3_, ...), custom_call_target="tpu_custom_call" | custom-call | flops 4000000000 | bytes 12000000 | tf_op jit(solution)/shard_map/softmax_stats/pallas_call | solution.py:225
  69.6 1.3 collective-permute-start.9
  71.6 1.8 collective-permute-done.11.refs_2_
  73.3 4.0 %softmax_stats.3 = (f32[8,1024]{1,0:T(8,128)S(1)}, f32[8,1024]{1,0:T(8,128)S(1)}) custom-call(s32[2]{0:T(128)S(1)} %pad_add_fusion.1.refs_0_, bf16[2,1024,128]{2,1,0:T(8,128)(2,1)S(1)} %copy-done.19, bf16[2,1024,128]{2,1,0:T(8,128)(2,1)S(1)} %collective-permute-done.11.refs_2_, bf16[1024,256]{1,0:T(8,128)(2,1)S(1)} %copy-done.17, ...), custom_call_target="tpu_custom_call" | custom-call | flops 4000000000 | bytes 12000000 | tf_op jit(solution)/shard_map/softmax_stats/pallas_call | solution.py:225
  78.4 2.8 %collective-permute-start.14 = (f32[8,1024]{1,0:T(8,128)S(1)}, f32[8,1024]{1,0:T(8,128)S(1)}, u32[]{:S(2)}, u32[]{:S(2)}) collective-permute-start(f32[8,1024]{1,0:T(8,128)S(1)} %get-tuple-element.68.refs_10_.refs_6_.refs_11_), channel_id=1, source_target_pairs={{0,24},{2,26},{4,28},{6,30},{8,0},{10,2},{12,4},{14,6},{16,8},{18,... | collective-permute-start | bytes 98312 | tf_op jit(solution)/shard_map/ppermute | solution.py:37
  81.2 9.7 %attention_grads.2 = (f32[2,1024,128]{2,1,0:T(8,128)S(1)}, bf16[2,1024,128]{2,1,0:T(8,128)(2,1)S(1)}, bf16[1024,256]{1,0:T(8,128)(2,1)S(1)}, f32[1024,256]{1,0:T(8,128)S(1)}) custom-call(s32[2]{0:T(128)S(1)} %pad_add_fusion.1.refs_0_, bf16[2,1024,128]{2,1,0:T(8,128)(2,1)} %get-tuple-element.63.refs_1_, bf16[2,1024,128]{2,1,0:T(8,128)(2,1)} %collective-permute-done.7.refs_2_, ...), custom_call_target="tpu_custom_call" | custom-call | flops 8000000000 | bytes 24000000 | tf_op jit(solution)/shard_map/attention_grads/pallas_call | solution.py:225
  91.9 1.5 collective-permute-start.17
  93.4 9.5 %attention_grads.3 = (f32[2,1024,128]{2,1,0:T(8,128)S(1)}, bf16[2,1024,256]{2,1,0:T(8,128)(2,1)}, bf16[1024,256]{1,0:T(8,128)(2,1)}, f32[1024,256]{1,0:T(8,128)S(1)}) custom-call(s32[2]{0:T(128)S(1)} %pad_add_fusion.1.refs_0_, bf16[2,1024,128]{2,1,0:T(8,128)(2,1)S(1)} %copy-done.19, bf16[2,1024,128]{2,1,0:T(8,128)(2,1)S(1)} %collective-permute-done.11.refs_2_, ...), custom_call_target="tpu_custom_call" | custom-call | flops 8000000000 | bytes 24000000 | tf_op jit(solution)/shard_map/attention_grads/pallas_call | solution.py:225
  103.0 2.4 %collective-permute-done.17.refs_6_ = bf16[1024,256]{1,0:T(8,128)(2,1)S(1)} collective-permute-done((bf16[1024,256]{1,0:T(8,128)(2,1)S(1)}, bf16[1024,256]{1,0:T(8,128)(2,1)S(1)}, u32[]{:S(2)}, u32[]{:S(2)}) %collective-permute-start.17) | collective-permute-done | bytes 524320 | tf_op jit(solution)/shard_map/ppermute | solution.py:31
  105.4 2.9 %spread.2 = (bf16[256,256]{1,0:T(8,128)(2,1)S(1)}, bf16[256,256]{1,0:T(8,128)(2,1)S(1)}, bf16[2,256,256]{2,1,0:T(8,128)(2,1)S(1)}, f32[4,256,256]{2,1,0:T(8,128)...) custom-call(s32[3]{0:T(128)S(1)} %pad_add_fusion.at_ref.refs_0_._, ...), custom_call_target="tpu_custom_call", output_to_operand_aliasing={{5}: (8, {})} | custom-call | tf_op jit(solution)/shard_map/spread/pallas_call | solution.py:315
  109.9 1.5 collective-permute-start.19
  111.5 3.1 %collective-permute-start.15 = (bf16[2,1024,256]{2,1,0:T(8,128)(2,1)}, bf16[2,1024,256]{2,1,0:T(8,128)(2,1)}, u32[]{:S(2)}, u32[]{:S(2)}) collective-permute-start(bf16[2,1024,256]{2,1,0:T(8,128)(2,1)} %get-tuple-element.73), channel_id=1, source_target_pairs={{0,8},{2,10},{4,12},{6,14},{8,16},{10,18},{12,20},{14,22},{16,24},... | collective-permute-start | bytes 3145736 | tf_op jit(solution)/shard_map/ppermute | solution.py:31
  114.6 1.5 collective-permute-start.16
  116.3 8.3 %collective-permute-done.19.refs_2_ = bf16[4,256,256]{2,1,0:T(8,128)(2,1)} collective-permute-done((bf16[4,256,256]{2,1,0:T(8,128)(2,1)}, bf16[4,256,256]{2,1,0:T(8,128)(2,1)}, u32[]{:S(2)}, u32[]{:S(2)}) %collective-permute-start.19) | collective-permute-done | bytes 524320 | tf_op jit(solution)/shard_map/ppermute | solution.py:51
  124.6 1.2 copy-done.15
  125.8 1.1 merge.4
  127.0 3.6 %collective-permute-done.16.refs_6_ = bf16[1024,256]{1,0:T(8,128)(2,1)} collective-permute-done((bf16[1024,256]{1,0:T(8,128)(2,1)}, bf16[1024,256]{1,0:T(8,128)(2,1)}, u32[]{:S(2)}, u32[]{:S(2)}) %collective-permute-start.16) | collective-permute-done | bytes 524320 | tf_op jit(solution)/shard_map/ppermute | solution.py:31
  130.6 2.8 %spread.3 = (bf16[256,512]{1,0:T(8,128)(2,1)S(1)}, bf16[256,512]{1,0:T(8,128)(2,1)S(1)}, bf16[2,256,512]{2,1,0:T(8,128)(2,1)S(1)}, f32[4,256,256]{2,1,0:T(8,128)S(1)}, bf16[4,256,256]{2,1,0:T(8,128)(2,1)S(1)}) custom-call(s32[3]{0:T(128)S(1)} %pad_add_fusion.at_ref.refs_0_._, bf16[256,2048]{1,0:T(8,128)(2,1)S(1)} %bitcast.11, ...), custom_call_target="tpu_custom_call" | custom-call | tf_op jit(solution)/shard_map/spread/pallas_call | solution.py:315
  134.0 2.7 %collective-permute-done.15.refs_3_ = bf16[2,1024,256]{2,1,0:T(8,128)(2,1)} collective-permute-done((bf16[2,1024,256]{2,1,0:T(8,128)(2,1)}, bf16[2,1024,256]{2,1,0:T(8,128)(2,1)}, u32[]{:S(2)}, u32[]{:S(2)}) %collective-permute-start.15) | collective-permute-done | bytes 1048608 | tf_op jit(solution)/shard_map/ppermute | solution.py:31
  136.7 1.5 settle_outs.1
  138.9 1.4 collective-permute-start.23
  140.3 2.5 %collective-permute-start.27 = (bf16[2,256,256]{2,1,0:T(8,128)(2,1)S(1)}, bf16[2,256,256]{2,1,0:T(8,128)(2,1)S(1)}, u32[]{:S(2)}, u32[]{:S(2)}) collective-permute-start(bf16[2,256,256]{2,1,0:T(8,128)(2,1)S(1)} %get-tuple-element.84.refs_10_), channel_id=1, source_target_pairs={{0,8},{1,9},{2,10},{3,11},{4,12},{5,13},{6,14},{7,15},{8,0},{9,1},... | collective-permute-start | bytes 786440 | tf_op jit(solution)/shard_map/ppermute | solution.py:47
  142.8 5.0 %collective-permute-done.25.refs_2_ = bf16[4,256,256]{2,1,0:T(8,128)(2,1)S(1)} collective-permute-done((bf16[4,256,256]{2,1,0:T(8,128)(2,1)S(1)}, bf16[4,256,256]{2,1,0:T(8,128)(2,1)S(1)}, u32[]{:S(2)}, u32[]{:S(2)}) %collective-permute-start.25) | collective-permute-done | bytes 524320 | tf_op jit(solution)/shard_map/ppermute | solution.py:51
  150.1 3.5 %collective-permute-start.28 = (bf16[1,256,256]{2,1,0:T(8,128)(2,1)S(1)}, bf16[1,256,256]{2,1,0:T(8,128)(2,1)S(1)}, u32[]{:S(2)}, u32[]{:S(2)}) collective-permute-start(bf16[1,256,256]{2,1,0:T(8,128)(2,1)S(1)} %get-tuple-element.102), channel_id=1, source_target_pairs={{0,16},{1,17},{2,18},{3,19},{4,20},{5,21},{6,22},{7,23},{8,24},{9,... | collective-permute-start | bytes 393224 | tf_op jit(solution)/shard_map/ppermute | solution.py:47
  154.3 4.9 %collective-permute-done.26.refs_2_ = bf16[2,256,256]{2,1,0:T(8,128)(2,1)S(1)} collective-permute-done((bf16[2,256,256]{2,1,0:T(8,128)(2,1)S(1)}, bf16[2,256,256]{2,1,0:T(8,128)(2,1)S(1)}, u32[]{:S(2)}, u32[]{:S(2)}) %collective-permute-start.26) | collective-permute-done | bytes 262176 | tf_op jit(solution)/shard_map/ppermute | solution.py:47
  159.9 6.9 %feature_grads.1 = (bf16[1,256,2048]{2,1,0:T(8,128)(2,1)}, f32[8,128]{1,0:T(8,128)S(1)}) custom-call(s32[3]{0:T(128)S(1)} %pad_add_fusion.at_ref.refs_0_._, bf16[256,512]{1,0:T(8,128)(2,1)S(1)} %get-tuple-element.91.refs_1_, bf16[2,256,512]{2,1,0:T(8,128)(2,1)S(1)} %collective-permute-done.22.refs_2_, ...), custom_call_target="tpu_custom_call" | custom-call | flops 6000000000 | bytes 18000000 | tf_op jit(solution)/shard_map/feature_grads/pallas_call | solution.py:579
  167.5 1.4 collective-permute-start.31
  169.4 1.7 place_heads.1
  171.0 2.8 %collective-permute-done.31.refs_3_ = f32[64,512]{1,0:T(8,128)S(1)} collective-permute-done((f32[64,512]{1,0:T(8,128)S(1)}, f32[64,512]{1,0:T(8,128)S(1)}, u32[]{:S(2)}, u32[]{:S(2)}) %collective-permute-start.31) | collective-permute-done | bytes 131104 | tf_op jit(solution)/shard_map/ppermute | solution.py:24
  173.9 1.9 %collective-permute-done.32.refs_4_ = f32[64,512]{1,0:T(8,128)S(1)} collective-permute-done((f32[64,512]{1,0:T(8,128)S(1)}, f32[64,512]{1,0:T(8,128)S(1)}, u32[]{:S(2)}, u32[]{:S(2)}) %collective-permute-start.32) | collective-permute-done | bytes 131104 | tf_op jit(solution)/shard_map/ppermute | solution.py:24
  175.8 1.4 place_weight.1
  (92 shorter events, 15.7 us)
Async XLA Ops:
  0.6 26.4 %collective-permute-start.4 = (bf16[256,2048]{1,0:T(8,128)(2,1)}, bf16[256,2048]{1,0:T(8,128)(2,1)S(1)}, u32[]{:S(2)}, u32[]{:S(2)}) collective-permute-start(bf16[256,2048]{1,0:T(8,128)(2,1)} %bitcast.7), channel_id=1, source_target_pairs={{0,4},{2,6},{4,0},{6,2},{8,12},{10,14},{12,8},{14,10},{16,20},{18,... | collective-permute-start | bytes 3145736 | tf_op jit(solution)/shard_map/ppermute | solution.py:24
  3.6 26.3 %collective-permute-start.3 = (bf16[256,2048]{1,0:T(8,128)(2,1)}, bf16[256,2048]{1,0:T(8,128)(2,1)S(1)}, u32[]{:S(2)}, u32[]{:S(2)}) collective-permute-start(bf16[256,2048]{1,0:T(8,128)(2,1)} %bitcast.8), channel_id=1, source_target_pairs={{0,2},{2,0},{4,6},{6,4},{8,10},{10,8},{12,14},{14,12},{16,18},{18,... | collective-permute-start | bytes 3145736 | tf_op jit(solution)/shard_map/ppermute | solution.py:24
  8.0 21.3 %copy-start.1 = (bf16[1024,2048]{1,0:T(8,128)(2,1)S(1)}, bf16[1024,2048]{1,0:T(8,128)(2,1)}, u32[]{:S(2)}) copy-start(bf16[1024,2048]{1,0:T(8,128)(2,1)} %refs_4_.1) | copy-start | bytes 12582916
  9.1 25.6 %collective-permute-start.6 = (bf16[1024,512]{1,0:T(8,128)(2,1)S(1)}, bf16[1024,512]{1,0:T(8,128)(2,1)S(1)}, u32[]{:S(2)}, u32[]{:S(2)}) collective-permute-start(bf16[1024,512]{1,0:T(8,128)(2,1)S(1)} %get-tuple-element.61.refs_5_), channel_id=1, source_target_pairs={{0,1},{1,0},{2,3},{3,2},{4,5},{5,4},{6,7},{7,6},{8,9},{9,8},{10,11... | collective-permute-start | bytes 3145736 | tf_op jit(solution)/shard_map/ppermute | solution.py:51
  27.0 7.7 %collective-permute-start.5 = (bf16[256,2048]{1,0:T(8,128)(2,1)S(1)}, bf16[256,2048]{1,0:T(8,128)(2,1)S(1)}, u32[]{:S(2)}, u32[]{:S(2)}) collective-permute-start(bf16[256,2048]{1,0:T(8,128)(2,1)S(1)} %collective-permute-done.4.refs_3_), channel_id=1, source_target_pairs={{0,2},{2,0},{4,6},{6,4},{8,10},{10,8},{12,14},{14,12},{16,18},{18,... | collective-permute-start | bytes 3145736 | tf_op jit(solution)/shard_map/ppermute | solution.py:24
  27.0 15.7 %collective-permute-start = (bf16[2,256,256]{2,1,0:T(8,128)(2,1)S(1)}, bf16[2,256,256]{2,1,0:T(8,128)(2,1)S(1)}, u32[]{:S(2)}, u32[]{:S(2)}) collective-permute-start(bf16[2,256,256]{2,1,0:T(8,128)(2,1)S(1)} %get-tuple-element.58), channel_id=1, source_target_pairs={{0,2},{2,0},{4,6},{6,4},{8,10},{10,8},{12,14},{14,12},{16,18},{18,... | collective-permute-start | bytes 786440 | tf_op jit(solution)/shard_map/ppermute | solution.py:24
  27.5 7.2 %copy-start.3 = (bf16[1,256,2048]{2,1,0:T(8,128)(2,1)S(1)}, bf16[1,256,2048]{2,1,0:T(8,128)(2,1)}, u32[]{:S(2)}) copy-start(bf16[1,256,2048]{2,1,0:T(8,128)(2,1)} %param.4) | copy-start | bytes 3145732
  27.5 15.2 %collective-permute-start.1 = (bf16[2,256,256]{2,1,0:T(8,128)(2,1)S(1)}, bf16[2,256,256]{2,1,0:T(8,128)(2,1)S(1)}, u32[]{:S(2)}, u32[]{:S(2)}) collective-permute-start(bf16[2,256,256]{2,1,0:T(8,128)(2,1)S(1)} %get-tuple-element.59), channel_id=1, source_target_pairs={{0,4},{2,6},{4,0},{6,2},{8,12},{10,14},{12,8},{14,10},{16,20},{18,... | collective-permute-start | bytes 786440 | tf_op jit(solution)/shard_map/ppermute | solution.py:24
  30.0 12.8 %collective-permute-start.2 = (bf16[2,256,256]{2,1,0:T(8,128)(2,1)S(1)}, bf16[2,256,256]{2,1,0:T(8,128)(2,1)S(1)}, u32[]{:S(2)}, u32[]{:S(2)}) collective-permute-start(bf16[2,256,256]{2,1,0:T(8,128)(2,1)S(1)} %get-tuple-element.60), channel_id=1, source_target_pairs={{0,6},{2,4},{4,2},{6,0},{8,14},{10,12},{12,10},{14,8},{16,22},{18,... | collective-permute-start | bytes 786440 | tf_op jit(solution)/shard_map/ppermute | solution.py:24
  34.8 3.7 %copy-start.4 = (bf16[256,2048]{1,0:T(8,128)(2,1)}, bf16[256,2048]{1,0:T(8,128)(2,1)S(1)}, u32[]{:S(2)}) copy-start(bf16[256,2048]{1,0:T(8,128)(2,1)S(1)} %collective-permute-done.5.refs_4_) | copy-start | bytes 3145732
  38.4 5.8 %copy-start.16 = (bf16[1024,256]{1,0:T(8,128)(2,1)}, bf16[1024,256]{1,0:T(8,128)(2,1)S(1)}, u32[]{:S(2)}) copy-start(bf16[1024,256]{1,0:T(8,128)(2,1)S(1)} %get-tuple-element.67.refs_3_) | copy-start | bytes 1572868
  38.4 16.8 %collective-permute-start.8 = (bf16[1024,256]{1,0:T(8,128)(2,1)}, bf16[1024,256]{1,0:T(8,128)(2,1)}, u32[]{:S(2)}, u32[]{:S(2)}) collective-permute-start(bf16[1024,256]{1,0:T(8,128)(2,1)} %get-tuple-element.62.refs_5_.refs_3_), channel_id=1, source_target_pairs={{0,8},{2,10},{4,12},{6,14},{8,16},{10,18},{12,20},{14,22},{16,24},... | collective-permute-start | bytes 1572872 | tf_op jit(solution)/shard_map/ppermute | solution.py:31
  46.4 17.1 %collective-permute-start.7 = (bf16[2,1024,128]{2,1,0:T(8,128)(2,1)}, bf16[2,1024,128]{2,1,0:T(8,128)(2,1)}, u32[]{:S(2)}, u32[]{:S(2)}) collective-permute-start(bf16[2,1024,128]{2,1,0:T(8,128)(2,1)} %get-tuple-element.63.refs_1_), channel_id=1, source_target_pairs={{8,0},{10,2},{12,4},{14,6},{16,8},{18,10},{20,12},{22,14},{24,16},... | collective-permute-start | bytes 1572872 | tf_op jit(solution)/shard_map/ppermute | solution.py:31
  47.7 23.2 %collective-permute-start.12 = (bf16[1024,256]{1,0:T(8,128)(2,1)}, bf16[1024,256]{1,0:T(8,128)(2,1)S(1)}, u32[]{:S(2)}, u32[]{:S(2)}) collective-permute-start(bf16[1024,256]{1,0:T(8,128)(2,1)} %copy-done.16), channel_id=1, source_target_pairs={{0,8},{2,10},{4,12},{6,14},{8,16},{10,18},{12,20},{14,22},{16,24},... | collective-permute-start | bytes 1572872 | tf_op jit(solution)/shard_map/ppermute | solution.py:31
  52.3 21.0 %collective-permute-start.11 = (bf16[2,1024,128]{2,1,0:T(8,128)(2,1)}, bf16[2,1024,128]{2,1,0:T(8,128)(2,1)S(1)}, u32[]{:S(2)}, u32[]{:S(2)}) collective-permute-start(bf16[2,1024,128]{2,1,0:T(8,128)(2,1)} %copy-done.18), channel_id=1, source_target_pairs={{8,0},{10,2},{12,4},{14,6},{16,8},{18,10},{20,12},{22,14},{24,16},... | collective-permute-start | bytes 1572872 | tf_op jit(solution)/shard_map/ppermute | solution.py:31
  53.6 51.7 %collective-permute-start.18 = (bf16[512,2048]{1,0:T(8,128)(2,1)}, bf16[512,2048]{1,0:T(8,128)(2,1)}, u32[]{:S(2)}, u32[]{:S(2)}) collective-permute-start(bf16[512,2048]{1,0:T(8,128)(2,1)} %copy-done.13), channel_id=1, source_target_pairs={{0,1},{1,0},{2,3},{3,2},{4,5},{5,4},{6,7},{7,6},{8,9},{9,8},{10,11... | collective-permute-start | bytes 6291464 | tf_op jit(solution)/shard_map/ppermute | solution.py:51
  68.7 4.6 %copy-start.17 = (bf16[1024,256]{1,0:T(8,128)(2,1)S(1)}, bf16[1024,256]{1,0:T(8,128)(2,1)}, u32[]{:S(2)}) copy-start(bf16[1024,256]{1,0:T(8,128)(2,1)} %copy-done.16) | copy-start | bytes 1572868
  68.7 4.6 %copy-start.19 = (bf16[2,1024,128]{2,1,0:T(8,128)(2,1)S(1)}, bf16[2,1024,128]{2,1,0:T(8,128)(2,1)}, u32[]{:S(2)}) copy-start(bf16[2,1024,128]{2,1,0:T(8,128)(2,1)} %copy-done.18) | copy-start | bytes 1572868
  68.8 12.4 %collective-permute-start.10 = (f32[8,1024]{1,0:T(8,128)S(1)}, f32[8,1024]{1,0:T(8,128)S(1)}, u32[]{:S(2)}, u32[]{:S(2)}) collective-permute-start(f32[8,1024]{1,0:T(8,128)S(1)} %get-tuple-element.64.refs_6_), channel_id=1, source_target_pairs={{0,24},{2,26},{4,28},{6,30},{8,0},{10,2},{12,4},{14,6},{16,8},{18,... | collective-permute-start | bytes 98312 | tf_op jit(solution)/shard_map/ppermute | solution.py:37
  69.6 11.6 %collective-permute-start.9 = (f32[8,1024]{1,0:T(8,128)S(1)}, f32[8,1024]{1,0:T(8,128)S(1)}, u32[]{:S(2)}, u32[]{:S(2)}) collective-permute-start(f32[8,1024]{1,0:T(8,128)S(1)} %get-tuple-element.65.refs_8_), channel_id=1, source_target_pairs={{0,8},{2,10},{4,12},{6,14},{8,16},{10,18},{12,20},{14,22},{16,24},... | collective-permute-start | bytes 98312 | tf_op jit(solution)/shard_map/ppermute | solution.py:37
  77.3 16.1 %collective-permute-start.13 = (f32[8,1024]{1,0:T(8,128)S(1)}, f32[8,1024]{1,0:T(8,128)S(1)}, u32[]{:S(2)}, u32[]{:S(2)}) collective-permute-start(f32[8,1024]{1,0:T(8,128)S(1)} %get-tuple-element.70.refs_8_), channel_id=1, source_target_pairs={{0,8},{2,10},{4,12},{6,14},{8,16},{10,18},{12,20},{14,22},{16,24},... | collective-permute-start | bytes 98312 | tf_op jit(solution)/shard_map/ppermute | solution.py:37
  78.4 15.0 %collective-permute-start.14 = (f32[8,1024]{1,0:T(8,128)S(1)}, f32[8,1024]{1,0:T(8,128)S(1)}, u32[]{:S(2)}, u32[]{:S(2)}) collective-permute-start(f32[8,1024]{1,0:T(8,128)S(1)} %get-tuple-element.68.refs_10_.refs_6_.refs_11_), channel_id=1, source_target_pairs={{0,24},{2,26},{4,28},{6,30},{8,0},{10,2},{12,4},{14,6},{16,8},{18,... | collective-permute-start | bytes 98312 | tf_op jit(solution)/shard_map/ppermute | solution.py:37
  91.9 13.5 %collective-permute-start.17 = (bf16[1024,256]{1,0:T(8,128)(2,1)S(1)}, bf16[1024,256]{1,0:T(8,128)(2,1)S(1)}, u32[]{:S(2)}, u32[]{:S(2)}) collective-permute-start(bf16[1024,256]{1,0:T(8,128)(2,1)S(1)} %get-tuple-element.77), channel_id=1, source_target_pairs={{8,0},{10,2},{12,4},{14,6},{16,8},{18,10},{20,12},{22,14},{24,16},... | collective-permute-start | bytes 1572872 | tf_op jit(solution)/shard_map/ppermute | solution.py:31
  93.4 11.9 %copy-start.5 = (bf16[256,2048]{1,0:T(8,128)(2,1)S(1)}, bf16[256,2048]{1,0:T(8,128)(2,1)}, u32[]{:S(2)}) copy-start(bf16[256,2048]{1,0:T(8,128)(2,1)} %copy-done.4) | copy-start | bytes 3145732
  103.0 5.3 %copy-start.7 = (f32[1024,256]{1,0:T(8,128)}, f32[1024,256]{1,0:T(8,128)S(1)}, u32[]{:S(2)}) copy-start(f32[1024,256]{1,0:T(8,128)S(1)} %get-tuple-element.74.refs_7_.refs_5_) | copy-start | bytes 3145732
  103.0 5.3 %copy-start.22 = (f32[2,1024,128]{2,1,0:T(8,128)}, f32[2,1024,128]{2,1,0:T(8,128)S(1)}, u32[]{:S(2)}) copy-start(f32[2,1024,128]{2,1,0:T(8,128)S(1)} %get-tuple-element.72.refs_2_) | copy-start | bytes 3145732
  109.9 49.9 %collective-permute-start.24 = (bf16[512,2048]{1,0:T(8,128)(2,1)}, bf16[512,2048]{1,0:T(8,128)(2,1)}, u32[]{:S(2)}, u32[]{:S(2)}) collective-permute-start(bf16[512,2048]{1,0:T(8,128)(2,1)} %get-tuple-element.94.refs_5_), channel_id=1, source_target_pairs={{0,2},{2,0},{4,6},{6,4},{8,10},{10,8},{12,14},{14,12},{16,18},{18,... | collective-permute-start | bytes 6291464 | tf_op jit(solution)/shard_map/ppermute | solution.py:24
  109.9 14.7 %collective-permute-start.19 = (bf16[4,256,256]{2,1,0:T(8,128)(2,1)}, bf16[4,256,256]{2,1,0:T(8,128)(2,1)}, u32[]{:S(2)}, u32[]{:S(2)}) collective-permute-start(bf16[4,256,256]{2,1,0:T(8,128)(2,1)} %get-tuple-element.83), channel_id=1, source_target_pairs={{0,1},{1,0},{2,3},{3,2},{4,5},{5,4},{6,7},{7,6},{8,9},{9,8},{10,11... | collective-permute-start | bytes 1572872 | tf_op jit(solution)/shard_map/ppermute | solution.py:51
  111.5 25.3 %collective-permute-start.15 = (bf16[2,1024,256]{2,1,0:T(8,128)(2,1)}, bf16[2,1024,256]{2,1,0:T(8,128)(2,1)}, u32[]{:S(2)}, u32[]{:S(2)}) collective-permute-start(bf16[2,1024,256]{2,1,0:T(8,128)(2,1)} %get-tuple-element.73), channel_id=1, source_target_pairs={{0,8},{2,10},{4,12},{6,14},{8,16},{10,18},{12,20},{14,22},{16,24},... | collective-permute-start | bytes 3145736 | tf_op jit(solution)/shard_map/ppermute | solution.py:31
  114.6 16.0 %collective-permute-start.16 = (bf16[1024,256]{1,0:T(8,128)(2,1)}, bf16[1024,256]{1,0:T(8,128)(2,1)}, u32[]{:S(2)}, u32[]{:S(2)}) collective-permute-start(bf16[1024,256]{1,0:T(8,128)(2,1)} %get-tuple-element.75), channel_id=1, source_target_pairs={{8,0},{10,2},{12,4},{14,6},{16,8},{18,10},{20,12},{22,14},{24,16},... | collective-permute-start | bytes 1572872 | tf_op jit(solution)/shard_map/ppermute | solution.py:31
  116.2 14.4 %copy-start.6 = (bf16[256,2048]{1,0:T(8,128)(2,1)S(1)}, bf16[256,2048]{1,0:T(8,128)(2,1)}, u32[]{:S(2)}) copy-start(bf16[256,2048]{1,0:T(8,128)(2,1)} %copy-done.4) | copy-start | bytes 3145732
  116.2 14.4 %copy-start.8 = (f32[1024,256]{1,0:T(8,128)S(1)}, f32[1024,256]{1,0:T(8,128)}, u32[]{:S(2)}) copy-start(f32[1024,256]{1,0:T(8,128)} %copy-done.7) | copy-start | bytes 3145732
  116.2 14.4 %copy-start.12 = (bf16[256,256]{1,0:T(8,128)(2,1)S(1)}, bf16[256,256]{1,0:T(8,128)(2,1)}, u32[]{:S(2)}) copy-start(bf16[256,256]{1,0:T(8,128)(2,1)} %copy-done.11) | copy-start | bytes 393220
  130.6 6.2 %copy-start.21 = (f32[2,1024,128]{2,1,0:T(8,128)S(1)}, f32[2,1024,128]{2,1,0:T(8,128)}, u32[]{:S(2)}) copy-start(f32[2,1024,128]{2,1,0:T(8,128)} %copy-done.20) | copy-start | bytes 3145732
  130.6 6.2 %copy-start.23 = (f32[2,1024,128]{2,1,0:T(8,128)S(1)}, f32[2,1024,128]{2,1,0:T(8,128)}, u32[]{:S(2)}) copy-start(f32[2,1024,128]{2,1,0:T(8,128)} %copy-done.22) | copy-start | bytes 3145732
  133.4 4.9 %collective-permute-start.22 = (bf16[2,256,512]{2,1,0:T(8,128)(2,1)S(1)}, bf16[2,256,512]{2,1,0:T(8,128)(2,1)S(1)}, u32[]{:S(2)}, u32[]{:S(2)}) collective-permute-start(bf16[2,256,512]{2,1,0:T(8,128)(2,1)S(1)} %get-tuple-element.92), channel_id=1, source_target_pairs={{0,2},{2,0},{4,6},{6,4},{8,10},{10,8},{12,14},{14,12},{16,18},{18,... | collective-permute-start | bytes 1572872 | tf_op jit(solution)/shard_map/ppermute | solution.py:24
  133.5 14.3 %collective-permute-start.25 = (bf16[4,256,256]{2,1,0:T(8,128)(2,1)S(1)}, bf16[4,256,256]{2,1,0:T(8,128)(2,1)S(1)}, u32[]{:S(2)}, u32[]{:S(2)}) collective-permute-start(bf16[4,256,256]{2,1,0:T(8,128)(2,1)S(1)} %get-tuple-element.85.refs_4_), channel_id=1, source_target_pairs={{0,1},{1,0},{2,3},{3,2},{4,5},{5,4},{6,7},{7,6},{8,9},{9,8},{10,11... | collective-permute-start | bytes 1572872 | tf_op jit(solution)/shard_map/ppermute | solution.py:51
  138.2 15.4 %collective-permute-start.20 = (bf16[2,2,256,256]{3,2,1,0:T(8,128)(2,1)S(1)}, bf16[2,2,256,256]{3,2,1,0:T(8,128)(2,1)S(1)}, u32[]{:S(2)}, u32[]{:S(2)}) collective-permute-start(bf16[2,2,256,256]{3,2,1,0:T(8,128)(2,1)S(1)} %get-tuple-element.87), channel_id=1, source_target_pairs={{0,2},{2,0},{4,6},{6,4},{8,10},{10,8},{12,14},{14,12},{16,18},{18,... | collective-permute-start | bytes 1572872 | tf_op jit(solution)/shard_map/ppermute | solution.py:24
  138.9 20.3 %collective-permute-start.23 = (bf16[2,256,512]{2,1,0:T(8,128)(2,1)S(1)}, bf16[2,256,512]{2,1,0:T(8,128)(2,1)S(1)}, u32[]{:S(2)}, u32[]{:S(2)}) collective-permute-start(bf16[2,256,512]{2,1,0:T(8,128)(2,1)S(1)} %mix.3), channel_id=1, source_target_pairs={{0,4},{2,6},{4,0},{6,2},{8,12},{10,14},{12,8},{14,10},{16,20},{18,... | collective-permute-start | bytes 1572872 | tf_op jit(solution)/shard_map/ppermute | solution.py:24
  140.3 9.2 %collective-permute-start.27 = (bf16[2,256,256]{2,1,0:T(8,128)(2,1)S(1)}, bf16[2,256,256]{2,1,0:T(8,128)(2,1)S(1)}, u32[]{:S(2)}, u32[]{:S(2)}) collective-permute-start(bf16[2,256,256]{2,1,0:T(8,128)(2,1)S(1)} %get-tuple-element.84.refs_10_), channel_id=1, source_target_pairs={{0,8},{1,9},{2,10},{3,11},{4,12},{5,13},{6,14},{7,15},{8,0},{9,1},... | collective-permute-start | bytes 786440 | tf_op jit(solution)/shard_map/ppermute | solution.py:47
  148.4 10.7 %collective-permute-start.26 = (bf16[2,256,256]{2,1,0:T(8,128)(2,1)S(1)}, bf16[2,256,256]{2,1,0:T(8,128)(2,1)S(1)}, u32[]{:S(2)}, u32[]{:S(2)}) collective-permute-start(bf16[2,256,256]{2,1,0:T(8,128)(2,1)S(1)} %get-tuple-element.97), channel_id=1, source_target_pairs={{0,8},{1,9},{2,10},{3,11},{4,12},{5,13},{6,14},{7,15},{8,0},{9,1},... | collective-permute-start | bytes 786440 | tf_op jit(solution)/shard_map/ppermute | solution.py:47
  150.1 16.7 %collective-permute-start.28 = (bf16[1,256,256]{2,1,0:T(8,128)(2,1)S(1)}, bf16[1,256,256]{2,1,0:T(8,128)(2,1)S(1)}, u32[]{:S(2)}, u32[]{:S(2)}) collective-permute-start(bf16[1,256,256]{2,1,0:T(8,128)(2,1)S(1)} %get-tuple-element.102), channel_id=1, source_target_pairs={{0,16},{1,17},{2,18},{3,19},{4,20},{5,21},{6,22},{7,23},{8,24},{9,... | collective-permute-start | bytes 393224 | tf_op jit(solution)/shard_map/ppermute | solution.py:47
  153.6 6.3 %copy-start.2 = (bf16[1024,2048]{1,0:T(8,128)(2,1)S(1)}, bf16[1024,2048]{1,0:T(8,128)(2,1)}, u32[]{:S(2)}) copy-start(bf16[1024,2048]{1,0:T(8,128)(2,1)} %refs_4_.1) | copy-start | bytes 12582916
  154.2 15.2 %collective-permute-start.21 = (bf16[2,2,256,256]{3,2,1,0:T(8,128)(2,1)S(1)}, bf16[2,2,256,256]{3,2,1,0:T(8,128)(2,1)S(1)}, u32[]{:S(2)}, u32[]{:S(2)}) collective-permute-start(bf16[2,2,256,256]{3,2,1,0:T(8,128)(2,1)S(1)} %mix.2), channel_id=1, source_target_pairs={{0,4},{2,6},{4,0},{6,2},{8,12},{10,14},{12,8},{14,10},{16,20},{18,... | collective-permute-start | bytes 1572872 | tf_op jit(solution)/shard_map/ppermute | solution.py:24
  159.8 7.0 %collective-permute-start.29 = (bf16[1,256,256]{2,1,0:T(8,128)(2,1)S(1)}, bf16[1,256,256]{2,1,0:T(8,128)(2,1)S(1)}, u32[]{:S(2)}, u32[]{:S(2)}) collective-permute-start(bf16[1,256,256]{2,1,0:T(8,128)(2,1)S(1)} %get-tuple-element.98.refs_7_), channel_id=1, source_target_pairs={{0,16},{1,17},{2,18},{3,19},{4,20},{5,21},{6,22},{7,23},{8,24},{9,... | collective-permute-start | bytes 393224 | tf_op jit(solution)/shard_map/ppermute | solution.py:47
  167.4 3.6 %collective-permute-start.30 = (f32[64,512]{1,0:T(8,128)S(1)}, f32[64,512]{1,0:T(8,128)S(1)}, u32[]{:S(2)}, u32[]{:S(2)}) collective-permute-start(f32[64,512]{1,0:T(8,128)S(1)} %get-tuple-element.106), channel_id=1, source_target_pairs={{0,2},{2,0},{4,6},{6,4},{8,10},{10,8},{12,14},{14,12},{16,18},{18,... | collective-permute-start | bytes 393224 | tf_op jit(solution)/shard_map/ppermute | solution.py:24
  167.5 6.4 %collective-permute-start.31 = (f32[64,512]{1,0:T(8,128)S(1)}, f32[64,512]{1,0:T(8,128)S(1)}, u32[]{:S(2)}, u32[]{:S(2)}) collective-permute-start(f32[64,512]{1,0:T(8,128)S(1)} %get-tuple-element.107), channel_id=1, source_target_pairs={{0,4},{2,6},{4,0},{6,2},{8,12},{10,14},{12,8},{14,10},{16,20},{18,... | collective-permute-start | bytes 393224 | tf_op jit(solution)/shard_map/ppermute | solution.py:24
  168.9 6.8 %collective-permute-start.32 = (f32[64,512]{1,0:T(8,128)S(1)}, f32[64,512]{1,0:T(8,128)S(1)}, u32[]{:S(2)}, u32[]{:S(2)}) collective-permute-start(f32[64,512]{1,0:T(8,128)S(1)} %get-tuple-element.108), channel_id=1, source_target_pairs={{0,6},{2,4},{4,2},{6,0},{8,14},{10,12},{12,10},{14,8},{16,22},{18,... | collective-permute-start | bytes 393224 | tf_op jit(solution)/shard_map/ppermute | solution.py:24
  (9 other events, 10.2 us)

commit v6 on v5

--- a/solution.py
+++ b/solution.py
@@ -93,13 +93,13 @@
         yield 1, turn, [(1, lane, "high" if lane == turn else None) for lane in range(turn, blocks)]
 
 
-def masked(score, near, edge, near_bias):
+def masked(score, edge):
     if edge:
         key_pos = lax.broadcasted_iota(jnp.int32, score.shape, 0)
         query_pos = lax.broadcasted_iota(jnp.int32, score.shape, 1)
         allowed = key_pos <= query_pos if edge == "low" else key_pos > query_pos
         score = jnp.where(allowed, score, MASKED)
-    return score + near_bias if near else score
+    return score
 
 
 def turn_kernel(_, near_ref, out_ref):
@@ -122,18 +122,20 @@
     outs = (own_out, next_out)
     for turn, (side, block, keys) in enumerate(visits(blocks)):
         held = slice(block * size, (block + 1) * size)
-        peak = jnp.full((8, size), MASKED, jnp.float32)
+        peaks = [jnp.full((8, size), MASKED, jnp.float32)] * 2
         for index, (near, lane, edge) in enumerate(keys):
             key = window[near][lane * size : (lane + 1) * size, :HEAD_DIM]
-            score = masked(product_minor(key, pairs[side][0, held]), near, edge, near_bias)
+            score = masked(product_minor(key, pairs[side][0, held]), edge)
             scores[turn % 2, index] = score
-            peak = jnp.maximum(peak, by_sublane(score, jnp.max))
-        peak = jnp.max(peak, axis=0, keepdims=True)
+            peaks[near] = jnp.maximum(peaks[near], by_sublane(score, jnp.max))
+        peaks = [jnp.max(found, axis=0, keepdims=True) for found in peaks]
+        peak = jnp.maximum(peaks[0], peaks[1] + near_bias)
+        bases = (peak, peak - near_bias)
         mass = jnp.zeros((8, size), jnp.float32)
         pull = jnp.zeros((8, size), jnp.float32)
         for index, (near, lane, edge) in enumerate(keys):
             value = window[near][lane * size : (lane + 1) * size, HEAD_DIM:]
-            grown = jnp.exp2((scores[turn % 2, index] - peak) * EXP2_SCALE)
+            grown = jnp.exp2((scores[turn % 2, index] - bases[near]) * EXP2_SCALE)
             mass = mass + by_sublane(grown, jnp.sum)
             pull = pull + by_sublane(grown * product_minor(value, pairs[side][1, held]), jnp.sum)
         out = outs[side]
@@ -188,11 +190,12 @@
         column = slice(side * row_tokens + block * size, side * row_tokens + (block + 1) * size)
         peak, share, centre = (figure[:, held] for figure in figures[side])
         scaled = share * SCORE_SCALE
+        bases = (peak, peak - near_bias)
         for near, lane, edge in keys:
             rows = slice(lane * size, (lane + 1) * size)
             score = product_minor(window[near][rows, :HEAD_DIM], pairs[side][0, held])
             dprob = product_minor(window[near][rows, HEAD_DIM:], pairs[side][1, held])
-            grown = jnp.exp2((masked(score, near, edge, near_bias) - peak) * EXP2_SCALE)
+            grown = jnp.exp2((masked(score, edge) - bases[near]) * EXP2_SCALE)
             weights[near][rows, column] = (grown * share).astype(jnp.bfloat16)
             dscores[near][rows, column] = (grown * ((dprob - centre) * scaled)).astype(jnp.bfloat16)
         rows = slice(block * size if side else 0, row_tokens)

time: 178 us -> 177 us (level)
  no operation moved by 1% of the time
where the time goes in v6:
time: 177 us
  waiting for transfers between devices  62.4 us (35%)
  Pallas kernels  59 us (33%)
  starting transfers between devices  43.9 us (25%)
  local copies, waits for them, and re-layouts  10.3 us (6%)
    pallas_call x4, Pallas kernels, kernel_call(): pl.pallas_call(ordered(functools.partial(kernel, blocks=blocks, size=size...  28.1 us
    pallas_call x16, Pallas kernels, small_call(): pl.pallas_call(ordered(kernel, len(operands), len(waits), len(out_shape),...  22.2 us
    ppermute x14, waiting for transfers between devices, exchanged(): lax.ppermute(value, 'seq', [(source, source ^ bits) for source in range(c...  21.1 us
    ppermute x4, waiting for transfers between devices, swapped(): return lax.ppermute(value, 'dp', [(0, 1), (1, 0)])  18.1 us
    ppermute x7, starting transfers between devices, shifted(): lax.ppermute(value, 'seq', [(source, source + steps) for source in range(...  17.4 us
    ppermute x7, waiting for transfers between devices, shifted(): lax.ppermute(value, 'seq', [(source, source + steps) for source in range(...  17.4 us
    unnamed x48, local copies, waits for them, and re-layouts  10.3 us
    ppermute x14, starting transfers between devices, exchanged(): lax.ppermute(value, 'seq', [(source, source ^ bits) for source in range(c...  9.07 us
  transfers between devices with their start and end apart: 33, of which 13 were waited for; matrix products, arithmetic and copies ran while one was open for 0% of the time, Pallas kernels for 31%

profile of v6, /device:TPU:0, one launch (start us, length us, event | category | flops | bytes accessed | tf_op | source)
XLA Modules:
  0.0 176.8 jit_solution(121428571959557917)
XLA Ops:
  0.6 3.0 %collective-permute-start.4 = (bf16[256,2048]{1,0:T(8,128)(2,1)}, bf16[256,2048]{1,0:T(8,128)(2,1)S(1)}, u32[]{:S(2)}, u32[]{:S(2)}) collective-permute-start(bf16[256,2048]{1,0:T(8,128)(2,1)} %bitcast.7), channel_id=1, source_target_pairs={{0,4},{2,6},{4,0},{6,2},{8,12},{10,14},{12,8},{14,10},{16,20},{18,... | collective-permute-start | bytes 3145736 | tf_op jit(solution)/shard_map/ppermute | solution.py:24
  3.7 2.2 %copy-done = bf16[1024,2048]{1,0:T(8,128)(2,1)S(1)} copy-done((bf16[1024,2048]{1,0:T(8,128)(2,1)S(1)}, bf16[1024,2048]{1,0:T(8,128)(2,1)}, u32[]{:S(2)}) %copy-start) | copy-done | bytes 4194328
  8.0 1.1 deal.1
  9.1 1.6 collective-permute-start.6
  10.7 16.3 %collective-permute-done.4.refs_3_ = bf16[256,2048]{1,0:T(8,128)(2,1)S(1)} collective-permute-done((bf16[256,2048]{1,0:T(8,128)(2,1)}, bf16[256,2048]{1,0:T(8,128)(2,1)S(1)}, u32[]{:S(2)}, u32[]{:S(2)}) %collective-permute-start.4) | collective-permute-done | bytes 1048608 | tf_op jit(solution)/shard_map/ppermute | solution.py:24
  27.5 1.7 collective-permute-start.1
  30.0 4.7 %collective-permute-done.6.refs_6_ = bf16[1024,512]{1,0:T(8,128)(2,1)S(1)} collective-permute-done((bf16[1024,512]{1,0:T(8,128)(2,1)S(1)}, bf16[1024,512]{1,0:T(8,128)(2,1)S(1)}, u32[]{:S(2)}, u32[]{:S(2)}) %collective-permute-start.6) | collective-permute-done | bytes 1048608 | tf_op jit(solution)/shard_map/ppermute | solution.py:51
  34.8 3.7 %project.1 = (bf16[1024,256]{1,0:T(8,128)(2,1)}, bf16[1024,256]{1,0:T(8,128)(2,1)S(1)}) custom-call(s32[3]{0:T(128)S(1)} %pad_add_fusion.at_ref.refs_0_._, bf16[256,2048]{1,0:T(8,128)(2,1)S(1)} %bitcast.9, bf16[256,2048]{1,0:T(8,128)(2,1)S(1)} %collective-permute-done.3.refs_2_, bf16[256,2048]{1,0:T(8,128)(2,1)S(1)} %collective-permute-done.4.refs_3_, ...), custom_call_target="tpu_custom_call" | custom-call | flops 4000000000 | bytes 12000000 | tf_op jit(solution)/shard_map/project/pallas_call | solution.py:318
  38.4 4.3 %collective-permute-start.8 = (bf16[1024,256]{1,0:T(8,128)(2,1)}, bf16[1024,256]{1,0:T(8,128)(2,1)}, u32[]{:S(2)}, u32[]{:S(2)}) collective-permute-start(bf16[1024,256]{1,0:T(8,128)(2,1)} %get-tuple-element.62.refs_5_.refs_3_), channel_id=1, source_target_pairs={{0,8},{2,10},{4,12},{6,14},{8,16},{10,18},{12,20},{14,22},{16,24},... | collective-permute-start | bytes 1572872 | tf_op jit(solution)/shard_map/ppermute | solution.py:31
  42.7 1.5 place_rows.1
  44.3 1.3 copy-done.13
  46.4 1.3 collective-permute-start.7
  47.7 4.6 %collective-permute-start.12 = (bf16[1024,256]{1,0:T(8,128)(2,1)}, bf16[1024,256]{1,0:T(8,128)(2,1)S(1)}, u32[]{:S(2)}, u32[]{:S(2)}) collective-permute-start(bf16[1024,256]{1,0:T(8,128)(2,1)} %copy-done.16), channel_id=1, source_target_pairs={{0,8},{2,10},{4,12},{6,14},{8,16},{10,18},{12,20},{14,22},{16,24},... | collective-permute-start | bytes 1572872 | tf_op jit(solution)/shard_map/ppermute | solution.py:31
  52.3 1.3 collective-permute-start.11
  53.6 1.6 collective-permute-start.18
  55.2 1.2 turn.2.refs_5_
  56.5 7.0 %collective-permute-done.7.refs_2_ = bf16[2,1024,128]{2,1,0:T(8,128)(2,1)} collective-permute-done((bf16[2,1024,128]{2,1,0:T(8,128)(2,1)}, bf16[2,1024,128]{2,1,0:T(8,128)(2,1)}, u32[]{:S(2)}, u32[]{:S(2)}) %collective-permute-start.7) | collective-permute-done | bytes 524320 | tf_op jit(solution)/shard_map/ppermute | solution.py:31
  63.4 5.3 %softmax_stats.2 = (f32[8,1024]{1,0:T(8,128)S(1)}, f32[8,1024]{1,0:T(8,128)S(1)}) custom-call(s32[2]{0:T(128)S(1)} %pad_add_fusion.1.refs_0_, bf16[2,1024,128]{2,1,0:T(8,128)(2,1)} %get-tuple-element.63.refs_1_, bf16[2,1024,128]{2,1,0:T(8,128)(2,1)} %collective-permute-done.7.refs_2_, bf16[1024,256]{1,0:T(8,128)(2,1)} %get-tuple-element.62.refs_5_.refs_3_, ...), custom_call_target="tpu_custom_call" | custom-call | flops 4000000000 | bytes 12000000 | tf_op jit(solution)/shard_map/softmax_stats/pallas_call | solution.py:228
  69.6 1.3 collective-permute-start.9
  71.6 1.8 %collective-permute-done.11.refs_2_ = bf16[2,1024,128]{2,1,0:T(8,128)(2,1)S(1)} collective-permute-done((bf16[2,1024,128]{2,1,0:T(8,128)(2,1)}, bf16[2,1024,128]{2,1,0:T(8,128)(2,1)S(1)}, u32[]{:S(2)}, u32[]{:S(2)}) %collective-permute-start.11) | collective-permute-done | bytes 524320 | tf_op jit(solution)/shard_map/ppermute | solution.py:31
  73.3 3.9 %softmax_stats.3 = (f32[8,1024]{1,0:T(8,128)S(1)}, f32[8,1024]{1,0:T(8,128)S(1)}) custom-call(s32[2]{0:T(128)S(1)} %pad_add_fusion.1.refs_0_, bf16[2,1024,128]{2,1,0:T(8,128)(2,1)S(1)} %copy-done.19, bf16[2,1024,128]{2,1,0:T(8,128)(2,1)S(1)} %collective-permute-done.11.refs_2_, bf16[1024,256]{1,0:T(8,128)(2,1)S(1)} %copy-done.17, ...), custom_call_target="tpu_custom_call" | custom-call | flops 4000000000 | bytes 12000000 | tf_op jit(solution)/shard_map/softmax_stats/pallas_call | solution.py:228
  78.3 2.8 %collective-permute-start.14 = (f32[8,1024]{1,0:T(8,128)S(1)}, f32[8,1024]{1,0:T(8,128)S(1)}, u32[]{:S(2)}, u32[]{:S(2)}) collective-permute-start(f32[8,1024]{1,0:T(8,128)S(1)} %get-tuple-element.68.refs_10_.refs_6_.refs_11_), channel_id=1, source_target_pairs={{0,24},{2,26},{4,28},{6,30},{8,0},{10,2},{12,4},{14,6},{16,8},{18,... | collective-permute-start | bytes 98312 | tf_op jit(solution)/shard_map/ppermute | solution.py:37
  81.2 9.6 %attention_grads.2 = (f32[2,1024,128]{2,1,0:T(8,128)S(1)}, bf16[2,1024,128]{2,1,0:T(8,128)(2,1)S(1)}, bf16[1024,256]{1,0:T(8,128)(2,1)S(1)}, f32[1024,256]{1,0:T(8,128)S(1)}) custom-call(s32[2]{0:T(128)S(1)} %pad_add_fusion.1.refs_0_, bf16[2,1024,128]{2,1,0:T(8,128)(2,1)} %get-tuple-element.63.refs_1_, bf16[2,1024,128]{2,1,0:T(8,128)(2,1)} %collective-permute-done.7.refs_2_, ...), custom_call_target="tpu_custom_call" | custom-call | flops 8000000000 | bytes 24000000 | tf_op jit(solution)/shard_map/attention_grads/pallas_call | solution.py:228
  91.7 1.5 collective-permute-start.17
  93.2 9.4 %attention_grads.3 = (f32[2,1024,128]{2,1,0:T(8,128)S(1)}, bf16[2,1024,256]{2,1,0:T(8,128)(2,1)}, bf16[1024,256]{1,0:T(8,128)(2,1)}, f32[1024,256]{1,0:T(8,128)S(1)}) custom-call(s32[2]{0:T(128)S(1)} %pad_add_fusion.1.refs_0_, bf16[2,1024,128]{2,1,0:T(8,128)(2,1)S(1)} %copy-done.19, bf16[2,1024,128]{2,1,0:T(8,128)(2,1)S(1)} %collective-permute-done.11.refs_2_, ...), custom_call_target="tpu_custom_call" | custom-call | flops 8000000000 | bytes 24000000 | tf_op jit(solution)/shard_map/attention_grads/pallas_call | solution.py:228
  102.6 2.5 %collective-permute-done.17.refs_6_ = bf16[1024,256]{1,0:T(8,128)(2,1)S(1)} collective-permute-done((bf16[1024,256]{1,0:T(8,128)(2,1)S(1)}, bf16[1024,256]{1,0:T(8,128)(2,1)S(1)}, u32[]{:S(2)}, u32[]{:S(2)}) %collective-permute-start.17) | collective-permute-done | bytes 524320 | tf_op jit(solution)/shard_map/ppermute | solution.py:31
  105.2 2.9 %spread.2 = (bf16[256,256]{1,0:T(8,128)(2,1)S(1)}, bf16[256,256]{1,0:T(8,128)(2,1)S(1)}, bf16[2,256,256]{2,1,0:T(8,128)(2,1)S(1)}, f32[4,256,256]{2,1,0:T(8,128)...) custom-call(s32[3]{0:T(128)S(1)} %pad_add_fusion.at_ref.refs_0_._, ...), custom_call_target="tpu_custom_call", output_to_operand_aliasing={{5}: (8, {})} | custom-call | tf_op jit(solution)/shard_map/spread/pallas_call | solution.py:318
  109.7 1.5 collective-permute-start.19
  111.3 2.9 %collective-permute-start.15 = (bf16[2,1024,256]{2,1,0:T(8,128)(2,1)}, bf16[2,1024,256]{2,1,0:T(8,128)(2,1)}, u32[]{:S(2)}, u32[]{:S(2)}) collective-permute-start(bf16[2,1024,256]{2,1,0:T(8,128)(2,1)} %get-tuple-element.73), channel_id=1, source_target_pairs={{0,8},{2,10},{4,12},{6,14},{8,16},{10,18},{12,20},{14,22},{16,24},... | collective-permute-start | bytes 3145736 | tf_op jit(solution)/shard_map/ppermute | solution.py:31
  114.2 1.5 collective-permute-start.16
  115.9 8.5 %collective-permute-done.19.refs_2_ = bf16[4,256,256]{2,1,0:T(8,128)(2,1)} collective-permute-done((bf16[4,256,256]{2,1,0:T(8,128)(2,1)}, bf16[4,256,256]{2,1,0:T(8,128)(2,1)}, u32[]{:S(2)}, u32[]{:S(2)}) %collective-permute-start.19) | collective-permute-done | bytes 524320 | tf_op jit(solution)/shard_map/ppermute | solution.py:51
  124.4 1.2 copy-done.15
  125.6 1.1 merge.4
  126.7 3.4 %collective-permute-done.16.refs_6_ = bf16[1024,256]{1,0:T(8,128)(2,1)} collective-permute-done((bf16[1024,256]{1,0:T(8,128)(2,1)}, bf16[1024,256]{1,0:T(8,128)(2,1)}, u32[]{:S(2)}, u32[]{:S(2)}) %collective-permute-start.16) | collective-permute-done | bytes 524320 | tf_op jit(solution)/shard_map/ppermute | solution.py:31
  130.2 2.8 %spread.3 = (bf16[256,512]{1,0:T(8,128)(2,1)S(1)}, bf16[256,512]{1,0:T(8,128)(2,1)S(1)}, bf16[2,256,512]{2,1,0:T(8,128)(2,1)S(1)}, f32[4,256,256]{2,1,0:T(8,128)S(1)}, bf16[4,256,256]{2,1,0:T(8,128)(2,1)S(1)}) custom-call(s32[3]{0:T(128)S(1)} %pad_add_fusion.at_ref.refs_0_._, bf16[256,2048]{1,0:T(8,128)(2,1)S(1)} %bitcast.11, ...), custom_call_target="tpu_custom_call" | custom-call | tf_op jit(solution)/shard_map/spread/pallas_call | solution.py:318
  133.7 2.7 %collective-permute-done.15.refs_3_ = bf16[2,1024,256]{2,1,0:T(8,128)(2,1)} collective-permute-done((bf16[2,1024,256]{2,1,0:T(8,128)(2,1)}, bf16[2,1024,256]{2,1,0:T(8,128)(2,1)}, u32[]{:S(2)}, u32[]{:S(2)}) %collective-permute-start.15) | collective-permute-done | bytes 1048608 | tf_op jit(solution)/shard_map/ppermute | solution.py:31
  136.3 1.5 settle_outs.1
  138.5 1.6 collective-permute-start.23
  140.1 2.5 %collective-permute-start.27 = (bf16[2,256,256]{2,1,0:T(8,128)(2,1)S(1)}, bf16[2,256,256]{2,1,0:T(8,128)(2,1)S(1)}, u32[]{:S(2)}, u32[]{:S(2)}) collective-permute-start(bf16[2,256,256]{2,1,0:T(8,128)(2,1)S(1)} %get-tuple-element.84.refs_10_), channel_id=1, source_target_pairs={{0,8},{1,9},{2,10},{3,11},{4,12},{5,13},{6,14},{7,15},{8,0},{9,1},... | collective-permute-start | bytes 786440 | tf_op jit(solution)/shard_map/ppermute | solution.py:47
  142.6 4.9 %collective-permute-done.25.refs_2_ = bf16[4,256,256]{2,1,0:T(8,128)(2,1)S(1)} collective-permute-done((bf16[4,256,256]{2,1,0:T(8,128)(2,1)S(1)}, bf16[4,256,256]{2,1,0:T(8,128)(2,1)S(1)}, u32[]{:S(2)}, u32[]{:S(2)}) %collective-permute-start.25) | collective-permute-done | bytes 524320 | tf_op jit(solution)/shard_map/ppermute | solution.py:51
  149.9 3.5 %collective-permute-start.28 = (bf16[1,256,256]{2,1,0:T(8,128)(2,1)S(1)}, bf16[1,256,256]{2,1,0:T(8,128)(2,1)S(1)}, u32[]{:S(2)}, u32[]{:S(2)}) collective-permute-start(bf16[1,256,256]{2,1,0:T(8,128)(2,1)S(1)} %get-tuple-element.102), channel_id=1, source_target_pairs={{0,16},{1,17},{2,18},{3,19},{4,20},{5,21},{6,22},{7,23},{8,24},{9,... | collective-permute-start | bytes 393224 | tf_op jit(solution)/shard_map/ppermute | solution.py:47
  154.1 4.7 %collective-permute-done.26.refs_2_ = bf16[2,256,256]{2,1,0:T(8,128)(2,1)S(1)} collective-permute-done((bf16[2,256,256]{2,1,0:T(8,128)(2,1)S(1)}, bf16[2,256,256]{2,1,0:T(8,128)(2,1)S(1)}, u32[]{:S(2)}, u32[]{:S(2)}) %collective-permute-start.26) | collective-permute-done | bytes 262176 | tf_op jit(solution)/shard_map/ppermute | solution.py:47
  159.5 6.9 %feature_grads.1 = (bf16[1,256,2048]{2,1,0:T(8,128)(2,1)}, f32[8,128]{1,0:T(8,128)S(1)}) custom-call(s32[3]{0:T(128)S(1)} %pad_add_fusion.at_ref.refs_0_._, bf16[256,512]{1,0:T(8,128)(2,1)S(1)} %get-tuple-element.91.refs_1_, bf16[2,256,512]{2,1,0:T(8,128)(2,1)S(1)} %collective-permute-done.22.refs_2_, ...), custom_call_target="tpu_custom_call" | custom-call | flops 6000000000 | bytes 18000000 | tf_op jit(solution)/shard_map/feature_grads/pallas_call | solution.py:582
  167.1 1.6 collective-permute-start.31
  169.0 1.7 place_heads.1
  170.7 2.8 %collective-permute-done.31.refs_3_ = f32[64,512]{1,0:T(8,128)S(1)} collective-permute-done((f32[64,512]{1,0:T(8,128)S(1)}, f32[64,512]{1,0:T(8,128)S(1)}, u32[]{:S(2)}, u32[]{:S(2)}) %collective-permute-start.31) | collective-permute-done | bytes 131104 | tf_op jit(solution)/shard_map/ppermute | solution.py:24
  173.5 1.9 %collective-permute-done.32.refs_4_ = f32[64,512]{1,0:T(8,128)S(1)} collective-permute-done((f32[64,512]{1,0:T(8,128)S(1)}, f32[64,512]{1,0:T(8,128)S(1)}, u32[]{:S(2)}, u32[]{:S(2)}) %collective-permute-start.32) | collective-permute-done | bytes 131104 | tf_op jit(solution)/shard_map/ppermute | solution.py:24
  175.4 1.4 place_weight.1
  (92 shorter events, 15.7 us)
Async XLA Ops:
  0.6 26.4 %collective-permute-start.4 = (bf16[256,2048]{1,0:T(8,128)(2,1)}, bf16[256,2048]{1,0:T(8,128)(2,1)S(1)}, u32[]{:S(2)}, u32[]{:S(2)}) collective-permute-start(bf16[256,2048]{1,0:T(8,128)(2,1)} %bitcast.7), channel_id=1, source_target_pairs={{0,4},{2,6},{4,0},{6,2},{8,12},{10,14},{12,8},{14,10},{16,20},{18,... | collective-permute-start | bytes 3145736 | tf_op jit(solution)/shard_map/ppermute | solution.py:24
  3.6 26.3 %collective-permute-start.3 = (bf16[256,2048]{1,0:T(8,128)(2,1)}, bf16[256,2048]{1,0:T(8,128)(2,1)S(1)}, u32[]{:S(2)}, u32[]{:S(2)}) collective-permute-start(bf16[256,2048]{1,0:T(8,128)(2,1)} %bitcast.8), channel_id=1, source_target_pairs={{0,2},{2,0},{4,6},{6,4},{8,10},{10,8},{12,14},{14,12},{16,18},{18,... | collective-permute-start | bytes 3145736 | tf_op jit(solution)/shard_map/ppermute | solution.py:24
  8.0 21.3 %copy-start.1 = (bf16[1024,2048]{1,0:T(8,128)(2,1)S(1)}, bf16[1024,2048]{1,0:T(8,128)(2,1)}, u32[]{:S(2)}) copy-start(bf16[1024,2048]{1,0:T(8,128)(2,1)} %refs_4_.1) | copy-start | bytes 12582916
  9.1 25.6 %collective-permute-start.6 = (bf16[1024,512]{1,0:T(8,128)(2,1)S(1)}, bf16[1024,512]{1,0:T(8,128)(2,1)S(1)}, u32[]{:S(2)}, u32[]{:S(2)}) collective-permute-start(bf16[1024,512]{1,0:T(8,128)(2,1)S(1)} %get-tuple-element.61.refs_5_), channel_id=1, source_target_pairs={{0,1},{1,0},{2,3},{3,2},{4,5},{5,4},{6,7},{7,6},{8,9},{9,8},{10,11... | collective-permute-start | bytes 3145736 | tf_op jit(solution)/shard_map/ppermute | solution.py:51
  27.0 7.7 %collective-permute-start.5 = (bf16[256,2048]{1,0:T(8,128)(2,1)S(1)}, bf16[256,2048]{1,0:T(8,128)(2,1)S(1)}, u32[]{:S(2)}, u32[]{:S(2)}) collective-permute-start(bf16[256,2048]{1,0:T(8,128)(2,1)S(1)} %collective-permute-done.4.refs_3_), channel_id=1, source_target_pairs={{0,2},{2,0},{4,6},{6,4},{8,10},{10,8},{12,14},{14,12},{16,18},{18,... | collective-permute-start | bytes 3145736 | tf_op jit(solution)/shard_map/ppermute | solution.py:24
  27.0 15.7 %collective-permute-start = (bf16[2,256,256]{2,1,0:T(8,128)(2,1)S(1)}, bf16[2,256,256]{2,1,0:T(8,128)(2,1)S(1)}, u32[]{:S(2)}, u32[]{:S(2)}) collective-permute-start(bf16[2,256,256]{2,1,0:T(8,128)(2,1)S(1)} %get-tuple-element.58), channel_id=1, source_target_pairs={{0,2},{2,0},{4,6},{6,4},{8,10},{10,8},{12,14},{14,12},{16,18},{18,... | collective-permute-start | bytes 786440 | tf_op jit(solution)/shard_map/ppermute | solution.py:24
  27.5 7.2 %copy-start.3 = (bf16[1,256,2048]{2,1,0:T(8,128)(2,1)S(1)}, bf16[1,256,2048]{2,1,0:T(8,128)(2,1)}, u32[]{:S(2)}) copy-start(bf16[1,256,2048]{2,1,0:T(8,128)(2,1)} %param.4) | copy-start | bytes 3145732
  27.5 15.2 %collective-permute-start.1 = (bf16[2,256,256]{2,1,0:T(8,128)(2,1)S(1)}, bf16[2,256,256]{2,1,0:T(8,128)(2,1)S(1)}, u32[]{:S(2)}, u32[]{:S(2)}) collective-permute-start(bf16[2,256,256]{2,1,0:T(8,128)(2,1)S(1)} %get-tuple-element.59), channel_id=1, source_target_pairs={{0,4},{2,6},{4,0},{6,2},{8,12},{10,14},{12,8},{14,10},{16,20},{18,... | collective-permute-start | bytes 786440 | tf_op jit(solution)/shard_map/ppermute | solution.py:24
  30.0 12.8 %collective-permute-start.2 = (bf16[2,256,256]{2,1,0:T(8,128)(2,1)S(1)}, bf16[2,256,256]{2,1,0:T(8,128)(2,1)S(1)}, u32[]{:S(2)}, u32[]{:S(2)}) collective-permute-start(bf16[2,256,256]{2,1,0:T(8,128)(2,1)S(1)} %get-tuple-element.60), channel_id=1, source_target_pairs={{0,6},{2,4},{4,2},{6,0},{8,14},{10,12},{12,10},{14,8},{16,22},{18,... | collective-permute-start | bytes 786440 | tf_op jit(solution)/shard_map/ppermute | solution.py:24
  34.8 3.7 %copy-start.4 = (bf16[256,2048]{1,0:T(8,128)(2,1)}, bf16[256,2048]{1,0:T(8,128)(2,1)S(1)}, u32[]{:S(2)}) copy-start(bf16[256,2048]{1,0:T(8,128)(2,1)S(1)} %collective-permute-done.5.refs_4_) | copy-start | bytes 3145732
  38.4 5.8 %copy-start.16 = (bf16[1024,256]{1,0:T(8,128)(2,1)}, bf16[1024,256]{1,0:T(8,128)(2,1)S(1)}, u32[]{:S(2)}) copy-start(bf16[1024,256]{1,0:T(8,128)(2,1)S(1)} %get-tuple-element.67.refs_3_) | copy-start | bytes 1572868
  38.4 16.8 %collective-permute-start.8 = (bf16[1024,256]{1,0:T(8,128)(2,1)}, bf16[1024,256]{1,0:T(8,128)(2,1)}, u32[]{:S(2)}, u32[]{:S(2)}) collective-permute-start(bf16[1024,256]{1,0:T(8,128)(2,1)} %get-tuple-element.62.refs_5_.refs_3_), channel_id=1, source_target_pairs={{0,8},{2,10},{4,12},{6,14},{8,16},{10,18},{12,20},{14,22},{16,24},... | collective-permute-start | bytes 1572872 | tf_op jit(solution)/shard_map/ppermute | solution.py:31
  46.4 17.1 %collective-permute-start.7 = (bf16[2,1024,128]{2,1,0:T(8,128)(2,1)}, bf16[2,1024,128]{2,1,0:T(8,128)(2,1)}, u32[]{:S(2)}, u32[]{:S(2)}) collective-permute-start(bf16[2,1024,128]{2,1,0:T(8,128)(2,1)} %get-tuple-element.63.refs_1_), channel_id=1, source_target_pairs={{8,0},{10,2},{12,4},{14,6},{16,8},{18,10},{20,12},{22,14},{24,16},... | collective-permute-start | bytes 1572872 | tf_op jit(solution)/shard_map/ppermute | solution.py:31
  47.7 23.1 %collective-permute-start.12 = (bf16[1024,256]{1,0:T(8,128)(2,1)}, bf16[1024,256]{1,0:T(8,128)(2,1)S(1)}, u32[]{:S(2)}, u32[]{:S(2)}) collective-permute-start(bf16[1024,256]{1,0:T(8,128)(2,1)} %copy-done.16), channel_id=1, source_target_pairs={{0,8},{2,10},{4,12},{6,14},{8,16},{10,18},{12,20},{14,22},{16,24},... | collective-permute-start | bytes 1572872 | tf_op jit(solution)/shard_map/ppermute | solution.py:31
  52.3 21.0 %collective-permute-start.11 = (bf16[2,1024,128]{2,1,0:T(8,128)(2,1)}, bf16[2,1024,128]{2,1,0:T(8,128)(2,1)S(1)}, u32[]{:S(2)}, u32[]{:S(2)}) collective-permute-start(bf16[2,1024,128]{2,1,0:T(8,128)(2,1)} %copy-done.18), channel_id=1, source_target_pairs={{8,0},{10,2},{12,4},{14,6},{16,8},{18,10},{20,12},{22,14},{24,16},... | collective-permute-start | bytes 1572872 | tf_op jit(solution)/shard_map/ppermute | solution.py:31
  53.6 51.5 %collective-permute-start.18 = (bf16[512,2048]{1,0:T(8,128)(2,1)}, bf16[512,2048]{1,0:T(8,128)(2,1)}, u32[]{:S(2)}, u32[]{:S(2)}) collective-permute-start(bf16[512,2048]{1,0:T(8,128)(2,1)} %copy-done.13), channel_id=1, source_target_pairs={{0,1},{1,0},{2,3},{3,2},{4,5},{5,4},{6,7},{7,6},{8,9},{9,8},{10,11... | collective-permute-start | bytes 6291464 | tf_op jit(solution)/shard_map/ppermute | solution.py:51
  68.7 4.6 %copy-start.17 = (bf16[1024,256]{1,0:T(8,128)(2,1)S(1)}, bf16[1024,256]{1,0:T(8,128)(2,1)}, u32[]{:S(2)}) copy-start(bf16[1024,256]{1,0:T(8,128)(2,1)} %copy-done.16) | copy-start | bytes 1572868
  68.7 4.6 %copy-start.19 = (bf16[2,1024,128]{2,1,0:T(8,128)(2,1)S(1)}, bf16[2,1024,128]{2,1,0:T(8,128)(2,1)}, u32[]{:S(2)}) copy-start(bf16[2,1024,128]{2,1,0:T(8,128)(2,1)} %copy-done.18) | copy-start | bytes 1572868
  68.7 12.4 %collective-permute-start.10 = (f32[8,1024]{1,0:T(8,128)S(1)}, f32[8,1024]{1,0:T(8,128)S(1)}, u32[]{:S(2)}, u32[]{:S(2)}) collective-permute-start(f32[8,1024]{1,0:T(8,128)S(1)} %get-tuple-element.64.refs_6_), channel_id=1, source_target_pairs={{0,24},{2,26},{4,28},{6,30},{8,0},{10,2},{12,4},{14,6},{16,8},{18,... | collective-permute-start | bytes 98312 | tf_op jit(solution)/shard_map/ppermute | solution.py:37
  69.6 11.6 %collective-permute-start.9 = (f32[8,1024]{1,0:T(8,128)S(1)}, f32[8,1024]{1,0:T(8,128)S(1)}, u32[]{:S(2)}, u32[]{:S(2)}) collective-permute-start(f32[8,1024]{1,0:T(8,128)S(1)} %get-tuple-element.65.refs_8_), channel_id=1, source_target_pairs={{0,8},{2,10},{4,12},{6,14},{8,16},{10,18},{12,20},{14,22},{16,24},... | collective-permute-start | bytes 98312 | tf_op jit(solution)/shard_map/ppermute | solution.py:37
  77.3 15.9 %collective-permute-start.13 = (f32[8,1024]{1,0:T(8,128)S(1)}, f32[8,1024]{1,0:T(8,128)S(1)}, u32[]{:S(2)}, u32[]{:S(2)}) collective-permute-start(f32[8,1024]{1,0:T(8,128)S(1)} %get-tuple-element.70.refs_8_), channel_id=1, source_target_pairs={{0,8},{2,10},{4,12},{6,14},{8,16},{10,18},{12,20},{14,22},{16,24},... | collective-permute-start | bytes 98312 | tf_op jit(solution)/shard_map/ppermute | solution.py:37
  78.3 14.9 %collective-permute-start.14 = (f32[8,1024]{1,0:T(8,128)S(1)}, f32[8,1024]{1,0:T(8,128)S(1)}, u32[]{:S(2)}, u32[]{:S(2)}) collective-permute-start(f32[8,1024]{1,0:T(8,128)S(1)} %get-tuple-element.68.refs_10_.refs_6_.refs_11_), channel_id=1, source_target_pairs={{0,24},{2,26},{4,28},{6,30},{8,0},{10,2},{12,4},{14,6},{16,8},{18,... | collective-permute-start | bytes 98312 | tf_op jit(solution)/shard_map/ppermute | solution.py:37
  91.7 13.4 %collective-permute-start.17 = (bf16[1024,256]{1,0:T(8,128)(2,1)S(1)}, bf16[1024,256]{1,0:T(8,128)(2,1)S(1)}, u32[]{:S(2)}, u32[]{:S(2)}) collective-permute-start(bf16[1024,256]{1,0:T(8,128)(2,1)S(1)} %get-tuple-element.77), channel_id=1, source_target_pairs={{8,0},{10,2},{12,4},{14,6},{16,8},{18,10},{20,12},{22,14},{24,16},... | collective-permute-start | bytes 1572872 | tf_op jit(solution)/shard_map/ppermute | solution.py:31
  93.2 11.9 %copy-start.5 = (bf16[256,2048]{1,0:T(8,128)(2,1)S(1)}, bf16[256,2048]{1,0:T(8,128)(2,1)}, u32[]{:S(2)}) copy-start(bf16[256,2048]{1,0:T(8,128)(2,1)} %copy-done.4) | copy-start | bytes 3145732
  102.6 5.5 %copy-start.7 = (f32[1024,256]{1,0:T(8,128)}, f32[1024,256]{1,0:T(8,128)S(1)}, u32[]{:S(2)}) copy-start(f32[1024,256]{1,0:T(8,128)S(1)} %get-tuple-element.74.refs_7_.refs_5_) | copy-start | bytes 3145732
  102.6 5.5 %copy-start.22 = (f32[2,1024,128]{2,1,0:T(8,128)}, f32[2,1024,128]{2,1,0:T(8,128)S(1)}, u32[]{:S(2)}) copy-start(f32[2,1024,128]{2,1,0:T(8,128)S(1)} %get-tuple-element.72.refs_2_) | copy-start | bytes 3145732
  109.7 49.8 %collective-permute-start.24 = (bf16[512,2048]{1,0:T(8,128)(2,1)}, bf16[512,2048]{1,0:T(8,128)(2,1)}, u32[]{:S(2)}, u32[]{:S(2)}) collective-permute-start(bf16[512,2048]{1,0:T(8,128)(2,1)} %get-tuple-element.94.refs_5_), channel_id=1, source_target_pairs={{0,2},{2,0},{4,6},{6,4},{8,10},{10,8},{12,14},{14,12},{16,18},{18,... | collective-permute-start | bytes 6291464 | tf_op jit(solution)/shard_map/ppermute | solution.py:24
  109.7 14.7 %collective-permute-start.19 = (bf16[4,256,256]{2,1,0:T(8,128)(2,1)}, bf16[4,256,256]{2,1,0:T(8,128)(2,1)}, u32[]{:S(2)}, u32[]{:S(2)}) collective-permute-start(bf16[4,256,256]{2,1,0:T(8,128)(2,1)} %get-tuple-element.83), channel_id=1, source_target_pairs={{0,1},{1,0},{2,3},{3,2},{4,5},{5,4},{6,7},{7,6},{8,9},{9,8},{10,11... | collective-permute-start | bytes 1572872 | tf_op jit(solution)/shard_map/ppermute | solution.py:51
  111.3 25.1 %collective-permute-start.15 = (bf16[2,1024,256]{2,1,0:T(8,128)(2,1)}, bf16[2,1024,256]{2,1,0:T(8,128)(2,1)}, u32[]{:S(2)}, u32[]{:S(2)}) collective-permute-start(bf16[2,1024,256]{2,1,0:T(8,128)(2,1)} %get-tuple-element.73), channel_id=1, source_target_pairs={{0,8},{2,10},{4,12},{6,14},{8,16},{10,18},{12,20},{14,22},{16,24},... | collective-permute-start | bytes 3145736 | tf_op jit(solution)/shard_map/ppermute | solution.py:31
  114.2 16.0 %collective-permute-start.16 = (bf16[1024,256]{1,0:T(8,128)(2,1)}, bf16[1024,256]{1,0:T(8,128)(2,1)}, u32[]{:S(2)}, u32[]{:S(2)}) collective-permute-start(bf16[1024,256]{1,0:T(8,128)(2,1)} %get-tuple-element.75), channel_id=1, source_target_pairs={{8,0},{10,2},{12,4},{14,6},{16,8},{18,10},{20,12},{22,14},{24,16},... | collective-permute-start | bytes 1572872 | tf_op jit(solution)/shard_map/ppermute | solution.py:31
  115.8 14.4 %copy-start.6 = (bf16[256,2048]{1,0:T(8,128)(2,1)S(1)}, bf16[256,2048]{1,0:T(8,128)(2,1)}, u32[]{:S(2)}) copy-start(bf16[256,2048]{1,0:T(8,128)(2,1)} %copy-done.4) | copy-start | bytes 3145732
  115.8 14.4 %copy-start.8 = (f32[1024,256]{1,0:T(8,128)S(1)}, f32[1024,256]{1,0:T(8,128)}, u32[]{:S(2)}) copy-start(f32[1024,256]{1,0:T(8,128)} %copy-done.7) | copy-start | bytes 3145732
  115.8 14.4 %copy-start.12 = (bf16[256,256]{1,0:T(8,128)(2,1)S(1)}, bf16[256,256]{1,0:T(8,128)(2,1)}, u32[]{:S(2)}) copy-start(bf16[256,256]{1,0:T(8,128)(2,1)} %copy-done.11) | copy-start | bytes 393220
  130.2 6.2 %copy-start.21 = (f32[2,1024,128]{2,1,0:T(8,128)S(1)}, f32[2,1024,128]{2,1,0:T(8,128)}, u32[]{:S(2)}) copy-start(f32[2,1024,128]{2,1,0:T(8,128)} %copy-done.20) | copy-start | bytes 3145732
  130.2 6.2 %copy-start.23 = (f32[2,1024,128]{2,1,0:T(8,128)S(1)}, f32[2,1024,128]{2,1,0:T(8,128)}, u32[]{:S(2)}) copy-start(f32[2,1024,128]{2,1,0:T(8,128)} %copy-done.22) | copy-start | bytes 3145732
  133.0 4.9 %collective-permute-start.22 = (bf16[2,256,512]{2,1,0:T(8,128)(2,1)S(1)}, bf16[2,256,512]{2,1,0:T(8,128)(2,1)S(1)}, u32[]{:S(2)}, u32[]{:S(2)}) collective-permute-start(bf16[2,256,512]{2,1,0:T(8,128)(2,1)S(1)} %get-tuple-element.92), channel_id=1, source_target_pairs={{0,2},{2,0},{4,6},{6,4},{8,10},{10,8},{12,14},{14,12},{16,18},{18,... | collective-permute-start | bytes 1572872 | tf_op jit(solution)/shard_map/ppermute | solution.py:24
  133.1 14.3 %collective-permute-start.25 = (bf16[4,256,256]{2,1,0:T(8,128)(2,1)S(1)}, bf16[4,256,256]{2,1,0:T(8,128)(2,1)S(1)}, u32[]{:S(2)}, u32[]{:S(2)}) collective-permute-start(bf16[4,256,256]{2,1,0:T(8,128)(2,1)S(1)} %get-tuple-element.85.refs_4_), channel_id=1, source_target_pairs={{0,1},{1,0},{2,3},{3,2},{4,5},{5,4},{6,7},{7,6},{8,9},{9,8},{10,11... | collective-permute-start | bytes 1572872 | tf_op jit(solution)/shard_map/ppermute | solution.py:51
  137.8 15.6 %collective-permute-start.20 = (bf16[2,2,256,256]{3,2,1,0:T(8,128)(2,1)S(1)}, bf16[2,2,256,256]{3,2,1,0:T(8,128)(2,1)S(1)}, u32[]{:S(2)}, u32[]{:S(2)}) collective-permute-start(bf16[2,2,256,256]{3,2,1,0:T(8,128)(2,1)S(1)} %get-tuple-element.87), channel_id=1, source_target_pairs={{0,2},{2,0},{4,6},{6,4},{8,10},{10,8},{12,14},{14,12},{16,18},{18,... | collective-permute-start | bytes 1572872 | tf_op jit(solution)/shard_map/ppermute | solution.py:24
  138.5 20.3 %collective-permute-start.23 = (bf16[2,256,512]{2,1,0:T(8,128)(2,1)S(1)}, bf16[2,256,512]{2,1,0:T(8,128)(2,1)S(1)}, u32[]{:S(2)}, u32[]{:S(2)}) collective-permute-start(bf16[2,256,512]{2,1,0:T(8,128)(2,1)S(1)} %mix.3), channel_id=1, source_target_pairs={{0,4},{2,6},{4,0},{6,2},{8,12},{10,14},{12,8},{14,10},{16,20},{18,... | collective-permute-start | bytes 1572872 | tf_op jit(solution)/shard_map/ppermute | solution.py:24
  140.1 9.2 %collective-permute-start.27 = (bf16[2,256,256]{2,1,0:T(8,128)(2,1)S(1)}, bf16[2,256,256]{2,1,0:T(8,128)(2,1)S(1)}, u32[]{:S(2)}, u32[]{:S(2)}) collective-permute-start(bf16[2,256,256]{2,1,0:T(8,128)(2,1)S(1)} %get-tuple-element.84.refs_10_), channel_id=1, source_target_pairs={{0,8},{1,9},{2,10},{3,11},{4,12},{5,13},{6,14},{7,15},{8,0},{9,1},... | collective-permute-start | bytes 786440 | tf_op jit(solution)/shard_map/ppermute | solution.py:47
  148.1 10.7 %collective-permute-start.26 = (bf16[2,256,256]{2,1,0:T(8,128)(2,1)S(1)}, bf16[2,256,256]{2,1,0:T(8,128)(2,1)S(1)}, u32[]{:S(2)}, u32[]{:S(2)}) collective-permute-start(bf16[2,256,256]{2,1,0:T(8,128)(2,1)S(1)} %get-tuple-element.97), channel_id=1, source_target_pairs={{0,8},{1,9},{2,10},{3,11},{4,12},{5,13},{6,14},{7,15},{8,0},{9,1},... | collective-permute-start | bytes 786440 | tf_op jit(solution)/shard_map/ppermute | solution.py:47
  149.9 16.6 %collective-permute-start.28 = (bf16[1,256,256]{2,1,0:T(8,128)(2,1)S(1)}, bf16[1,256,256]{2,1,0:T(8,128)(2,1)S(1)}, u32[]{:S(2)}, u32[]{:S(2)}) collective-permute-start(bf16[1,256,256]{2,1,0:T(8,128)(2,1)S(1)} %get-tuple-element.102), channel_id=1, source_target_pairs={{0,16},{1,17},{2,18},{3,19},{4,20},{5,21},{6,22},{7,23},{8,24},{9,... | collective-permute-start | bytes 393224 | tf_op jit(solution)/shard_map/ppermute | solution.py:47
  153.4 6.1 %copy-start.2 = (bf16[1024,2048]{1,0:T(8,128)(2,1)S(1)}, bf16[1024,2048]{1,0:T(8,128)(2,1)}, u32[]{:S(2)}) copy-start(bf16[1024,2048]{1,0:T(8,128)(2,1)} %refs_4_.1) | copy-start | bytes 12582916
  154.0 15.0 %collective-permute-start.21 = (bf16[2,2,256,256]{3,2,1,0:T(8,128)(2,1)S(1)}, bf16[2,2,256,256]{3,2,1,0:T(8,128)(2,1)S(1)}, u32[]{:S(2)}, u32[]{:S(2)}) collective-permute-start(bf16[2,2,256,256]{3,2,1,0:T(8,128)(2,1)S(1)} %mix.2), channel_id=1, source_target_pairs={{0,4},{2,6},{4,0},{6,2},{8,12},{10,14},{12,8},{14,10},{16,20},{18,... | collective-permute-start | bytes 1572872 | tf_op jit(solution)/shard_map/ppermute | solution.py:24
  159.4 7.0 %collective-permute-start.29 = (bf16[1,256,256]{2,1,0:T(8,128)(2,1)S(1)}, bf16[1,256,256]{2,1,0:T(8,128)(2,1)S(1)}, u32[]{:S(2)}, u32[]{:S(2)}) collective-permute-start(bf16[1,256,256]{2,1,0:T(8,128)(2,1)S(1)} %get-tuple-element.98.refs_7_), channel_id=1, source_target_pairs={{0,16},{1,17},{2,18},{3,19},{4,20},{5,21},{6,22},{7,23},{8,24},{9,... | collective-permute-start | bytes 393224 | tf_op jit(solution)/shard_map/ppermute | solution.py:47
  167.1 3.6 %collective-permute-start.30 = (f32[64,512]{1,0:T(8,128)S(1)}, f32[64,512]{1,0:T(8,128)S(1)}, u32[]{:S(2)}, u32[]{:S(2)}) collective-permute-start(f32[64,512]{1,0:T(8,128)S(1)} %get-tuple-element.106), channel_id=1, source_target_pairs={{0,2},{2,0},{4,6},{6,4},{8,10},{10,8},{12,14},{14,12},{16,18},{18,... | collective-permute-start | bytes 393224 | tf_op jit(solution)/shard_map/ppermute | solution.py:24
  167.1 6.4 %collective-permute-start.31 = (f32[64,512]{1,0:T(8,128)S(1)}, f32[64,512]{1,0:T(8,128)S(1)}, u32[]{:S(2)}, u32[]{:S(2)}) collective-permute-start(f32[64,512]{1,0:T(8,128)S(1)} %get-tuple-element.107), channel_id=1, source_target_pairs={{0,4},{2,6},{4,0},{6,2},{8,12},{10,14},{12,8},{14,10},{16,20},{18,... | collective-permute-start | bytes 393224 | tf_op jit(solution)/shard_map/ppermute | solution.py:24
  168.7 6.7 %collective-permute-start.32 = (f32[64,512]{1,0:T(8,128)S(1)}, f32[64,512]{1,0:T(8,128)S(1)}, u32[]{:S(2)}, u32[]{:S(2)}) collective-permute-start(f32[64,512]{1,0:T(8,128)S(1)} %get-tuple-element.108), channel_id=1, source_target_pairs={{0,6},{2,4},{4,2},{6,0},{8,14},{10,12},{12,10},{14,8},{16,22},{18,... | collective-permute-start | bytes 393224 | tf_op jit(solution)/shard_map/ppermute | solution.py:24
  (9 other events, 10.2 us)

commit v7 on v6

--- a/solution.py
+++ b/solution.py
@@ -265,7 +265,7 @@
     return kernel_call(
         gradient_kernel, "attention_grads", at, own_pair, next_pair, kvs, (*stats, *earlier),
         [
-            jax.ShapeDtypeStruct((2, row_tokens, HEAD_DIM), jnp.float32),
+            jax.ShapeDtypeStruct((2, row_tokens, HEAD_DIM), low),
             jax.ShapeDtypeStruct((2, row_tokens, width), low),
             jax.ShapeDtypeStruct((row_tokens, 2 * HEAD_DIM), low),
             jax.ShapeDtypeStruct((row_tokens, 2 * HEAD_DIM), jnp.float32),
@@ -441,7 +441,8 @@
         rows = at_offset(at_ref[0] ^ bits, size)
         for head, own_out in enumerate(own_outs):
             column = slice(head * HEAD_DIM, (head + 1) * HEAD_DIM)
-            whole = own_out[:, rows] + arrived[:, rows, column].astype(jnp.float32)
+            whole = own_out[:, rows].astype(jnp.float32)
+            whole = whole + arrived[:, rows, column].astype(jnp.float32)
             out[:, :, column] = whole.astype(jnp.bfloat16)
 
 

time: 177 us -> 177 us (level)
  no operation moved by 1% of the time
where the time goes in v7:
time: 177 us
  waiting for transfers between devices  62.4 us (35%)
  Pallas kernels  58.9 us (33%)
  starting transfers between devices  43.9 us (25%)
  local copies, waits for them, and re-layouts  10.2 us (6%)
    pallas_call x4, Pallas kernels, kernel_call(): pl.pallas_call(ordered(functools.partial(kernel, blocks=blocks, size=size...  28.1 us
    pallas_call x16, Pallas kernels, small_call(): pl.pallas_call(ordered(kernel, len(operands), len(waits), len(out_shape),...  22.1 us
    ppermute x14, waiting for transfers between devices, exchanged(): lax.ppermute(value, 'seq', [(source, source ^ bits) for source in range(c...  21.1 us
    ppermute x4, waiting for transfers between devices, swapped(): return lax.ppermute(value, 'dp', [(0, 1), (1, 0)])  18 us
    ppermute x7, waiting for transfers between devices, shifted(): lax.ppermute(value, 'seq', [(source, source + steps) for source in range(...  17.5 us
    ppermute x7, starting transfers between devices, shifted(): lax.ppermute(value, 'seq', [(source, source + steps) for source in range(...  17.5 us
    unnamed x48, local copies, waits for them, and re-layouts  10.2 us
    ppermute x14, starting transfers between devices, exchanged(): lax.ppermute(value, 'seq', [(source, source ^ bits) for source in range(c...  9.1 us
  transfers between devices with their start and end apart: 33, of which 13 were waited for; matrix products, arithmetic and copies ran while one was open for 0% of the time, Pallas kernels for 31%

profile of v7, /device:TPU:0, one launch (start us, length us, event | category | flops | bytes accessed | tf_op | source)
XLA Modules:
  0.0 176.7 jit_solution(11395028068347234961)
XLA Ops:
  0.6 3.0 %collective-permute-start.4 = (bf16[256,2048]{1,0:T(8,128)(2,1)}, bf16[256,2048]{1,0:T(8,128)(2,1)S(1)}, u32[]{:S(2)}, u32[]{:S(2)}) collective-permute-start(bf16[256,2048]{1,0:T(8,128)(2,1)} %bitcast.7), channel_id=1, source_target_pairs={{0,4},{2,6},{4,0},{6,2},{8,12},{10,14},{12,8},{14,10},{16,20},{18,... | collective-permute-start | bytes 3145736 | tf_op jit(solution)/shard_map/ppermute | solution.py:24
  3.7 2.2 %copy-done = bf16[1024,2048]{1,0:T(8,128)(2,1)S(1)} copy-done((bf16[1024,2048]{1,0:T(8,128)(2,1)S(1)}, bf16[1024,2048]{1,0:T(8,128)(2,1)}, u32[]{:S(2)}) %copy-start) | copy-done | bytes 4194328
  9.1 1.6 collective-permute-start.6
  10.7 16.3 %collective-permute-done.4.refs_3_ = bf16[256,2048]{1,0:T(8,128)(2,1)S(1)} collective-permute-done((bf16[256,2048]{1,0:T(8,128)(2,1)}, bf16[256,2048]{1,0:T(8,128)(2,1)S(1)}, u32[]{:S(2)}, u32[]{:S(2)}) %collective-permute-start.4) | collective-permute-done | bytes 1048608 | tf_op jit(solution)/shard_map/ppermute | solution.py:24
  27.5 1.7 collective-permute-start.1
  30.0 4.7 %collective-permute-done.6.refs_6_ = bf16[1024,512]{1,0:T(8,128)(2,1)S(1)} collective-permute-done((bf16[1024,512]{1,0:T(8,128)(2,1)S(1)}, bf16[1024,512]{1,0:T(8,128)(2,1)S(1)}, u32[]{:S(2)}, u32[]{:S(2)}) %collective-permute-start.6) | collective-permute-done | bytes 1048608 | tf_op jit(solution)/shard_map/ppermute | solution.py:51
  34.8 3.7 %project.1 = (bf16[1024,256]{1,0:T(8,128)(2,1)}, bf16[1024,256]{1,0:T(8,128)(2,1)S(1)}) custom-call(s32[3]{0:T(128)S(1)} %pad_add_fusion.at_ref.refs_0_._, bf16[256,2048]{1,0:T(8,128)(2,1)S(1)} %bitcast.9, bf16[256,2048]{1,0:T(8,128)(2,1)S(1)} %collective-permute-done.3.refs_2_, bf16[256,2048]{1,0:T(8,128)(2,1)S(1)} %collective-permute-done.4.refs_3_, ...), custom_call_target="tpu_custom_call" | custom-call | flops 4000000000 | bytes 12000000 | tf_op jit(solution)/shard_map/project/pallas_call | solution.py:318
  38.4 4.3 %collective-permute-start.8 = (bf16[1024,256]{1,0:T(8,128)(2,1)}, bf16[1024,256]{1,0:T(8,128)(2,1)}, u32[]{:S(2)}, u32[]{:S(2)}) collective-permute-start(bf16[1024,256]{1,0:T(8,128)(2,1)} %get-tuple-element.62.refs_5_.refs_3_), channel_id=1, source_target_pairs={{0,8},{2,10},{4,12},{6,14},{8,16},{10,18},{12,20},{14,22},{16,24},... | collective-permute-start | bytes 1572872 | tf_op jit(solution)/shard_map/ppermute | solution.py:31
  42.7 1.5 place_rows.1
  44.3 1.3 copy-done.13
  46.4 1.3 collective-permute-start.7
  47.7 4.6 %collective-permute-start.12 = (bf16[1024,256]{1,0:T(8,128)(2,1)}, bf16[1024,256]{1,0:T(8,128)(2,1)S(1)}, u32[]{:S(2)}, u32[]{:S(2)}) collective-permute-start(bf16[1024,256]{1,0:T(8,128)(2,1)} %copy-done.16), channel_id=1, source_target_pairs={{0,8},{2,10},{4,12},{6,14},{8,16},{10,18},{12,20},{14,22},{16,24},... | collective-permute-start | bytes 1572872 | tf_op jit(solution)/shard_map/ppermute | solution.py:31
  52.3 1.3 collective-permute-start.11
  53.6 1.6 collective-permute-start.18
  55.2 1.2 turn.2.refs_5_
  56.5 7.0 %collective-permute-done.7.refs_2_ = bf16[2,1024,128]{2,1,0:T(8,128)(2,1)} collective-permute-done((bf16[2,1024,128]{2,1,0:T(8,128)(2,1)}, bf16[2,1024,128]{2,1,0:T(8,128)(2,1)}, u32[]{:S(2)}, u32[]{:S(2)}) %collective-permute-start.7) | collective-permute-done | bytes 524320 | tf_op jit(solution)/shard_map/ppermute | solution.py:31
  63.4 5.3 %softmax_stats.2 = (f32[8,1024]{1,0:T(8,128)S(1)}, f32[8,1024]{1,0:T(8,128)S(1)}) custom-call(s32[2]{0:T(128)S(1)} %pad_add_fusion.1.refs_0_, bf16[2,1024,128]{2,1,0:T(8,128)(2,1)} %get-tuple-element.63.refs_1_, bf16[2,1024,128]{2,1,0:T(8,128)(2,1)} %collective-permute-done.7.refs_2_, bf16[1024,256]{1,0:T(8,128)(2,1)} %get-tuple-element.62.refs_5_.refs_3_, ...), custom_call_target="tpu_custom_call" | custom-call | flops 4000000000 | bytes 12000000 | tf_op jit(solution)/shard_map/softmax_stats/pallas_call | solution.py:228
  69.6 1.3 collective-permute-start.9
  71.6 1.8 %collective-permute-done.11.refs_2_ = bf16[2,1024,128]{2,1,0:T(8,128)(2,1)S(1)} collective-permute-done((bf16[2,1024,128]{2,1,0:T(8,128)(2,1)}, bf16[2,1024,128]{2,1,0:T(8,128)(2,1)S(1)}, u32[]{:S(2)}, u32[]{:S(2)}) %collective-permute-start.11) | collective-permute-done | bytes 524320 | tf_op jit(solution)/shard_map/ppermute | solution.py:31
  73.3 3.9 %softmax_stats.3 = (f32[8,1024]{1,0:T(8,128)S(1)}, f32[8,1024]{1,0:T(8,128)S(1)}) custom-call(s32[2]{0:T(128)S(1)} %pad_add_fusion.1.refs_0_, bf16[2,1024,128]{2,1,0:T(8,128)(2,1)S(1)} %copy-done.19, bf16[2,1024,128]{2,1,0:T(8,128)(2,1)S(1)} %collective-permute-done.11.refs_2_, bf16[1024,256]{1,0:T(8,128)(2,1)S(1)} %copy-done.17, ...), custom_call_target="tpu_custom_call" | custom-call | flops 4000000000 | bytes 12000000 | tf_op jit(solution)/shard_map/softmax_stats/pallas_call | solution.py:228
  78.3 2.8 %collective-permute-start.14 = (f32[8,1024]{1,0:T(8,128)S(1)}, f32[8,1024]{1,0:T(8,128)S(1)}, u32[]{:S(2)}, u32[]{:S(2)}) collective-permute-start(f32[8,1024]{1,0:T(8,128)S(1)} %get-tuple-element.68.refs_10_.refs_6_.refs_11_), channel_id=1, source_target_pairs={{0,24},{2,26},{4,28},{6,30},{8,0},{10,2},{12,4},{14,6},{16,8},{18,... | collective-permute-start | bytes 98312 | tf_op jit(solution)/shard_map/ppermute | solution.py:37
  81.2 9.6 %attention_grads.2 = (bf16[2,1024,128]{2,1,0:T(8,128)(2,1)S(1)}, bf16[2,1024,128]{2,1,0:T(8,128)(2,1)S(1)}, bf16[1024,256]{1,0:T(8,128)(2,1)S(1)}, f32[1024,256]{1,0:T(8,128)S(1)}) custom-call(s32[2]{0:T(128)S(1)} %pad_add_fusion.1.refs_0_, bf16[2,1024,128]{2,1,0:T(8,128)(2,1)} %get-tuple-element.63.refs_1_, ...), custom_call_target="tpu_custom_call" | custom-call | flops 8000000000 | bytes 24000000 | tf_op jit(solution)/shard_map/attention_grads/pallas_call | solution.py:228
  91.5 1.5 collective-permute-start.17
  93.1 9.3 %attention_grads.3 = (bf16[2,1024,128]{2,1,0:T(8,128)(2,1)S(1)}, bf16[2,1024,256]{2,1,0:T(8,128)(2,1)}, bf16[1024,256]{1,0:T(8,128)(2,1)}, f32[1024,256]{1,0:T(8,128)S(1)}) custom-call(s32[2]{0:T(128)S(1)} %pad_add_fusion.1.refs_0_, bf16[2,1024,128]{2,1,0:T(8,128)(2,1)S(1)} %copy-done.19, bf16[2,1024,128]{2,1,0:T(8,128)(2,1)S(1)} %collective-permute-done.11.refs_2_, ...), custom_call_target="tpu_custom_call" | custom-call | flops 8000000000 | bytes 24000000 | tf_op jit(solution)/shard_map/attention_grads/pallas_call | solution.py:228
  102.4 2.6 %collective-permute-done.17.refs_6_ = bf16[1024,256]{1,0:T(8,128)(2,1)S(1)} collective-permute-done((bf16[1024,256]{1,0:T(8,128)(2,1)S(1)}, bf16[1024,256]{1,0:T(8,128)(2,1)S(1)}, u32[]{:S(2)}, u32[]{:S(2)}) %collective-permute-start.17) | collective-permute-done | bytes 524320 | tf_op jit(solution)/shard_map/ppermute | solution.py:31
  105.0 2.9 %spread.2 = (bf16[256,256]{1,0:T(8,128)(2,1)S(1)}, bf16[256,256]{1,0:T(8,128)(2,1)S(1)}, bf16[2,256,256]{2,1,0:T(8,128)(2,1)S(1)}, f32[4,256,256]{2,1,0:T(8,128)...) custom-call(s32[3]{0:T(128)S(1)} %pad_add_fusion.at_ref.refs_0_._, ...), custom_call_target="tpu_custom_call", output_to_operand_aliasing={{5}: (8, {})} | custom-call | tf_op jit(solution)/shard_map/spread/pallas_call | solution.py:318
  109.6 1.5 collective-permute-start.19
  111.2 3.0 %collective-permute-start.15 = (bf16[2,1024,256]{2,1,0:T(8,128)(2,1)}, bf16[2,1024,256]{2,1,0:T(8,128)(2,1)}, u32[]{:S(2)}, u32[]{:S(2)}) collective-permute-start(bf16[2,1024,256]{2,1,0:T(8,128)(2,1)} %get-tuple-element.73), channel_id=1, source_target_pairs={{0,8},{2,10},{4,12},{6,14},{8,16},{10,18},{12,20},{14,22},{16,24},... | collective-permute-start | bytes 3145736 | tf_op jit(solution)/shard_map/ppermute | solution.py:31
  114.1 1.5 collective-permute-start.16
  115.8 8.5 %collective-permute-done.19.refs_2_ = bf16[4,256,256]{2,1,0:T(8,128)(2,1)} collective-permute-done((bf16[4,256,256]{2,1,0:T(8,128)(2,1)}, bf16[4,256,256]{2,1,0:T(8,128)(2,1)}, u32[]{:S(2)}, u32[]{:S(2)}) %collective-permute-start.19) | collective-permute-done | bytes 524320 | tf_op jit(solution)/shard_map/ppermute | solution.py:51
  124.3 1.2 copy-done.15
  125.5 1.1 merge.4
  126.7 3.4 %collective-permute-done.16.refs_6_ = bf16[1024,256]{1,0:T(8,128)(2,1)} collective-permute-done((bf16[1024,256]{1,0:T(8,128)(2,1)}, bf16[1024,256]{1,0:T(8,128)(2,1)}, u32[]{:S(2)}, u32[]{:S(2)}) %collective-permute-start.16) | collective-permute-done | bytes 524320 | tf_op jit(solution)/shard_map/ppermute | solution.py:31
  130.1 2.7 %spread.3 = (bf16[256,512]{1,0:T(8,128)(2,1)S(1)}, bf16[256,512]{1,0:T(8,128)(2,1)S(1)}, bf16[2,256,512]{2,1,0:T(8,128)(2,1)S(1)}, f32[4,256,256]{2,1,0:T(8,128)S(1)}, bf16[4,256,256]{2,1,0:T(8,128)(2,1)S(1)}) custom-call(s32[3]{0:T(128)S(1)} %pad_add_fusion.at_ref.refs_0_._, bf16[256,2048]{1,0:T(8,128)(2,1)S(1)} %bitcast.11, ...), custom_call_target="tpu_custom_call" | custom-call | tf_op jit(solution)/shard_map/spread/pallas_call | solution.py:318
  133.5 2.7 %collective-permute-done.15.refs_3_ = bf16[2,1024,256]{2,1,0:T(8,128)(2,1)} collective-permute-done((bf16[2,1024,256]{2,1,0:T(8,128)(2,1)}, bf16[2,1024,256]{2,1,0:T(8,128)(2,1)}, u32[]{:S(2)}, u32[]{:S(2)}) %collective-permute-start.15) | collective-permute-done | bytes 1048608 | tf_op jit(solution)/shard_map/ppermute | solution.py:31
  136.2 1.5 settle_outs.1
  138.4 1.6 collective-permute-start.23
  140.1 2.5 %collective-permute-start.27 = (bf16[2,256,256]{2,1,0:T(8,128)(2,1)S(1)}, bf16[2,256,256]{2,1,0:T(8,128)(2,1)S(1)}, u32[]{:S(2)}, u32[]{:S(2)}) collective-permute-start(bf16[2,256,256]{2,1,0:T(8,128)(2,1)S(1)} %get-tuple-element.84.refs_10_), channel_id=1, source_target_pairs={{0,8},{1,9},{2,10},{3,11},{4,12},{5,13},{6,14},{7,15},{8,0},{9,1},... | collective-permute-start | bytes 786440 | tf_op jit(solution)/shard_map/ppermute | solution.py:47
  142.5 4.8 %collective-permute-done.25.refs_2_ = bf16[4,256,256]{2,1,0:T(8,128)(2,1)S(1)} collective-permute-done((bf16[4,256,256]{2,1,0:T(8,128)(2,1)S(1)}, bf16[4,256,256]{2,1,0:T(8,128)(2,1)S(1)}, u32[]{:S(2)}, u32[]{:S(2)}) %collective-permute-start.25) | collective-permute-done | bytes 524320 | tf_op jit(solution)/shard_map/ppermute | solution.py:51
  148.0 1.2 collective-permute-done.27.refs_2_
  149.8 3.5 %collective-permute-start.28 = (bf16[1,256,256]{2,1,0:T(8,128)(2,1)S(1)}, bf16[1,256,256]{2,1,0:T(8,128)(2,1)S(1)}, u32[]{:S(2)}, u32[]{:S(2)}) collective-permute-start(bf16[1,256,256]{2,1,0:T(8,128)(2,1)S(1)} %get-tuple-element.102), channel_id=1, source_target_pairs={{0,16},{1,17},{2,18},{3,19},{4,20},{5,21},{6,22},{7,23},{8,24},{9,... | collective-permute-start | bytes 393224 | tf_op jit(solution)/shard_map/ppermute | solution.py:47
  154.0 4.7 %collective-permute-done.26.refs_2_ = bf16[2,256,256]{2,1,0:T(8,128)(2,1)S(1)} collective-permute-done((bf16[2,256,256]{2,1,0:T(8,128)(2,1)S(1)}, bf16[2,256,256]{2,1,0:T(8,128)(2,1)S(1)}, u32[]{:S(2)}, u32[]{:S(2)}) %collective-permute-start.26) | collective-permute-done | bytes 262176 | tf_op jit(solution)/shard_map/ppermute | solution.py:47
  159.4 6.9 %feature_grads.1 = (bf16[1,256,2048]{2,1,0:T(8,128)(2,1)}, f32[8,128]{1,0:T(8,128)S(1)}) custom-call(s32[3]{0:T(128)S(1)} %pad_add_fusion.at_ref.refs_0_._, bf16[256,512]{1,0:T(8,128)(2,1)S(1)} %get-tuple-element.91.refs_1_, bf16[2,256,512]{2,1,0:T(8,128)(2,1)S(1)} %collective-permute-done.22.refs_2_, ...), custom_call_target="tpu_custom_call" | custom-call | flops 6000000000 | bytes 18000000 | tf_op jit(solution)/shard_map/feature_grads/pallas_call | solution.py:583
  167.0 1.6 collective-permute-start.31
  168.9 1.7 place_heads.1
  170.5 2.8 %collective-permute-done.31.refs_3_ = f32[64,512]{1,0:T(8,128)S(1)} collective-permute-done((f32[64,512]{1,0:T(8,128)S(1)}, f32[64,512]{1,0:T(8,128)S(1)}, u32[]{:S(2)}, u32[]{:S(2)}) %collective-permute-start.31) | collective-permute-done | bytes 131104 | tf_op jit(solution)/shard_map/ppermute | solution.py:24
  173.4 1.9 %collective-permute-done.32.refs_4_ = f32[64,512]{1,0:T(8,128)S(1)} collective-permute-done((f32[64,512]{1,0:T(8,128)S(1)}, f32[64,512]{1,0:T(8,128)S(1)}, u32[]{:S(2)}, u32[]{:S(2)}) %collective-permute-start.32) | collective-permute-done | bytes 131104 | tf_op jit(solution)/shard_map/ppermute | solution.py:24
  175.3 1.4 place_weight.1
  (92 shorter events, 15.5 us)
Async XLA Ops:
  0.6 26.4 %collective-permute-start.4 = (bf16[256,2048]{1,0:T(8,128)(2,1)}, bf16[256,2048]{1,0:T(8,128)(2,1)S(1)}, u32[]{:S(2)}, u32[]{:S(2)}) collective-permute-start(bf16[256,2048]{1,0:T(8,128)(2,1)} %bitcast.7), channel_id=1, source_target_pairs={{0,4},{2,6},{4,0},{6,2},{8,12},{10,14},{12,8},{14,10},{16,20},{18,... | collective-permute-start | bytes 3145736 | tf_op jit(solution)/shard_map/ppermute | solution.py:24
  3.6 26.3 %collective-permute-start.3 = (bf16[256,2048]{1,0:T(8,128)(2,1)}, bf16[256,2048]{1,0:T(8,128)(2,1)S(1)}, u32[]{:S(2)}, u32[]{:S(2)}) collective-permute-start(bf16[256,2048]{1,0:T(8,128)(2,1)} %bitcast.8), channel_id=1, source_target_pairs={{0,2},{2,0},{4,6},{6,4},{8,10},{10,8},{12,14},{14,12},{16,18},{18,... | collective-permute-start | bytes 3145736 | tf_op jit(solution)/shard_map/ppermute | solution.py:24
  8.0 21.3 %copy-start.1 = (bf16[1024,2048]{1,0:T(8,128)(2,1)S(1)}, bf16[1024,2048]{1,0:T(8,128)(2,1)}, u32[]{:S(2)}) copy-start(bf16[1024,2048]{1,0:T(8,128)(2,1)} %refs_4_.1) | copy-start | bytes 12582916
  9.1 25.6 %collective-permute-start.6 = (bf16[1024,512]{1,0:T(8,128)(2,1)S(1)}, bf16[1024,512]{1,0:T(8,128)(2,1)S(1)}, u32[]{:S(2)}, u32[]{:S(2)}) collective-permute-start(bf16[1024,512]{1,0:T(8,128)(2,1)S(1)} %get-tuple-element.61.refs_5_), channel_id=1, source_target_pairs={{0,1},{1,0},{2,3},{3,2},{4,5},{5,4},{6,7},{7,6},{8,9},{9,8},{10,11... | collective-permute-start | bytes 3145736 | tf_op jit(solution)/shard_map/ppermute | solution.py:51
  27.0 7.7 %collective-permute-start.5 = (bf16[256,2048]{1,0:T(8,128)(2,1)S(1)}, bf16[256,2048]{1,0:T(8,128)(2,1)S(1)}, u32[]{:S(2)}, u32[]{:S(2)}) collective-permute-start(bf16[256,2048]{1,0:T(8,128)(2,1)S(1)} %collective-permute-done.4.refs_3_), channel_id=1, source_target_pairs={{0,2},{2,0},{4,6},{6,4},{8,10},{10,8},{12,14},{14,12},{16,18},{18,... | collective-permute-start | bytes 3145736 | tf_op jit(solution)/shard_map/ppermute | solution.py:24
  27.0 15.7 %collective-permute-start = (bf16[2,256,256]{2,1,0:T(8,128)(2,1)S(1)}, bf16[2,256,256]{2,1,0:T(8,128)(2,1)S(1)}, u32[]{:S(2)}, u32[]{:S(2)}) collective-permute-start(bf16[2,256,256]{2,1,0:T(8,128)(2,1)S(1)} %get-tuple-element.58), channel_id=1, source_target_pairs={{0,2},{2,0},{4,6},{6,4},{8,10},{10,8},{12,14},{14,12},{16,18},{18,... | collective-permute-start | bytes 786440 | tf_op jit(solution)/shard_map/ppermute | solution.py:24
  27.5 7.2 %copy-start.3 = (bf16[1,256,2048]{2,1,0:T(8,128)(2,1)S(1)}, bf16[1,256,2048]{2,1,0:T(8,128)(2,1)}, u32[]{:S(2)}) copy-start(bf16[1,256,2048]{2,1,0:T(8,128)(2,1)} %param.4) | copy-start | bytes 3145732
  27.5 15.2 %collective-permute-start.1 = (bf16[2,256,256]{2,1,0:T(8,128)(2,1)S(1)}, bf16[2,256,256]{2,1,0:T(8,128)(2,1)S(1)}, u32[]{:S(2)}, u32[]{:S(2)}) collective-permute-start(bf16[2,256,256]{2,1,0:T(8,128)(2,1)S(1)} %get-tuple-element.59), channel_id=1, source_target_pairs={{0,4},{2,6},{4,0},{6,2},{8,12},{10,14},{12,8},{14,10},{16,20},{18,... | collective-permute-start | bytes 786440 | tf_op jit(solution)/shard_map/ppermute | solution.py:24
  30.0 12.8 %collective-permute-start.2 = (bf16[2,256,256]{2,1,0:T(8,128)(2,1)S(1)}, bf16[2,256,256]{2,1,0:T(8,128)(2,1)S(1)}, u32[]{:S(2)}, u32[]{:S(2)}) collective-permute-start(bf16[2,256,256]{2,1,0:T(8,128)(2,1)S(1)} %get-tuple-element.60), channel_id=1, source_target_pairs={{0,6},{2,4},{4,2},{6,0},{8,14},{10,12},{12,10},{14,8},{16,22},{18,... | collective-permute-start | bytes 786440 | tf_op jit(solution)/shard_map/ppermute | solution.py:24
  34.8 3.7 %copy-start.4 = (bf16[256,2048]{1,0:T(8,128)(2,1)}, bf16[256,2048]{1,0:T(8,128)(2,1)S(1)}, u32[]{:S(2)}) copy-start(bf16[256,2048]{1,0:T(8,128)(2,1)S(1)} %collective-permute-done.5.refs_4_) | copy-start | bytes 3145732
  38.4 5.8 %copy-start.16 = (bf16[1024,256]{1,0:T(8,128)(2,1)}, bf16[1024,256]{1,0:T(8,128)(2,1)S(1)}, u32[]{:S(2)}) copy-start(bf16[1024,256]{1,0:T(8,128)(2,1)S(1)} %get-tuple-element.67.refs_3_) | copy-start | bytes 1572868
  38.4 16.8 %collective-permute-start.8 = (bf16[1024,256]{1,0:T(8,128)(2,1)}, bf16[1024,256]{1,0:T(8,128)(2,1)}, u32[]{:S(2)}, u32[]{:S(2)}) collective-permute-start(bf16[1024,256]{1,0:T(8,128)(2,1)} %get-tuple-element.62.refs_5_.refs_3_), channel_id=1, source_target_pairs={{0,8},{2,10},{4,12},{6,14},{8,16},{10,18},{12,20},{14,22},{16,24},... | collective-permute-start | bytes 1572872 | tf_op jit(solution)/shard_map/ppermute | solution.py:31
  46.4 17.1 %collective-permute-start.7 = (bf16[2,1024,128]{2,1,0:T(8,128)(2,1)}, bf16[2,1024,128]{2,1,0:T(8,128)(2,1)}, u32[]{:S(2)}, u32[]{:S(2)}) collective-permute-start(bf16[2,1024,128]{2,1,0:T(8,128)(2,1)} %get-tuple-element.63.refs_1_), channel_id=1, source_target_pairs={{8,0},{10,2},{12,4},{14,6},{16,8},{18,10},{20,12},{22,14},{24,16},... | collective-permute-start | bytes 1572872 | tf_op jit(solution)/shard_map/ppermute | solution.py:31
  47.7 23.1 %collective-permute-start.12 = (bf16[1024,256]{1,0:T(8,128)(2,1)}, bf16[1024,256]{1,0:T(8,128)(2,1)S(1)}, u32[]{:S(2)}, u32[]{:S(2)}) collective-permute-start(bf16[1024,256]{1,0:T(8,128)(2,1)} %copy-done.16), channel_id=1, source_target_pairs={{0,8},{2,10},{4,12},{6,14},{8,16},{10,18},{12,20},{14,22},{16,24},... | collective-permute-start | bytes 1572872 | tf_op jit(solution)/shard_map/ppermute | solution.py:31
  52.3 21.0 %collective-permute-start.11 = (bf16[2,1024,128]{2,1,0:T(8,128)(2,1)}, bf16[2,1024,128]{2,1,0:T(8,128)(2,1)S(1)}, u32[]{:S(2)}, u32[]{:S(2)}) collective-permute-start(bf16[2,1024,128]{2,1,0:T(8,128)(2,1)} %copy-done.18), channel_id=1, source_target_pairs={{8,0},{10,2},{12,4},{14,6},{16,8},{18,10},{20,12},{22,14},{24,16},... | collective-permute-start | bytes 1572872 | tf_op jit(solution)/shard_map/ppermute | solution.py:31
  53.6 51.3 %collective-permute-start.18 = (bf16[512,2048]{1,0:T(8,128)(2,1)}, bf16[512,2048]{1,0:T(8,128)(2,1)}, u32[]{:S(2)}, u32[]{:S(2)}) collective-permute-start(bf16[512,2048]{1,0:T(8,128)(2,1)} %copy-done.13), channel_id=1, source_target_pairs={{0,1},{1,0},{2,3},{3,2},{4,5},{5,4},{6,7},{7,6},{8,9},{9,8},{10,11... | collective-permute-start | bytes 6291464 | tf_op jit(solution)/shard_map/ppermute | solution.py:51
  68.7 4.6 %copy-start.17 = (bf16[1024,256]{1,0:T(8,128)(2,1)S(1)}, bf16[1024,256]{1,0:T(8,128)(2,1)}, u32[]{:S(2)}) copy-start(bf16[1024,256]{1,0:T(8,128)(2,1)} %copy-done.16) | copy-start | bytes 1572868
  68.7 4.6 %copy-start.19 = (bf16[2,1024,128]{2,1,0:T(8,128)(2,1)S(1)}, bf16[2,1024,128]{2,1,0:T(8,128)(2,1)}, u32[]{:S(2)}) copy-start(bf16[2,1024,128]{2,1,0:T(8,128)(2,1)} %copy-done.18) | copy-start | bytes 1572868
  68.7 12.4 %collective-permute-start.10 = (f32[8,1024]{1,0:T(8,128)S(1)}, f32[8,1024]{1,0:T(8,128)S(1)}, u32[]{:S(2)}, u32[]{:S(2)}) collective-permute-start(f32[8,1024]{1,0:T(8,128)S(1)} %get-tuple-element.64.refs_6_), channel_id=1, source_target_pairs={{0,24},{2,26},{4,28},{6,30},{8,0},{10,2},{12,4},{14,6},{16,8},{18,... | collective-permute-start | bytes 98312 | tf_op jit(solution)/shard_map/ppermute | solution.py:37
  69.6 11.6 %collective-permute-start.9 = (f32[8,1024]{1,0:T(8,128)S(1)}, f32[8,1024]{1,0:T(8,128)S(1)}, u32[]{:S(2)}, u32[]{:S(2)}) collective-permute-start(f32[8,1024]{1,0:T(8,128)S(1)} %get-tuple-element.65.refs_8_), channel_id=1, source_target_pairs={{0,8},{2,10},{4,12},{6,14},{8,16},{10,18},{12,20},{14,22},{16,24},... | collective-permute-start | bytes 98312 | tf_op jit(solution)/shard_map/ppermute | solution.py:37
  77.3 15.8 %collective-permute-start.13 = (f32[8,1024]{1,0:T(8,128)S(1)}, f32[8,1024]{1,0:T(8,128)S(1)}, u32[]{:S(2)}, u32[]{:S(2)}) collective-permute-start(f32[8,1024]{1,0:T(8,128)S(1)} %get-tuple-element.70.refs_8_), channel_id=1, source_target_pairs={{0,8},{2,10},{4,12},{6,14},{8,16},{10,18},{12,20},{14,22},{16,24},... | collective-permute-start | bytes 98312 | tf_op jit(solution)/shard_map/ppermute | solution.py:37
  78.3 14.7 %collective-permute-start.14 = (f32[8,1024]{1,0:T(8,128)S(1)}, f32[8,1024]{1,0:T(8,128)S(1)}, u32[]{:S(2)}, u32[]{:S(2)}) collective-permute-start(f32[8,1024]{1,0:T(8,128)S(1)} %get-tuple-element.68.refs_10_.refs_6_.refs_11_), channel_id=1, source_target_pairs={{0,24},{2,26},{4,28},{6,30},{8,0},{10,2},{12,4},{14,6},{16,8},{18,... | collective-permute-start | bytes 98312 | tf_op jit(solution)/shard_map/ppermute | solution.py:37
  91.5 13.4 %collective-permute-start.17 = (bf16[1024,256]{1,0:T(8,128)(2,1)S(1)}, bf16[1024,256]{1,0:T(8,128)(2,1)S(1)}, u32[]{:S(2)}, u32[]{:S(2)}) collective-permute-start(bf16[1024,256]{1,0:T(8,128)(2,1)S(1)} %get-tuple-element.77), channel_id=1, source_target_pairs={{8,0},{10,2},{12,4},{14,6},{16,8},{18,10},{20,12},{22,14},{24,16},... | collective-permute-start | bytes 1572872 | tf_op jit(solution)/shard_map/ppermute | solution.py:31
  93.1 11.9 %copy-start.5 = (bf16[256,2048]{1,0:T(8,128)(2,1)S(1)}, bf16[256,2048]{1,0:T(8,128)(2,1)}, u32[]{:S(2)}) copy-start(bf16[256,2048]{1,0:T(8,128)(2,1)} %copy-done.4) | copy-start | bytes 3145732
  102.4 5.6 %copy-start.7 = (f32[1024,256]{1,0:T(8,128)}, f32[1024,256]{1,0:T(8,128)S(1)}, u32[]{:S(2)}) copy-start(f32[1024,256]{1,0:T(8,128)S(1)} %get-tuple-element.74.refs_7_.refs_5_) | copy-start | bytes 3145732
  102.4 5.6 %copy-start.22 = (bf16[2,1024,128]{2,1,0:T(8,128)(2,1)}, bf16[2,1024,128]{2,1,0:T(8,128)(2,1)S(1)}, u32[]{:S(2)}) copy-start(bf16[2,1024,128]{2,1,0:T(8,128)(2,1)S(1)} %get-tuple-element.72.refs_2_) | copy-start | bytes 1572868
  109.6 49.7 %collective-permute-start.24 = (bf16[512,2048]{1,0:T(8,128)(2,1)}, bf16[512,2048]{1,0:T(8,128)(2,1)}, u32[]{:S(2)}, u32[]{:S(2)}) collective-permute-start(bf16[512,2048]{1,0:T(8,128)(2,1)} %get-tuple-element.94.refs_5_), channel_id=1, source_target_pairs={{0,2},{2,0},{4,6},{6,4},{8,10},{10,8},{12,14},{14,12},{16,18},{18,... | collective-permute-start | bytes 6291464 | tf_op jit(solution)/shard_map/ppermute | solution.py:24
  109.6 14.7 %collective-permute-start.19 = (bf16[4,256,256]{2,1,0:T(8,128)(2,1)}, bf16[4,256,256]{2,1,0:T(8,128)(2,1)}, u32[]{:S(2)}, u32[]{:S(2)}) collective-permute-start(bf16[4,256,256]{2,1,0:T(8,128)(2,1)} %get-tuple-element.83), channel_id=1, source_target_pairs={{0,1},{1,0},{2,3},{3,2},{4,5},{5,4},{6,7},{7,6},{8,9},{9,8},{10,11... | collective-permute-start | bytes 1572872 | tf_op jit(solution)/shard_map/ppermute | solution.py:51
  111.2 25.1 %collective-permute-start.15 = (bf16[2,1024,256]{2,1,0:T(8,128)(2,1)}, bf16[2,1024,256]{2,1,0:T(8,128)(2,1)}, u32[]{:S(2)}, u32[]{:S(2)}) collective-permute-start(bf16[2,1024,256]{2,1,0:T(8,128)(2,1)} %get-tuple-element.73), channel_id=1, source_target_pairs={{0,8},{2,10},{4,12},{6,14},{8,16},{10,18},{12,20},{14,22},{16,24},... | collective-permute-start | bytes 3145736 | tf_op jit(solution)/shard_map/ppermute | solution.py:31
  114.1 16.0 %collective-permute-start.16 = (bf16[1024,256]{1,0:T(8,128)(2,1)}, bf16[1024,256]{1,0:T(8,128)(2,1)}, u32[]{:S(2)}, u32[]{:S(2)}) collective-permute-start(bf16[1024,256]{1,0:T(8,128)(2,1)} %get-tuple-element.75), channel_id=1, source_target_pairs={{8,0},{10,2},{12,4},{14,6},{16,8},{18,10},{20,12},{22,14},{24,16},... | collective-permute-start | bytes 1572872 | tf_op jit(solution)/shard_map/ppermute | solution.py:31
  115.7 14.4 %copy-start.6 = (bf16[256,2048]{1,0:T(8,128)(2,1)S(1)}, bf16[256,2048]{1,0:T(8,128)(2,1)}, u32[]{:S(2)}) copy-start(bf16[256,2048]{1,0:T(8,128)(2,1)} %copy-done.4) | copy-start | bytes 3145732
  115.7 14.4 %copy-start.8 = (f32[1024,256]{1,0:T(8,128)S(1)}, f32[1024,256]{1,0:T(8,128)}, u32[]{:S(2)}) copy-start(f32[1024,256]{1,0:T(8,128)} %copy-done.7) | copy-start | bytes 3145732
  115.7 14.4 %copy-start.12 = (bf16[256,256]{1,0:T(8,128)(2,1)S(1)}, bf16[256,256]{1,0:T(8,128)(2,1)}, u32[]{:S(2)}) copy-start(bf16[256,256]{1,0:T(8,128)(2,1)} %copy-done.11) | copy-start | bytes 393220
  130.1 6.1 %copy-start.21 = (bf16[2,1024,128]{2,1,0:T(8,128)(2,1)S(1)}, bf16[2,1024,128]{2,1,0:T(8,128)(2,1)}, u32[]{:S(2)}) copy-start(bf16[2,1024,128]{2,1,0:T(8,128)(2,1)} %copy-done.20) | copy-start | bytes 1572868
  130.1 6.1 %copy-start.23 = (bf16[2,1024,128]{2,1,0:T(8,128)(2,1)S(1)}, bf16[2,1024,128]{2,1,0:T(8,128)(2,1)}, u32[]{:S(2)}) copy-start(bf16[2,1024,128]{2,1,0:T(8,128)(2,1)} %copy-done.22) | copy-start | bytes 1572868
  132.9 4.9 %collective-permute-start.22 = (bf16[2,256,512]{2,1,0:T(8,128)(2,1)S(1)}, bf16[2,256,512]{2,1,0:T(8,128)(2,1)S(1)}, u32[]{:S(2)}, u32[]{:S(2)}) collective-permute-start(bf16[2,256,512]{2,1,0:T(8,128)(2,1)S(1)} %get-tuple-element.92), channel_id=1, source_target_pairs={{0,2},{2,0},{4,6},{6,4},{8,10},{10,8},{12,14},{14,12},{16,18},{18,... | collective-permute-start | bytes 1572872 | tf_op jit(solution)/shard_map/ppermute | solution.py:24
  133.0 14.3 %collective-permute-start.25 = (bf16[4,256,256]{2,1,0:T(8,128)(2,1)S(1)}, bf16[4,256,256]{2,1,0:T(8,128)(2,1)S(1)}, u32[]{:S(2)}, u32[]{:S(2)}) collective-permute-start(bf16[4,256,256]{2,1,0:T(8,128)(2,1)S(1)} %get-tuple-element.85.refs_4_), channel_id=1, source_target_pairs={{0,1},{1,0},{2,3},{3,2},{4,5},{5,4},{6,7},{7,6},{8,9},{9,8},{10,11... | collective-permute-start | bytes 1572872 | tf_op jit(solution)/shard_map/ppermute | solution.py:51
  137.8 15.6 %collective-permute-start.20 = (bf16[2,2,256,256]{3,2,1,0:T(8,128)(2,1)S(1)}, bf16[2,2,256,256]{3,2,1,0:T(8,128)(2,1)S(1)}, u32[]{:S(2)}, u32[]{:S(2)}) collective-permute-start(bf16[2,2,256,256]{3,2,1,0:T(8,128)(2,1)S(1)} %get-tuple-element.87), channel_id=1, source_target_pairs={{0,2},{2,0},{4,6},{6,4},{8,10},{10,8},{12,14},{14,12},{16,18},{18,... | collective-permute-start | bytes 1572872 | tf_op jit(solution)/shard_map/ppermute | solution.py:24
  138.4 20.3 %collective-permute-start.23 = (bf16[2,256,512]{2,1,0:T(8,128)(2,1)S(1)}, bf16[2,256,512]{2,1,0:T(8,128)(2,1)S(1)}, u32[]{:S(2)}, u32[]{:S(2)}) collective-permute-start(bf16[2,256,512]{2,1,0:T(8,128)(2,1)S(1)} %mix.3), channel_id=1, source_target_pairs={{0,4},{2,6},{4,0},{6,2},{8,12},{10,14},{12,8},{14,10},{16,20},{18,... | collective-permute-start | bytes 1572872 | tf_op jit(solution)/shard_map/ppermute | solution.py:24
  140.1 9.2 %collective-permute-start.27 = (bf16[2,256,256]{2,1,0:T(8,128)(2,1)S(1)}, bf16[2,256,256]{2,1,0:T(8,128)(2,1)S(1)}, u32[]{:S(2)}, u32[]{:S(2)}) collective-permute-start(bf16[2,256,256]{2,1,0:T(8,128)(2,1)S(1)} %get-tuple-element.84.refs_10_), channel_id=1, source_target_pairs={{0,8},{1,9},{2,10},{3,11},{4,12},{5,13},{6,14},{7,15},{8,0},{9,1},... | collective-permute-start | bytes 786440 | tf_op jit(solution)/shard_map/ppermute | solution.py:47
  147.9 10.7 %collective-permute-start.26 = (bf16[2,256,256]{2,1,0:T(8,128)(2,1)S(1)}, bf16[2,256,256]{2,1,0:T(8,128)(2,1)S(1)}, u32[]{:S(2)}, u32[]{:S(2)}) collective-permute-start(bf16[2,256,256]{2,1,0:T(8,128)(2,1)S(1)} %get-tuple-element.97), channel_id=1, source_target_pairs={{0,8},{1,9},{2,10},{3,11},{4,12},{5,13},{6,14},{7,15},{8,0},{9,1},... | collective-permute-start | bytes 786440 | tf_op jit(solution)/shard_map/ppermute | solution.py:47
  149.8 16.5 %collective-permute-start.28 = (bf16[1,256,256]{2,1,0:T(8,128)(2,1)S(1)}, bf16[1,256,256]{2,1,0:T(8,128)(2,1)S(1)}, u32[]{:S(2)}, u32[]{:S(2)}) collective-permute-start(bf16[1,256,256]{2,1,0:T(8,128)(2,1)S(1)} %get-tuple-element.102), channel_id=1, source_target_pairs={{0,16},{1,17},{2,18},{3,19},{4,20},{5,21},{6,22},{7,23},{8,24},{9,... | collective-permute-start | bytes 393224 | tf_op jit(solution)/shard_map/ppermute | solution.py:47
  153.4 6.0 %copy-start.2 = (bf16[1024,2048]{1,0:T(8,128)(2,1)S(1)}, bf16[1024,2048]{1,0:T(8,128)(2,1)}, u32[]{:S(2)}) copy-start(bf16[1024,2048]{1,0:T(8,128)(2,1)} %refs_4_.1) | copy-start | bytes 12582916
  153.9 14.9 %collective-permute-start.21 = (bf16[2,2,256,256]{3,2,1,0:T(8,128)(2,1)S(1)}, bf16[2,2,256,256]{3,2,1,0:T(8,128)(2,1)S(1)}, u32[]{:S(2)}, u32[]{:S(2)}) collective-permute-start(bf16[2,2,256,256]{3,2,1,0:T(8,128)(2,1)S(1)} %mix.2), channel_id=1, source_target_pairs={{0,4},{2,6},{4,0},{6,2},{8,12},{10,14},{12,8},{14,10},{16,20},{18,... | collective-permute-start | bytes 1572872 | tf_op jit(solution)/shard_map/ppermute | solution.py:24
  159.3 7.0 %collective-permute-start.29 = (bf16[1,256,256]{2,1,0:T(8,128)(2,1)S(1)}, bf16[1,256,256]{2,1,0:T(8,128)(2,1)S(1)}, u32[]{:S(2)}, u32[]{:S(2)}) collective-permute-start(bf16[1,256,256]{2,1,0:T(8,128)(2,1)S(1)} %get-tuple-element.98.refs_7_), channel_id=1, source_target_pairs={{0,16},{1,17},{2,18},{3,19},{4,20},{5,21},{6,22},{7,23},{8,24},{9,... | collective-permute-start | bytes 393224 | tf_op jit(solution)/shard_map/ppermute | solution.py:47
  166.9 3.6 %collective-permute-start.30 = (f32[64,512]{1,0:T(8,128)S(1)}, f32[64,512]{1,0:T(8,128)S(1)}, u32[]{:S(2)}, u32[]{:S(2)}) collective-permute-start(f32[64,512]{1,0:T(8,128)S(1)} %get-tuple-element.106), channel_id=1, source_target_pairs={{0,2},{2,0},{4,6},{6,4},{8,10},{10,8},{12,14},{14,12},{16,18},{18,... | collective-permute-start | bytes 393224 | tf_op jit(solution)/shard_map/ppermute | solution.py:24
  167.0 6.4 %collective-permute-start.31 = (f32[64,512]{1,0:T(8,128)S(1)}, f32[64,512]{1,0:T(8,128)S(1)}, u32[]{:S(2)}, u32[]{:S(2)}) collective-permute-start(f32[64,512]{1,0:T(8,128)S(1)} %get-tuple-element.107), channel_id=1, source_target_pairs={{0,4},{2,6},{4,0},{6,2},{8,12},{10,14},{12,8},{14,10},{16,20},{18,... | collective-permute-start | bytes 393224 | tf_op jit(solution)/shard_map/ppermute | solution.py:24
  168.6 6.6 %collective-permute-start.32 = (f32[64,512]{1,0:T(8,128)S(1)}, f32[64,512]{1,0:T(8,128)S(1)}, u32[]{:S(2)}, u32[]{:S(2)}) collective-permute-start(f32[64,512]{1,0:T(8,128)S(1)} %get-tuple-element.108), channel_id=1, source_target_pairs={{0,6},{2,4},{4,2},{6,0},{8,14},{10,12},{12,10},{14,8},{16,22},{18,... | collective-permute-start | bytes 393224 | tf_op jit(solution)/shard_map/ppermute | solution.py:24
  (9 other events, 10.1 us)
